TPU v7x, 32 devices: a whole 2x2x4 slice. The times are simulated.
32 devices in a mesh: dp: 4 (over z), op: 8 (over y, x, core).
Axes of the slice: x: 2, y: 2, z: 4, core: 2. Of those that a mesh axis runs over, the one named last changes fastest.
Arguments:
- inputs: bfloat16 [384, 512, 768], P(('dp', 'op')), may hold values from -6 to 6
- candidate: int32 [384, 2], P(('dp', 'op')), may hold values from 0 to 39, as said below
- attn_qkv: bfloat16 [2, 8, 768, 2304], P(None, 'op'), may hold values from -0.21875 to 0.21875
- attn_out: bfloat16 [2, 8, 768, 768], P(None, 'op'), may hold values from -2.5 to 2.5
- ffn_up: bfloat16 [2, 8, 768, 3072], P(None, 'op'), may hold values from -0.21875 to 0.21875
- ffn_down: bfloat16 [2, 8, 3072, 768], P(None, 'op'), may hold values from -0.109375 to 0.109375
- conv_taps: bfloat16 [2, 8, 15, 768], P(None, 'op'), may hold values from -2.5 to 2.5
- conv_point: bfloat16 [2, 8, 3, 768, 768], P(None, 'op'), may hold values from -0.21875 to 0.21875
- norm_gain: bfloat16 [2, 8, 5, 768], P(None, 'op'), may hold values from 0.5 to 1.5
- norm_bias: bfloat16 [2, 8, 5, 768], P(None, 'op'), may hold values from -2.5 to 2.5
- cotangent: bfloat16 [384, 512, 768], P(('dp', 'op')), may hold values from -6 to 6
Outputs:
- outputs: bfloat16 [384, 512, 768], P(('dp', 'op'))
- input_grad: bfloat16 [384, 512, 768], P(('dp', 'op'))
- attn_qkv_grad: float32 [2, 8, 768, 2304], P(None, 'op', 'dp')
- attn_out_grad: float32 [2, 8, 768, 768], P(None, 'op', 'dp')
- ffn_up_grad: float32 [2, 8, 768, 3072], P(None, 'op', 'dp')
- ffn_down_grad: float32 [2, 8, 3072, 768], P(None, 'op', 'dp')
- conv_taps_grad: float32 [2, 8, 15, 768], P(None, 'op', None, 'dp')
- conv_point_grad: float32 [2, 8, 3, 768, 768], P(None, 'op', None, 'dp')
- norm_gain_grad: float32 [2, 8, 5, 768], P(None, 'op', None, 'dp')
- norm_bias_grad: float32 [2, 8, 5, 768], P(None, 'op', None, 'dp')
Inputs may be any that keep to these rules, and one draw needn't show every extreme that they name: candidate[n, b] = k * 8 + owner. In each block the 12 sequences of one device go at most 2 to one owner, and some owner gets exactly 2 of them; every owner receives exactly 12 sequences a block from the devices of its dp group, each of its 5 candidates between 1 and 3 of them, one candidate exactly 3.
All inputs are finite; a program needn't handle non-finite values.
Results may differ from a plain program's by a relative error of at most 0.015.
Values may be sent and summed in bfloat16 or wider, within the bound.
No kernel may reach another device: no remote copies, remote signals or barrier semaphores. Data moves between devices by JAX's collectives and lax.ppermute only.
A program may use at most 704 MiB of HBM per device.

v0:
```python
import jax
import jax.numpy as jnp
from jax import lax
from jax.sharding import PartitionSpec as P

HEADS = 12
KINDS = 5
BLOCKS = 2
OWN_CAP = 3


def layer_norm(summed, gain_row, norm_shift):
    center = summed - jnp.mean(summed, axis=-1, keepdims=True)
    spread = jnp.mean(center * center, axis=-1, keepdims=True)
    return center * lax.rsqrt(spread + 1e-05) * gain_row + norm_shift


def gelu_exact(values):
    return jax.nn.gelu(values, approximate=False)


def matrix_product(operand_a, operand_b, einsum_form):
    return jnp.einsum(einsum_form, operand_a, operand_b, preferred_element_type=jnp.float32)


def take_rows(source_rows, row_ids, present):
    return jnp.where(present[:, None, None], source_rows[row_ids], jnp.zeros((), source_rows.dtype))


def plan_route(chosen, owner_count, peer_cap):
    seq_count = chosen.shape[0]
    owner_of = chosen % owner_count
    kind_of = chosen // owner_count
    seq_ids = jnp.arange(seq_count, dtype=jnp.int32)
    earlier = (owner_of[None, :] == owner_of[:, None]) & (seq_ids[None, :] < seq_ids[:, None])
    position = owner_of * peer_cap + jnp.sum(earlier, axis=1)
    send_ids = jnp.arange(owner_count * peer_cap, dtype=jnp.int32)
    matches = position[None, :] == send_ids[:, None]
    source = jnp.sum(jnp.where(matches, seq_ids[None, :], 0), axis=1)
    filled = jnp.any(matches, axis=1)
    kind_tags = jnp.where(filled, kind_of[source], KINDS)
    return (position, source, filled, kind_tags)


def owner_slots(arrived_kinds):
    row_ids = jnp.arange(arrived_kinds.shape[0], dtype=jnp.int32)
    earlier = (arrived_kinds[None, :] == arrived_kinds[:, None]) & (
        row_ids[None, :] < row_ids[:, None]
    )
    slot_of = (arrived_kinds * OWN_CAP + jnp.sum(earlier, axis=1)).astype(jnp.int32)
    wanted = jnp.arange(KINDS * OWN_CAP, dtype=jnp.int32)
    matches = slot_of[None, :] == wanted[:, None]
    picked = jnp.sum(jnp.where(matches, row_ids[None, :], 0), axis=1)
    present = jnp.any(matches, axis=1)
    return (jnp.minimum(slot_of, KINDS * OWN_CAP - 1), picked, present)


def attention_parts(block_activation, query_key_value_weight):
    packed_rows = matrix_product(block_activation, query_key_value_weight, "wtz,zk->wtk").astype(
        jnp.bfloat16
    )
    seq_count, length, triple = packed_rows.shape
    head_size = triple // (3 * HEADS)
    split_heads = packed_rows.reshape(seq_count, length, 3, HEADS, head_size)
    queries = split_heads[:, :, 0]
    key_rows = split_heads[:, :, 1]
    values = split_heads[:, :, 2]
    scores = matrix_product(queries, key_rows, "sqhe,skhe->shqk") * head_size ** (-0.5)
    row_max = jnp.max(scores, axis=-1, keepdims=True)
    exponent = jnp.exp(scores - row_max)
    attn_probs = exponent / jnp.sum(exponent, axis=-1, keepdims=True)
    probs_low = attn_probs.astype(jnp.bfloat16)
    attention_result = (
        matrix_product(probs_low, values, "shqk,skhe->sqhe")
        .reshape(seq_count, length, triple // 3)
        .astype(jnp.bfloat16)
    )
    return (queries, key_rows, values, attn_probs, probs_low, attention_result)


def attention_back(
    block_activation, query_key_value_weight, output_weight, stored_pieces, branch_gradient
):
    queries, key_rows, values, attn_probs, probs_low, attention_result = stored_pieces
    seq_count, length, model_width = attention_result.shape
    score_scale = (model_width // HEADS) ** (-0.5)
    output_weight_gradient = matrix_product(attention_result, branch_gradient, "uxv,uxm->vm")
    mixed_gradient = (
        matrix_product(branch_gradient, output_weight, "ujt,at->uja")
        .astype(jnp.bfloat16)
        .reshape(seq_count, length, HEADS, -1)
    )
    grad_values = matrix_product(probs_low, mixed_gradient, "shqk,sqhe->skhe").astype(jnp.bfloat16)
    grad_probs = matrix_product(mixed_gradient, values, "sqhe,skhe->shqk")
    grad_scores = (
        attn_probs * (grad_probs - jnp.sum(attn_probs * grad_probs, axis=-1, keepdims=True))
    ).astype(jnp.bfloat16)
    grad_queries = (matrix_product(grad_scores, key_rows, "shqk,skhe->sqhe") * score_scale).astype(
        jnp.bfloat16
    )
    grad_keys = (matrix_product(grad_scores, queries, "shqk,sqhe->skhe") * score_scale).astype(
        jnp.bfloat16
    )
    packed_gradient = jnp.stack([grad_queries, grad_keys, grad_values], axis=2).reshape(
        seq_count, length, 3 * model_width
    )
    query_key_value_weight_gradient = matrix_product(
        block_activation, packed_gradient, "uxv,uxm->vm"
    )
    input_gradient_rows = matrix_product(packed_gradient, query_key_value_weight, "ujt,at->uja")
    return (input_gradient_rows, (query_key_value_weight_gradient, output_weight_gradient))


def conv_parts(block_activation, tap_rows):
    tap_count = tap_rows.shape[0]
    half_width = tap_count // 2
    length = block_activation.shape[1]
    padded = jnp.pad(
        block_activation.astype(jnp.float32), ((0, 0), (half_width, half_width), (0, 0))
    )
    mixed = jnp.zeros(block_activation.shape, jnp.float32)
    for offset in range(tap_count):
        mixed = mixed + padded[:, offset : offset + length] * tap_rows[offset].astype(jnp.float32)
    return (padded, mixed.astype(jnp.bfloat16))


def conv_back(tap_rows, pointwise_weight, stored_pieces, branch_gradient):
    padded, mixed_reduced = stored_pieces
    tap_count = tap_rows.shape[0]
    half_width = tap_count // 2
    length = branch_gradient.shape[1]
    pointwise_weight_gradient = matrix_product(mixed_reduced, branch_gradient, "uxv,uxm->vm")
    mixed_gradient = matrix_product(branch_gradient, pointwise_weight, "ujt,at->uja")
    grad_taps = jnp.stack(
        [
            jnp.sum(padded[:, offset : offset + length] * mixed_gradient, axis=(0, 1))
            for offset in range(tap_count)
        ]
    )
    grad_padded = jnp.pad(mixed_gradient, ((0, 0), (half_width, half_width), (0, 0)))
    input_gradient_rows = jnp.zeros(mixed_gradient.shape, jnp.float32)
    for offset in range(tap_count):
        start_row = tap_count - 1 - offset
        input_gradient_rows = input_gradient_rows + grad_padded[
            :, start_row : start_row + length
        ] * tap_rows[offset].astype(jnp.float32)
    return (input_gradient_rows, (grad_taps, pointwise_weight_gradient))


def kind_forward(block_activation, kind_number, params):
    (
        query_key_value_weight,
        output_weight,
        up_weight,
        down_weight,
        tap_rows,
        pointwise_weight,
        norm_gains,
        norm_shifts,
    ) = params
    if kind_number == 0:
        stored_pieces = attention_parts(block_activation, query_key_value_weight)
        return (matrix_product(stored_pieces[5], output_weight, "wtz,zk->wtk"), stored_pieces)
    if kind_number == KINDS - 1:
        hidden_activation = matrix_product(block_activation, up_weight, "hnw,wk->hnk")
        active, gelu_derivative = jax.vjp(gelu_exact, hidden_activation)
        active_reduced = active.astype(jnp.bfloat16)
        return (
            matrix_product(active_reduced, down_weight, "knj,jh->knh"),
            (gelu_derivative, active_reduced),
        )
    first_row = kind_number * kind_number - 1
    stored_pieces = conv_parts(
        block_activation, tap_rows[first_row : first_row + 2 * kind_number + 1]
    )
    return (
        matrix_product(stored_pieces[1], pointwise_weight[kind_number - 1], "wtz,zk->wtk"),
        stored_pieces,
    )


def kind_backward(block_activation, kind_number, params, stored_pieces, branch_gradient):
    (
        query_key_value_weight,
        output_weight,
        up_weight,
        down_weight,
        tap_rows,
        pointwise_weight,
        norm_gains,
        norm_shifts,
    ) = params
    if kind_number == 0:
        return attention_back(
            block_activation, query_key_value_weight, output_weight, stored_pieces, branch_gradient
        )
    if kind_number == KINDS - 1:
        gelu_derivative, active_reduced = stored_pieces
        down_weight_gradient = matrix_product(active_reduced, branch_gradient, "vry,vrw->yw")
        active_gradient = matrix_product(branch_gradient, down_weight, "oyg,hg->oyh")
        hidden_gradient = gelu_derivative(active_gradient)[0].astype(jnp.bfloat16)
        up_weight_gradient = matrix_product(block_activation, hidden_gradient, "kye,kyg->eg")
        return (
            matrix_product(hidden_gradient, up_weight, "ayi,hi->ayh"),
            (up_weight_gradient, down_weight_gradient),
        )
    first_row = kind_number * kind_number - 1
    return conv_back(
        tap_rows[first_row : first_row + 2 * kind_number + 1],
        pointwise_weight[kind_number - 1],
        stored_pieces,
        branch_gradient,
    )


def owner_forward(owner_x, params):
    norm_gains, norm_shifts = (params[6], params[7])
    per_kind = owner_x.shape[0] // KINDS
    results = []
    for kind_number in range(KINDS):
        block_activation = owner_x[kind_number * per_kind : (kind_number + 1) * per_kind]
        branch = kind_forward(block_activation, kind_number, params)[0]
        summed = block_activation.astype(jnp.float32) + branch
        normed = layer_norm(
            summed,
            norm_gains[kind_number].astype(jnp.float32),
            norm_shifts[kind_number].astype(jnp.float32),
        )
        results.append(normed.astype(jnp.bfloat16))
    return jnp.concatenate(results, axis=0)


def owner_backward(owner_x, owner_grad, params):
    norm_gains, norm_shifts = (params[6], params[7])
    per_kind = owner_x.shape[0] // KINDS
    grad_rows = []
    kind_grads = []
    gain_grads = []
    shift_grads = []
    for kind_number in range(KINDS):
        block_activation = owner_x[kind_number * per_kind : (kind_number + 1) * per_kind]
        branch, stored_pieces = kind_forward(block_activation, kind_number, params)
        summed = block_activation.astype(jnp.float32) + branch
        normed, norm_back = jax.vjp(
            layer_norm,
            summed,
            norm_gains[kind_number].astype(jnp.float32),
            norm_shifts[kind_number].astype(jnp.float32),
        )
        grad_sum, grad_gain, grad_shift = norm_back(
            owner_grad[kind_number * per_kind : (kind_number + 1) * per_kind].astype(jnp.float32)
        )
        grad_branch_x, grad_set = kind_backward(
            block_activation, kind_number, params, stored_pieces, grad_sum.astype(jnp.bfloat16)
        )
        grad_rows.append((grad_sum + grad_branch_x).astype(jnp.bfloat16))
        kind_grads.append(grad_set)
        gain_grads.append(grad_gain)
        shift_grads.append(grad_shift)
    grad_taps = jnp.concatenate(
        [kind_grads[kind_number][0] for kind_number in range(1, KINDS - 1)], axis=0
    )
    pointwise_weight_gradient = jnp.stack(
        [kind_grads[kind_number][1] for kind_number in range(1, KINDS - 1)]
    )
    grad_set = (
        kind_grads[0][0],
        kind_grads[0][1],
        kind_grads[KINDS - 1][0],
        kind_grads[KINDS - 1][1],
        grad_taps,
        pointwise_weight_gradient,
        jnp.stack(gain_grads),
        jnp.stack(shift_grads),
    )
    return (jnp.concatenate(grad_rows, axis=0), grad_set)


def scale_grads(shares, totals):
    (
        query_key_value_weight_gradient,
        output_weight_gradient,
        up_weight_gradient,
        down_weight_gradient,
        grad_taps,
        pointwise_weight_gradient,
        grad_gains,
        grad_shifts,
    ) = shares
    tap_scale = jnp.concatenate(
        [
            jnp.ones((2 * kind_number + 1,), jnp.float32) * totals[kind_number]
            for kind_number in range(1, KINDS - 1)
        ]
    )
    return (
        query_key_value_weight_gradient / totals[0],
        output_weight_gradient / totals[0],
        up_weight_gradient / totals[KINDS - 1],
        down_weight_gradient / totals[KINDS - 1],
        grad_taps / tap_scale[:, None],
        pointwise_weight_gradient / totals[1 : KINDS - 1][:, None, None],
        grad_gains / totals[:, None],
        grad_shifts / totals[:, None],
    )


def per_device(
    inputs,
    candidate,
    attn_qkv,
    attn_out,
    ffn_up,
    ffn_down,
    conv_taps,
    conv_point,
    norm_gain,
    norm_bias,
    cotangent,
):
    owner_count = lax.axis_size("op")
    peer_cap = -(-inputs.shape[0] // owner_count)
    weights = (attn_qkv, attn_out, ffn_up, ffn_down, conv_taps, conv_point, norm_gain, norm_bias)
    block_inputs = []
    route_plans = []
    kept_owner = []
    tallies = []
    current = inputs
    for block_no in range(BLOCKS):
        params = tuple((stacked[block_no, 0] for stacked in weights))
        position, source, filled, kind_tags = plan_route(
            candidate[:, block_no], owner_count, peer_cap
        )
        outgoing = take_rows(current, source, filled)
        arrived, arrived_kinds = (
            lax.all_to_all(outgoing, "op", split_axis=0, concat_axis=0, tiled=True),
            lax.all_to_all(kind_tags, "op", split_axis=0, concat_axis=0, tiled=True),
        )
        slot_of, picked, present = owner_slots(arrived_kinds)
        owner_x = take_rows(arrived, picked, present)
        owner_y = owner_forward(owner_x, params)
        returned = lax.all_to_all(owner_y[slot_of], "op", split_axis=0, concat_axis=0, tiled=True)
        block_inputs.append(current)
        route_plans.append((position, source, filled, kind_tags))
        kept_owner.append((owner_x, slot_of, picked, present))
        tallies.append(jnp.sum(present.reshape(KINDS, OWN_CAP).astype(jnp.float32), axis=1))
        current = returned[position]
    totals = lax.psum(jnp.stack(tallies), "dp")
    grad_state = cotangent
    block_grads = [None, None]
    for block_no in reversed(range(BLOCKS)):
        params = tuple((stacked[block_no, 0] for stacked in weights))
        position, source, filled, kind_tags = route_plans[block_no]
        outgoing = take_rows(grad_state, source, filled)
        resent = take_rows(block_inputs[block_no], source, filled)
        arrived_grad, arrived_x, arrived_kinds = (
            lax.all_to_all(outgoing, "op", split_axis=0, concat_axis=0, tiled=True),
            lax.all_to_all(resent, "op", split_axis=0, concat_axis=0, tiled=True),
            lax.all_to_all(kind_tags, "op", split_axis=0, concat_axis=0, tiled=True),
        )
        slot_of, picked, present = owner_slots(arrived_kinds)
        owner_x = take_rows(arrived_x, picked, present)
        owner_grad = take_rows(arrived_grad, picked, present)
        owner_dx, grad_set = owner_backward(owner_x, owner_grad, params)
        returned = lax.all_to_all(owner_dx[slot_of], "op", split_axis=0, concat_axis=0, tiled=True)
        grad_state = returned[position]
        block_grads[block_no] = grad_set
    stacked_qkv = jnp.stack([block_grads[0][0], block_grads[1][0]])
    stacked_out = jnp.stack([block_grads[0][1], block_grads[1][1]])
    stacked_up = jnp.stack([block_grads[0][2], block_grads[1][2]])
    stacked_down = jnp.stack([block_grads[0][3], block_grads[1][3]])
    stacked_taps = jnp.stack([block_grads[0][4], block_grads[1][4]])
    stacked_point = jnp.stack([block_grads[0][5], block_grads[1][5]])
    stacked_gains = jnp.stack([block_grads[0][6], block_grads[1][6]])
    stacked_shifts = jnp.stack([block_grads[0][7], block_grads[1][7]])
    summed = (
        lax.psum_scatter(
            stacked_qkv.astype(jnp.bfloat16), "dp", scatter_dimension=1, tiled=True
        ).astype(jnp.float32),
        lax.psum_scatter(
            stacked_out.astype(jnp.bfloat16), "dp", scatter_dimension=1, tiled=True
        ).astype(jnp.float32),
        lax.psum_scatter(
            stacked_up.astype(jnp.bfloat16), "dp", scatter_dimension=1, tiled=True
        ).astype(jnp.float32),
        lax.psum_scatter(
            stacked_down.astype(jnp.bfloat16), "dp", scatter_dimension=1, tiled=True
        ).astype(jnp.float32),
        lax.psum_scatter(
            stacked_taps.astype(jnp.bfloat16), "dp", scatter_dimension=2, tiled=True
        ).astype(jnp.float32),
        lax.psum_scatter(
            stacked_point.astype(jnp.bfloat16), "dp", scatter_dimension=2, tiled=True
        ).astype(jnp.float32),
        lax.psum_scatter(
            stacked_gains.astype(jnp.bfloat16), "dp", scatter_dimension=2, tiled=True
        ).astype(jnp.float32),
        lax.psum_scatter(
            stacked_shifts.astype(jnp.bfloat16), "dp", scatter_dimension=2, tiled=True
        ).astype(jnp.float32),
    )
    finished = [
        scale_grads(tuple((member[block_no] for member in summed)), totals[block_no])
        for block_no in range(BLOCKS)
    ]
    grad_outputs = tuple(
        (
            jnp.stack([finished[0][index_no], finished[1][index_no]])[:, None]
            for index_no in range(8)
        )
    )
    return (current, grad_state) + grad_outputs


def solution(mesh):
    placed = (
        P(("dp", "op"), None, None),
        P(("dp", "op"), None),
        P(None, "op", None, None),
        P(None, "op", None, None),
        P(None, "op", None, None),
        P(None, "op", None, None),
        P(None, "op", None, None),
        P(None, "op", None, None, None),
        P(None, "op", None, None),
        P(None, "op", None, None),
        P(("dp", "op"), None, None),
    )
    return jax.shard_map(
        per_device,
        mesh=mesh,
        in_specs=placed,
        out_specs=(
            P(("dp", "op"), None, None),
            P(("dp", "op"), None, None),
            P(None, "op", "dp", None),
            P(None, "op", "dp", None),
            P(None, "op", "dp", None),
            P(None, "op", "dp", None),
            P(None, "op", None, "dp"),
            P(None, "op", None, "dp", None),
            P(None, "op", None, "dp"),
            P(None, "op", None, "dp"),
        ),
        check_vma=False,
    )
```

profile of v0, /device:TPU:0, one launch (start us, length us, event | category | flops | bytes accessed | tf_op | source)
XLA Modules:
  0.0 2501.3 jit_solution(14049616177243368878)
XLA Ops:
  32.5 10.8 broadcast_select_fusion.1
  55.1 133.1 %all-to-all-done.2 = bf16[16,512,768]{2,1,0:T(8,128)(2,1)} async-done(((bf16[16,512,768]{2,1,0:T(8,128)(2,1)}), bf16[16,512,768]{2,1,0:T(8,128)(2,1)}, u32[]{:S(2)}, u32[]{:S(2)}) %all-to-all-start.2) | async-done | bytes 12582944 | tf_op jit(solution)/shard_map/all_to_all | solution.py:336
  188.3 10.7 gather_fusion.3
  223.4 10.3 copy.206
  271.1 19.8 fusion.98
  290.9 44.9 %multiply_convert_fusion.3 = (bf16[3,512,3072]{2,1,0:T(8,128)(2,1)S(1)}, f32[3,512,3072]{2,1,0:T(8,128)}) fusion(f32[3,512,3072]{2,1,0:T(8,128)} %get-tuple-element.311, u8[512,3072]{1,0:T(8,128)(4,1)S(1)} %get-tuple-element.63, u8[512,3072]{1,0:T(8,128)(4,1)S(1)} %get-tuple-element.62), kind=kLoop, calls=%fused_computation.59 | loop fusion | flops 330301440 | bytes 50331648 | tf_op jit(solution)/shard_map/convert_element_type | solution.py:167
  335.8 15.3 fusion.270
  354.5 19.5 fusion.265
  374.0 15.8 fusion.154
  409.0 10.9 gather_fusion.4
  435.4 128.8 %all-to-all-done.3 = bf16[16,512,768]{2,1,0:T(8,128)(2,1)} async-done(((bf16[16,512,768]{2,1,0:T(8,128)(2,1)}), bf16[16,512,768]{2,1,0:T(8,128)(2,1)}, u32[]{:S(2)}, u32[]{:S(2)}) %all-to-all-start.3) | async-done | bytes 12582944 | tf_op jit(solution)/shard_map/all_to_all | solution.py:342
  584.7 13.7 broadcast_select_fusion.2
  598.4 142.6 %all_to_all.62 = bf16[16,512,768]{2,1,0:T(8,128)(2,1)} all-to-all(bf16[16,512,768]{2,1,0:T(8,128)(2,1)S(1)} %get-tuple-element.299), channel_id=1, replica_groups=mesh['dp'=4,'op'=8] {'op'}, dimensions={0} | all-to-all | bytes 25165824 | tf_op jit(solution)/shard_map/all_to_all | solution.py:357
  747.8 10.8 gather_fusion.11
  758.6 127.0 %all-to-all-done.4 = bf16[16,512,768]{2,1,0:T(8,128)(2,1)} async-done(((bf16[16,512,768]{2,1,0:T(8,128)(2,1)}), bf16[16,512,768]{2,1,0:T(8,128)(2,1)}, u32[]{:S(2)}, u32[]{:S(2)}) %all-to-all-start.4) | async-done | bytes 12582944 | tf_op jit(solution)/shard_map/all_to_all | solution.py:336
  885.6 10.8 gather_fusion.7
  896.4 12.9 broadcast_select_fusion.6
  909.2 12.3 convolution_convert_fusion
  926.9 21.0 fusion.99
  975.5 14.3 add_convert_fusion.14
  1004.5 45.3 %multiply_convert_fusion.2 = (bf16[3,512,3072]{2,1,0:T(8,128)(2,1)S(1)}, f32[3,512,3072]{2,1,0:T(8,128)}) fusion(f32[3,512,3072]{2,1,0:T(8,128)} %get-tuple-element.314, u8[512,3072]{1,0:T(8,128)(4,1)S(1)} %copy-done.27, u8[512,3072]{1,0:T(8,128)(4,1)S(1)} %copy-done.26), kind=kLoop, calls=%fused_computation.45 | loop fusion | flops 330301440 | bytes 50331648 | tf_op jit(solution)/shard_map/convert_element_type | solution.py:167
  1049.8 15.1 fusion.271
  1065.0 18.9 fusion.274
  1083.9 15.9 fusion.159
  1105.1 11.0 fusion.59
  1136.4 14.6 convert_bitcast_fusion.1
  1151.0 25.4 %multiply_reduce_fusion.1 = (f32[3,12,512]{2,1,0:T(8,128)S(1)}, f32[3,12,512,512]{2,3,1,0:T(8,128)}) fusion(f32[3,12,512,512]{2,3,1,0:T(8,128)} %get-tuple-element.322, f32[3,12,512]{2,1,0:T(8,128)S(1)} %get-tuple-element.321, bf16[3,512,12,64]{1,3,2,0:T(8,128)(2,1)} %bitcast.587, bf16[3,512,3,12,64]{1,4,3,2,0:T(8,128)(2,1)} %bitcast.569), kind=kOutput, calls=%fused_computation.23 | convolution fusion | flops 1236252672 | bytes 80363520 | tf_op jit(solution)/shard_map/sqhe,skhe->shqk/dot_general | solution.py:23
  1176.4 31.3 %multiply_convert_fusion.1 = bf16[3,12,512,512]{2,3,1,0:T(8,128)(2,1)} fusion(f32[3,12,512,512]{2,3,1,0:T(8,128)} %get-tuple-element.328, f32[3,12,512]{2,1,0:T(8,128)S(1)} %get-tuple-element.327, f32[3,12,512,512]{2,3,1,0:T(8,128)} %get-tuple-element.322, f32[3,12,512]{2,1,0:T(8,128)S(1)} %get-tuple-element.321), kind=kLoop, calls=%fused_computation.22 | loop fusion | flops 37748736 | bytes 94519296 | tf_op jit(solution)/shard_map/convert_element_type | solution.py:97
  1207.7 10.5 fusion.135
  1218.3 10.4 fusion.134
  1258.2 12.1 fusion.136
  1270.4 24.6 add_convert_fusion.1
  1295.1 31.1 %multiply_reduce_fusion.4 = (bf16[768]{0:T(1024)(128)(2,1)S(1)}, bf16[768]{0:T(1024)(128)(2,1)S(1)}, bf16[768]{0:T(1024)(128)(2,1)S(1)}, bf16[768]{0:T(1024)(128...) fusion(f32[3,512,768]{2,1,0:T(8,128)} %get-tuple-element.240, ...), kind=kOutput, calls=%fused_computation.193 | convolution fusion | flops 1861473024 | bytes 43697664 | tf_op jit(solution)/shard_map/ujt,at->uja/dot_general | solution.py:23
  1326.4 12.7 fusion.137
  1339.2 17.9 fusion.138
  1366.5 13.2 fusion.140
  1379.7 10.8 gather_fusion.12
  1396.0 139.0 %all-to-all-done.7 = bf16[16,512,768]{2,1,0:T(8,128)(2,1)} async-done(((bf16[16,512,768]{2,1,0:T(8,128)(2,1)}), bf16[16,512,768]{2,1,0:T(8,128)(2,1)}, u32[]{:S(2)}, u32[]{:S(2)}) %all-to-all-start.7) | async-done | bytes 12582944 | tf_op jit(solution)/shard_map/all_to_all | solution.py:365
  1555.4 10.8 broadcast_select_fusion
  1605.2 105.6 %all-to-all-done.8 = bf16[16,512,768]{2,1,0:T(8,128)(2,1)} async-done(((bf16[16,512,768]{2,1,0:T(8,128)(2,1)}), bf16[16,512,768]{2,1,0:T(8,128)(2,1)}, u32[]{:S(2)}, u32[]{:S(2)}) %all-to-all-start.8) | async-done | bytes 12582944 | tf_op jit(solution)/shard_map/all_to_all | solution.py:357
  1710.8 11.5 gather_fusion.15
  1780.4 34.3 %multiply_reduce_fusion.19 = (bf16[768]{0:T(1024)(128)(2,1)S(1)}, bf16[768]{0:T(1024)(128)(2,1)S(1)}, bf16[768]{0:T(1024)(128)(2,1)S(1)}, bf16[768]{0:T(1024)(12...) fusion(f32[3,512,768]{2,1,0:T(8,128)} %get-tuple-element.242, ...), kind=kOutput, calls=%fused_computation.208 | convolution fusion | flops 1861473024 | bytes 43697664 | tf_op jit(solution)/shard_map/ujt,at->uja/dot_general | solution.py:23
  1863.3 25.8 %multiply_reduce_fusion = (f32[3,12,512]{2,1,0:T(8,128)S(1)}, f32[3,12,512,512]{2,3,1,0:T(8,128)}) fusion(f32[3,12,512,512]{2,3,1,0:T(8,128)} %get-tuple-element.302, f32[3,12,512]{2,1,0:T(8,128)S(1)} %copy-done.78, bf16[3,512,12,64]{1,3,2,0:T(8,128)(2,1)S(1)} %bitcast.584, bf16[3,512,3,12,64]{1,4,3,2,0:T(8,128)(2,1)} %bitcast.564), kind=kOutput, calls=%fused_computation.21 | convolution fusion | flops 1236252672 | bytes 80363520 | tf_op jit(solution)/shard_map/sqhe,skhe->shqk/dot_general | solution.py:23
  1889.2 32.2 %multiply_convert_fusion = bf16[3,12,512,512]{2,3,1,0:T(8,128)(2,1)} fusion(f32[3,12,512,512]{2,3,1,0:T(8,128)} %get-tuple-element.330, f32[3,12,512]{2,1,0:T(8,128)S(1)} %get-tuple-element.329, f32[3,12,512,512]{2,3,1,0:T(8,128)} %get-tuple-element.302, f32[3,12,512]{2,1,0:T(8,128)S(1)} %copy-done.78), kind=kLoop, calls=%fused_computation.20 | loop fusion | flops 37748736 | bytes 94519296 | tf_op jit(solution)/shard_map/convert_element_type | solution.py:97
  1921.3 10.4 fusion.142
  1931.8 10.4 fusion.141
  1942.2 14.3 convert_bitcast_fusion
  1970.8 16.6 fusion.105
  1987.5 17.0 fusion.104
  2017.3 11.0 gather_fusion.8
  2034.0 12.3 fusion.103
  2046.3 25.3 %add_convert_fusion = bf16[3,512,3072]{2,1,0:T(8,128)(2,1)} fusion(f32[3,512,3072]{2,1,0:T(8,128)} %get-tuple-element.236, f32[3,512,3072]{2,1,0:T(8,128)} %get-tuple-element.311, bf16[2,1,3072,768]{3,2,1,0:T(8,128)(2,1)} %param.16, f32[3,512]{1,0:T(4,128)S(1)} %negate_multiply_fusion.2, f32[3,512,768]{2,1,0:T(8,128)} %copy-done.4, ...), kind=kOutput, calls=%fused_computation.43 | convolution fusion | flops 7324434432 | bytes 59010048 | tf_op jit(solution)/shard_map/oyg,hg->oyh/dot_general | solution.py:23
  2071.6 12.3 fusion.102
  2093.0 13.1 fusion.143
  2106.3 11.6 fusion.144
  2118.1 15.6 fusion.145
  2133.8 20.6 fusion.146
  2154.4 13.2 fusion.147
  2167.6 11.0 gather_fusion.16
  2184.4 12.8 psum.7
  2202.1 10.5 gather_fusion.9
  2221.3 101.7 %all-to-all-done.9 = bf16[16,512,768]{2,1,0:T(8,128)(2,1)} async-done(((bf16[16,512,768]{2,1,0:T(8,128)(2,1)}), bf16[16,512,768]{2,1,0:T(8,128)(2,1)}, u32[]{:S(2)}, u32[]{:S(2)}) %all-to-all-start.9) | async-done | bytes 12582944 | tf_op jit(solution)/shard_map/all_to_all | solution.py:365
  2323.0 10.4 gather_fusion.17
  2348.0 136.7 %reduce-scatter.19.cloned.1.call-done = bf16[2,192,3072]{2,1,0:T(8,128)(2,1)} async-done(((bf16[2,768,3072]{2,1,0:T(8,128)(2,1)}), bf16[2,192,3072]{2,1,0:T(8,128)(2,1)}) %reduce-scatter.19.cloned.1.call-update) | async-done | bytes 2359312 | tf_op jit(solution)/shard_map/reduce_scatter | solution.py:383
  (977 shorter events, 530.2 us)
Async XLA Ops:
  10.9 17.3 all-to-all-start.1
  28.3 15.0 all-to-all-start
  43.3 145.0 %all-to-all-start.2 = ((bf16[16,512,768]{2,1,0:T(8,128)(2,1)}), bf16[16,512,768]{2,1,0:T(8,128)(2,1)}, u32[]{:S(2)}, u32[]{:S(2)}) async-start(bf16[16,512,768]{2,1,0:T(8,128)(2,1)} %broadcast_select_fusion.1), calls=%async_computation.2 | async-start | bytes 25165824 | tf_op jit(solution)/shard_map/all_to_all | solution.py:336
  50.0 183.8 %copy-start.181 = (f32[768]{0:T(1024)}, f32[768]{0:T(1024)S(1)}, u32[]{:S(2)}) copy-start(f32[768]{0:T(1024)S(1)} %get-tuple-element.203) | copy-start | bytes 9220
  50.0 183.8 %copy-start.183 = (f32[768]{0:T(1024)}, f32[768]{0:T(1024)S(1)}, u32[]{:S(2)}) copy-start(f32[768]{0:T(1024)S(1)} %get-tuple-element.204) | copy-start | bytes 9220
  50.0 183.8 %copy-start.185 = (f32[768]{0:T(1024)}, f32[768]{0:T(1024)S(1)}, u32[]{:S(2)}) copy-start(f32[768]{0:T(1024)S(1)} %get-tuple-element.205) | copy-start | bytes 9220
  50.0 197.9 %copy-start.171 = (f32[768]{0:T(1024)}, f32[768]{0:T(1024)S(1)}, u32[]{:S(2)}) copy-start(f32[768]{0:T(1024)S(1)} %get-tuple-element.198) | copy-start | bytes 9220
  50.0 197.9 %copy-start.173 = (f32[768]{0:T(1024)}, f32[768]{0:T(1024)S(1)}, u32[]{:S(2)}) copy-start(f32[768]{0:T(1024)S(1)} %get-tuple-element.199) | copy-start | bytes 9220
  50.0 197.9 %copy-start.175 = (f32[768]{0:T(1024)}, f32[768]{0:T(1024)S(1)}, u32[]{:S(2)}) copy-start(f32[768]{0:T(1024)S(1)} %get-tuple-element.200) | copy-start | bytes 9220
  50.0 197.9 %copy-start.177 = (f32[768]{0:T(1024)}, f32[768]{0:T(1024)S(1)}, u32[]{:S(2)}) copy-start(f32[768]{0:T(1024)S(1)} %get-tuple-element.201) | copy-start | bytes 9220
  50.0 197.9 %copy-start.179 = (f32[768]{0:T(1024)}, f32[768]{0:T(1024)S(1)}, u32[]{:S(2)}) copy-start(f32[768]{0:T(1024)S(1)} %get-tuple-element.202) | copy-start | bytes 9220
  50.0 208.9 %copy-start.133 = (f32[768]{0:T(1024)}, f32[768]{0:T(1024)S(1)}, u32[]{:S(2)}) copy-start(f32[768]{0:T(1024)S(1)} %get-tuple-element.197) | copy-start | bytes 9220
  52.1 206.8 %copy-start.135 = (f32[768]{0:T(1024)}, f32[768]{0:T(1024)S(1)}, u32[]{:S(2)}) copy-start(f32[768]{0:T(1024)S(1)} %get-tuple-element.190) | copy-start | bytes 9220
  52.1 206.8 %copy-start.137 = (f32[768]{0:T(1024)}, f32[768]{0:T(1024)S(1)}, u32[]{:S(2)}) copy-start(f32[768]{0:T(1024)S(1)} %get-tuple-element.191) | copy-start | bytes 9220
  52.1 206.8 %copy-start.139 = (f32[768]{0:T(1024)}, f32[768]{0:T(1024)S(1)}, u32[]{:S(2)}) copy-start(f32[768]{0:T(1024)S(1)} %get-tuple-element.192) | copy-start | bytes 9220
  52.1 206.8 %copy-start.141 = (f32[768]{0:T(1024)}, f32[768]{0:T(1024)S(1)}, u32[]{:S(2)}) copy-start(f32[768]{0:T(1024)S(1)} %get-tuple-element.193) | copy-start | bytes 9220
  52.1 206.8 %copy-start.143 = (f32[768]{0:T(1024)}, f32[768]{0:T(1024)S(1)}, u32[]{:S(2)}) copy-start(f32[768]{0:T(1024)S(1)} %get-tuple-element.194) | copy-start | bytes 9220
  52.1 206.9 %copy-start.145 = (f32[768]{0:T(1024)}, f32[768]{0:T(1024)S(1)}, u32[]{:S(2)}) copy-start(f32[768]{0:T(1024)S(1)} %get-tuple-element.195) | copy-start | bytes 9220
  55.0 133.3 %copy-start.234 = (s32[1024]{0:T(1024)}, s32[1024]{0:T(1024)S(1)}, u32[]{:S(2)}) copy-start(s32[1024]{0:T(1024)S(1)} %pad_clamp_fusion.5) | copy-start | bytes 12292
  55.1 143.9 %copy-start.237 = (pred[15]{0:T(512)(128)(4,1)}, pred[15]{0:T(512)(128)(4,1)S(1)}, u32[]{:S(2)}) copy-start(pred[15]{0:T(512)(128)(4,1)S(1)} %fusion.220) | copy-start | bytes 49
  245.1 153.2 %copy-start.36 = (f32[3,512]{1,0:T(4,128)}, f32[3,512]{1,0:T(4,128)S(1)}, u32[]{:S(2)}) copy-start(f32[3,512]{1,0:T(4,128)S(1)} %broadcast_multiply_fusion.8) | copy-start | bytes 18436
  247.9 150.4 %copy-start.62 = (f32[3,512]{1,0:T(4,128)}, f32[3,512]{1,0:T(4,128)S(1)}, u32[]{:S(2)}) copy-start(f32[3,512]{1,0:T(4,128)S(1)} %fusion.229) | copy-start | bytes 18436
  256.1 146.9 %copy-start.33 = (f32[3,512]{1,0:T(4,128)}, f32[3,512]{1,0:T(4,128)S(1)}, u32[]{:S(2)}) copy-start(f32[3,512]{1,0:T(4,128)S(1)} %broadcast_multiply_fusion.7) | copy-start | bytes 18436
  258.9 144.1 %copy-start.58 = (f32[3,512]{1,0:T(4,128)}, f32[3,512]{1,0:T(4,128)S(1)}, u32[]{:S(2)}) copy-start(f32[3,512]{1,0:T(4,128)S(1)} %fusion.230) | copy-start | bytes 18436
  268.2 136.8 %copy-start.30 = (f32[3,512]{1,0:T(4,128)}, f32[3,512]{1,0:T(4,128)S(1)}, u32[]{:S(2)}) copy-start(f32[3,512]{1,0:T(4,128)S(1)} %broadcast_multiply_fusion.6) | copy-start | bytes 18436
  271.1 133.9 %copy-start.55 = (f32[3,512]{1,0:T(4,128)}, f32[3,512]{1,0:T(4,128)S(1)}, u32[]{:S(2)}) copy-start(f32[3,512]{1,0:T(4,128)S(1)} %fusion.231) | copy-start | bytes 18436
  351.1 55.9 %copy-start.40 = (f32[3,512]{1,0:T(4,128)}, f32[3,512]{1,0:T(4,128)S(1)}, u32[]{:S(2)}) copy-start(f32[3,512]{1,0:T(4,128)S(1)} %broadcast_multiply_fusion.5) | copy-start | bytes 18436
  354.5 52.5 %copy-start.108 = (f32[3,512]{1,0:T(4,128)}, f32[3,512]{1,0:T(4,128)S(1)}, u32[]{:S(2)}) copy-start(f32[3,512]{1,0:T(4,128)S(1)} %fusion.232) | copy-start | bytes 18436
  419.8 144.4 %all-to-all-start.3 = ((bf16[16,512,768]{2,1,0:T(8,128)(2,1)}), bf16[16,512,768]{2,1,0:T(8,128)(2,1)}, u32[]{:S(2)}, u32[]{:S(2)}) async-start(bf16[16,512,768]{2,1,0:T(8,128)(2,1)} %gather_fusion.4), calls=%async_computation.3 | async-start | bytes 25165824 | tf_op jit(solution)/shard_map/all_to_all | solution.py:342
  435.4 139.1 %copy-start.235 = (s32[1024]{0:T(1024)}, s32[1024]{0:T(1024)S(1)}, u32[]{:S(2)}) copy-start(s32[1024]{0:T(1024)S(1)} %pad_clamp_fusion.3) | copy-start | bytes 12292
  740.9 144.7 %all-to-all-start.4 = ((bf16[16,512,768]{2,1,0:T(8,128)(2,1)}), bf16[16,512,768]{2,1,0:T(8,128)(2,1)}, u32[]{:S(2)}, u32[]{:S(2)}) async-start(bf16[16,512,768]{2,1,0:T(8,128)(2,1)} %get-tuple-element.300), calls=%async_computation.4 | async-start | bytes 25165824 | tf_op jit(solution)/shard_map/all_to_all | solution.py:336
  747.8 148.6 %copy-start.242 = (pred[15]{0:T(512)(128)(4,1)}, pred[15]{0:T(512)(128)(4,1)S(1)}, u32[]{:S(2)}) copy-start(pred[15]{0:T(512)(128)(4,1)S(1)} %fusion.222) | copy-start | bytes 49
  958.2 31.6 %slice-start.48 = ((s8[11796480]{0:T(1024)(128)(4,1)}), s8[4194304]{0:T(1024)(128)(4,1)S(1)}, s32[]{:S(2)}) async-start(s8[11796480]{0:T(1024)(128)(4,1)} %bitcast.560), calls=%async_computation.74 | async-start | bytes 8388608
  996.2 120.0 %copy-start.48 = (f32[3,512]{1,0:T(4,128)}, f32[3,512]{1,0:T(4,128)S(1)}, u32[]{:S(2)}) copy-start(f32[3,512]{1,0:T(4,128)S(1)} %broadcast_multiply_fusion.1) | copy-start | bytes 18436
  1004.5 321.7 %copy-start.53 = (f32[3,512]{1,0:T(4,128)}, f32[3,512]{1,0:T(4,128)S(1)}, u32[]{:S(2)}) copy-start(f32[3,512]{1,0:T(4,128)S(1)} %broadcast_multiply_fusion.3) | copy-start | bytes 18436
  1065.0 58.6 %copy-start.50 = (f32[3,512]{1,0:T(4,128)}, f32[3,512]{1,0:T(4,128)S(1)}, u32[]{:S(2)}) copy-start(f32[3,512]{1,0:T(4,128)S(1)} %broadcast_multiply_fusion) | copy-start | bytes 18436
  1228.6 137.8 %copy-start.227 = (f32[3,512]{1,0:T(4,128)}, f32[3,512]{1,0:T(4,128)S(1)}, u32[]{:S(2)}) copy-start(f32[3,512]{1,0:T(4,128)S(1)} %negate_multiply_fusion.7) | copy-start | bytes 18436
  1228.7 97.5 %copy-start.94 = (f32[3,512]{1,0:T(4,128)}, f32[3,512]{1,0:T(4,128)S(1)}, u32[]{:S(2)}) copy-start(f32[3,512]{1,0:T(4,128)S(1)} %get-tuple-element.267) | copy-start | bytes 18436
  1228.7 97.5 %copy-start.96 = (f32[3,512]{1,0:T(4,128)}, f32[3,512]{1,0:T(4,128)S(1)}, u32[]{:S(2)}) copy-start(f32[3,512]{1,0:T(4,128)S(1)} %get-tuple-element.268) | copy-start | bytes 18436
  1233.4 92.8 %copy-start.202 = (f32[3,512]{1,0:T(4,128)}, f32[3,512]{1,0:T(4,128)S(1)}, u32[]{:S(2)}) copy-start(f32[3,512]{1,0:T(4,128)S(1)} %negate_multiply_fusion.10) | copy-start | bytes 18436
  1295.0 31.2 %copy-start.188 = (f32[768]{0:T(1024)S(1)}, f32[768]{0:T(1024)}, u32[]{:S(2)}) copy-start(f32[768]{0:T(1024)} %get-tuple-element.187) | copy-start | bytes 9220
  1295.0 31.2 %copy-start.190 = (f32[768]{0:T(1024)S(1)}, f32[768]{0:T(1024)}, u32[]{:S(2)}) copy-start(f32[768]{0:T(1024)} %get-tuple-element.188) | copy-start | bytes 9220
  1295.0 31.2 %copy-start.192 = (f32[768]{0:T(1024)S(1)}, f32[768]{0:T(1024)}, u32[]{:S(2)}) copy-start(f32[768]{0:T(1024)} %get-tuple-element.189) | copy-start | bytes 9220
  1295.1 31.2 %copy-start.221 = (f32[768]{0:T(1024)S(1)}, f32[768]{0:T(1024)}, u32[]{:S(2)}) copy-start(f32[768]{0:T(1024)} %get-tuple-element.219) | copy-start | bytes 9220
  1326.3 30.8 %slice-start.36 = ((s8[4718592]{0:T(1024)(128)(4,1)}), s8[4194304]{0:T(1024)(128)(4,1)S(1)}, s32[]{:S(2)}) async-start(s8[4718592]{0:T(1024)(128)(4,1)} %bitcast.548), calls=%async_computation.62 | async-start | bytes 8388608
  1390.5 144.5 %all-to-all-start.7 = ((bf16[16,512,768]{2,1,0:T(8,128)(2,1)}), bf16[16,512,768]{2,1,0:T(8,128)(2,1)}, u32[]{:S(2)}, u32[]{:S(2)}) async-start(bf16[16,512,768]{2,1,0:T(8,128)(2,1)} %gather_fusion.12), calls=%async_computation.7 | async-start | bytes 25165824 | tf_op jit(solution)/shard_map/all_to_all | solution.py:365
  1396.0 149.2 %copy-start.236 = (s32[1024]{0:T(1024)}, s32[1024]{0:T(1024)S(1)}, u32[]{:S(2)}) copy-start(s32[1024]{0:T(1024)S(1)} %pad_clamp_fusion) | copy-start | bytes 12292
  1566.2 144.6 %all-to-all-start.8 = ((bf16[16,512,768]{2,1,0:T(8,128)(2,1)}), bf16[16,512,768]{2,1,0:T(8,128)(2,1)}, u32[]{:S(2)}, u32[]{:S(2)}) async-start(bf16[16,512,768]{2,1,0:T(8,128)(2,1)} %broadcast_select_fusion), calls=%async_computation.8 | async-start | bytes 25165824 | tf_op jit(solution)/shard_map/all_to_all | solution.py:357
  1571.8 640.7 %reduce-scatter.27.cloned.1.call-start = ((), (), s32[]{:S(2)}) async-start(), calls=%async_computation.24 | async-start | bytes 245760
  1605.2 117.1 %copy-start.238 = (pred[15]{0:T(512)(128)(4,1)S(1)}, pred[15]{0:T(512)(128)(4,1)}, u32[]{:S(2)}) copy-start(pred[15]{0:T(512)(128)(4,1)} %copy-done.237) | copy-start | bytes 49
  1728.6 33.5 %copy-start = (bf16[15,512,768]{2,1,0:T(8,128)(2,1)}, bf16[15,512,768]{2,1,0:T(8,128)(2,1)S(1)}, u32[]{:S(2)}) copy-start(bf16[15,512,768]{2,1,0:T(8,128)(2,1)S(1)} %broadcast_select_fusion.4) | copy-start | bytes 35389444
  1740.0 40.4 %copy-start.79 = (f32[3,512]{1,0:T(4,128)}, f32[3,512]{1,0:T(4,128)S(1)}, u32[]{:S(2)}) copy-start(f32[3,512]{1,0:T(4,128)S(1)} %multiply_multiply_fusion.11) | copy-start | bytes 18436
  1740.1 33.3 %copy-start.88 = (f32[3,512]{1,0:T(4,128)}, f32[3,512]{1,0:T(4,128)S(1)}, u32[]{:S(2)}) copy-start(f32[3,512]{1,0:T(4,128)S(1)} %multiply_multiply_fusion.12) | copy-start | bytes 18436
  1748.1 32.2 %copy-start.193 = (f32[3,512]{1,0:T(4,128)}, f32[3,512]{1,0:T(4,128)S(1)}, u32[]{:S(2)}) copy-start(f32[3,512]{1,0:T(4,128)S(1)} %negate_multiply_fusion.3) | copy-start | bytes 18436
  1766.2 447.3 %reduce-scatter.29.cloned.1.call-start = ((), (), s32[]{:S(2)}) async-start(), calls=%async_computation.25 | async-start | bytes 245760
  1816.4 399.6 %reduce-scatter.25.cloned.1.call-start = ((), (), s32[]{:S(2)}) async-start(), calls=%async_computation.23 | async-start | bytes 245760
  1817.9 399.8 %reduce-scatter.17.cloned.1.call-start = ((), (), s32[]{:S(2)}) async-start(), calls=%async_computation.19 | async-start | bytes 2949120 | tf_op jit(solution)/shard_map/reduce_scatter | solution.py:380
  1821.3 512.1 %reduce-scatter.23.cloned.1.call-start = ((), (), s32[]{:S(2)}) async-start(), calls=%async_computation.22 | async-start | bytes 8847360 | tf_op jit(solution)/shard_map/reduce_scatter | solution.py:392
  1861.5 473.7 %reduce-scatter.15.cloned.1.call-start = ((), (), s32[]{:S(2)}) async-start(), calls=%async_computation.18 | async-start | bytes 8847360 | tf_op jit(solution)/shard_map/reduce_scatter | solution.py:377
  1970.2 372.8 %reduce-scatter.21.cloned.1.call-start = ((), (), s32[]{:S(2)}) async-start(), calls=%async_computation.21 | async-start | bytes 11796480 | tf_op jit(solution)/shard_map/reduce_scatter | solution.py:386
  2028.2 150.3 %all-to-all-start.5 = ((bf16[16,512,768]{2,1,0:T(8,128)(2,1)}), bf16[16,512,768]{2,1,0:T(8,128)(2,1)}, u32[]{:S(2)}, u32[]{:S(2)}) async-start(bf16[16,512,768]{2,1,0:T(8,128)(2,1)} %gather_fusion.8), calls=%async_computation.5 | async-start | bytes 25165824 | tf_op jit(solution)/shard_map/all_to_all | solution.py:342
  2033.6 451.1 %reduce-scatter.19.cloned.1.call-start = ((), (), s32[]{:S(2)}) async-start(), calls=%async_computation.20 | async-start | bytes 11796480 | tf_op jit(solution)/shard_map/reduce_scatter | solution.py:383
  2118.0 36.3 %slice-start.24 = ((s8[4718592]{0:T(1024)(128)(4,1)}), s8[4194304]{0:T(1024)(128)(4,1)S(1)}, s32[]{:S(2)}) async-start(s8[4718592]{0:T(1024)(128)(4,1)} %bitcast.536), calls=%async_computation.50 | async-start | bytes 8388608
  2178.5 144.5 %all-to-all-start.9 = ((bf16[16,512,768]{2,1,0:T(8,128)(2,1)}), bf16[16,512,768]{2,1,0:T(8,128)(2,1)}, u32[]{:S(2)}, u32[]{:S(2)}) async-start(bf16[16,512,768]{2,1,0:T(8,128)(2,1)} %gather_fusion.16), calls=%async_computation.9 | async-start | bytes 25165824 | tf_op jit(solution)/shard_map/all_to_all | solution.py:365
  (271 other events, 2545.0 us)
Sparse Core Ops, SparseCore 0:
  1766.4 18.8 reduce-scatter.26
  1816.5 18.8 reduce-scatter.28
  1837.7 17.5 reduce-scatter.24
  1857.6 46.2 reduce-scatter.16
  1906.1 122.9 reduce-scatter.22
  2031.4 124.0 reduce-scatter.14
  2157.9 162.0 reduce-scatter.20
  2322.5 162.1 reduce-scatter.18
where the time goes:
time: 2510 us; the launch traced here: 2500 us
  waiting for transfers between devices  872 us (35%)
  matrix products  654 us (26%)
  other arithmetic  509 us (20%)
  local copies, waits for them, and re-layouts  242 us (10%)
  blocking collectives  155 us (6%)
  starting transfers between devices  49.1 us (2%)
    dot_general x52, matrix products, matrix_product(): jnp.einsum(einsum_form, operand_a, operand_b, preferred_element_type=jnp....  616 us
    all_to_all x3, waiting for transfers between devices, per_device(): lax.all_to_all(outgoing, 'op', split_axis=0, concat_axis=0, tiled=True)  366 us
    all_to_all x2, waiting for transfers between devices, per_device(): lax.all_to_all(owner_dx[slot_of], 'op', split_axis=0, concat_axis=0, tile...  241 us
    all_to_all x1, blocking collectives, per_device(): lax.all_to_all(outgoing, 'op', split_axis=0, concat_axis=0, tiled=True)  143 us
    reduce_scatter x1, waiting for transfers between devices, per_device(): lax.psum_scatter(stacked_up.astype(jnp.bfloat16), 'dp', scatter_dimension...  137 us
    all_to_all x2, waiting for transfers between devices, per_device(): lax.all_to_all(owner_y[slot_of], 'op', split_axis=0, concat_axis=0, tiled...  129 us
    unnamed x44, other arithmetic  110 us
    convert_element_type x2, other arithmetic, kind_forward(): active_reduced = active.astype(jnp.bfloat16)  90.2 us
  transfers between devices with their start and end apart: 17, of which 7 were waited for; matrix products, arithmetic and copies ran while one was open for 21% of the time, Pallas kernels for 0%

commit v1 on v0

v1 whole, which is shorter than its diff:
```python
import jax
import jax.numpy as jnp
from jax import lax
from jax.experimental import pallas as pl
from jax.experimental.pallas import tpu as pltpu
from jax.sharding import PartitionSpec as P

HEADS = 12
KINDS = 5
BLOCKS = 2
OWN_CAP = 3
FF_PART = 1024
FF_SUB = 512
LANES = 128
BF16 = jnp.bfloat16
F32 = jnp.float32
VMEM_BYTES = 60 * 2**20


def params_of(axes):
    return pltpu.CompilerParams(
        dimension_semantics=("arbitrary",) * axes, vmem_limit_bytes=VMEM_BYTES
    )


def nn(a, b):
    return lax.dot_general(a, b, (((1,), (0,)), ((), ())), preferred_element_type=F32)


def nt(a, b):
    return lax.dot_general(a, b, (((1,), (1,)), ((), ())), preferred_element_type=F32)


def tn(a, b):
    return lax.dot_general(a, b, (((0,), (0,)), ((), ())), preferred_element_type=F32)


def table_kernel(owners, cap, seqs, cand, me_ref, src, pos, rows, counts, relay_in, relay_out, fill):
    me = me_ref[0]
    slots = owners * cap
    for b in range(BLOCKS):

        def clear_slot(s, _):
            src[b * slots + s] = -1
            return 0

        lax.fori_loop(0, slots, clear_slot, 0)

        def clear_fill(o, _):
            fill[o] = 0
            return 0

        lax.fori_loop(0, owners, clear_fill, 0)
        for k in range(8):
            counts[b * 8 + k] = 0

        def one_home(h, _):
            def one_seq(j, _):
                c = cand[(h * seqs + j) * BLOCKS + b]
                o = lax.rem(c, owners)
                k = lax.div(c, owners)
                stamp = h * (cap + 1)
                before = fill[o]
                r = jnp.minimum(jnp.maximum(before - stamp, 0), cap - 1)
                fill[o] = stamp + r + 1

                @pl.when(h == me)
                def _():
                    src[b * slots + o * cap + r] = j
                    pos[b * seqs + j] = o * cap + r

                @pl.when(o == me)
                def _():
                    n = jnp.minimum(counts[b * 8 + k], OWN_CAP - 1)
                    rows[b * KINDS * OWN_CAP + k * OWN_CAP + n] = h * cap + r
                    counts[b * 8 + k] = n + 1

                return 0

            return lax.fori_loop(0, seqs, one_seq, 0)

        lax.fori_loop(0, owners, one_home, 0)
        for k in range(KINDS):
            base = b * KINDS * OWN_CAP + k * OWN_CAP
            for i in range(1, OWN_CAP):
                rows[base + i] = jnp.where(
                    i < counts[b * 8 + k], rows[base + i], rows[base + i - 1]
                )

        def fill_slot(s, last):
            now = src[b * slots + s]
            now = jnp.where(now < 0, last, now)
            src[b * slots + s] = now
            return now

        lax.fori_loop(0, slots, fill_slot, 0)

    def relays(s, _):
        relay_in[s] = pos[src[slots + s]]
        relay_out[s] = pos[seqs + src[s]]
        return 0

    lax.fori_loop(0, slots, relays, 0)


def make_tables(group, me, owners, cap, seqs):
    slots = owners * cap

    def kernel(*refs):
        table_kernel(owners, cap, seqs, *refs)

    smem = pl.BlockSpec(memory_space=pltpu.SMEM)
    shape = lambda n: jax.ShapeDtypeStruct((n,), jnp.int32)
    return pl.pallas_call(
        kernel,
        in_specs=[smem, smem],
        out_specs=[smem] * 6,
        out_shape=[
            shape(BLOCKS * slots),
            shape(BLOCKS * seqs),
            shape(BLOCKS * KINDS * OWN_CAP),
            shape(BLOCKS * 8),
            shape(slots),
            shape(slots),
        ],
        scratch_shapes=[pltpu.SMEM((max(owners, 8),), jnp.int32)],
        name="tables",
    )(group, me)


def permute_rows(table, source, start, count):
    length, width = source.shape[1:]

    def kernel(table_ref, in_ref, out_ref):
        out_ref[...] = in_ref[...]

    return pl.pallas_call(
        kernel,
        grid_spec=pltpu.PrefetchScalarGridSpec(
            num_scalar_prefetch=1,
            grid=(count,),
            in_specs=[pl.BlockSpec((1, length, width), lambda i, t: (t[start + i], 0, 0))],
            out_specs=pl.BlockSpec((1, length, width), lambda i, t: (i, 0, 0)),
        ),
        out_shape=jax.ShapeDtypeStruct((count, length, width), source.dtype),
        compiler_params=params_of(1),
        cost_estimate=pl.CostEstimate(
            flops=0, transcendentals=0, bytes_accessed=4 * count * length * width
        ),
        name="permute",
    )(table, source)


def norm_forward(summed, gain_row, shift_row):
    center = summed - jnp.mean(summed, axis=-1, keepdims=True)
    spread = jnp.mean(center * center, axis=-1, keepdims=True)
    scale = lax.rsqrt(spread + 1e-05)
    normed = center * scale
    return normed, normed * gain_row + shift_row, scale


def finish_forward(x, branch, gain_row, shift_row, y_ref, zn_ref, rstd_ref):
    normed, result, scale = norm_forward(x.astype(F32) + branch, gain_row, shift_row)
    y_ref[0] = result.astype(BF16)
    zn_ref[0] = normed.astype(BF16)
    rstd_ref[0] = jnp.broadcast_to(scale, rstd_ref.shape[1:])


def norm_backward(dy_ref, zn_ref, rstd_ref, gain_row):
    dy = dy_ref[0].astype(F32)
    normed = zn_ref[0].astype(F32)
    scale = rstd_ref[0][:, :1]
    scaled = dy * gain_row
    first = jnp.mean(scaled, axis=-1, keepdims=True)
    second = jnp.mean(scaled * normed, axis=-1, keepdims=True)
    gain_grad = jnp.sum(dy * normed, axis=0, keepdims=True)
    shift_grad = jnp.sum(dy, axis=0, keepdims=True)
    return (scaled - first - normed * second) * scale, gain_grad, shift_grad


def head_masks(length):
    lane = lax.broadcasted_iota(jnp.int32, (length, LANES), 1)
    low = lane < LANES // 2
    return low


def attention_forward(b, tables, x, weights, norms, y_in):
    rows, counts = tables
    attn_qkv, attn_out = weights
    gains, shifts = norms
    slots, length, width = x.shape
    score_scale = (width // HEADS) ** (-0.5)
    base = b * KINDS * OWN_CAP

    def kernel(rows_ref, counts_ref, x_ref, qkv_w, out_w, gain, shift, *rest):
        y_ref, qkv_ref, o_ref, zn_ref, rstd_ref = rest[-5:]
        i = pl.program_id(0)

        @pl.when(i < counts_ref[b * 8])
        def _():
            xv = x_ref[0]
            for part in range(3):
                cols = slice(part * width, (part + 1) * width)
                qkv_ref[0, :, cols] = nn(xv, qkv_w[:, cols]).astype(BF16)
            low = head_masks(length)
            zero = jnp.zeros((), BF16)
            for pair in range(width // LANES):
                at = pair * LANES
                q2 = qkv_ref[0, :, at : at + LANES] * jnp.asarray(score_scale, BF16)
                k2 = qkv_ref[0, :, width + at : width + at + LANES]
                v2 = qkv_ref[0, :, 2 * width + at : 2 * width + at + LANES]
                mixed = []
                for half in range(2):
                    qm = jnp.where(low if half == 0 else ~low, q2, zero)
                    s = nt(qm, k2)
                    e = jnp.exp(s - jnp.max(s, axis=-1, keepdims=True))
                    total = jnp.sum(e, axis=-1, keepdims=True)
                    mixed.append(nn(e.astype(BF16), v2) / total)
                o_ref[0, :, at : at + LANES] = jnp.where(low, mixed[0], mixed[1]).astype(BF16)
            branch = nn(o_ref[0], out_w[...])
            finish_forward(
                xv, branch, gain[0:1, :], shift[0:1, :], y_ref, zn_ref, rstd_ref
            )

    def at_row(i, r, c):
        return (r[base + i], 0, 0)

    def at_step(i, r, c):
        return (jnp.minimum(i, c[b * 8] - 1), 0, 0)

    seq = (1, length, width)
    in_specs = [
        pl.BlockSpec(seq, at_row),
        pl.BlockSpec(
            (None, None, width, 3 * width), lambda i, r, c: (b, 0, 0, 0), pipeline_mode=pl.Buffered(1)
        ),
        pl.BlockSpec(
            (None, None, width, width), lambda i, r, c: (b, 0, 0, 0), pipeline_mode=pl.Buffered(1)
        ),
        pl.BlockSpec((8, width), lambda i, r, c: (0, 0)),
        pl.BlockSpec((8, width), lambda i, r, c: (0, 0)),
    ]
    args = [rows, counts, x, attn_qkv, attn_out, gains, shifts]
    alias = {}
    if y_in is not None:
        in_specs.append(pl.BlockSpec(memory_space=pl.ANY))
        alias = {len(args): 0}
        args.append(y_in)
    flops = OWN_CAP * length * width * (8 * width + 4 * length)
    return pl.pallas_call(
        kernel,
        grid_spec=pltpu.PrefetchScalarGridSpec(
            num_scalar_prefetch=2,
            grid=(OWN_CAP,),
            in_specs=in_specs,
            out_specs=[
                pl.BlockSpec(seq, at_row),
                pl.BlockSpec((1, length, 3 * width), at_step),
                pl.BlockSpec(seq, at_step),
                pl.BlockSpec(seq, at_step),
                pl.BlockSpec((1, length, LANES), at_step),
            ],
        ),
        out_shape=[
            jax.ShapeDtypeStruct((slots, length, width), BF16),
            jax.ShapeDtypeStruct((OWN_CAP, length, 3 * width), BF16),
            jax.ShapeDtypeStruct((OWN_CAP, length, width), BF16),
            jax.ShapeDtypeStruct((OWN_CAP, length, width), BF16),
            jax.ShapeDtypeStruct((OWN_CAP, length, LANES), F32),
        ],
        input_output_aliases=alias,
        compiler_params=params_of(1),
        cost_estimate=pl.CostEstimate(
            flops=2 * flops, transcendentals=OWN_CAP * HEADS * length * length, bytes_accessed=30 * 2**20
        ),
        name="attention_forward",
    )(*args)


def attention_backward(b, tables, x, dy, kept, weights, gains, dx_in):
    rows, counts = tables
    attn_qkv, attn_out = weights
    qkv, o, zn, rstd = kept
    slots, length, width = x.shape
    score_scale = (width // HEADS) ** (-0.5)
    base = b * KINDS * OWN_CAP

    def kernel(rows_ref, counts_ref, x_ref, dy_ref, qkv_ref, o_ref, zn_ref, rstd_ref, qkv_w, out_w, gain, *rest):
        dx_ref, dqkv_w_ref, dout_w_ref, small_ref, acc_qkv, acc_out, do_scr, dqkv_scr = rest[-8:]
        i = pl.program_id(0)

        @pl.when(i == 0)
        def _():
            acc_qkv[...] = jnp.zeros_like(acc_qkv)
            acc_out[...] = jnp.zeros_like(acc_out)
            small_ref[...] = jnp.zeros_like(small_ref)

        @pl.when(i < counts_ref[b * 8])
        def _():
            dz, gain_grad, shift_grad = norm_backward(dy_ref, zn_ref, rstd_ref, gain[0:1, :])
            small_ref[0:1, :] += gain_grad
            small_ref[1:2, :] += shift_grad
            dh = dz.astype(BF16)
            acc_out[...] += tn(o_ref[0], dh)
            do_scr[...] = nt(dh, out_w[...]).astype(BF16)
            low = head_masks(length)
            zero = jnp.zeros((), BF16)
            for pair in range(width // LANES):
                at = pair * LANES
                q2 = qkv_ref[0, :, at : at + LANES] * jnp.asarray(score_scale, BF16)
                k2 = qkv_ref[0, :, width + at : width + at + LANES]
                v2 = qkv_ref[0, :, 2 * width + at : 2 * width + at + LANES]
                do2 = do_scr[:, at : at + LANES]
                dqs, dks, dvs = [], [], []
                for half in range(2):
                    mask = low if half == 0 else ~low
                    st = nt(jnp.where(mask, k2, zero), q2)
                    e = jnp.exp(st - jnp.max(st, axis=0, keepdims=True))
                    p = e * (1.0 / jnp.sum(e, axis=0, keepdims=True))
                    dvs.append(nn(p.astype(BF16), do2))
                    t = p * nt(jnp.where(mask, v2, zero), do2)
                    ds = (t - p * jnp.sum(t, axis=0, keepdims=True)).astype(BF16)
                    dks.append(nn(ds, q2))
                    dqs.append(tn(ds, k2))
                dqkv_scr[:, at : at + LANES] = (jnp.where(low, dqs[0], dqs[1]) * score_scale).astype(BF16)
                dqkv_scr[:, width + at : width + at + LANES] = jnp.where(low, dks[0], dks[1]).astype(BF16)
                dqkv_scr[:, 2 * width + at : 2 * width + at + LANES] = jnp.where(low, dvs[0], dvs[1]).astype(BF16)
            xv = x_ref[0]
            total = dz
            for part in range(3):
                cols = slice(part * width, (part + 1) * width)
                piece = dqkv_scr[:, cols]
                acc_qkv[:, cols] += tn(xv, piece)
                total = total + nt(piece, qkv_w[:, cols])
            dx_ref[0] = total.astype(BF16)

        @pl.when(i == OWN_CAP - 1)
        def _():
            dqkv_w_ref[...] = acc_qkv[...].astype(BF16)
            dout_w_ref[...] = acc_out[...].astype(BF16)

    def at_row(i, r, c):
        return (r[base + i], 0, 0)

    def at_step(i, r, c):
        return (jnp.minimum(i, c[b * 8] - 1), 0, 0)

    def whole(i, r, c):
        return (0, 0)

    seq = (1, length, width)
    in_specs = [
        pl.BlockSpec(seq, at_row),
        pl.BlockSpec(seq, at_row),
        pl.BlockSpec((1, length, 3 * width), at_step),
        pl.BlockSpec(seq, at_step),
        pl.BlockSpec(seq, at_step),
        pl.BlockSpec((1, length, LANES), at_step),
        pl.BlockSpec(
            (None, None, width, 3 * width), lambda i, r, c: (b, 0, 0, 0), pipeline_mode=pl.Buffered(1)
        ),
        pl.BlockSpec(
            (None, None, width, width), lambda i, r, c: (b, 0, 0, 0), pipeline_mode=pl.Buffered(1)
        ),
        pl.BlockSpec((8, width), whole),
    ]
    args = [rows, counts, x, dy, qkv, o, zn, rstd, attn_qkv, attn_out, gains]
    alias = {}
    if dx_in is not None:
        in_specs.append(pl.BlockSpec(memory_space=pl.ANY))
        alias = {len(args): 0}
        args.append(dx_in)
    flops = 2 * OWN_CAP * length * width * (8 * width + 4 * length)
    return pl.pallas_call(
        kernel,
        grid_spec=pltpu.PrefetchScalarGridSpec(
            num_scalar_prefetch=2,
            grid=(OWN_CAP,),
            in_specs=in_specs,
            out_specs=[
                pl.BlockSpec(seq, at_row),
                pl.BlockSpec((width, 3 * width), whole),
                pl.BlockSpec((width, width), whole),
                pl.BlockSpec((8, width), whole),
            ],
            scratch_shapes=[
                pltpu.VMEM((width, 3 * width), F32),
                pltpu.VMEM((width, width), F32),
                pltpu.VMEM((length, width), BF16),
                pltpu.VMEM((length, 3 * width), BF16),
            ],
        ),
        out_shape=[
            jax.ShapeDtypeStruct((slots, length, width), BF16),
            jax.ShapeDtypeStruct((width, 3 * width), BF16),
            jax.ShapeDtypeStruct((width, width), BF16),
            jax.ShapeDtypeStruct((8, width), F32),
        ],
        input_output_aliases=alias,
        compiler_params=params_of(1),
        cost_estimate=pl.CostEstimate(
            flops=2 * flops, transcendentals=OWN_CAP * HEADS * length * length, bytes_accessed=40 * 2**20
        ),
        name="attention_backward",
    )(*args)


def feed_forward(b, tables, x, weights, norms, y_in):
    rows, counts = tables
    ffn_up, ffn_down = weights
    gains, shifts = norms
    slots, length, width = x.shape
    hidden = ffn_up.shape[-1]
    parts = hidden // FF_PART
    kind = KINDS - 1
    base = b * KINDS * OWN_CAP + kind * OWN_CAP

    def kernel(rows_ref, counts_ref, x_ref, up, down, gain, shift, *rest):
        y_ref, g_ref, slope_ref, zn_ref, rstd_ref, x_scr, h_scr = rest[-7:]
        c, i = pl.program_id(0), pl.program_id(1)

        @pl.when(i < counts_ref[b * 8 + kind])
        def _():
            @pl.when(c == 0)
            def _():
                x_scr[i] = x_ref[0]

            xv = x_scr[i]
            branch = None
            for sub in range(FF_PART // FF_SUB):
                cols = slice(sub * FF_SUB, (sub + 1) * FF_SUB)
                a = nn(xv, up[:, cols])
                phi = 0.5 + 0.5 * lax.erf(a * (0.5**0.5))
                slope = phi + a * (jnp.exp(a * a * -0.5) * 0.3989422804014327)
                g = (a * phi).astype(BF16)
                g_ref[0, :, cols] = g
                slope_ref[0, :, cols] = slope.astype(BF16)
                term = nn(g, down[cols, :])
                branch = term if branch is None else branch + term

            @pl.when(c == 0)
            def _():
                h_scr[i] = branch

            @pl.when(jnp.logical_and(c > 0, c < parts - 1))
            def _():
                h_scr[i] += branch

            @pl.when(c == parts - 1)
            def _():
                finish_forward(
                    xv,
                    h_scr[i] + branch,
                    gain[kind : kind + 1, :],
                    shift[kind : kind + 1, :],
                    y_ref,
                    zn_ref,
                    rstd_ref,
                )

    def in_row(c, i, r, n):
        return (r[base + jnp.where(c == 0, i, OWN_CAP - 1)], 0, 0)

    def out_row(c, i, r, n):
        return (r[base + jnp.where(c == parts - 1, i, 0)], 0, 0)

    def out_step(c, i, r, n):
        return (jnp.where(c == parts - 1, jnp.minimum(i, n[b * 8 + kind] - 1), 0), 0, 0)

    def part_step(c, i, r, n):
        return (jnp.minimum(i, n[b * 8 + kind] - 1), 0, c)

    seq = (1, length, width)
    in_specs = [
        pl.BlockSpec(seq, in_row),
        pl.BlockSpec((None, None, width, FF_PART), lambda c, i, r, n: (b, 0, 0, c)),
        pl.BlockSpec((None, None, FF_PART, width), lambda c, i, r, n: (b, 0, c, 0)),
        pl.BlockSpec((8, width), lambda c, i, r, n: (0, 0)),
        pl.BlockSpec((8, width), lambda c, i, r, n: (0, 0)),
    ]
    args = [rows, counts, x, ffn_up, ffn_down, gains, shifts]
    alias = {}
    if y_in is not None:
        in_specs.append(pl.BlockSpec(memory_space=pl.ANY))
        alias = {len(args): 0}
        args.append(y_in)
    return pl.pallas_call(
        kernel,
        grid_spec=pltpu.PrefetchScalarGridSpec(
            num_scalar_prefetch=2,
            grid=(parts, OWN_CAP),
            in_specs=in_specs,
            out_specs=[
                pl.BlockSpec(seq, out_row),
                pl.BlockSpec((1, length, FF_PART), part_step),
                pl.BlockSpec((1, length, FF_PART), part_step),
                pl.BlockSpec(seq, out_step),
                pl.BlockSpec((1, length, LANES), out_step),
            ],
            scratch_shapes=[
                pltpu.VMEM((OWN_CAP, length, width), BF16),
                pltpu.VMEM((OWN_CAP, length, width), F32),
            ],
        ),
        out_shape=[
            jax.ShapeDtypeStruct((slots, length, width), BF16),
            jax.ShapeDtypeStruct((OWN_CAP, length, hidden), BF16),
            jax.ShapeDtypeStruct((OWN_CAP, length, hidden), BF16),
            jax.ShapeDtypeStruct((OWN_CAP, length, width), BF16),
            jax.ShapeDtypeStruct((OWN_CAP, length, LANES), F32),
        ],
        input_output_aliases=alias,
        compiler_params=params_of(2),
        cost_estimate=pl.CostEstimate(
            flops=4 * OWN_CAP * length * width * hidden,
            transcendentals=2 * OWN_CAP * length * hidden,
            bytes_accessed=40 * 2**20,
        ),
        name="feed_forward",
    )(*args)


def feed_backward(b, tables, x, dy, kept, weights, gains, dx_in):
    rows, counts = tables
    ffn_up, ffn_down = weights
    g, slope, zn, rstd = kept
    slots, length, width = x.shape
    hidden = ffn_up.shape[-1]
    parts = hidden // FF_PART
    kind = KINDS - 1
    base = b * KINDS * OWN_CAP + kind * OWN_CAP

    def kernel(
        rows_ref, counts_ref, x_ref, dy_ref, g_ref, slope_ref, zn_ref, rstd_ref, up, down, gain, *rest
    ):
        dx_ref, dup_ref, ddown_ref, small_ref, x_scr, dh_scr, dx_scr, acc_up, acc_down = rest[-9:]
        c, i = pl.program_id(0), pl.program_id(1)

        @pl.when(jnp.logical_and(c == 0, i == 0))
        def _():
            small_ref[...] = jnp.zeros_like(small_ref)

        @pl.when(i == 0)
        def _():
            acc_up[...] = jnp.zeros_like(acc_up)
            acc_down[...] = jnp.zeros_like(acc_down)

        @pl.when(i < counts_ref[b * 8 + kind])
        def _():
            @pl.when(c == 0)
            def _():
                dz, gain_grad, shift_grad = norm_backward(
                    dy_ref, zn_ref, rstd_ref, gain[kind : kind + 1, :]
                )
                small_ref[0:1, :] += gain_grad
                small_ref[1:2, :] += shift_grad
                x_scr[i] = x_ref[0]
                dh_scr[i] = dz.astype(BF16)
                dx_scr[i] = dz

            xv = x_scr[i]
            dh = dh_scr[i]
            total = None
            for sub in range(FF_PART // FF_SUB):
                cols = slice(sub * FF_SUB, (sub + 1) * FF_SUB)
                dg = nt(dh, down[cols, :])
                da = (dg * slope_ref[0, :, cols].astype(F32)).astype(BF16)
                acc_up[:, cols] += tn(xv, da)
                acc_down[cols, :] += tn(g_ref[0, :, cols], dh)
                term = nt(da, up[:, cols])
                total = term if total is None else total + term

            @pl.when(c < parts - 1)
            def _():
                dx_scr[i] += total

            @pl.when(c == parts - 1)
            def _():
                dx_ref[0] = (dx_scr[i] + total).astype(BF16)

        @pl.when(i == OWN_CAP - 1)
        def _():
            dup_ref[...] = acc_up[...].astype(BF16)
            ddown_ref[...] = acc_down[...].astype(BF16)

    def in_row(c, i, r, n):
        return (r[base + jnp.where(c == 0, i, OWN_CAP - 1)], 0, 0)

    def in_step(c, i, r, n):
        last = n[b * 8 + kind] - 1
        return (jnp.where(c == 0, jnp.minimum(i, last), last), 0, 0)

    def out_row(c, i, r, n):
        return (r[base + jnp.where(c == parts - 1, i, 0)], 0, 0)

    def part_step(c, i, r, n):
        return (jnp.minimum(i, n[b * 8 + kind] - 1), 0, c)

    seq = (1, length, width)
    in_specs = [
        pl.BlockSpec(seq, in_row),
        pl.BlockSpec(seq, in_row),
        pl.BlockSpec((1, length, FF_PART), part_step),
        pl.BlockSpec((1, length, FF_PART), part_step),
        pl.BlockSpec(seq, in_step),
        pl.BlockSpec((1, length, LANES), in_step),
        pl.BlockSpec((None, None, width, FF_PART), lambda c, i, r, n: (b, 0, 0, c)),
        pl.BlockSpec((None, None, FF_PART, width), lambda c, i, r, n: (b, 0, c, 0)),
        pl.BlockSpec((8, width), lambda c, i, r, n: (0, 0)),
    ]
    args = [rows, counts, x, dy, g, slope, zn, rstd, ffn_up, ffn_down, gains]
    alias = {}
    if dx_in is not None:
        in_specs.append(pl.BlockSpec(memory_space=pl.ANY))
        alias = {len(args): 0}
        args.append(dx_in)
    return pl.pallas_call(
        kernel,
        grid_spec=pltpu.PrefetchScalarGridSpec(
            num_scalar_prefetch=2,
            grid=(parts, OWN_CAP),
            in_specs=in_specs,
            out_specs=[
                pl.BlockSpec(seq, out_row),
                pl.BlockSpec((width, FF_PART), lambda c, i, r, n: (0, c)),
                pl.BlockSpec((FF_PART, width), lambda c, i, r, n: (c, 0)),
                pl.BlockSpec((8, width), lambda c, i, r, n: (0, 0)),
            ],
            scratch_shapes=[
                pltpu.VMEM((OWN_CAP, length, width), BF16),
                pltpu.VMEM((OWN_CAP, length, width), BF16),
                pltpu.VMEM((OWN_CAP, length, width), F32),
                pltpu.VMEM((width, FF_PART), F32),
                pltpu.VMEM((FF_PART, width), F32),
            ],
        ),
        out_shape=[
            jax.ShapeDtypeStruct((slots, length, width), BF16),
            jax.ShapeDtypeStruct((width, hidden), BF16),
            jax.ShapeDtypeStruct((hidden, width), BF16),
            jax.ShapeDtypeStruct((8, width), F32),
        ],
        input_output_aliases=alias,
        compiler_params=params_of(2),
        cost_estimate=pl.CostEstimate(
            flops=8 * OWN_CAP * length * width * hidden,
            transcendentals=0,
            bytes_accessed=50 * 2**20,
        ),
        name="feed_backward",
    )(*args)


PAD = 8
ROW_TILE = 128
COL_TILE = 256


def fill_padded(padded, values):
    length = values.shape[0]
    edge = jnp.zeros((PAD, values.shape[1]), F32)
    padded[0:PAD, :] = edge
    padded[PAD + length : PAD + length + PAD, :] = edge
    padded[PAD : PAD + length, :] = values


def conv_forward(b, tables, x, weights, norms, y_in):
    rows, counts = tables
    taps, conv_point = weights
    gains, shifts = norms
    slots, length, width = x.shape
    base = b * KINDS * OWN_CAP + OWN_CAP
    steps = (KINDS - 2) * OWN_CAP

    def kernel(rows_ref, counts_ref, x_ref, point, taps_ref, gain, shift, *rest):
        y_ref, u_ref, zn_ref, rstd_ref, xpad = rest[-5:]
        step = pl.program_id(0)
        which, j = step // OWN_CAP, step % OWN_CAP
        for kind in range(1, KINDS - 1):
            taps_n = 2 * kind + 1
            first = kind * kind - 1

            @pl.when(jnp.logical_and(which == kind - 1, j < counts_ref[b * 8 + kind]))
            def _():
                fill_padded(xpad, x_ref[0].astype(F32))
                for r in range(0, length, ROW_TILE):
                    for col in range(0, width, COL_TILE):
                        cols = slice(col, col + COL_TILE)
                        mixed = None
                        for t in range(taps_n):
                            start = PAD + r + t - kind
                            term = xpad[start : start + ROW_TILE, cols] * taps_ref[first + t : first + t + 1, cols]
                            mixed = term if mixed is None else mixed + term
                        u_ref[0, r : r + ROW_TILE, cols] = mixed.astype(BF16)
                branch = nn(u_ref[0], point[...])
                finish_forward(
                    x_ref[0],
                    branch,
                    gain[kind : kind + 1, :],
                    shift[kind : kind + 1, :],
                    y_ref,
                    zn_ref,
                    rstd_ref,
                )

    def at_row(i, r, c):
        return (r[base + i], 0, 0)

    def at_step(i, r, c):
        which = i // OWN_CAP
        last = c[b * 8 + 1 + which] - 1
        return (which * OWN_CAP + jnp.minimum(i % OWN_CAP, last), 0, 0)

    def whole(i, r, c):
        return (0, 0)

    seq = (1, length, width)
    in_specs = [
        pl.BlockSpec(seq, at_row),
        pl.BlockSpec((None, None, None, width, width), lambda i, r, c: (b, 0, i // OWN_CAP, 0, 0)),
        pl.BlockSpec((16, width), whole),
        pl.BlockSpec((8, width), whole),
        pl.BlockSpec((8, width), whole),
    ]
    args = [rows, counts, x, conv_point, taps, gains, shifts]
    alias = {}
    if y_in is not None:
        in_specs.append(pl.BlockSpec(memory_space=pl.ANY))
        alias = {len(args): 0}
        args.append(y_in)
    return pl.pallas_call(
        kernel,
        grid_spec=pltpu.PrefetchScalarGridSpec(
            num_scalar_prefetch=2,
            grid=(steps,),
            in_specs=in_specs,
            out_specs=[
                pl.BlockSpec(seq, at_row),
                pl.BlockSpec(seq, at_step),
                pl.BlockSpec(seq, at_step),
                pl.BlockSpec((1, length, LANES), at_step),
            ],
            scratch_shapes=[pltpu.VMEM((length + 2 * PAD, width), F32)],
        ),
        out_shape=[
            jax.ShapeDtypeStruct((slots, length, width), BF16),
            jax.ShapeDtypeStruct((steps, length, width), BF16),
            jax.ShapeDtypeStruct((steps, length, width), BF16),
            jax.ShapeDtypeStruct((steps, length, LANES), F32),
        ],
        input_output_aliases=alias,
        compiler_params=params_of(1),
        cost_estimate=pl.CostEstimate(
            flops=2 * steps * length * width * width, transcendentals=0, bytes_accessed=36 * 2**20
        ),
        name="conv_forward",
    )(*args)


def conv_backward(b, tables, x, dy, kept, weights, gains, dx_in):
    rows, counts = tables
    taps, conv_point = weights
    u, zn, rstd = kept
    slots, length, width = x.shape
    base = b * KINDS * OWN_CAP + OWN_CAP
    steps = (KINDS - 2) * OWN_CAP

    def kernel(rows_ref, counts_ref, x_ref, dy_ref, u_ref, zn_ref, rstd_ref, point, taps_ref, gain, *rest):
        dx_ref, dpoint_ref, small_ref, acc, xpad, dupad, dz_scr = rest[-7:]
        step = pl.program_id(0)
        which, j = step // OWN_CAP, step % OWN_CAP

        @pl.when(step == 0)
        def _():
            small_ref[...] = jnp.zeros_like(small_ref)

        @pl.when(j == 0)
        def _():
            acc[...] = jnp.zeros_like(acc)

        for kind in range(1, KINDS - 1):
            taps_n = 2 * kind + 1
            first = kind * kind - 1

            @pl.when(jnp.logical_and(which == kind - 1, j < counts_ref[b * 8 + kind]))
            def _():
                dz, gain_grad, shift_grad = norm_backward(
                    dy_ref, zn_ref, rstd_ref, gain[kind : kind + 1, :]
                )
                small_ref[14 + kind : 15 + kind, :] += gain_grad
                small_ref[17 + kind : 18 + kind, :] += shift_grad
                dz_scr[...] = dz
                dh = dz.astype(BF16)
                acc[...] += tn(u_ref[0], dh)
                fill_padded(xpad, x_ref[0].astype(F32))
                fill_padded(dupad, nt(dh, point[...]))
                for col in range(0, width, COL_TILE):
                    cols = slice(col, col + COL_TILE)
                    sums = [None] * taps_n
                    for r in range(0, length, ROW_TILE):
                        here = dupad[PAD + r : PAD + r + ROW_TILE, cols]
                        total = dz_scr[r : r + ROW_TILE, cols]
                        for t in range(taps_n):
                            back = PAD + r - t + kind
                            total = total + dupad[back : back + ROW_TILE, cols] * taps_ref[first + t : first + t + 1, cols]
                            ahead = PAD + r + t - kind
                            part = jnp.sum(
                                xpad[ahead : ahead + ROW_TILE, cols] * here, axis=0, keepdims=True
                            )
                            sums[t] = part if sums[t] is None else sums[t] + part
                        dx_ref[0, r : r + ROW_TILE, cols] = total.astype(BF16)
                    for t in range(taps_n):
                        small_ref[first + t : first + t + 1, cols] += sums[t]

        @pl.when(j == OWN_CAP - 1)
        def _():
            dpoint_ref[...] = acc[...].astype(BF16)

    def at_row(i, r, c):
        return (r[base + i], 0, 0)

    def at_step(i, r, c):
        which = i // OWN_CAP
        last = c[b * 8 + 1 + which] - 1
        return (which * OWN_CAP + jnp.minimum(i % OWN_CAP, last), 0, 0)

    def whole(i, r, c):
        return (0, 0)

    seq = (1, length, width)
    in_specs = [
        pl.BlockSpec(seq, at_row),
        pl.BlockSpec(seq, at_row),
        pl.BlockSpec(seq, at_step),
        pl.BlockSpec(seq, at_step),
        pl.BlockSpec((1, length, LANES), at_step),
        pl.BlockSpec((None, None, None, width, width), lambda i, r, c: (b, 0, i // OWN_CAP, 0, 0)),
        pl.BlockSpec((16, width), whole),
        pl.BlockSpec((8, width), whole),
    ]
    args = [rows, counts, x, dy, u, zn, rstd, conv_point, taps, gains]
    alias = {}
    if dx_in is not None:
        in_specs.append(pl.BlockSpec(memory_space=pl.ANY))
        alias = {len(args): 0}
        args.append(dx_in)
    return pl.pallas_call(
        kernel,
        grid_spec=pltpu.PrefetchScalarGridSpec(
            num_scalar_prefetch=2,
            grid=(steps,),
            in_specs=in_specs,
            out_specs=[
                pl.BlockSpec(seq, at_row),
                pl.BlockSpec((None, width, width), lambda i, r, c: (i // OWN_CAP, 0, 0)),
                pl.BlockSpec((24, width), whole),
            ],
            scratch_shapes=[
                pltpu.VMEM((width, width), F32),
                pltpu.VMEM((length + 2 * PAD, width), F32),
                pltpu.VMEM((length + 2 * PAD, width), F32),
                pltpu.VMEM((length, width), F32),
            ],
        ),
        out_shape=[
            jax.ShapeDtypeStruct((slots, length, width), BF16),
            jax.ShapeDtypeStruct((KINDS - 2, width, width), BF16),
            jax.ShapeDtypeStruct((24, width), F32),
        ],
        input_output_aliases=alias,
        compiler_params=params_of(1),
        cost_estimate=pl.CostEstimate(
            flops=4 * steps * length * width * width, transcendentals=0, bytes_accessed=50 * 2**20
        ),
        name="conv_backward",
    )(*args)


def owner_forward(b, tables, x, weights, small_weights):
    attn_qkv, attn_out, ffn_up, ffn_down, conv_point = weights
    taps, gains, shifts = small_weights
    norms = (gains, shifts)
    y, g, slope, zn_f, rstd_f = feed_forward(b, tables, x, (ffn_up, ffn_down), norms, None)
    y, qkv, o, zn_a, rstd_a = attention_forward(b, tables, x, (attn_qkv, attn_out), norms, y)
    y, u, zn_c, rstd_c = conv_forward(b, tables, x, (taps, conv_point), norms, y)
    return y, ((g, slope, zn_f, rstd_f), (qkv, o, zn_a, rstd_a), (u, zn_c, rstd_c))


def owner_backward(b, tables, x, dy, kept, weights, small_weights):
    attn_qkv, attn_out, ffn_up, ffn_down, conv_point = weights
    taps, gains, shifts = small_weights
    kept_f, kept_a, kept_c = kept
    dx, dup, ddown, small_f = feed_backward(b, tables, x, dy, kept_f, (ffn_up, ffn_down), gains, None)
    dx, dqkv, dout, small_a = attention_backward(
        b, tables, x, dy, kept_a, (attn_qkv, attn_out), gains, dx
    )
    dx, dpoint, small_c = conv_backward(b, tables, x, dy, kept_c, (taps, conv_point), gains, dx)
    small = jnp.concatenate(
        [
            small_c[:15],
            small_a[0:1],
            small_c[15:18],
            small_f[0:1],
            small_a[1:2],
            small_c[18:21],
            small_f[1:2],
        ]
    )
    return dx, (dup, ddown, dqkv, dout, dpoint, small)


def small_params(b, conv_taps, norm_gain, norm_bias):
    taps = jnp.pad(conv_taps[b, 0].astype(F32), ((0, 1), (0, 0)))
    gains = jnp.pad(norm_gain[b, 0].astype(F32), ((0, 3), (0, 0)))
    shifts = jnp.pad(norm_bias[b, 0].astype(F32), ((0, 3), (0, 0)))
    return taps, gains, shifts


def exchange(rows):
    return lax.all_to_all(rows, "op", split_axis=0, concat_axis=0, tiled=True)


def per_device(
    inputs,
    candidate,
    attn_qkv,
    attn_out,
    ffn_up,
    ffn_down,
    conv_taps,
    conv_point,
    norm_gain,
    norm_bias,
    cotangent,
):
    owners = lax.axis_size("op")
    groups = lax.axis_size("dp")
    seqs = inputs.shape[0]
    width = inputs.shape[-1]
    cap = -(-seqs // owners)
    slots = owners * cap
    weights = (attn_qkv, attn_out, ffn_up, ffn_down, conv_point)
    smalls = [small_params(b, conv_taps, norm_gain, norm_bias) for b in range(BLOCKS)]
    me = lax.axis_index("op")
    everyone = lax.all_gather(candidate, ("dp", "op"), axis=0, tiled=True)
    group = lax.dynamic_slice_in_dim(
        everyone, lax.axis_index("dp") * (owners * seqs), owners * seqs, axis=0
    )
    own = jnp.arange(KINDS, dtype=jnp.int32) * owners + me
    totals = jnp.sum((everyone[:, :, None] == own).astype(F32), axis=0)
    src, pos, rows, counts, relay_in, relay_out = make_tables(
        group.reshape(-1), me.astype(jnp.int32)[None], owners, cap, seqs
    )
    tables = (rows, counts)

    x0 = exchange(permute_rows(src, inputs, 0, slots))
    dy1 = exchange(permute_rows(src, cotangent, slots, slots))
    y0, kept0 = owner_forward(0, tables, x0, weights, smalls[0])
    x1 = exchange(permute_rows(relay_in, exchange(y0), 0, slots))
    y1, kept1 = owner_forward(1, tables, x1, weights, smalls[1])
    outputs = permute_rows(pos, exchange(y1), seqs, seqs)
    dx1, grads1 = owner_backward(1, tables, x1, dy1, kept1, weights, smalls[1])
    dy0 = exchange(permute_rows(relay_out, exchange(dx1), 0, slots))
    dx0, grads0 = owner_backward(0, tables, x0, dy0, kept0, weights, smalls[0])
    input_grad = permute_rows(pos, exchange(dx0), 0, seqs)

    def scatter(grad, dim):
        return lax.psum_scatter(grad, "dp", scatter_dimension=dim, tiled=True).astype(F32)

    finished = [None, None]
    for b, (dup, ddown, dqkv, dout, dpoint, small) in ((1, grads1), (0, grads0)):
        total = totals[b]
        small = small.reshape(25, groups, width // groups).transpose(1, 0, 2).astype(BF16)
        small = lax.psum_scatter(small, "dp", scatter_dimension=0, tiled=True)[0].astype(F32)
        tap_total = jnp.repeat(
            total[1 : KINDS - 1], jnp.array([3, 5, 7]), total_repeat_length=15
        )
        finished[b] = (
            scatter(dqkv, 0) / total[0],
            scatter(dout, 0) / total[0],
            scatter(dup, 0) / total[KINDS - 1],
            scatter(ddown, 0) / total[KINDS - 1],
            small[:15] / tap_total[:, None],
            scatter(dpoint, 1) / total[1 : KINDS - 1, None, None],
            small[15:20] / total[:, None],
            small[20:25] / total[:, None],
        )
    grads = tuple(
        jnp.stack([finished[0][n], finished[1][n]])[:, None] for n in range(8)
    )
    return (outputs, input_grad) + grads


def solution(mesh):
    placed = (
        P(("dp", "op"), None, None),
        P(("dp", "op"), None),
        P(None, "op", None, None),
        P(None, "op", None, None),
        P(None, "op", None, None),
        P(None, "op", None, None),
        P(None, "op", None, None),
        P(None, "op", None, None, None),
        P(None, "op", None, None),
        P(None, "op", None, None),
        P(("dp", "op"), None, None),
    )
    return jax.shard_map(
        per_device,
        mesh=mesh,
        in_specs=placed,
        out_specs=(
            P(("dp", "op"), None, None),
            P(("dp", "op"), None, None),
            P(None, "op", "dp", None),
            P(None, "op", "dp", None),
            P(None, "op", "dp", None),
            P(None, "op", "dp", None),
            P(None, "op", None, "dp"),
            P(None, "op", None, "dp", None),
            P(None, "op", None, "dp"),
            P(None, "op", None, "dp"),
        ),
        check_vma=False,
    )
```

time: 2510 us -> 1750 us (0.70)
  matrix products: 654 us -> 0 us
  Pallas kernels: 0 us -> 507 us
  other arithmetic: 509 us -> 44.6 us
  local copies, waits for them, and re-layouts: 242 us -> 7.28 us
  blocking collectives: 155 us -> 191 us
  waiting for transfers between devices: 872 us -> 907 us
    dot_general x52 -> x0, matrix products: 616 us -> none  [matrix_product(): jnp.einsum(einsum_form, operand_a, operand_b, preferred_element_type=jnp....]
    pallas_call x0 -> x19, Pallas kernels: none -> 507 us  [the longest x2 94.4 us: attention_backward(): pl.pallas_call(kernel, grid_spec=pltpu.PrefetchScalarGridSpec(num_scalar_...]
    convert_element_type x26 -> x2, other arithmetic: 215 us -> 1.44 us  [per_device(): lax.psum_scatter(small, 'dp', scatter_dimension=0, tiled=True)[0]]
    gather x18 -> x1, local copies, waits for them, and re-layouts: 171 us -> 0.66 us  [per_device(): jnp.repeat(total[1:KINDS - 1], jnp.array([3, 5, 7]), total_repeat_length=15)]
    unnamed x44 -> x5, other arithmetic: 110 us -> 10.2 us
    reduce_sum x25 -> x1, other arithmetic: 70.8 us -> 0.15 us  [per_device(): totals = jnp.sum((everyone[:, :, None] == own).astype(F32), axis=0)]
    select_n x20 -> x0, other arithmetic: 62.2 us -> none  [the longest x6 60.6 us: take_rows(): jnp.where(present[:, None, None], source_rows[row_ids], jnp.zeros((), sou...]
    all_gather x0 -> x1, blocking collectives: none -> 43.5 us  [per_device(): everyone = lax.all_gather(candidate, ('dp', 'op'), axis=0, tiled=True)]
  transfers between devices with their start and end apart: 17 -> 19, of which waited for: 7 -> 8; matrix products, arithmetic and copies ran while one was open for 21% -> 3% of each run, Pallas kernels for 0% -> 14%
where the time goes in v1:
time: 1750 us; the launch traced here: 1740 us
  waiting for transfers between devices  907 us (52%)
  Pallas kernels  507 us (29%)
  blocking collectives  191 us (11%)
  starting transfers between devices  70.5 us (4%)
  other arithmetic  44.6 us (3%)
    all_to_all x7, waiting for transfers between devices, exchange(): return lax.all_to_all(rows, 'op', split_axis=0, concat_axis=0, tiled=True)  742 us
    reduce_scatter x10, waiting for transfers between devices, scatter(): lax.psum_scatter(grad, 'dp', scatter_dimension=dim, tiled=True).astype(F32)  159 us
    all_to_all x1, blocking collectives, exchange(): return lax.all_to_all(rows, 'op', split_axis=0, concat_axis=0, tiled=True)  148 us
    pallas_call x2, Pallas kernels, attention_backward(): pl.pallas_call(kernel, grid_spec=pltpu.PrefetchScalarGridSpec(num_scalar_...  94.4 us
    pallas_call x2, Pallas kernels, conv_backward(): pl.pallas_call(kernel, grid_spec=pltpu.PrefetchScalarGridSpec(num_scalar_...  87.7 us
    pallas_call x2, Pallas kernels, feed_backward(): pl.pallas_call(kernel, grid_spec=pltpu.PrefetchScalarGridSpec(num_scalar_...  87.6 us
    pallas_call x6, Pallas kernels, permute_rows(): pl.pallas_call(kernel, grid_spec=pltpu.PrefetchScalarGridSpec(num_scalar_...  87 us
    all_to_all x7, starting transfers between devices, exchange(): return lax.all_to_all(rows, 'op', split_axis=0, concat_axis=0, tiled=True)  70 us
  transfers between devices with their start and end apart: 19, of which 8 were waited for; matrix products, arithmetic and copies ran while one was open for 3% of the time, Pallas kernels for 14%

profile of v1, /device:TPU:0, one launch (start us, length us, event | category | flops | bytes accessed | tf_op | source)
XLA Modules:
  0.0 1742.1 jit_solution(13379414449465066821)
XLA Ops:
  7.2 43.5 %all-gather = s32[32,12,2]{1,2,0:T(2,128)S(1)} all-gather(s32[1,12,2]{1,2,0:T(2,128)} %bitcast.136), channel_id=1, replica_groups=mesh['dp'=4,'op'=8] {'dp','op'}, dimensions={0}, use_global_device_ids=true | all-gather | bytes 3168 | tf_op jit(solution)/shard_map/all_gather | solution.py:945
  51.6 0.7 reshape.213.refs_0_
  52.3 6.5 tables.1
  58.8 15.7 permute.6
  74.5 5.5 all-to-all-start
  81.5 137.5 %all-to-all-done.x_ref = bf16[16,512,768]{2,1,0:T(8,128)(2,1)} async-done(((bf16[16,512,768]{2,1,0:T(8,128)(2,1)}), bf16[16,512,768]{2,1,0:T(8,128)(2,1)}, u32[]{:S(2)}, u32[]{:S(2)}) %all-to-all-start) | async-done | bytes 12582944 | tf_op jit(solution)/shard_map/all_to_all | solution.py:920
  219.0 29.3 %feed_forward.2 = (bf16[16,512,768]{2,1,0:T(8,128)(2,1)}, bf16[3,512,3072]{2,1,0:T(8,128)(2,1)}, bf16[3,512,3072]{2,1,0:T(8,128)(2,1)}, bf16[3,512,768]{2,1,0:T(8,128)(2,1)}, f32[3,512,128]{2,1,0:T(8,128)}) custom-call(s32[30]{0:T(128)} %get-tuple-element.92.rows_ref, s32[16]{0:T(128)} %get-tuple-element.93.counts_ref, ...), custom_call_target="tpu_custom_call" | custom-call | flops 14495514624 | bytes 41943040 | tf_op jit(solution)/shard_map/feed_forward/pallas_call | solution.py:487
  248.3 20.0 %attention_forward.2 = (bf16[16,512,768]{2,1,0:T(8,128)(2,1)}, bf16[3,512,2304]{2,1,0:T(8,128)(2,1)}, bf16[3,512,768]{2,1,0:T(8,128)(2,1)}, bf16[3,512,768]{2,1,0:T(8,128)(2,1)}, f32[3,512,128]{2,1,0:T(8,128)}) custom-call(s32[30]{0:T(128)} %get-tuple-element.92.rows_ref, s32[16]{0:T(128)} %get-tuple-element.93.counts_ref, ...), custom_call_target="tpu_custom_call", output_to_operand_aliasing={{0}: (7, {})} | custom-call | flops 19327352832 | bytes 31457280 | tf_op jit(solution)/shard_map/attention_forward/pallas_call | solution.py:250
  268.4 23.6 %conv_forward.2 = (bf16[16,512,768]{2,1,0:T(8,128)(2,1)}, bf16[9,512,768]{2,1,0:T(8,128)(2,1)}, bf16[9,512,768]{2,1,0:T(8,128)(2,1)}, f32[9,512,128]{2,1,0:T(8,128)}) custom-call(s32[30]{0:T(128)} %get-tuple-element.92.rows_ref, s32[16]{0:T(128)} %get-tuple-element.93.counts_ref, ...), custom_call_target="tpu_custom_call", output_to_operand_aliasing={{0}: (7, {})} | custom-call | flops 5435817984 | bytes 37748736 | tf_op jit(solution)/shard_map/conv_forward/pallas_call | solution.py:731
  292.0 147.9 %all_to_all.40.in_ref = bf16[16,512,768]{2,1,0:T(8,128)(2,1)} all-to-all(bf16[16,512,768]{2,1,0:T(8,128)(2,1)} %get-tuple-element.98), channel_id=1, replica_groups=mesh['dp'=4,'op'=8] {'op'}, dimensions={0} | all-to-all | bytes 25165824 | tf_op jit(solution)/shard_map/all_to_all | solution.py:920
  439.9 15.6 permute.7
  455.5 5.3 all-to-all-start.2
  460.9 15.6 permute.9
  476.5 123.4 %all-to-all-done.2.x_ref = bf16[16,512,768]{2,1,0:T(8,128)(2,1)} async-done(((bf16[16,512,768]{2,1,0:T(8,128)(2,1)}), bf16[16,512,768]{2,1,0:T(8,128)(2,1)}, u32[]{:S(2)}, u32[]{:S(2)}) %all-to-all-start.2) | async-done | bytes 12582944 | tf_op jit(solution)/shard_map/all_to_all | solution.py:920
  599.9 5.3 all-to-all-start.4
  607.1 26.9 %feed_forward.3 = (bf16[16,512,768]{2,1,0:T(8,128)(2,1)}, bf16[3,512,3072]{2,1,0:T(8,128)(2,1)}, bf16[3,512,3072]{2,1,0:T(8,128)(2,1)}, bf16[3,512,768]{2,1,0:T(8,128)(2,1)}, f32[3,512,128]{2,1,0:T(8,128)}) custom-call(s32[30]{0:T(128)} %get-tuple-element.92.rows_ref, s32[16]{0:T(128)} %get-tuple-element.93.counts_ref, ...), custom_call_target="tpu_custom_call" | custom-call | flops 14495514624 | bytes 41943040 | tf_op jit(solution)/shard_map/feed_forward/pallas_call | solution.py:487
  634.0 20.0 %attention_forward.3 = (bf16[16,512,768]{2,1,0:T(8,128)(2,1)}, bf16[3,512,2304]{2,1,0:T(8,128)(2,1)}, bf16[3,512,768]{2,1,0:T(8,128)(2,1)}, bf16[3,512,768]{2,1,0:T(8,128)(2,1)}, f32[3,512,128]{2,1,0:T(8,128)}) custom-call(s32[30]{0:T(128)} %get-tuple-element.92.rows_ref, s32[16]{0:T(128)} %get-tuple-element.93.counts_ref, ...), custom_call_target="tpu_custom_call", output_to_operand_aliasing={{0}: (7, {})} | custom-call | flops 19327352832 | bytes 31457280 | tf_op jit(solution)/shard_map/attention_forward/pallas_call | solution.py:250
  654.1 23.4 %conv_forward.3 = (bf16[16,512,768]{2,1,0:T(8,128)(2,1)}, bf16[9,512,768]{2,1,0:T(8,128)(2,1)}, bf16[9,512,768]{2,1,0:T(8,128)(2,1)}, f32[9,512,128]{2,1,0:T(8,128)}) custom-call(s32[30]{0:T(128)} %get-tuple-element.92.rows_ref, s32[16]{0:T(128)} %get-tuple-element.93.counts_ref, ...), custom_call_target="tpu_custom_call", output_to_operand_aliasing={{0}: (7, {})} | custom-call | flops 5435817984 | bytes 37748736 | tf_op jit(solution)/shard_map/conv_forward/pallas_call | solution.py:731
  677.5 66.7 %all-to-all-done.4.dy_ref = bf16[16,512,768]{2,1,0:T(8,128)(2,1)} async-done(((bf16[16,512,768]{2,1,0:T(8,128)(2,1)}), bf16[16,512,768]{2,1,0:T(8,128)(2,1)}, u32[]{:S(2)}, u32[]{:S(2)}) %all-to-all-start.4) | async-done | bytes 12582944 | tf_op jit(solution)/shard_map/all_to_all | solution.py:920
  744.2 40.7 %feed_backward.2 = (bf16[16,512,768]{2,1,0:T(8,128)(2,1)}, bf16[768,3072]{1,0:T(8,128)(2,1)}, bf16[3072,768]{1,0:T(8,128)(2,1)}, f32[8,768]{1,0:T(8,128)}) custom-call(s32[30]{0:T(128)} %get-tuple-element.92.rows_ref, s32[16]{0:T(128)} %get-tuple-element.93.counts_ref, bf16[16,512,768]{2,1,0:T(8,128)(2,1)} %all-to-all-done.2.x_ref, ...), custom_call_target="tpu_custom_call" | custom-call | flops 28991029248 | bytes 52428800 | tf_op jit(solution)/shard_map/feed_backward/pallas_call | solution.py:617
  784.9 47.2 %attention_backward.2 = (bf16[16,512,768]{2,1,0:T(8,128)(2,1)}, bf16[768,2304]{1,0:T(8,128)(2,1)}, bf16[768,768]{1,0:T(8,128)(2,1)}, f32[8,768]{1,0:T(8,128)}) custom-call(s32[30]{0:T(128)} %get-tuple-element.92.rows_ref, s32[16]{0:T(128)} %get-tuple-element.93.counts_ref, ...), custom_call_target="tpu_custom_call", output_to_operand_aliasing={{0}: (11, {})} | custom-call | flops 38654705664 | bytes 41943040 | tf_op jit(solution)/shard_map/attention_backward/pallas_call | solution.py:374
  832.1 44.4 %conv_backward.2 = (bf16[16,512,768]{2,1,0:T(8,128)(2,1)}, bf16[3,768,768]{2,1,0:T(8,128)(2,1)}, f32[24,768]{1,0:T(8,128)}) custom-call(s32[30]{0:T(128)} %get-tuple-element.92.rows_ref, s32[16]{0:T(128)} %get-tuple-element.93.counts_ref, bf16[16,512,768]{2,1,0:T(8,128)(2,1)} %all-to-all-done.2.x_ref, ...), custom_call_target="tpu_custom_call", output_to_operand_aliasing={{0}: (10, {})} | custom-call | flops 10871635968 | bytes 52428800 | tf_op jit(solution)/shard_map/conv_backward/pallas_call | solution.py:847
  876.6 0.9 convert.61
  878.5 0.7 reduce-scatter.19.cloned.1.call-update
  879.2 0.7 reduce-scatter.35.cloned.1.call-update
  879.9 24.8 %all-to-all-start.5 = ((bf16[16,512,768]{2,1,0:T(8,128)(2,1)}), bf16[16,512,768]{2,1,0:T(8,128)(2,1)}, u32[]{:S(2)}, u32[]{:S(2)}) async-start(bf16[16,512,768]{2,1,0:T(8,128)(2,1)} %get-tuple-element.116), calls=%async_computation.5 | async-start | bytes 25165824 | tf_op jit(solution)/shard_map/all_to_all | solution.py:920
  905.3 138.5 %all-to-all-done.5.in_ref = bf16[16,512,768]{2,1,0:T(8,128)(2,1)} async-done(((bf16[16,512,768]{2,1,0:T(8,128)(2,1)}), bf16[16,512,768]{2,1,0:T(8,128)(2,1)}, u32[]{:S(2)}, u32[]{:S(2)}) %all-to-all-start.5) | async-done | bytes 12582944 | tf_op jit(solution)/shard_map/all_to_all | solution.py:920
  1043.8 15.7 permute.10
  1059.5 5.3 all-to-all-start.6
  1066.1 137.8 %all-to-all-done.6.dy_ref = bf16[16,512,768]{2,1,0:T(8,128)(2,1)} async-done(((bf16[16,512,768]{2,1,0:T(8,128)(2,1)}), bf16[16,512,768]{2,1,0:T(8,128)(2,1)}, u32[]{:S(2)}, u32[]{:S(2)}) %all-to-all-start.6) | async-done | bytes 12582944 | tf_op jit(solution)/shard_map/all_to_all | solution.py:920
  1203.9 46.9 %feed_backward.3 = (bf16[16,512,768]{2,1,0:T(8,128)(2,1)}, bf16[768,3072]{1,0:T(8,128)(2,1)}, bf16[3072,768]{1,0:T(8,128)(2,1)}, f32[8,768]{1,0:T(8,128)}) custom-call(s32[30]{0:T(128)} %get-tuple-element.92.rows_ref, s32[16]{0:T(128)} %get-tuple-element.93.counts_ref, bf16[16,512,768]{2,1,0:T(8,128)(2,1)} %all-to-all-done.x_ref, ...), custom_call_target="tpu_custom_call" | custom-call | flops 28991029248 | bytes 52428800 | tf_op jit(solution)/shard_map/feed_backward/pallas_call | solution.py:617
  1250.8 47.2 %attention_backward.3 = (bf16[16,512,768]{2,1,0:T(8,128)(2,1)}, bf16[768,2304]{1,0:T(8,128)(2,1)}, bf16[768,768]{1,0:T(8,128)(2,1)}, f32[8,768]{1,0:T(8,128)}) custom-call(s32[30]{0:T(128)} %get-tuple-element.92.rows_ref, s32[16]{0:T(128)} %get-tuple-element.93.counts_ref, ...), custom_call_target="tpu_custom_call", output_to_operand_aliasing={{0}: (11, {})} | custom-call | flops 38654705664 | bytes 41943040 | tf_op jit(solution)/shard_map/attention_backward/pallas_call | solution.py:374
  1298.0 0.7 convert.59
  1298.8 43.3 %conv_backward.3 = (bf16[16,512,768]{2,1,0:T(8,128)(2,1)}, bf16[3,768,768]{2,1,0:T(8,128)(2,1)}, f32[24,768]{1,0:T(8,128)}) custom-call(s32[30]{0:T(128)} %get-tuple-element.92.rows_ref, s32[16]{0:T(128)} %get-tuple-element.93.counts_ref, bf16[16,512,768]{2,1,0:T(8,128)(2,1)} %all-to-all-done.x_ref, ...), custom_call_target="tpu_custom_call", output_to_operand_aliasing={{0}: (10, {})} | custom-call | flops 10871635968 | bytes 52428800 | tf_op jit(solution)/shard_map/conv_backward/pallas_call | solution.py:847
  1342.0 0.9 convert.58
  1343.9 0.7 reduce-scatter.17.cloned.1.call-update
  1344.7 0.7 reduce-scatter.33.cloned.1.call-update
  1345.9 18.3 %all-to-all-start.3 = ((bf16[16,512,768]{2,1,0:T(8,128)(2,1)}), bf16[16,512,768]{2,1,0:T(8,128)(2,1)}, u32[]{:S(2)}, u32[]{:S(2)}) async-start(bf16[16,512,768]{2,1,0:T(8,128)(2,1)} %get-tuple-element.101), calls=%async_computation.3 | async-start | bytes 25165824 | tf_op jit(solution)/shard_map/all_to_all | solution.py:920
  1364.3 0.7 reduce-scatter.25.cloned.1.call-update
  1365.0 138.4 %all-to-all-done.3.in_ref = bf16[16,512,768]{2,1,0:T(8,128)(2,1)} async-done(((bf16[16,512,768]{2,1,0:T(8,128)(2,1)}), bf16[16,512,768]{2,1,0:T(8,128)(2,1)}, u32[]{:S(2)}, u32[]{:S(2)}) %all-to-all-start.3) | async-done | bytes 12582944 | tf_op jit(solution)/shard_map/all_to_all | solution.py:920
  1503.3 5.4 all-to-all-start.7
  1510.5 0.7 fusion.22
  1511.2 3.7 select_select_fusion.1
  1514.9 0.7 convert_element_type.107
  1515.8 1.7 divide_bitcast_fusion.8
  1517.5 2.6 divide_bitcast_fusion.4
  1520.1 3.2 divide_bitcast_fusion.6
  1523.3 3.5 divide_bitcast_fusion
  1526.8 2.2 divide_bitcast_fusion.2
  1529.0 12.2 permute.8
  1541.2 0.7 convert_element_type.104
  1543.9 1.7 divide_bitcast_fusion.9
  1545.6 1.1 maximum_bitcast_fusion.4
  1546.7 1.5 divide_bitcast_fusion.5
  1548.5 2.0 maximum_bitcast_fusion.3
  1550.5 2.4 divide_bitcast_fusion.7
  1552.9 2.0 maximum_bitcast_fusion.2
  1554.9 75.3 %reduce-scatter.25.cloned.1.call-done = bf16[768,768]{1,0:T(8,128)(2,1)} async-done(((bf16[3072,768]{1,0:T(8,128)(2,1)}), bf16[768,768]{1,0:T(8,128)(2,1)}) %reduce-scatter.25.cloned.1.call-update) | async-done | bytes 1179664 | tf_op jit(solution)/shard_map/reduce_scatter | solution.py:968
  1630.2 2.2 divide_bitcast_fusion.1
  1632.5 2.5 maximum_bitcast_fusion.1
  1634.9 83.2 %reduce-scatter.21.cloned.1.call-done = bf16[192,3072]{1,0:T(8,128)(2,1)} async-done(((bf16[768,3072]{1,0:T(8,128)(2,1)}), bf16[192,3072]{1,0:T(8,128)(2,1)}) %reduce-scatter.21.cloned.1.call-update) | async-done | bytes 1179664 | tf_op jit(solution)/shard_map/reduce_scatter | solution.py:968
  1718.2 2.1 divide_bitcast_fusion.3
  1720.3 2.6 maximum_bitcast_fusion
  1722.9 12.2 permute.11
  (108 shorter events, 12.7 us)
Async XLA Ops:
  50.8 0.6 copy-start.9
  74.5 5.5 copy-start.4
  74.5 5.6 copy-start.5
  74.5 5.6 copy-start.3
  74.5 144.5 %all-to-all-start = ((bf16[16,512,768]{2,1,0:T(8,128)(2,1)}), bf16[16,512,768]{2,1,0:T(8,128)(2,1)}, u32[]{:S(2)}, u32[]{:S(2)}) async-start(bf16[16,512,768]{2,1,0:T(8,128)(2,1)} %permute.6), calls=%async_computation | async-start | bytes 25165824 | tf_op jit(solution)/shard_map/all_to_all | solution.py:920
  455.5 144.4 %all-to-all-start.2 = ((bf16[16,512,768]{2,1,0:T(8,128)(2,1)}), bf16[16,512,768]{2,1,0:T(8,128)(2,1)}, u32[]{:S(2)}, u32[]{:S(2)}) async-start(bf16[16,512,768]{2,1,0:T(8,128)(2,1)} %permute.7), calls=%async_computation.2 | async-start | bytes 25165824 | tf_op jit(solution)/shard_map/all_to_all | solution.py:920
  599.9 144.3 %all-to-all-start.4 = ((bf16[16,512,768]{2,1,0:T(8,128)(2,1)}), bf16[16,512,768]{2,1,0:T(8,128)(2,1)}, u32[]{:S(2)}, u32[]{:S(2)}) async-start(bf16[16,512,768]{2,1,0:T(8,128)(2,1)} %permute.9), calls=%async_computation.4 | async-start | bytes 25165824 | tf_op jit(solution)/shard_map/all_to_all | solution.py:920
  605.2 909.7 %reduce-scatter.31.cloned.1.call-start = ((), (), s32[]{:S(2)}) async-start(), calls=%async_computation.29 | async-start | bytes 81920 | tf_op jit(solution)/shard_map/reduce_scatter | solution.py:974
  832.1 45.4 %copy-start.7 = (f32[8,768]{1,0:T(8,128)S(1)}, f32[8,768]{1,0:T(8,128)}, u32[]{:S(2)}) copy-start(f32[8,768]{1,0:T(8,128)} %get-tuple-element.143) | copy-start | bytes 73732
  832.1 45.4 %copy-start.6 = (f32[8,768]{1,0:T(8,128)S(1)}, f32[8,768]{1,0:T(8,128)}, u32[]{:S(2)}) copy-start(f32[8,768]{1,0:T(8,128)} %get-tuple-element.144) | copy-start | bytes 73732
  878.4 637.4 %reduce-scatter.19.cloned.1.call-start = ((), (), s32[]{:S(2)}) async-start(), calls=%async_computation.23 | async-start | bytes 1474560 | tf_op jit(solution)/shard_map/reduce_scatter | solution.py:968
  879.2 638.3 %reduce-scatter.35.cloned.1.call-start = ((), (), s32[]{:S(2)}) async-start(), calls=%async_computation.31 | async-start | bytes 4423680 | tf_op jit(solution)/shard_map/reduce_scatter | solution.py:968
  879.9 163.9 %all-to-all-start.5 = ((bf16[16,512,768]{2,1,0:T(8,128)(2,1)}), bf16[16,512,768]{2,1,0:T(8,128)(2,1)}, u32[]{:S(2)}, u32[]{:S(2)}) async-start(bf16[16,512,768]{2,1,0:T(8,128)(2,1)} %get-tuple-element.116), calls=%async_computation.5 | async-start | bytes 25165824 | tf_op jit(solution)/shard_map/all_to_all | solution.py:920
  904.7 615.4 %reduce-scatter.15.cloned.1.call-start = ((), (), s32[]{:S(2)}) async-start(), calls=%async_computation.21 | async-start | bytes 4423680 | tf_op jit(solution)/shard_map/reduce_scatter | solution.py:968
  1059.5 144.4 %all-to-all-start.6 = ((bf16[16,512,768]{2,1,0:T(8,128)(2,1)}), bf16[16,512,768]{2,1,0:T(8,128)(2,1)}, u32[]{:S(2)}, u32[]{:S(2)}) async-start(bf16[16,512,768]{2,1,0:T(8,128)(2,1)} %permute.10), calls=%async_computation.6 | async-start | bytes 25165824 | tf_op jit(solution)/shard_map/all_to_all | solution.py:920
  1064.8 458.4 %reduce-scatter.27.cloned.1.call-start = ((), (), s32[]{:S(2)}) async-start(), calls=%async_computation.27 | async-start | bytes 5898240 | tf_op jit(solution)/shard_map/reduce_scatter | solution.py:968
  1065.4 461.3 %reduce-scatter.23.cloned.1.call-start = ((), (), s32[]{:S(2)}) async-start(), calls=%async_computation.25 | async-start | bytes 5898240 | tf_op jit(solution)/shard_map/reduce_scatter | solution.py:968
  1066.0 475.1 %reduce-scatter.29.cloned.1.call-start = ((), (), s32[]{:S(2)}) async-start(), calls=%async_computation.28 | async-start | bytes 81920 | tf_op jit(solution)/shard_map/reduce_scatter | solution.py:974
  1250.8 48.0 %copy-start.8 = (f32[8,768]{1,0:T(8,128)S(1)}, f32[8,768]{1,0:T(8,128)}, u32[]{:S(2)}) copy-start(f32[8,768]{1,0:T(8,128)} %get-tuple-element.141) | copy-start | bytes 73732
  1343.9 200.1 %reduce-scatter.17.cloned.1.call-start = ((), (), s32[]{:S(2)}) async-start(), calls=%async_computation.22 | async-start | bytes 1474560 | tf_op jit(solution)/shard_map/reduce_scatter | solution.py:968
  1344.6 202.1 %reduce-scatter.33.cloned.1.call-start = ((), (), s32[]{:S(2)}) async-start(), calls=%async_computation.30 | async-start | bytes 4423680 | tf_op jit(solution)/shard_map/reduce_scatter | solution.py:968
  1345.3 205.1 %reduce-scatter.13.cloned.1.call-start = ((), (), s32[]{:S(2)}) async-start(), calls=%async_computation.20 | async-start | bytes 4423680 | tf_op jit(solution)/shard_map/reduce_scatter | solution.py:968
  1345.9 157.4 %all-to-all-start.3 = ((bf16[16,512,768]{2,1,0:T(8,128)(2,1)}), bf16[16,512,768]{2,1,0:T(8,128)(2,1)}, u32[]{:S(2)}, u32[]{:S(2)}) async-start(bf16[16,512,768]{2,1,0:T(8,128)(2,1)} %get-tuple-element.101), calls=%async_computation.3 | async-start | bytes 25165824 | tf_op jit(solution)/shard_map/all_to_all | solution.py:920
  1364.2 266.0 %reduce-scatter.25.cloned.1.call-start = ((), (), s32[]{:S(2)}) async-start(), calls=%async_computation.26 | async-start | bytes 5898240 | tf_op jit(solution)/shard_map/reduce_scatter | solution.py:968
  1503.3 219.6 %all-to-all-start.7 = ((bf16[16,512,768]{2,1,0:T(8,128)(2,1)}), bf16[16,512,768]{2,1,0:T(8,128)(2,1)}, u32[]{:S(2)}, u32[]{:S(2)}) async-start(bf16[16,512,768]{2,1,0:T(8,128)(2,1)} %get-tuple-element.130), calls=%async_computation.7 | async-start | bytes 25165824 | tf_op jit(solution)/shard_map/all_to_all | solution.py:920
  1508.7 0.7 copy-start.10
  1508.7 2.5 copy-start.11
  1508.7 2.4 copy-start.12
  1508.7 209.4 %reduce-scatter.21.cloned.1.call-start = ((), (), s32[]{:S(2)}) async-start(), calls=%async_computation.24 | async-start | bytes 5898240 | tf_op jit(solution)/shard_map/reduce_scatter | solution.py:968
  1546.7 1.7 copy-start.2
  1550.5 2.4 copy-start.1
  1630.2 2.2 copy-start
Sparse Core Ops, SparseCore 0:
  878.5 38.2 reduce-scatter.30
  919.9 27.3 reduce-scatter.18
  950.3 65.0 reduce-scatter.34
  1018.2 66.6 reduce-scatter.14
  1087.7 85.5 reduce-scatter.26
  1176.1 85.7 reduce-scatter.22
  1344.0 31.7 reduce-scatter.28
  1378.1 27.4 reduce-scatter.16
  1407.8 65.0 reduce-scatter.32
  1475.7 66.6 reduce-scatter.12
  1544.7 85.5 reduce-scatter.24
  1632.4 85.7 reduce-scatter.20

commit v2 on v1

--- a/solution.py
+++ b/solution.py
@@ -9,9 +9,12 @@
 KINDS = 5
 BLOCKS = 2
 OWN_CAP = 3
-FF_PART = 1024
-FF_SUB = 512
+HALVES = 2
+SLOTS = KINDS * OWN_CAP
+FF_PART = 768
+FF_SUB = 256
 LANES = 128
+SMALL_ROWS = 16
 BF16 = jnp.bfloat16
 F32 = jnp.float32
 VMEM_BYTES = 60 * 2**20
@@ -35,120 +38,240 @@
     return lax.dot_general(a, b, (((0,), (0,)), ((), ())), preferred_element_type=F32)
 
 
-def table_kernel(owners, cap, seqs, cand, me_ref, src, pos, rows, counts, relay_in, relay_out, fill):
-    me = me_ref[0]
-    slots = owners * cap
+def home_kernel(owners, seqs, cand, send, relay, tags, color, partner, first, tally):
     for b in range(BLOCKS):
 
-        def clear_slot(s, _):
-            src[b * slots + s] = -1
+        def clear_owner(o, _):
+            first[b * owners + o] = -1
+            for half in range(HALVES):
+                send[(b * HALVES + half) * owners + o] = -1
+                relay[(b * HALVES + half) * owners + o] = -1
+                tags[o * BLOCKS * HALVES + b * HALVES + half] = KINDS
             return 0
 
-        lax.fori_loop(0, slots, clear_slot, 0)
-
-        def clear_fill(o, _):
-            fill[o] = 0
-            return 0
-
-        lax.fori_loop(0, owners, clear_fill, 0)
-        for k in range(8):
-            counts[b * 8 + k] = 0
-
-        def one_home(h, _):
-            def one_seq(j, _):
-                c = cand[(h * seqs + j) * BLOCKS + b]
-                o = lax.rem(c, owners)
-                k = lax.div(c, owners)
-                stamp = h * (cap + 1)
-                before = fill[o]
-                r = jnp.minimum(jnp.maximum(before - stamp, 0), cap - 1)
-                fill[o] = stamp + r + 1
-
-                @pl.when(h == me)
-                def _():
-                    src[b * slots + o * cap + r] = j
-                    pos[b * seqs + j] = o * cap + r
-
-                @pl.when(o == me)
-                def _():
-                    n = jnp.minimum(counts[b * 8 + k], OWN_CAP - 1)
-                    rows[b * KINDS * OWN_CAP + k * OWN_CAP + n] = h * cap + r
-                    counts[b * 8 + k] = n + 1
-
-                return 0
-
-            return lax.fori_loop(0, seqs, one_seq, 0)
-
-        lax.fori_loop(0, owners, one_home, 0)
-        for k in range(KINDS):
-            base = b * KINDS * OWN_CAP + k * OWN_CAP
-            for i in range(1, OWN_CAP):
-                rows[base + i] = jnp.where(
-                    i < counts[b * 8 + k], rows[base + i], rows[base + i - 1]
-                )
-
-        def fill_slot(s, last):
-            now = src[b * slots + s]
-            now = jnp.where(now < 0, last, now)
-            src[b * slots + s] = now
-            return now
-
-        lax.fori_loop(0, slots, fill_slot, 0)
-
-    def relays(s, _):
-        relay_in[s] = pos[src[slots + s]]
-        relay_out[s] = pos[seqs + src[s]]
+        lax.fori_loop(0, owners, clear_owner, 0)
+    for half in range(HALVES):
+        tally[half] = 0
+
+    def pair_up(j, _):
+        color[j] = -1
+        for b in range(BLOCKS):
+            o = b * owners + lax.rem(cand[j * BLOCKS + b], owners)
+            other = first[o]
+            partner[b * seqs + j] = other
+            first[o] = j
+
+            @pl.when(other >= 0)
+            def _():
+                partner[b * seqs + other] = j
+
         return 0
 
-    lax.fori_loop(0, slots, relays, 0)
-
-
-def make_tables(group, me, owners, cap, seqs):
-    slots = owners * cap
-
+    lax.fori_loop(0, seqs, pair_up, 0)
+
+    def give(j, shade):
+        color[j] = shade
+        tally[shade] = tally[shade] + 1
+
+    def paint(j, _):
+        @pl.when(color[j] < 0)
+        def _():
+            shade = jnp.where(tally[0] > tally[1], 1, 0).astype(jnp.int32)
+            give(j, shade)
+            for side in range(2):
+
+                def more(state):
+                    return state[0] >= 0
+
+                def walk(state):
+                    now, use, tone = state
+                    after = partner[use * seqs + now]
+                    free = jnp.logical_and(after >= 0, color[jnp.maximum(after, 0)] < 0)
+
+                    @pl.when(free)
+                    def _():
+                        give(after, 1 - tone)
+
+                    return (jnp.where(free, after, -1), 1 - use, 1 - tone)
+
+                lax.while_loop(more, walk, (j, jnp.int32(side), shade))
+
+        return 0
+
+    lax.fori_loop(0, seqs, paint, 0)
+
+    def place(j, _):
+        half = color[j]
+        spots = []
+        for b in range(BLOCKS):
+            c = cand[j * BLOCKS + b]
+            o = lax.rem(c, owners)
+            spots.append(o)
+            send[(b * HALVES + half) * owners + o] = j
+            tags[o * BLOCKS * HALVES + b * HALVES + half] = lax.div(c, owners)
+        relay[half * owners + spots[1]] = spots[0]
+        relay[(HALVES + half) * owners + spots[0]] = spots[1]
+        return 0
+
+    lax.fori_loop(0, seqs, place, 0)
+
+
+SMEM_SPEC = pl.BlockSpec(memory_space=pltpu.SMEM)
+ANY_SPEC = pl.BlockSpec(memory_space=pl.ANY)
+
+
+def int_shape(n):
+    return jax.ShapeDtypeStruct((n,), jnp.int32)
+
+
+def home_tables(cand, owners, seqs):
     def kernel(*refs):
-        table_kernel(owners, cap, seqs, *refs)
-
-    smem = pl.BlockSpec(memory_space=pltpu.SMEM)
-    shape = lambda n: jax.ShapeDtypeStruct((n,), jnp.int32)
+        home_kernel(owners, seqs, *refs)
+
+    size = BLOCKS * HALVES * owners
     return pl.pallas_call(
         kernel,
-        in_specs=[smem, smem],
-        out_specs=[smem] * 6,
-        out_shape=[
-            shape(BLOCKS * slots),
-            shape(BLOCKS * seqs),
-            shape(BLOCKS * KINDS * OWN_CAP),
-            shape(BLOCKS * 8),
-            shape(slots),
-            shape(slots),
+        in_specs=[SMEM_SPEC],
+        out_specs=[SMEM_SPEC] * 3,
+        out_shape=[int_shape(size)] * 3,
+        scratch_shapes=[
+            pltpu.SMEM((seqs,), jnp.int32),
+            pltpu.SMEM((BLOCKS * seqs,), jnp.int32),
+            pltpu.SMEM((BLOCKS * owners,), jnp.int32),
+            pltpu.SMEM((HALVES,), jnp.int32),
         ],
-        scratch_shapes=[pltpu.SMEM((max(owners, 8),), jnp.int32)],
-        name="tables",
-    )(group, me)
-
-
-def permute_rows(table, source, start, count):
-    length, width = source.shape[1:]
-
-    def kernel(table_ref, in_ref, out_ref):
-        out_ref[...] = in_ref[...]
+        name="home_tables",
+    )(cand)
+
+
+def owner_kernel(owners, tags, rows, counts):
+    for b in range(BLOCKS):
+        for half in range(HALVES):
+            part = b * HALVES + half
+            for k in range(8):
+                counts[part * 8 + k] = 0
+
+            def arrive(h, free):
+                k = tags[h * BLOCKS * HALVES + part]
+                there = k < KINDS
+
+                @pl.when(there)
+                def _():
+                    n = jnp.minimum(counts[part * 8 + k], OWN_CAP - 1)
+                    rows[part * SLOTS + k * OWN_CAP + n] = h
+                    counts[part * 8 + k] = n + 1
+
+                return jnp.where(there, free, h)
+
+            free = lax.fori_loop(0, owners, arrive, jnp.int32(0))
+
+            def spare(k, otherwise):
+                return jnp.where(
+                    counts[part * 8 + k] > 0, rows[part * SLOTS + k * OWN_CAP], otherwise
+                )
+
+            conv_spare = free
+            for k in reversed(range(1, KINDS - 1)):
+                conv_spare = spare(k, conv_spare)
+            attn_spare = spare(0, conv_spare)
+            feed_spare = spare(KINDS - 1, attn_spare)
+            last = conv_spare
+            for k, start in ((1, None), (2, None), (3, None), (0, attn_spare), (KINDS - 1, feed_spare)):
+                last = last if start is None else start
+                for i in range(OWN_CAP):
+                    at = part * SLOTS + k * OWN_CAP + i
+                    last = jnp.where(i < counts[part * 8 + k], rows[at], last)
+                    rows[at] = last
+
+
+def owner_tables(tags, owners):
+    def kernel(*refs):
+        owner_kernel(owners, *refs)
+
+    return pl.pallas_call(
+        kernel,
+        in_specs=[SMEM_SPEC],
+        out_specs=[SMEM_SPEC] * 2,
+        out_shape=[int_shape(BLOCKS * HALVES * SLOTS), int_shape(BLOCKS * HALVES * 8)],
+        name="owner_tables",
+    )(tags)
+
+
+def move_rows(table, starts, sources, count, scatter, name, wait_for=()):
+    length, width = sources[0].shape[1:]
+    each = table.shape[0] // (BLOCKS * HALVES)
+    total = each * len(sources)
+
+    def kernel(table_ref, *refs):
+        ins = refs[: len(sources)]
+        out_ref, buf, sem_in, sem_out = refs[-4:]
+
+        def load(part, s):
+            idx = table_ref[starts[part] + s]
+            at = s if scatter else idx
+            to = part * each + s
+            return pltpu.make_async_copy(ins[part].at[at], buf.at[to], sem_in.at[to])
+
+        def store(part, s):
+            idx = table_ref[starts[part] + s]
+            at = part * each + s
+            to = idx if scatter else at
+            return pltpu.make_async_copy(buf.at[at], out_ref.at[to], sem_out.at[at])
+
+        todo = [(part, s) for part in range(len(sources)) for s in range(each)]
+        for part, s in todo:
+
+            @pl.when(table_ref[starts[part] + s] >= 0)
+            def _():
+                load(part, s).start()
+
+        for part, s in todo:
+
+            @pl.when(table_ref[starts[part] + s] >= 0)
+            def _():
+                load(part, s).wait()
+                store(part, s).start()
+
+        for part, s in todo:
+
+            @pl.when(table_ref[starts[part] + s] >= 0)
+            def _():
+                store(part, s).wait()
 
     return pl.pallas_call(
         kernel,
         grid_spec=pltpu.PrefetchScalarGridSpec(
             num_scalar_prefetch=1,
-            grid=(count,),
-            in_specs=[pl.BlockSpec((1, length, width), lambda i, t: (t[start + i], 0, 0))],
-            out_specs=pl.BlockSpec((1, length, width), lambda i, t: (i, 0, 0)),
-        ),
-        out_shape=jax.ShapeDtypeStruct((count, length, width), source.dtype),
+            grid=(1,),
+            in_specs=[ANY_SPEC] * (len(sources) + len(wait_for)),
+            out_specs=ANY_SPEC,
+            scratch_shapes=[
+                pltpu.VMEM((total, length, width), BF16),
+                pltpu.SemaphoreType.DMA((total,)),
+                pltpu.SemaphoreType.DMA((total,)),
+            ],
+        ),
+        out_shape=jax.ShapeDtypeStruct((count, length, width), BF16),
         compiler_params=params_of(1),
         cost_estimate=pl.CostEstimate(
-            flops=0, transcendentals=0, bytes_accessed=4 * count * length * width
-        ),
-        name="permute",
-    )(table, source)
+            flops=0, transcendentals=0, bytes_accessed=4 * total * length * width
+        ),
+        name=name,
+    )(table, *sources, *wait_for)
+
+
+def after(value, earlier):
+    def kernel(*refs):
+        return
+
+    return pl.pallas_call(
+        kernel,
+        in_specs=[ANY_SPEC] * (1 + len(earlier)),
+        out_specs=ANY_SPEC,
+        out_shape=jax.ShapeDtypeStruct(value.shape, value.dtype),
+        input_output_aliases={0: 0},
+        name="after",
+    )(value, *earlier)
 
 
 def norm_forward(summed, gain_row, shift_row):
@@ -184,23 +307,24 @@
     return low
 
 
-def attention_forward(b, tables, x, weights, norms, y_in):
+def attention_forward(part, tables, x, weights, norms, y_in):
     rows, counts = tables
+    b = part // HALVES
     attn_qkv, attn_out = weights
     gains, shifts = norms
     slots, length, width = x.shape
     score_scale = (width // HEADS) ** (-0.5)
-    base = b * KINDS * OWN_CAP
+    base = part * SLOTS
 
     def kernel(rows_ref, counts_ref, x_ref, qkv_w, out_w, gain, shift, *rest):
         y_ref, qkv_ref, o_ref, zn_ref, rstd_ref = rest[-5:]
         i = pl.program_id(0)
 
-        @pl.when(i < counts_ref[b * 8])
+        @pl.when(i < counts_ref[part * 8])
         def _():
             xv = x_ref[0]
-            for part in range(3):
-                cols = slice(part * width, (part + 1) * width)
+            for third in range(3):
+                cols = slice(third * width, (third + 1) * width)
                 qkv_ref[0, :, cols] = nn(xv, qkv_w[:, cols]).astype(BF16)
             low = head_masks(length)
             zero = jnp.zeros((), BF16)
@@ -226,7 +350,7 @@
         return (r[base + i], 0, 0)
 
     def at_step(i, r, c):
-        return (jnp.minimum(i, c[b * 8] - 1), 0, 0)
+        return (jnp.maximum(jnp.minimum(i, c[part * 8] - 1), 0), 0, 0)
 
     seq = (1, length, width)
     in_specs = [
@@ -277,31 +401,53 @@
     )(*args)
 
 
-def attention_backward(b, tables, x, dy, kept, weights, gains, dx_in):
+def attention_backward(part, tables, x, dy, kept, weights, gains, dx_in, sums, packed):
     rows, counts = tables
+    b = part // HALVES
     attn_qkv, attn_out = weights
     qkv, o, zn, rstd = kept
     slots, length, width = x.shape
     score_scale = (width // HEADS) ** (-0.5)
-    base = b * KINDS * OWN_CAP
+    base = part * SLOTS
+    first = sums is None
+    n_out = 4 if first else 3
 
     def kernel(rows_ref, counts_ref, x_ref, dy_ref, qkv_ref, o_ref, zn_ref, rstd_ref, qkv_w, out_w, gain, *rest):
-        dx_ref, dqkv_w_ref, dout_w_ref, small_ref, acc_qkv, acc_out, do_scr, dqkv_scr = rest[-8:]
+        ins = rest[: len(rest) - n_out - 7]
+        outs = rest[len(ins) : len(ins) + n_out]
+        acc_qkv, acc_out, do_scr, dqkv_scr, dh_scr, dz_scr, sems = rest[-7:]
+        dx_ref, small_ref = outs[0], outs[1]
         i = pl.program_id(0)
+        here = i < counts_ref[part * 8]
+
+        def copies():
+            if first:
+                pairs = ((acc_qkv, outs[2]), (acc_out, outs[3]))
+            else:
+                pairs = ((ins[0], acc_qkv), (ins[1], acc_out))
+            return [
+                pltpu.make_async_copy(source, target, sems.at[n])
+                for n, (source, target) in enumerate(pairs)
+            ]
 
         @pl.when(i == 0)
         def _():
-            acc_qkv[...] = jnp.zeros_like(acc_qkv)
-            acc_out[...] = jnp.zeros_like(acc_out)
             small_ref[...] = jnp.zeros_like(small_ref)
-
-        @pl.when(i < counts_ref[b * 8])
+            if first:
+                acc_qkv[...] = jnp.zeros_like(acc_qkv)
+                acc_out[...] = jnp.zeros_like(acc_out)
+            else:
+                for copy in copies():
+                    copy.start()
+
+        @pl.when(here)
         def _():
             dz, gain_grad, shift_grad = norm_backward(dy_ref, zn_ref, rstd_ref, gain[0:1, :])
             small_ref[0:1, :] += gain_grad
             small_ref[1:2, :] += shift_grad
+            dz_scr[...] = dz
             dh = dz.astype(BF16)
-            acc_out[...] += tn(o_ref[0], dh)
+            dh_scr[...] = dh
             do_scr[...] = nt(dh, out_w[...]).astype(BF16)
             low = head_masks(length)
             zero = jnp.zeros((), BF16)
@@ -325,25 +471,51 @@
                 dqkv_scr[:, at : at + LANES] = (jnp.where(low, dqs[0], dqs[1]) * score_scale).astype(BF16)
                 dqkv_scr[:, width + at : width + at + LANES] = jnp.where(low, dks[0], dks[1]).astype(BF16)
                 dqkv_scr[:, 2 * width + at : 2 * width + at + LANES] = jnp.where(low, dvs[0], dvs[1]).astype(BF16)
+            total = dz_scr[...]
+            for third in range(3):
+                cols = slice(third * width, (third + 1) * width)
+                total = total + nt(dqkv_scr[:, cols], qkv_w[:, cols])
+            dx_ref[0] = total.astype(BF16)
+
+        if not first:
+
+            @pl.when(i == 0)
+            def _():
+                for copy in copies():
+                    copy.wait()
+
+        @pl.when(here)
+        def _():
             xv = x_ref[0]
-            total = dz
-            for part in range(3):
-                cols = slice(part * width, (part + 1) * width)
-                piece = dqkv_scr[:, cols]
-                acc_qkv[:, cols] += tn(xv, piece)
-                total = total + nt(piece, qkv_w[:, cols])
-            dx_ref[0] = total.astype(BF16)
+            for third in range(3):
+                cols = slice(third * width, (third + 1) * width)
+                acc_qkv[:, cols] += tn(xv, dqkv_scr[:, cols])
+            acc_out[...] += tn(o_ref[0], dh_scr[...])
 
         @pl.when(i == OWN_CAP - 1)
         def _():
-            dqkv_w_ref[...] = acc_qkv[...].astype(BF16)
-            dout_w_ref[...] = acc_out[...].astype(BF16)
+            if first:
+                for copy in copies():
+                    copy.start()
+                for copy in copies():
+                    copy.wait()
+            else:
+                packed_ref = outs[2]
+                groups, tall = packed_ref.shape[0], packed_ref.shape[1] // 4
+                for third in range(3):
+                    piece = acc_qkv[:, third * width : (third + 1) * width].astype(BF16)
+                    packed_ref[:, third * tall : (third + 1) * tall, :] = piece.reshape(
+                        groups, tall, width
+                    )
+                packed_ref[:, 3 * tall : 4 * tall, :] = (
+                    acc_out[...].astype(BF16).reshape(groups, tall, width)
+                )
 
     def at_row(i, r, c):
         return (r[base + i], 0, 0)
 
     def at_step(i, r, c):
-        return (jnp.minimum(i, c[b * 8] - 1), 0, 0)
+        return (jnp.maximum(jnp.minimum(i, c[part * 8] - 1), 0), 0, 0)
 
     def whole(i, r, c):
         return (0, 0)
@@ -365,11 +537,28 @@
         pl.BlockSpec((8, width), whole),
     ]
     args = [rows, counts, x, dy, qkv, o, zn, rstd, attn_qkv, attn_out, gains]
-    alias = {}
-    if dx_in is not None:
-        in_specs.append(pl.BlockSpec(memory_space=pl.ANY))
-        alias = {len(args): 0}
-        args.append(dx_in)
+    out_specs = [pl.BlockSpec(seq, at_row), pl.BlockSpec((8, width), whole)]
+    out_shape = [
+        jax.ShapeDtypeStruct((slots, length, width), BF16),
+        jax.ShapeDtypeStruct((8, width), F32),
+    ]
+    if first:
+        out_specs += [ANY_SPEC, ANY_SPEC]
+        out_shape += [
+            jax.ShapeDtypeStruct((width, 3 * width), F32),
+            jax.ShapeDtypeStruct((width, width), F32),
+        ]
+    else:
+        groups, total_rows = packed
+        out_specs.append(
+            pl.BlockSpec((groups, 4 * width // groups, width), lambda i, r, c: (0, 0, 0))
+        )
+        out_shape.append(jax.ShapeDtypeStruct((groups, total_rows, width), BF16))
+        in_specs += [ANY_SPEC, ANY_SPEC]
+        args += list(sums)
+    in_specs.append(ANY_SPEC)
+    alias = {len(args): 0}
+    args.append(dx_in)
     flops = 2 * OWN_CAP * length * width * (8 * width + 4 * length)
     return pl.pallas_call(
         kernel,
@@ -377,56 +566,49 @@
             num_scalar_prefetch=2,
             grid=(OWN_CAP,),
             in_specs=in_specs,
-            out_specs=[
-                pl.BlockSpec(seq, at_row),
-                pl.BlockSpec((width, 3 * width), whole),
-                pl.BlockSpec((width, width), whole),
-                pl.BlockSpec((8, width), whole),
-            ],
+            out_specs=out_specs,
             scratch_shapes=[
                 pltpu.VMEM((width, 3 * width), F32),
                 pltpu.VMEM((width, width), F32),
                 pltpu.VMEM((length, width), BF16),
                 pltpu.VMEM((length, 3 * width), BF16),
+                pltpu.VMEM((length, width), BF16),
+                pltpu.VMEM((length, width), F32),
+                pltpu.SemaphoreType.DMA((2,)),
             ],
         ),
-        out_shape=[
-            jax.ShapeDtypeStruct((slots, length, width), BF16),
-            jax.ShapeDtypeStruct((width, 3 * width), BF16),
-            jax.ShapeDtypeStruct((width, width), BF16),
-            jax.ShapeDtypeStruct((8, width), F32),
-        ],
+        out_shape=out_shape,
         input_output_aliases=alias,
         compiler_params=params_of(1),
         cost_estimate=pl.CostEstimate(
-            flops=2 * flops, transcendentals=OWN_CAP * HEADS * length * length, bytes_accessed=40 * 2**20
+            flops=flops, transcendentals=OWN_CAP * HEADS * length * length // 2, bytes_accessed=40 * 2**20
         ),
         name="attention_backward",
     )(*args)
 
 
-def feed_forward(b, tables, x, weights, norms, y_in):
+def feed_forward(part, tables, x, weights, norms, y_in):
     rows, counts = tables
+    b = part // HALVES
     ffn_up, ffn_down = weights
     gains, shifts = norms
     slots, length, width = x.shape
     hidden = ffn_up.shape[-1]
     parts = hidden // FF_PART
     kind = KINDS - 1
-    base = b * KINDS * OWN_CAP + kind * OWN_CAP
+    base = part * SLOTS + kind * OWN_CAP
 
     def kernel(rows_ref, counts_ref, x_ref, up, down, gain, shift, *rest):
         y_ref, g_ref, slope_ref, zn_ref, rstd_ref, x_scr, h_scr = rest[-7:]
         c, i = pl.program_id(0), pl.program_id(1)
 
-        @pl.when(i < counts_ref[b * 8 + kind])
+        @pl.when(i < counts_ref[part * 8 + kind])
         def _():
             @pl.when(c == 0)
             def _():
                 x_scr[i] = x_ref[0]
 
             xv = x_scr[i]
-            branch = None
             for sub in range(FF_PART // FF_SUB):
                 cols = slice(sub * FF_SUB, (sub + 1) * FF_SUB)
                 a = nn(xv, up[:, cols])
@@ -435,8 +617,7 @@
                 g = (a * phi).astype(BF16)
                 g_ref[0, :, cols] = g
                 slope_ref[0, :, cols] = slope.astype(BF16)
-                term = nn(g, down[cols, :])
-                branch = term if branch is None else branch + term
+            branch = nn(g_ref[0], down[...])
 
             @pl.when(c == 0)
             def _():
@@ -465,10 +646,10 @@
         return (r[base + jnp.where(c == parts - 1, i, 0)], 0, 0)
 
     def out_step(c, i, r, n):
-        return (jnp.where(c == parts - 1, jnp.minimum(i, n[b * 8 + kind] - 1), 0), 0, 0)
+        return (jnp.where(c == parts - 1, jnp.maximum(jnp.minimum(i, n[part * 8 + kind] - 1), 0), 0), 0, 0)
 
     def part_step(c, i, r, n):
-        return (jnp.minimum(i, n[b * 8 + kind] - 1), 0, c)
+        return (jnp.maximum(jnp.minimum(i, n[part * 8 + kind] - 1), 0), 0, c)
 
     seq = (1, length, width)
     in_specs = [
@@ -520,20 +701,30 @@
     )(*args)
 
 
-def feed_backward(b, tables, x, dy, kept, weights, gains, dx_in):
+def feed_backward(part, tables, x, dy, kept, weights, gains, sums, packed):
     rows, counts = tables
+    b = part // HALVES
     ffn_up, ffn_down = weights
     g, slope, zn, rstd = kept
     slots, length, width = x.shape
     hidden = ffn_up.shape[-1]
     parts = hidden // FF_PART
     kind = KINDS - 1
-    base = b * KINDS * OWN_CAP + kind * OWN_CAP
+    base = part * SLOTS + kind * OWN_CAP
+    first = sums is None
+    groups = packed[0]
+    tall = width // groups
+    deep = hidden // groups
 
     def kernel(
         rows_ref, counts_ref, x_ref, dy_ref, g_ref, slope_ref, zn_ref, rstd_ref, up, down, gain, *rest
     ):
-        dx_ref, dup_ref, ddown_ref, small_ref, x_scr, dh_scr, dx_scr, acc_up, acc_down = rest[-9:]
+        if first:
+            dx_ref, small_ref, acc_up, acc_down = rest[:4]
+        else:
+            sum_up, sum_down, dx_ref, small_ref, packed_ref = rest[:5]
+            acc_up, acc_down, low_up, low_down, sems = rest[-5:]
+        x_scr, dh_scr, dx_scr, da_scr = rest[-4:] if first else rest[-9:-5]
         c, i = pl.program_id(0), pl.program_id(1)
 
         @pl.when(jnp.logical_and(c == 0, i == 0))
@@ -542,10 +733,14 @@
 
         @pl.when(i == 0)
         def _():
-            acc_up[...] = jnp.zeros_like(acc_up)
-            acc_down[...] = jnp.zeros_like(acc_down)
-
-        @pl.when(i < counts_ref[b * 8 + kind])
+            if first:
+                acc_up[...] = jnp.zeros_like(acc_up)
+                acc_down[...] = jnp.zeros_like(acc_down)
+            else:
+                acc_up[...] = sum_up[...]
+                acc_down[...] = sum_down[...]
+
+        @pl.when(i < counts_ref[part * 8 + kind])
         def _():
             @pl.when(c == 0)
             def _():
@@ -558,43 +753,63 @@
                 dh_scr[i] = dz.astype(BF16)
                 dx_scr[i] = dz
 
-            xv = x_scr[i]
             dh = dh_scr[i]
-            total = None
             for sub in range(FF_PART // FF_SUB):
                 cols = slice(sub * FF_SUB, (sub + 1) * FF_SUB)
                 dg = nt(dh, down[cols, :])
-                da = (dg * slope_ref[0, :, cols].astype(F32)).astype(BF16)
-                acc_up[:, cols] += tn(xv, da)
-                acc_down[cols, :] += tn(g_ref[0, :, cols], dh)
-                term = nt(da, up[:, cols])
-                total = term if total is None else total + term
+                da_scr[:, cols] = (dg * slope_ref[0, :, cols].astype(F32)).astype(BF16)
+            acc_down[...] += tn(g_ref[0], dh)
+            acc_up[...] += tn(x_scr[i], da_scr[...])
+            total = dx_scr[i] + nt(da_scr[...], up[...])
 
             @pl.when(c < parts - 1)
             def _():
-                dx_scr[i] += total
+                dx_scr[i] = total
 
             @pl.when(c == parts - 1)
             def _():
-                dx_ref[0] = (dx_scr[i] + total).astype(BF16)
-
-        @pl.when(i == OWN_CAP - 1)
-        def _():
-            dup_ref[...] = acc_up[...].astype(BF16)
-            ddown_ref[...] = acc_down[...].astype(BF16)
+                dx_ref[0] = total.astype(BF16)
+
+        if not first:
+
+            @pl.when(i == OWN_CAP - 1)
+            def _():
+                low_up[...] = acc_up[...].astype(BF16)
+                low_down[...] = acc_down[...].astype(BF16)
+                copies = [
+                    pltpu.make_async_copy(
+                        low_up.at[pl.ds(z * tall, tall)],
+                        packed_ref.at[z, pl.ds(c * tall, tall)],
+                        sems.at[z],
+                    )
+                    for z in range(groups)
+                ]
+                shares = FF_PART // deep
+                copies += [
+                    pltpu.make_async_copy(
+                        low_down.at[pl.ds(m * deep, deep)],
+                        packed_ref.at[c * shares + m, pl.ds(parts * tall, deep)],
+                        sems.at[groups + m],
+                    )
+                    for m in range(shares)
+                ]
+                for copy in copies:
+                    copy.start()
+                for copy in copies:
+                    copy.wait()
 
     def in_row(c, i, r, n):
         return (r[base + jnp.where(c == 0, i, OWN_CAP - 1)], 0, 0)
 
     def in_step(c, i, r, n):
-        last = n[b * 8 + kind] - 1
+        last = jnp.maximum(n[part * 8 + kind] - 1, 0)
         return (jnp.where(c == 0, jnp.minimum(i, last), last), 0, 0)
 
     def out_row(c, i, r, n):
         return (r[base + jnp.where(c == parts - 1, i, 0)], 0, 0)
 
     def part_step(c, i, r, n):
-        return (jnp.minimum(i, n[b * 8 + kind] - 1), 0, c)
+        return (jnp.maximum(jnp.minimum(i, n[part * 8 + kind] - 1), 0), 0, c)
 
     seq = (1, length, width)
     in_specs = [
@@ -609,41 +824,50 @@
         pl.BlockSpec((8, width), lambda c, i, r, n: (0, 0)),
     ]
     args = [rows, counts, x, dy, g, slope, zn, rstd, ffn_up, ffn_down, gains]
-    alias = {}
-    if dx_in is not None:
-        in_specs.append(pl.BlockSpec(memory_space=pl.ANY))
-        alias = {len(args): 0}
-        args.append(dx_in)
+    up_spec = pl.BlockSpec((width, FF_PART), lambda c, i, r, n: (0, c))
+    down_spec = pl.BlockSpec((FF_PART, width), lambda c, i, r, n: (c, 0))
+    out_specs = [pl.BlockSpec(seq, out_row), pl.BlockSpec((8, width), lambda c, i, r, n: (0, 0))]
+    out_shape = [
+        jax.ShapeDtypeStruct((slots, length, width), BF16),
+        jax.ShapeDtypeStruct((8, width), F32),
+    ]
+    scratch = [
+        pltpu.VMEM((OWN_CAP, length, width), BF16),
+        pltpu.VMEM((OWN_CAP, length, width), BF16),
+        pltpu.VMEM((OWN_CAP, length, width), F32),
+        pltpu.VMEM((length, FF_PART), BF16),
+    ]
+    if first:
+        out_specs += [up_spec, down_spec]
+        out_shape += [
+            jax.ShapeDtypeStruct((width, hidden), F32),
+            jax.ShapeDtypeStruct((hidden, width), F32),
+        ]
+    else:
+        in_specs += [up_spec, down_spec]
+        args += list(sums)
+        out_specs.append(ANY_SPEC)
+        out_shape.append(jax.ShapeDtypeStruct((groups, parts * tall + deep, width), BF16))
+        scratch += [
+            pltpu.VMEM((width, FF_PART), F32),
+            pltpu.VMEM((FF_PART, width), F32),
+            pltpu.VMEM((width, FF_PART), BF16),
+            pltpu.VMEM((FF_PART, width), BF16),
+            pltpu.SemaphoreType.DMA((groups + FF_PART // deep,)),
+        ]
     return pl.pallas_call(
         kernel,
         grid_spec=pltpu.PrefetchScalarGridSpec(
             num_scalar_prefetch=2,
             grid=(parts, OWN_CAP),
             in_specs=in_specs,
-            out_specs=[
-                pl.BlockSpec(seq, out_row),
-                pl.BlockSpec((width, FF_PART), lambda c, i, r, n: (0, c)),
-                pl.BlockSpec((FF_PART, width), lambda c, i, r, n: (c, 0)),
-                pl.BlockSpec((8, width), lambda c, i, r, n: (0, 0)),
-            ],
-            scratch_shapes=[
-                pltpu.VMEM((OWN_CAP, length, width), BF16),
-                pltpu.VMEM((OWN_CAP, length, width), BF16),
-                pltpu.VMEM((OWN_CAP, length, width), F32),
-                pltpu.VMEM((width, FF_PART), F32),
-                pltpu.VMEM((FF_PART, width), F32),
-            ],
-        ),
-        out_shape=[
-            jax.ShapeDtypeStruct((slots, length, width), BF16),
-            jax.ShapeDtypeStruct((width, hidden), BF16),
-            jax.ShapeDtypeStruct((hidden, width), BF16),
-            jax.ShapeDtypeStruct((8, width), F32),
-        ],
-        input_output_aliases=alias,
+            out_specs=out_specs,
+            scratch_shapes=scratch,
+        ),
+        out_shape=out_shape,
         compiler_params=params_of(2),
         cost_estimate=pl.CostEstimate(
-            flops=8 * OWN_CAP * length * width * hidden,
+            flops=4 * OWN_CAP * length * width * hidden,
             transcendentals=0,
             bytes_accessed=50 * 2**20,
         ),
@@ -664,12 +888,13 @@
     padded[PAD : PAD + length, :] = values
 
 
-def conv_forward(b, tables, x, weights, norms, y_in):
+def conv_forward(part, tables, x, weights, norms, y_in):
     rows, counts = tables
+    b = part // HALVES
     taps, conv_point = weights
     gains, shifts = norms
     slots, length, width = x.shape
-    base = b * KINDS * OWN_CAP + OWN_CAP
+    base = part * SLOTS + OWN_CAP
     steps = (KINDS - 2) * OWN_CAP
 
     def kernel(rows_ref, counts_ref, x_ref, point, taps_ref, gain, shift, *rest):
@@ -680,7 +905,7 @@
             taps_n = 2 * kind + 1
             first = kind * kind - 1
 
-            @pl.when(jnp.logical_and(which == kind - 1, j < counts_ref[b * 8 + kind]))
+            @pl.when(jnp.logical_and(which == kind - 1, j < counts_ref[part * 8 + kind]))
             def _():
                 fill_padded(xpad, x_ref[0].astype(F32))
                 for r in range(0, length, ROW_TILE):
@@ -708,8 +933,8 @@
 
     def at_step(i, r, c):
         which = i // OWN_CAP
-        last = c[b * 8 + 1 + which] - 1
-        return (which * OWN_CAP + jnp.minimum(i % OWN_CAP, last), 0, 0)
+        last = c[part * 8 + 1 + which] - 1
+        return (which * OWN_CAP + jnp.maximum(jnp.minimum(i % OWN_CAP, last), 0), 0, 0)
 
     def whole(i, r, c):
         return (0, 0)
@@ -757,16 +982,23 @@
     )(*args)
 
 
-def conv_backward(b, tables, x, dy, kept, weights, gains, dx_in):
+def conv_backward(part, tables, x, dy, kept, weights, gains, dx_in, sums, packed):
     rows, counts = tables
+    b = part // HALVES
     taps, conv_point = weights
     u, zn, rstd = kept
     slots, length, width = x.shape
-    base = b * KINDS * OWN_CAP + OWN_CAP
+    base = part * SLOTS + OWN_CAP
     steps = (KINDS - 2) * OWN_CAP
+    first_half = sums is None
+    groups = packed[0]
 
     def kernel(rows_ref, counts_ref, x_ref, dy_ref, u_ref, zn_ref, rstd_ref, point, taps_ref, gain, *rest):
-        dx_ref, dpoint_ref, small_ref, acc, xpad, dupad, dz_scr = rest[-7:]
+        if first_half:
+            dx_ref, small_ref, acc, xpad, dupad, dz_scr = rest[-6:]
+        else:
+            sum_ref = rest[0]
+            dx_ref, small_ref, packed_ref, xpad, dupad, dz_scr, acc = rest[-7:]
         step = pl.program_id(0)
         which, j = step // OWN_CAP, step % OWN_CAP
 
@@ -776,13 +1008,13 @@
 
         @pl.when(j == 0)
         def _():
-            acc[...] = jnp.zeros_like(acc)
+            acc[...] = jnp.zeros_like(acc) if first_half else sum_ref[...]
 
         for kind in range(1, KINDS - 1):
             taps_n = 2 * kind + 1
             first = kind * kind - 1
 
-            @pl.when(jnp.logical_and(which == kind - 1, j < counts_ref[b * 8 + kind]))
+            @pl.when(jnp.logical_and(which == kind - 1, j < counts_ref[part * 8 + kind]))
             def _():
                 dz, gain_grad, shift_grad = norm_backward(
                     dy_ref, zn_ref, rstd_ref, gain[kind : kind + 1, :]
@@ -812,17 +1044,19 @@
                     for t in range(taps_n):
                         small_ref[first + t : first + t + 1, cols] += sums[t]
 
-        @pl.when(j == OWN_CAP - 1)
-        def _():
-            dpoint_ref[...] = acc[...].astype(BF16)
+        if not first_half:
+
+            @pl.when(j == OWN_CAP - 1)
+            def _():
+                packed_ref[...] = acc[...].astype(BF16).reshape(packed_ref.shape)
 
     def at_row(i, r, c):
         return (r[base + i], 0, 0)
 
     def at_step(i, r, c):
         which = i // OWN_CAP
-        last = c[b * 8 + 1 + which] - 1
-        return (which * OWN_CAP + jnp.minimum(i % OWN_CAP, last), 0, 0)
+        last = c[part * 8 + 1 + which] - 1
+        return (which * OWN_CAP + jnp.maximum(jnp.minimum(i % OWN_CAP, last), 0), 0, 0)
 
     def whole(i, r, c):
         return (0, 0)
@@ -839,63 +1073,66 @@
         pl.BlockSpec((8, width), whole),
     ]
     args = [rows, counts, x, dy, u, zn, rstd, conv_point, taps, gains]
+    sum_spec = pl.BlockSpec((None, width, width), lambda i, r, c: (i // OWN_CAP, 0, 0))
+    out_specs = [pl.BlockSpec(seq, at_row), pl.BlockSpec((24, width), whole)]
+    out_shape = [
+        jax.ShapeDtypeStruct((slots, length, width), BF16),
+        jax.ShapeDtypeStruct((24, width), F32),
+    ]
+    scratch = [
+        pltpu.VMEM((length + 2 * PAD, width), F32),
+        pltpu.VMEM((length + 2 * PAD, width), F32),
+        pltpu.VMEM((length, width), F32),
+    ]
     alias = {}
-    if dx_in is not None:
-        in_specs.append(pl.BlockSpec(memory_space=pl.ANY))
-        alias = {len(args): 0}
-        args.append(dx_in)
+    if first_half:
+        out_specs.append(sum_spec)
+        out_shape.append(jax.ShapeDtypeStruct((KINDS - 2, width, width), F32))
+    else:
+        in_specs.append(sum_spec)
+        args.append(sums)
+        out_specs.append(
+            pl.BlockSpec((groups, width // groups, width), lambda i, r, c: (0, 4 + i // OWN_CAP, 0))
+        )
+        out_shape.append(jax.ShapeDtypeStruct(packed[1].shape, BF16))
+        in_specs.append(ANY_SPEC)
+        alias = {len(args): 2}
+        args.append(packed[1])
+        scratch.append(pltpu.VMEM((width, width), F32))
+    in_specs.append(ANY_SPEC)
+    alias = {**alias, len(args): 0}
+    args.append(dx_in)
     return pl.pallas_call(
         kernel,
         grid_spec=pltpu.PrefetchScalarGridSpec(
             num_scalar_prefetch=2,
             grid=(steps,),
             in_specs=in_specs,
-            out_specs=[
-                pl.BlockSpec(seq, at_row),
-                pl.BlockSpec((None, width, width), lambda i, r, c: (i // OWN_CAP, 0, 0)),
-                pl.BlockSpec((24, width), whole),
-            ],
-            scratch_shapes=[
-                pltpu.VMEM((width, width), F32),
-                pltpu.VMEM((length + 2 * PAD, width), F32),
-                pltpu.VMEM((length + 2 * PAD, width), F32),
-                pltpu.VMEM((length, width), F32),
-            ],
-        ),
-        out_shape=[
-            jax.ShapeDtypeStruct((slots, length, width), BF16),
-            jax.ShapeDtypeStruct((KINDS - 2, width, width), BF16),
-            jax.ShapeDtypeStruct((24, width), F32),
-        ],
+            out_specs=out_specs,
+            scratch_shapes=scratch,
+        ),
+        out_shape=out_shape,
         input_output_aliases=alias,
         compiler_params=params_of(1),
         cost_estimate=pl.CostEstimate(
-            flops=4 * steps * length * width * width, transcendentals=0, bytes_accessed=50 * 2**20
+            flops=3 * steps * length * width * width, transcendentals=0, bytes_accessed=50 * 2**20
         ),
         name="conv_backward",
     )(*args)
 
 
-def owner_forward(b, tables, x, weights, small_weights):
+def owner_forward(part, tables, x, weights, small_weights):
     attn_qkv, attn_out, ffn_up, ffn_down, conv_point = weights
     taps, gains, shifts = small_weights
     norms = (gains, shifts)
-    y, g, slope, zn_f, rstd_f = feed_forward(b, tables, x, (ffn_up, ffn_down), norms, None)
-    y, qkv, o, zn_a, rstd_a = attention_forward(b, tables, x, (attn_qkv, attn_out), norms, y)
-    y, u, zn_c, rstd_c = conv_forward(b, tables, x, (taps, conv_point), norms, y)
+    y, g, slope, zn_f, rstd_f = feed_forward(part, tables, x, (ffn_up, ffn_down), norms, None)
+    y, qkv, o, zn_a, rstd_a = attention_forward(part, tables, x, (attn_qkv, attn_out), norms, y)
+    y, u, zn_c, rstd_c = conv_forward(part, tables, x, (taps, conv_point), norms, y)
     return y, ((g, slope, zn_f, rstd_f), (qkv, o, zn_a, rstd_a), (u, zn_c, rstd_c))
 
 
-def owner_backward(b, tables, x, dy, kept, weights, small_weights):
-    attn_qkv, attn_out, ffn_up, ffn_down, conv_point = weights
-    taps, gains, shifts = small_weights
-    kept_f, kept_a, kept_c = kept
-    dx, dup, ddown, small_f = feed_backward(b, tables, x, dy, kept_f, (ffn_up, ffn_down), gains, None)
-    dx, dqkv, dout, small_a = attention_backward(
-        b, tables, x, dy, kept_a, (attn_qkv, attn_out), gains, dx
-    )
-    dx, dpoint, small_c = conv_backward(b, tables, x, dy, kept_c, (taps, conv_point), gains, dx)
-    small = jnp.concatenate(
+def join_small(small_f, small_a, small_c):
+    return jnp.concatenate(
         [
             small_c[:15],
             small_a[0:1],
@@ -906,7 +1143,50 @@
             small_f[1:2],
         ]
     )
-    return dx, (dup, ddown, dqkv, dout, dpoint, small)
+
+
+def owner_backward(b, tables, x, dy, kept, weights, small_weights, groups):
+    attn_qkv, attn_out, ffn_up, ffn_down, conv_point = weights
+    taps, gains, shifts = small_weights
+    width = x[0].shape[-1]
+    rest_rows = 7 * width // groups + SMALL_ROWS
+    dx, smalls = [None, None], [None, None]
+    sums = None
+    for half in range(HALVES):
+        part = b * HALVES + half
+        kept_f, kept_a, kept_c = kept[half]
+        xh, dyh = x[half], dy[half]
+        first = half == 0
+        if first:
+            d, small_f, *sum_f = feed_backward(
+                part, tables, xh, dyh, kept_f, (ffn_up, ffn_down), gains, None, (groups,)
+            )
+            d, small_a, *sum_a = attention_backward(
+                part, tables, xh, dyh, kept_a, (attn_qkv, attn_out), gains, d, None, None
+            )
+            d, small_c, sum_c = conv_backward(
+                part, tables, xh, dyh, kept_c, (taps, conv_point), gains, d, None, (groups,)
+            )
+        else:
+            d, small_f, feed_pack = feed_backward(
+                part, tables, xh, dyh, kept_f, (ffn_up, ffn_down), gains, sum_f, (groups,)
+            )
+            d, small_a, rest_pack = attention_backward(
+                part, tables, xh, dyh, kept_a, (attn_qkv, attn_out), gains, d, sum_a, (groups, rest_rows)
+            )
+            d, small_c, rest_pack = conv_backward(
+                part, tables, xh, dyh, kept_c, (taps, conv_point), gains, d, sum_c, (groups, rest_pack)
+            )
+        dx[half] = d
+        smalls[half] = join_small(small_f, small_a, small_c)
+    counts = tables[1].reshape(BLOCKS, HALVES, 8)[b].sum(axis=0).astype(BF16)
+    small = (smalls[0] + smalls[1]).reshape(25, groups, width // groups)
+    small = small.transpose(1, 0, 2).reshape(groups, -1).astype(BF16)
+    small = jnp.pad(small, ((0, 0), (0, (SMALL_ROWS - 1) * width - small.shape[1])))
+    last = jnp.pad(jnp.broadcast_to(counts, (groups, 8)), ((0, 0), (0, width - 8)))
+    small = jnp.concatenate([small, last], axis=1).reshape(groups, SMALL_ROWS, width)
+    rest_pack = lax.dynamic_update_slice(rest_pack, small, (0, rest_rows - SMALL_ROWS, 0))
+    return dx, feed_pack, rest_pack
 
 
 def small_params(b, conv_taps, norm_gain, norm_bias):
@@ -937,51 +1217,74 @@
     groups = lax.axis_size("dp")
     seqs = inputs.shape[0]
     width = inputs.shape[-1]
-    cap = -(-seqs // owners)
-    slots = owners * cap
+    hidden = ffn_up.shape[-1]
     weights = (attn_qkv, attn_out, ffn_up, ffn_down, conv_point)
     smalls = [small_params(b, conv_taps, norm_gain, norm_bias) for b in range(BLOCKS)]
-    me = lax.axis_index("op")
-    everyone = lax.all_gather(candidate, ("dp", "op"), axis=0, tiled=True)
-    group = lax.dynamic_slice_in_dim(
-        everyone, lax.axis_index("dp") * (owners * seqs), owners * seqs, axis=0
+    send, relay, tags = home_tables(candidate.reshape(-1), owners, seqs)
+    arrived = exchange(tags.reshape(owners, BLOCKS * HALVES))
+    tables = owner_tables(arrived.reshape(-1), owners)
+    both = range(HALVES)
+
+    def start(b, half):
+        return (b * HALVES + half) * owners
+
+    x0 = [
+        exchange(move_rows(send, [start(0, h)], [inputs], owners, False, "send_inputs"))
+        for h in both
+    ]
+    y0, kept0 = zip(*[owner_forward(h, tables, x0[h], weights, smalls[0]) for h in both])
+    x1 = []
+    for h in both:
+        back = exchange(y0[h])
+        x1.append(exchange(move_rows(relay, [start(0, h)], [back], owners, False, "relay_x")))
+    dy1 = [
+        exchange(
+            move_rows(
+                send, [start(1, h)], [cotangent], owners, False, "send_cotangent", (x1[0],)
+            )
+        )
+        for h in both
+    ]
+    y1, kept1 = zip(
+        *[owner_forward(HALVES + h, tables, x1[h], weights, smalls[1]) for h in both]
     )
-    own = jnp.arange(KINDS, dtype=jnp.int32) * owners + me
-    totals = jnp.sum((everyone[:, :, None] == own).astype(F32), axis=0)
-    src, pos, rows, counts, relay_in, relay_out = make_tables(
-        group.reshape(-1), me.astype(jnp.int32)[None], owners, cap, seqs
-    )
-    tables = (rows, counts)
-
-    x0 = exchange(permute_rows(src, inputs, 0, slots))
-    dy1 = exchange(permute_rows(src, cotangent, slots, slots))
-    y0, kept0 = owner_forward(0, tables, x0, weights, smalls[0])
-    x1 = exchange(permute_rows(relay_in, exchange(y0), 0, slots))
-    y1, kept1 = owner_forward(1, tables, x1, weights, smalls[1])
-    outputs = permute_rows(pos, exchange(y1), seqs, seqs)
-    dx1, grads1 = owner_backward(1, tables, x1, dy1, kept1, weights, smalls[1])
-    dy0 = exchange(permute_rows(relay_out, exchange(dx1), 0, slots))
-    dx0, grads0 = owner_backward(0, tables, x0, dy0, kept0, weights, smalls[0])
-    input_grad = permute_rows(pos, exchange(dx0), 0, seqs)
-
-    def scatter(grad, dim):
-        return lax.psum_scatter(grad, "dp", scatter_dimension=dim, tiled=True).astype(F32)
-
-    finished = [None, None]
-    for b, (dup, ddown, dqkv, dout, dpoint, small) in ((1, grads1), (0, grads0)):
-        total = totals[b]
-        small = small.reshape(25, groups, width // groups).transpose(1, 0, 2).astype(BF16)
-        small = lax.psum_scatter(small, "dp", scatter_dimension=0, tiled=True)[0].astype(F32)
-        tap_total = jnp.repeat(
-            total[1 : KINDS - 1], jnp.array([3, 5, 7]), total_repeat_length=15
+    dx1, feed1, rest1 = owner_backward(1, tables, x1, dy1, kept1, weights, smalls[1], groups)
+    dy0 = []
+    for h in both:
+        back = exchange(dx1[h])
+        dy0.append(exchange(move_rows(relay, [start(1, h)], [back], owners, False, "relay_dx")))
+    dx0, feed0, rest0 = owner_backward(0, tables, x0, dy0, kept0, weights, smalls[0], groups)
+    starts = [start(1, h) for h in both]
+    y_home = [exchange(after(y1[h], (dy0[1],))) for h in both]
+    outputs = move_rows(send, starts, y_home, seqs, True, "outputs")
+    starts = [start(0, h) for h in both]
+    dx_home = [exchange(dx0[h]) for h in both]
+    input_grad = move_rows(send, starts, dx_home, seqs, True, "input_grad")
+
+    tall, deep, parts = width // groups, hidden // groups, hidden // FF_PART
+    finished, earlier = [None, None], None
+    for b, feed, rest in ((1, feed1, rest1), (0, feed0, rest0)):
+        if earlier is not None:
+            feed = after(feed, (earlier,))
+        feed = lax.psum_scatter(feed, "dp", scatter_dimension=0, tiled=False)
+        rest = after(rest, (feed,))
+        earlier = lax.psum_scatter(rest, "dp", scatter_dimension=0, tiled=False)
+        feed, rest = feed.astype(F32), earlier.astype(F32)
+        total = rest[-1, :KINDS]
+        small = rest[7 * tall : -1].reshape(-1)[: 25 * tall].reshape(25, tall)
+        up = feed[: parts * tall].reshape(parts, tall, FF_PART).transpose(1, 0, 2)
+        qkv = rest[: 3 * tall].reshape(3, tall, width).transpose(1, 0, 2)
+        point = rest[4 * tall : 7 * tall].reshape(KINDS - 2, tall, width)
+        tap_total = jnp.concatenate(
+            [jnp.broadcast_to(total[k], (2 * k + 1,)) for k in range(1, KINDS - 1)]
         )
         finished[b] = (
-            scatter(dqkv, 0) / total[0],
-            scatter(dout, 0) / total[0],
-            scatter(dup, 0) / total[KINDS - 1],
-            scatter(ddown, 0) / total[KINDS - 1],
+            qkv.reshape(tall, 3 * width) / total[0],
+            rest[3 * tall : 4 * tall] / total[0],
+            up.reshape(tall, hidden) / total[KINDS - 1],
+            feed[parts * tall :] / total[KINDS - 1],
             small[:15] / tap_total[:, None],
-            scatter(dpoint, 1) / total[1 : KINDS - 1, None, None],
+            point / total[1 : KINDS - 1, None, None],
             small[15:20] / total[:, None],
             small[20:25] / total[:, None],
         )

time: 1750 us -> 1710 us (0.977)
  waiting for transfers between devices: 907 us -> 672 us
  Pallas kernels: 507 us -> 663 us
  blocking collectives: 191 us -> 76.9 us
  starting transfers between devices: 70.5 us -> 171 us
  local copies, waits for them, and re-layouts: 7.28 us -> 58.8 us
    reduce_scatter x12 -> x4, waiting for transfers between devices: 159 us -> 0.03 us  [the longest x2 0.02 us: per_device(): earlier = lax.psum_scatter(rest, 'dp', scatter_dimension=0, tiled=False)]
    all_to_all x7 -> x16, starting transfers between devices: 70 us -> 171 us  [exchange(): return lax.all_to_all(rows, 'op', split_axis=0, concat_axis=0, tiled=True)]
    all_to_all x1, blocking collectives: 148 us -> 76.9 us  [exchange(): return lax.all_to_all(rows, 'op', split_axis=0, concat_axis=0, tiled=True)]
    all_to_all x7 -> x16, waiting for transfers between devices: 742 us -> 672 us  [exchange(): return lax.all_to_all(rows, 'op', split_axis=0, concat_axis=0, tiled=True)]
    pallas_call x2 -> x4, Pallas kernels: 87.6 us -> 147 us  [feed_backward(): pl.pallas_call(kernel, grid_spec=pltpu.PrefetchScalarGridSpec(num_scalar_...]
    all_gather x1 -> x0, blocking collectives: 43.5 us -> none  [per_device(): everyone = lax.all_gather(candidate, ('dp', 'op'), axis=0, tiled=True)]
    pallas_call x2 -> x4, Pallas kernels: 87.7 us -> 125 us  [conv_backward(): pl.pallas_call(kernel, grid_spec=pltpu.PrefetchScalarGridSpec(num_scalar_...]
    pallas_call x7 -> x17, Pallas kernels: 93.5 us -> 58.2 us  [the longest x10 54 us: move_rows(): pl.pallas_call(kernel, grid_spec=pltpu.PrefetchScalarGridSpec(num_scalar_...]
  transfers between devices with their start and end apart: 19 -> 20, of which waited for: 8 -> 13; matrix products, arithmetic and copies ran while one was open for 3% -> 3% of each run, Pallas kernels for 14% -> 37%
where the time goes in v2:
time: 1710 us; the launch traced here: 1700 us
  waiting for transfers between devices  672 us (39%)
  Pallas kernels  663 us (39%)
  starting transfers between devices  171 us (10%)
  blocking collectives  76.9 us (4%)
  local copies, waits for them, and re-layouts  58.8 us (3%)
  other arithmetic  42.4 us (2%)
    all_to_all x16, waiting for transfers between devices, exchange(): return lax.all_to_all(rows, 'op', split_axis=0, concat_axis=0, tiled=True)  672 us
    all_to_all x16, starting transfers between devices, exchange(): return lax.all_to_all(rows, 'op', split_axis=0, concat_axis=0, tiled=True)  171 us
    pallas_call x4, Pallas kernels, feed_backward(): pl.pallas_call(kernel, grid_spec=pltpu.PrefetchScalarGridSpec(num_scalar_...  147 us
    pallas_call x4, Pallas kernels, conv_backward(): pl.pallas_call(kernel, grid_spec=pltpu.PrefetchScalarGridSpec(num_scalar_...  125 us
    pallas_call x4, Pallas kernels, attention_backward(): pl.pallas_call(kernel, grid_spec=pltpu.PrefetchScalarGridSpec(num_scalar_...  119 us
    pallas_call x4, Pallas kernels, feed_forward(): pl.pallas_call(kernel, grid_spec=pltpu.PrefetchScalarGridSpec(num_scalar_...  91.3 us
    all_to_all x1, blocking collectives, exchange(): return lax.all_to_all(rows, 'op', split_axis=0, concat_axis=0, tiled=True)  76.9 us
    pallas_call x4, Pallas kernels, conv_forward(): pl.pallas_call(kernel, grid_spec=pltpu.PrefetchScalarGridSpec(num_scalar_...  71.1 us
  transfers between devices with their start and end apart: 20, of which 13 were waited for; matrix products, arithmetic and copies ran while one was open for 3% of the time, Pallas kernels for 37%

profile of v2, /device:TPU:0, one launch (start us, length us, event | category | flops | bytes accessed | tf_op | source)
XLA Modules:
  0.0 1698.6 jit_solution(17921371013293148259)
XLA Ops:
  12.3 5.2 all-to-all-start
  17.4 4.7 send_inputs.2
  22.1 4.8 all-to-all-start.1
  26.9 4.7 send_inputs.3
  31.7 66.8 %all-to-all-done.1.x_ref = bf16[8,512,768]{2,1,0:T(8,128)(2,1)} async-done(((bf16[8,512,768]{2,1,0:T(8,128)(2,1)}), bf16[8,512,768]{2,1,0:T(8,128)(2,1)}, u32[]{:S(2)}, u32[]{:S(2)}) %all-to-all-start.1) | async-done | bytes 6291488 | tf_op jit(solution)/shard_map/all_to_all | solution.py:1200
  98.5 4.7 all-to-all-start.4
  108.9 29.2 %feed_forward.4 = (bf16[8,512,768]{2,1,0:T(8,128)(2,1)}, bf16[3,512,3072]{2,1,0:T(8,128)(2,1)}, bf16[3,512,3072]{2,1,0:T(8,128)(2,1)}, bf16[3,512,768]{2,1,0:T(8,128)(2,1)}, f32[3,512,128]{2,1,0:T(8,128)}) custom-call(s32[60]{0:T(128)} %get-tuple-element.113.rows_ref, s32[32]{0:T(128)} %get-tuple-element.114.counts_ref, ...), custom_call_target="tpu_custom_call" | custom-call | flops 14495514624 | bytes 41943040 | tf_op jit(solution)/shard_map/feed_forward/pallas_call | solution.py:668
  138.2 20.0 %attention_forward.4 = (bf16[8,512,768]{2,1,0:T(8,128)(2,1)}, bf16[3,512,2304]{2,1,0:T(8,128)(2,1)}, bf16[3,512,768]{2,1,0:T(8,128)(2,1)}, bf16[3,512,768]{2,1,0:T(8,128)(2,1)}, f32[3,512,128]{2,1,0:T(8,128)}) custom-call(s32[60]{0:T(128)} %get-tuple-element.113.rows_ref, s32[32]{0:T(128)} %get-tuple-element.114.counts_ref, ...), custom_call_target="tpu_custom_call", output_to_operand_aliasing={{0}: (7, {})} | custom-call | flops 19327352832 | bytes 31457280 | tf_op jit(solution)/shard_map/attention_forward/pallas_call | solution.py:374
  158.2 14.0 conv_forward.4
  174.9 5.1 all-to-all-start.2
  180.0 20.7 %feed_forward.6 = (bf16[8,512,768]{2,1,0:T(8,128)(2,1)}, bf16[3,512,3072]{2,1,0:T(8,128)(2,1)}, bf16[3,512,3072]{2,1,0:T(8,128)(2,1)}, bf16[3,512,768]{2,1,0:T(8,128)(2,1)}, f32[3,512,128]{2,1,0:T(8,128)}) custom-call(s32[60]{0:T(128)} %get-tuple-element.113.rows_ref, s32[32]{0:T(128)} %get-tuple-element.114.counts_ref, ...), custom_call_target="tpu_custom_call" | custom-call | flops 14495514624 | bytes 41943040 | tf_op jit(solution)/shard_map/feed_forward/pallas_call | solution.py:668
  200.7 5.6 attention_forward.6
  206.3 20.7 %conv_forward.6 = (bf16[8,512,768]{2,1,0:T(8,128)(2,1)}, bf16[9,512,768]{2,1,0:T(8,128)(2,1)}, bf16[9,512,768]{2,1,0:T(8,128)(2,1)}, f32[9,512,128]{2,1,0:T(8,128)}) custom-call(s32[60]{0:T(128)} %get-tuple-element.113.rows_ref, s32[32]{0:T(128)} %get-tuple-element.114.counts_ref, ...), custom_call_target="tpu_custom_call", output_to_operand_aliasing={{0}: (7, {})} | custom-call | flops 5435817984 | bytes 37748736 | tf_op jit(solution)/shard_map/conv_forward/pallas_call | solution.py:956
  227.0 24.6 %all-to-all-done.2.refs_0_ = bf16[8,512,768]{2,1,0:T(8,128)(2,1)} async-done(((bf16[8,512,768]{2,1,0:T(8,128)(2,1)}), bf16[8,512,768]{2,1,0:T(8,128)(2,1)}, u32[]{:S(2)}, u32[]{:S(2)}) %all-to-all-start.2) | async-done | bytes 6291488 | tf_op jit(solution)/shard_map/all_to_all | solution.py:1200
  251.6 4.8 all-to-all-start.5
  256.4 4.7 relay_x.2
  261.2 66.8 %all-to-all-done.5.refs_0_ = bf16[8,512,768]{2,1,0:T(8,128)(2,1)} async-done(((bf16[8,512,768]{2,1,0:T(8,128)(2,1)}), bf16[8,512,768]{2,1,0:T(8,128)(2,1)}, u32[]{:S(2)}, u32[]{:S(2)}) %all-to-all-start.5) | async-done | bytes 6291488 | tf_op jit(solution)/shard_map/all_to_all | solution.py:1200
  328.0 4.7 all-to-all-start.3
  332.8 4.7 relay_x.3
  337.5 66.9 %all-to-all-done.3.x_ref.refs_1_ = bf16[8,512,768]{2,1,0:T(8,128)(2,1)} async-done(((bf16[8,512,768]{2,1,0:T(8,128)(2,1)}), bf16[8,512,768]{2,1,0:T(8,128)(2,1)}, u32[]{:S(2)}, u32[]{:S(2)}) %all-to-all-start.3) | async-done | bytes 6291488 | tf_op jit(solution)/shard_map/all_to_all | solution.py:1200
  404.4 4.8 all-to-all-start.6
  409.2 4.8 send_cotangent.3
  414.0 66.8 %all-to-all-done.6.x_ref = bf16[8,512,768]{2,1,0:T(8,128)(2,1)} async-done(((bf16[8,512,768]{2,1,0:T(8,128)(2,1)}), bf16[8,512,768]{2,1,0:T(8,128)(2,1)}, u32[]{:S(2)}, u32[]{:S(2)}) %all-to-all-start.6) | async-done | bytes 6291488 | tf_op jit(solution)/shard_map/all_to_all | solution.py:1200
  480.8 4.8 all-to-all-start.8
  485.6 4.7 send_cotangent.2
  490.3 66.9 %all-to-all-done.8.dy_ref = bf16[8,512,768]{2,1,0:T(8,128)(2,1)} async-done(((bf16[8,512,768]{2,1,0:T(8,128)(2,1)}), bf16[8,512,768]{2,1,0:T(8,128)(2,1)}, u32[]{:S(2)}, u32[]{:S(2)}) %all-to-all-start.8) | async-done | bytes 6291488 | tf_op jit(solution)/shard_map/all_to_all | solution.py:1200
  557.2 4.8 all-to-all-start.7
  563.3 20.8 %feed_forward.5 = (bf16[8,512,768]{2,1,0:T(8,128)(2,1)}, bf16[3,512,3072]{2,1,0:T(8,128)(2,1)}, bf16[3,512,3072]{2,1,0:T(8,128)(2,1)}, bf16[3,512,768]{2,1,0:T(8,128)(2,1)}, f32[3,512,128]{2,1,0:T(8,128)}) custom-call(s32[60]{0:T(128)} %get-tuple-element.113.rows_ref, s32[32]{0:T(128)} %get-tuple-element.114.counts_ref, ...), custom_call_target="tpu_custom_call" | custom-call | flops 14495514624 | bytes 41943040 | tf_op jit(solution)/shard_map/feed_forward/pallas_call | solution.py:668
  584.1 20.6 %feed_forward.7 = (bf16[8,512,768]{2,1,0:T(8,128)(2,1)}, bf16[3,512,3072]{2,1,0:T(8,128)(2,1)}, bf16[3,512,3072]{2,1,0:T(8,128)(2,1)}, bf16[3,512,768]{2,1,0:T(8,128)(2,1)}, f32[3,512,128]{2,1,0:T(8,128)}) custom-call(s32[60]{0:T(128)} %get-tuple-element.113.rows_ref, s32[32]{0:T(128)} %get-tuple-element.114.counts_ref, ...), custom_call_target="tpu_custom_call" | custom-call | flops 14495514624 | bytes 41943040 | tf_op jit(solution)/shard_map/feed_forward/pallas_call | solution.py:668
  604.7 31.8 %feed_backward.4 = (bf16[8,512,768]{2,1,0:T(8,128)(2,1)}, f32[8,768]{1,0:T(8,128)}, f32[768,3072]{1,0:T(8,128)}, f32[3072,768]{1,0:T(8,128)}) custom-call(s32[60]{0:T(128)} %get-tuple-element.113.rows_ref, s32[32]{0:T(128)} %get-tuple-element.114.counts_ref, bf16[8,512,768]{2,1,0:T(8,128)(2,1)} %all-to-all-done.3.x_ref.refs_1_, ...), custom_call_target="tpu_custom_call" | custom-call | flops 14495514624 | bytes 52428800 | tf_op jit(solution)/shard_map/feed_backward/pallas_call | solution.py:858
  636.5 35.7 %feed_backward.5 = (bf16[8,512,768]{2,1,0:T(8,128)(2,1)}, f32[8,768]{1,0:T(8,128)}, bf16[4,1536,768]{2,1,0:T(8,128)(2,1)}) custom-call(s32[60]{0:T(128)} %get-tuple-element.113.rows_ref, s32[32]{0:T(128)} %get-tuple-element.114.counts_ref, bf16[8,512,768]{2,1,0:T(8,128)(2,1)} %all-to-all-done.6.x_ref, bf16[8,512,768]{2,1,0:T(8,128)(2,1)} %all-to-all-done.7.dy_ref, ...), custom_call_target="tpu_custom_call" | custom-call | flops 14495514624 | bytes 52428800 | tf_op jit(solution)/shard_map/feed_backward/pallas_call | solution.py:858
  674.3 20.0 %attention_forward.5 = (bf16[8,512,768]{2,1,0:T(8,128)(2,1)}, bf16[3,512,2304]{2,1,0:T(8,128)(2,1)}, bf16[3,512,768]{2,1,0:T(8,128)(2,1)}, bf16[3,512,768]{2,1,0:T(8,128)(2,1)}, f32[3,512,128]{2,1,0:T(8,128)}) custom-call(s32[60]{0:T(128)} %get-tuple-element.113.rows_ref, s32[32]{0:T(128)} %get-tuple-element.114.counts_ref, ...), custom_call_target="tpu_custom_call", output_to_operand_aliasing={{0}: (7, {})} | custom-call | flops 19327352832 | bytes 31457280 | tf_op jit(solution)/shard_map/attention_forward/pallas_call | solution.py:374
  694.3 15.1 conv_forward.5
  709.5 47.5 %attention_backward.4 = (bf16[8,512,768]{2,1,0:T(8,128)(2,1)}, f32[8,768]{1,0:T(8,128)}, f32[768,2304]{1,0:T(8,128)}, f32[768,768]{1,0:T(8,128)}) custom-call(s32[60]{0:T(128)} %get-tuple-element.113.rows_ref, s32[32]{0:T(128)} %get-tuple-element.114.counts_ref, bf16[8,512,768]{2,1,0:T(8,128)(2,1)} %all-to-all-done.3.x_ref.refs_1_, ...), custom_call_target="tpu_custom_call", output_to_operand_aliasing={{0}: (11, {})} | custom-call | flops 19327352832 | bytes 41943040 | tf_op jit(solution)/shard_map/attention_backward/pallas_call | solution.py:563
  756.9 25.7 %conv_backward.4 = (bf16[8,512,768]{2,1,0:T(8,128)(2,1)}, f32[24,768]{1,0:T(8,128)}, f32[3,768,768]{2,1,0:T(8,128)}) custom-call(s32[60]{0:T(128)} %get-tuple-element.113.rows_ref, s32[32]{0:T(128)} %get-tuple-element.114.counts_ref, bf16[8,512,768]{2,1,0:T(8,128)(2,1)} %all-to-all-done.3.x_ref.refs_1_, ...), custom_call_target="tpu_custom_call", output_to_operand_aliasing={{0}: (10, {})} | custom-call | flops 8153726976 | bytes 52428800 | tf_op jit(solution)/shard_map/conv_backward/pallas_call | solution.py:1105
  782.6 44.7 %all-to-all-start.13 = ((bf16[8,512,768]{2,1,0:T(8,128)(2,1)}), bf16[8,512,768]{2,1,0:T(8,128)(2,1)}, u32[]{:S(2)}, u32[]{:S(2)}) async-start(bf16[8,512,768]{2,1,0:T(8,128)(2,1)} %get-tuple-element.161), calls=%async_computation.13 | async-start | bytes 12582912 | tf_op jit(solution)/shard_map/all_to_all | solution.py:1200
  827.3 5.7 attention_forward.7
  833.0 21.3 %conv_forward.7 = (bf16[8,512,768]{2,1,0:T(8,128)(2,1)}, bf16[9,512,768]{2,1,0:T(8,128)(2,1)}, bf16[9,512,768]{2,1,0:T(8,128)(2,1)}, f32[9,512,128]{2,1,0:T(8,128)}) custom-call(s32[60]{0:T(128)} %get-tuple-element.113.rows_ref, s32[32]{0:T(128)} %get-tuple-element.114.counts_ref, ...), custom_call_target="tpu_custom_call", output_to_operand_aliasing={{0}: (7, {})} | custom-call | flops 5435817984 | bytes 37748736 | tf_op jit(solution)/shard_map/conv_forward/pallas_call | solution.py:956
  857.6 11.9 attention_backward.5
  870.5 38.8 %conv_backward.5 = (bf16[8,512,768]{2,1,0:T(8,128)(2,1)}, f32[24,768]{1,0:T(8,128)}, bf16[4,1360,768]{2,1,0:T(8,128)(2,1)}) custom-call(s32[60]{0:T(128)} %get-tuple-element.113.rows_ref, s32[32]{0:T(128)} %get-tuple-element.114.counts_ref, bf16[8,512,768]{2,1,0:T(8,128)(2,1)} %all-to-all-done.6.x_ref, ...), custom_call_target="tpu_custom_call", output_to_operand_aliasing={{2}: (11, {}), {0}: (12, {})} | custom-call | flops 8153726976 | bytes 52428800 | tf_op jit(solution)/shard_map/conv_backward/pallas_call | solution.py:1105
  911.6 40.3 %all-to-all-start.9 = ((bf16[8,512,768]{2,1,0:T(8,128)(2,1)}), bf16[8,512,768]{2,1,0:T(8,128)(2,1)}, u32[]{:S(2)}, u32[]{:S(2)}) async-start(bf16[8,512,768]{2,1,0:T(8,128)(2,1)} %get-tuple-element.159), calls=%async_computation.9 | async-start | bytes 12582912 | tf_op jit(solution)/shard_map/all_to_all | solution.py:1200
  952.7 4.7 relay_dx.3
  957.4 66.2 %all-to-all-done.9.refs_0_ = bf16[8,512,768]{2,1,0:T(8,128)(2,1)} async-done(((bf16[8,512,768]{2,1,0:T(8,128)(2,1)}), bf16[8,512,768]{2,1,0:T(8,128)(2,1)}, u32[]{:S(2)}, u32[]{:S(2)}) %all-to-all-start.9) | async-done | bytes 6291488 | tf_op jit(solution)/shard_map/all_to_all | solution.py:1200
  1023.6 4.7 all-to-all-start.14
  1028.4 4.9 relay_dx.2
  1033.3 66.7 %all-to-all-done.14.dy_ref = bf16[8,512,768]{2,1,0:T(8,128)(2,1)} async-done(((bf16[8,512,768]{2,1,0:T(8,128)(2,1)}), bf16[8,512,768]{2,1,0:T(8,128)(2,1)}, u32[]{:S(2)}, u32[]{:S(2)}) %all-to-all-start.14) | async-done | bytes 6291488 | tf_op jit(solution)/shard_map/all_to_all | solution.py:1200
  1100.0 4.8 all-to-all-start.10
  1104.8 43.9 %feed_backward.6 = (bf16[8,512,768]{2,1,0:T(8,128)(2,1)}, f32[8,768]{1,0:T(8,128)}, f32[768,3072]{1,0:T(8,128)}, f32[3072,768]{1,0:T(8,128)}) custom-call(s32[60]{0:T(128)} %get-tuple-element.113.rows_ref, s32[32]{0:T(128)} %get-tuple-element.114.counts_ref, bf16[8,512,768]{2,1,0:T(8,128)(2,1)} %all-to-all-done.1.x_ref, ...), custom_call_target="tpu_custom_call" | custom-call | flops 14495514624 | bytes 52428800 | tf_op jit(solution)/shard_map/feed_backward/pallas_call | solution.py:858
  1148.8 27.6 %all-to-all-done.10.refs_1_.dy_ref = bf16[8,512,768]{2,1,0:T(8,128)(2,1)} async-done(((bf16[8,512,768]{2,1,0:T(8,128)(2,1)}), bf16[8,512,768]{2,1,0:T(8,128)(2,1)}, u32[]{:S(2)}, u32[]{:S(2)}) %all-to-all-start.10) | async-done | bytes 6291488 | tf_op jit(solution)/shard_map/all_to_all | solution.py:1200
  1176.4 35.3 %feed_backward.7 = (bf16[8,512,768]{2,1,0:T(8,128)(2,1)}, f32[8,768]{1,0:T(8,128)}, bf16[4,1536,768]{2,1,0:T(8,128)(2,1)}) custom-call(s32[60]{0:T(128)} %get-tuple-element.113.rows_ref, s32[32]{0:T(128)} %get-tuple-element.114.counts_ref, bf16[8,512,768]{2,1,0:T(8,128)(2,1)} %all-to-all-done.4.x_ref, bf16[8,512,768]{2,1,0:T(8,128)(2,1)} %all-to-all-done.10.refs_1_.dy_ref, ...), custom_call_target="tpu_custom_call" | custom-call | flops 14495514624 | bytes 52428800 | tf_op jit(solution)/shard_map/feed_backward/pallas_call | solution.py:858
  1211.7 47.5 %attention_backward.6 = (bf16[8,512,768]{2,1,0:T(8,128)(2,1)}, f32[8,768]{1,0:T(8,128)}, f32[768,2304]{1,0:T(8,128)}, f32[768,768]{1,0:T(8,128)}) custom-call(s32[60]{0:T(128)} %get-tuple-element.113.rows_ref, s32[32]{0:T(128)} %get-tuple-element.114.counts_ref, bf16[8,512,768]{2,1,0:T(8,128)(2,1)} %all-to-all-done.1.x_ref, ...), custom_call_target="tpu_custom_call", output_to_operand_aliasing={{0}: (11, {})} | custom-call | flops 19327352832 | bytes 41943040 | tf_op jit(solution)/shard_map/attention_backward/pallas_call | solution.py:563
  1259.3 23.3 %conv_backward.6 = (bf16[8,512,768]{2,1,0:T(8,128)(2,1)}, f32[24,768]{1,0:T(8,128)}, f32[3,768,768]{2,1,0:T(8,128)}) custom-call(s32[60]{0:T(128)} %get-tuple-element.113.rows_ref, s32[32]{0:T(128)} %get-tuple-element.114.counts_ref, bf16[8,512,768]{2,1,0:T(8,128)(2,1)} %all-to-all-done.1.x_ref, ...), custom_call_target="tpu_custom_call", output_to_operand_aliasing={{0}: (10, {})} | custom-call | flops 8153726976 | bytes 52428800 | tf_op jit(solution)/shard_map/conv_backward/pallas_call | solution.py:1105
  1282.6 22.9 %all-to-all-start.15 = ((bf16[8,512,768]{2,1,0:T(8,128)(2,1)}), bf16[8,512,768]{2,1,0:T(8,128)(2,1)}, u32[]{:S(2)}, u32[]{:S(2)}) async-start(bf16[8,512,768]{2,1,0:T(8,128)(2,1)} %get-tuple-element.175), calls=%async_computation.15 | async-start | bytes 12582912 | tf_op jit(solution)/shard_map/all_to_all | solution.py:1200
  1307.6 12.3 attention_backward.7
  1319.9 57.3 %all-to-all-done.15.refs_0_ = bf16[8,512,768]{2,1,0:T(8,128)(2,1)} async-done(((bf16[8,512,768]{2,1,0:T(8,128)(2,1)}), bf16[8,512,768]{2,1,0:T(8,128)(2,1)}, u32[]{:S(2)}, u32[]{:S(2)}) %all-to-all-start.15) | async-done | bytes 6291488 | tf_op jit(solution)/shard_map/all_to_all | solution.py:1200
  1377.2 4.8 all-to-all-start.11
  1384.3 37.3 %conv_backward.7 = (bf16[8,512,768]{2,1,0:T(8,128)(2,1)}, f32[24,768]{1,0:T(8,128)}, bf16[4,1360,768]{2,1,0:T(8,128)(2,1)}) custom-call(s32[60]{0:T(128)} %get-tuple-element.113.rows_ref, s32[32]{0:T(128)} %get-tuple-element.114.counts_ref, bf16[8,512,768]{2,1,0:T(8,128)(2,1)} %all-to-all-done.4.x_ref, ...), custom_call_target="tpu_custom_call", output_to_operand_aliasing={{2}: (11, {}), {0}: (12, {})} | custom-call | flops 8153726976 | bytes 52428800 | tf_op jit(solution)/shard_map/conv_backward/pallas_call | solution.py:1105
  1424.7 28.8 %all-to-all-done.11.refs_0_ = bf16[8,512,768]{2,1,0:T(8,128)(2,1)} async-done(((bf16[8,512,768]{2,1,0:T(8,128)(2,1)}), bf16[8,512,768]{2,1,0:T(8,128)(2,1)}, u32[]{:S(2)}, u32[]{:S(2)}) %all-to-all-start.11) | async-done | bytes 6291488 | tf_op jit(solution)/shard_map/all_to_all | solution.py:1200
  1453.5 76.9 %all_to_all.89.refs_1_ = bf16[8,512,768]{2,1,0:T(8,128)(2,1)} all-to-all(bf16[8,512,768]{2,1,0:T(8,128)(2,1)} %after.6), channel_id=1, replica_groups=mesh['dp'=4,'op'=8] {'op'}, dimensions={0} | all-to-all | bytes 12582912 | tf_op jit(solution)/shard_map/all_to_all | solution.py:1200
  1530.5 4.8 all-to-all-start.16
  1535.3 8.1 outputs.1
  1543.5 63.4 %all-to-all-done.16.refs_1_ = bf16[8,512,768]{2,1,0:T(8,128)(2,1)} async-done(((bf16[8,512,768]{2,1,0:T(8,128)(2,1)}), bf16[8,512,768]{2,1,0:T(8,128)(2,1)}, u32[]{:S(2)}, u32[]{:S(2)}) %all-to-all-start.16) | async-done | bytes 6291488 | tf_op jit(solution)/shard_map/all_to_all | solution.py:1200
  1606.9 8.0 input_grad.1
  1656.2 4.7 fusion.1
  (213 shorter events, 103.7 us)
Async XLA Ops:
  12.3 9.8 all-to-all-start
  22.1 76.4 %all-to-all-start.1 = ((bf16[8,512,768]{2,1,0:T(8,128)(2,1)}), bf16[8,512,768]{2,1,0:T(8,128)(2,1)}, u32[]{:S(2)}, u32[]{:S(2)}) async-start(bf16[8,512,768]{2,1,0:T(8,128)(2,1)} %send_inputs.2), calls=%async_computation.1 | async-start | bytes 12582912 | tf_op jit(solution)/shard_map/all_to_all | solution.py:1200
  31.7 71.6 %copy-start.15 = (bf16[2,1,5,768]{3,0,2,1:T(2,128)(2,1)S(1)}, bf16[2,1,5,768]{3,0,2,1:T(2,128)(2,1)}, u32[]{:S(2)}) copy-start(bf16[2,1,5,768]{3,0,2,1:T(2,128)(2,1)} %param.19) | copy-start | bytes 46084
  31.7 71.7 %copy-start.16 = (bf16[2,1,5,768]{3,0,2,1:T(2,128)(2,1)S(1)}, bf16[2,1,5,768]{3,0,2,1:T(2,128)(2,1)}, u32[]{:S(2)}) copy-start(bf16[2,1,5,768]{3,0,2,1:T(2,128)(2,1)} %param.20) | copy-start | bytes 46084
  31.7 71.7 %copy-start.11 = (bf16[2,1,15,768]{3,0,2,1:T(2,128)(2,1)S(1)}, bf16[2,1,15,768]{3,0,2,1:T(2,128)(2,1)}, u32[]{:S(2)}) copy-start(bf16[2,1,15,768]{3,0,2,1:T(2,128)(2,1)} %param.17) | copy-start | bytes 138244
  98.5 76.3 %all-to-all-start.4 = ((bf16[8,512,768]{2,1,0:T(8,128)(2,1)}), bf16[8,512,768]{2,1,0:T(8,128)(2,1)}, u32[]{:S(2)}, u32[]{:S(2)}) async-start(bf16[8,512,768]{2,1,0:T(8,128)(2,1)} %send_inputs.3), calls=%async_computation.4 | async-start | bytes 12582912 | tf_op jit(solution)/shard_map/all_to_all | solution.py:1200
  174.9 76.8 %all-to-all-start.2 = ((bf16[8,512,768]{2,1,0:T(8,128)(2,1)}), bf16[8,512,768]{2,1,0:T(8,128)(2,1)}, u32[]{:S(2)}, u32[]{:S(2)}) async-start(bf16[8,512,768]{2,1,0:T(8,128)(2,1)} %get-tuple-element.118), calls=%async_computation.2 | async-start | bytes 12582912 | tf_op jit(solution)/shard_map/all_to_all | solution.py:1200
  251.6 76.4 %all-to-all-start.5 = ((bf16[8,512,768]{2,1,0:T(8,128)(2,1)}), bf16[8,512,768]{2,1,0:T(8,128)(2,1)}, u32[]{:S(2)}, u32[]{:S(2)}) async-start(bf16[8,512,768]{2,1,0:T(8,128)(2,1)} %get-tuple-element.124), calls=%async_computation.5 | async-start | bytes 12582912 | tf_op jit(solution)/shard_map/all_to_all | solution.py:1200
  328.0 76.4 %all-to-all-start.3 = ((bf16[8,512,768]{2,1,0:T(8,128)(2,1)}), bf16[8,512,768]{2,1,0:T(8,128)(2,1)}, u32[]{:S(2)}, u32[]{:S(2)}) async-start(bf16[8,512,768]{2,1,0:T(8,128)(2,1)} %relay_x.2), calls=%async_computation.3 | async-start | bytes 12582912 | tf_op jit(solution)/shard_map/all_to_all | solution.py:1200
  404.4 76.4 %all-to-all-start.6 = ((bf16[8,512,768]{2,1,0:T(8,128)(2,1)}), bf16[8,512,768]{2,1,0:T(8,128)(2,1)}, u32[]{:S(2)}, u32[]{:S(2)}) async-start(bf16[8,512,768]{2,1,0:T(8,128)(2,1)} %relay_x.3), calls=%async_computation.6 | async-start | bytes 12582912 | tf_op jit(solution)/shard_map/all_to_all | solution.py:1200
  480.8 76.4 %all-to-all-start.8 = ((bf16[8,512,768]{2,1,0:T(8,128)(2,1)}), bf16[8,512,768]{2,1,0:T(8,128)(2,1)}, u32[]{:S(2)}, u32[]{:S(2)}) async-start(bf16[8,512,768]{2,1,0:T(8,128)(2,1)} %send_cotangent.3), calls=%async_computation.8 | async-start | bytes 12582912 | tf_op jit(solution)/shard_map/all_to_all | solution.py:1200
  557.2 79.3 %all-to-all-start.7 = ((bf16[8,512,768]{2,1,0:T(8,128)(2,1)}), bf16[8,512,768]{2,1,0:T(8,128)(2,1)}, u32[]{:S(2)}, u32[]{:S(2)}) async-start(bf16[8,512,768]{2,1,0:T(8,128)(2,1)} %send_cotangent.2), calls=%async_computation.7 | async-start | bytes 12582912 | tf_op jit(solution)/shard_map/all_to_all | solution.py:1200
  562.0 390.8 %reduce-scatter.5.cloned.1.call-start = ((), (), s32[]{:S(2)}) async-start(), calls=%async_computation.21 | async-start | bytes 11796480 | tf_op jit(solution)/shard_map/reduce_scatter | solution.py:1269
  672.2 0.8 copy-start.12
  672.2 1.4 copy-start.17
  782.6 129.0 %all-to-all-start.13 = ((bf16[8,512,768]{2,1,0:T(8,128)(2,1)}), bf16[8,512,768]{2,1,0:T(8,128)(2,1)}, u32[]{:S(2)}, u32[]{:S(2)}) async-start(bf16[8,512,768]{2,1,0:T(8,128)(2,1)} %get-tuple-element.161), calls=%async_computation.13 | async-start | bytes 12582912 | tf_op jit(solution)/shard_map/all_to_all | solution.py:1200
  833.0 23.2 %copy-start.14 = (f32[24,768]{1,0:T(8,128)S(1)}, f32[24,768]{1,0:T(8,128)}, u32[]{:S(2)}) copy-start(f32[24,768]{1,0:T(8,128)} %get-tuple-element.205) | copy-start | bytes 221188
  911.6 112.0 %all-to-all-start.9 = ((bf16[8,512,768]{2,1,0:T(8,128)(2,1)}), bf16[8,512,768]{2,1,0:T(8,128)(2,1)}, u32[]{:S(2)}, u32[]{:S(2)}) async-start(bf16[8,512,768]{2,1,0:T(8,128)(2,1)} %get-tuple-element.159), calls=%async_computation.9 | async-start | bytes 12582912 | tf_op jit(solution)/shard_map/all_to_all | solution.py:1200
  951.9 259.7 %reduce-scatter.7.cloned.1.call-start = ((), (), s32[]{:S(2)}) async-start(), calls=%async_computation.22 | async-start | bytes 10444800 | tf_op jit(solution)/shard_map/reduce_scatter | solution.py:1271
  1023.6 76.3 %all-to-all-start.14 = ((bf16[8,512,768]{2,1,0:T(8,128)(2,1)}), bf16[8,512,768]{2,1,0:T(8,128)(2,1)}, u32[]{:S(2)}, u32[]{:S(2)}) async-start(bf16[8,512,768]{2,1,0:T(8,128)(2,1)} %relay_dx.3), calls=%async_computation.14 | async-start | bytes 12582912 | tf_op jit(solution)/shard_map/all_to_all | solution.py:1200
  1100.0 76.4 %all-to-all-start.10 = ((bf16[8,512,768]{2,1,0:T(8,128)(2,1)}), bf16[8,512,768]{2,1,0:T(8,128)(2,1)}, u32[]{:S(2)}, u32[]{:S(2)}) async-start(bf16[8,512,768]{2,1,0:T(8,128)(2,1)} %relay_dx.2), calls=%async_computation.10 | async-start | bytes 12582912 | tf_op jit(solution)/shard_map/all_to_all | solution.py:1200
  1104.8 319.9 %reduce-scatter.9.cloned.1.call-start = ((), (), s32[]{:S(2)}) async-start(), calls=%async_computation.23 | async-start | bytes 11796480 | tf_op jit(solution)/shard_map/reduce_scatter | solution.py:1269
  1282.6 22.9 %copy-start.18 = (s32[16]{0:T(128)S(1)}, s32[16]{0:T(128)}, u32[]{:S(2)}) copy-start(s32[16]{0:T(128)} %get-tuple-element.294) | copy-start | bytes 196
  1282.6 25.0 %copy-start.13 = (f32[24,768]{1,0:T(8,128)S(1)}, f32[24,768]{1,0:T(8,128)}, u32[]{:S(2)}) copy-start(f32[24,768]{1,0:T(8,128)} %get-tuple-element.197) | copy-start | bytes 221188
  1282.6 94.5 %all-to-all-start.15 = ((bf16[8,512,768]{2,1,0:T(8,128)(2,1)}), bf16[8,512,768]{2,1,0:T(8,128)(2,1)}, u32[]{:S(2)}, u32[]{:S(2)}) async-start(bf16[8,512,768]{2,1,0:T(8,128)(2,1)} %get-tuple-element.175), calls=%async_computation.15 | async-start | bytes 12582912 | tf_op jit(solution)/shard_map/all_to_all | solution.py:1200
  1377.2 76.4 %all-to-all-start.11 = ((bf16[8,512,768]{2,1,0:T(8,128)(2,1)}), bf16[8,512,768]{2,1,0:T(8,128)(2,1)}, u32[]{:S(2)}, u32[]{:S(2)}) async-start(bf16[8,512,768]{2,1,0:T(8,128)(2,1)} %after.5), calls=%async_computation.11 | async-start | bytes 12582912 | tf_op jit(solution)/shard_map/all_to_all | solution.py:1200
  1381.9 266.1 %reduce-scatter.11.cloned.1.call-start = ((), (), s32[]{:S(2)}) async-start(), calls=%async_computation.24 | async-start | bytes 10444800 | tf_op jit(solution)/shard_map/reduce_scatter | solution.py:1271
  1530.5 76.4 %all-to-all-start.16 = ((bf16[8,512,768]{2,1,0:T(8,128)(2,1)}), bf16[8,512,768]{2,1,0:T(8,128)(2,1)}, u32[]{:S(2)}, u32[]{:S(2)}) async-start(bf16[8,512,768]{2,1,0:T(8,128)(2,1)} %get-tuple-element.195), calls=%async_computation.16 | async-start | bytes 12582912 | tf_op jit(solution)/shard_map/all_to_all | solution.py:1200
  1543.5 71.5 %copy-start.1 = (bf16[1,1536,768]{2,1,0:T(8,128)(2,1)S(1)}, bf16[1,1536,768]{2,1,0:T(8,128)(2,1)}, u32[]{:S(2)}) copy-start(bf16[1,1536,768]{2,1,0:T(8,128)(2,1)} %reduce-scatter.5.cloned.1.call-done) | copy-start | bytes 7077892
  1614.9 1.6 copy-start.7
  1616.9 2.0 copy-start
  1632.3 13.2 copy-start.2
  1674.3 3.9 copy-start.19
  1676.8 1.7 copy-start.9
  1678.3 2.3 copy-start.5
  1678.3 3.7 copy-start.6
  1682.0 2.7 copy-start.3
  1682.0 4.1 copy-start.4
  1686.1 3.8 copy-start.8
  1686.1 3.8 copy-start.10
Sparse Core Ops, SparseCore 0:
  672.4 183.5 reduce-scatter.4
  955.1 147.2 reduce-scatter.6
  1211.8 173.0 reduce-scatter.8
  1424.9 140.3 reduce-scatter.10

commit v3 on v2

--- a/solution.py
+++ b/solution.py
@@ -14,7 +14,8 @@
 FF_PART = 768
 FF_SUB = 256
 LANES = 128
-SMALL_ROWS = 16
+SMALL_ROWS = 32
+COUNT_ROWS = 16
 BF16 = jnp.bfloat16
 F32 = jnp.float32
 VMEM_BYTES = 60 * 2**20
@@ -723,8 +724,8 @@
             dx_ref, small_ref, acc_up, acc_down = rest[:4]
         else:
             sum_up, sum_down, dx_ref, small_ref, packed_ref = rest[:5]
-            acc_up, acc_down, low_up, low_down, sems = rest[-5:]
-        x_scr, dh_scr, dx_scr, da_scr = rest[-4:] if first else rest[-9:-5]
+            acc_up, acc_down, low_up, low_down, tally, sems = rest[-6:]
+        x_scr, dh_scr, dx_scr, da_scr = rest[-4:] if first else rest[-10:-6]
         c, i = pl.program_id(0), pl.program_id(1)
 
         @pl.when(jnp.logical_and(c == 0, i == 0))
@@ -785,6 +786,20 @@
                     for z in range(groups)
                 ]
                 shares = FF_PART // deep
+                lane = lax.broadcasted_iota(jnp.int32, (COUNT_ROWS, width), 1)
+                counted = jnp.zeros((COUNT_ROWS, width), F32)
+                for k in range(KINDS):
+                    there = sum(counts_ref[(b * HALVES + half) * 8 + k] for half in range(HALVES))
+                    counted = jnp.where(lane == k, there.astype(F32), counted)
+                tally[...] = counted.astype(BF16)
+                copies += [
+                    pltpu.make_async_copy(
+                        tally,
+                        packed_ref.at[z, pl.ds(parts * tall + deep, COUNT_ROWS)],
+                        sems.at[groups + shares + z],
+                    )
+                    for z in range(groups)
+                ]
                 copies += [
                     pltpu.make_async_copy(
                         low_down.at[pl.ds(m * deep, deep)],
@@ -847,13 +862,16 @@
         in_specs += [up_spec, down_spec]
         args += list(sums)
         out_specs.append(ANY_SPEC)
-        out_shape.append(jax.ShapeDtypeStruct((groups, parts * tall + deep, width), BF16))
+        out_shape.append(
+            jax.ShapeDtypeStruct((groups, parts * tall + deep + COUNT_ROWS, width), BF16)
+        )
         scratch += [
             pltpu.VMEM((width, FF_PART), F32),
             pltpu.VMEM((FF_PART, width), F32),
             pltpu.VMEM((width, FF_PART), BF16),
             pltpu.VMEM((FF_PART, width), BF16),
-            pltpu.SemaphoreType.DMA((groups + FF_PART // deep,)),
+            pltpu.VMEM((COUNT_ROWS, width), BF16),
+            pltpu.SemaphoreType.DMA((2 * groups + FF_PART // deep,)),
         ]
     return pl.pallas_call(
         kernel,
@@ -1179,14 +1197,109 @@
             )
         dx[half] = d
         smalls[half] = join_small(small_f, small_a, small_c)
-    counts = tables[1].reshape(BLOCKS, HALVES, 8)[b].sum(axis=0).astype(BF16)
-    small = (smalls[0] + smalls[1]).reshape(25, groups, width // groups)
-    small = small.transpose(1, 0, 2).reshape(groups, -1).astype(BF16)
-    small = jnp.pad(small, ((0, 0), (0, (SMALL_ROWS - 1) * width - small.shape[1])))
-    last = jnp.pad(jnp.broadcast_to(counts, (groups, 8)), ((0, 0), (0, width - 8)))
-    small = jnp.concatenate([small, last], axis=1).reshape(groups, SMALL_ROWS, width)
+    small = (smalls[0] + smalls[1]).astype(BF16).reshape(25, groups, width // groups)
+    small = small.transpose(1, 0, 2)
+    small = jnp.pad(small, ((0, 0), (0, SMALL_ROWS - 25), (0, width - width // groups)))
     rest_pack = lax.dynamic_update_slice(rest_pack, small, (0, rest_rows - SMALL_ROWS, 0))
     return dx, feed_pack, rest_pack
+
+
+def finish_feed(b, feed, up_out, down_out, shapes):
+    parts = shapes[0].shape[-1] // FF_PART
+    tall, width = shapes[0].shape[2], FF_PART
+    count_block = 2 * parts * tall // COUNT_ROWS
+
+    def kernel(up_ref, down_ref, count_ref, *rest):
+        up_to, down_to = rest[-2:]
+        scale = 1.0 / count_ref[0:1, KINDS - 1 : KINDS].astype(F32)
+        up_to[...] = up_ref[...].astype(F32) * scale
+        down_to[...] = down_ref[...].astype(F32) * scale
+
+    old = [] if up_out is None else [up_out, down_out]
+    return pl.pallas_call(
+        kernel,
+        grid=(parts,),
+        in_specs=[
+            pl.BlockSpec((tall, width), lambda c: (c, 0)),
+            pl.BlockSpec((tall, width), lambda c: (parts + c, 0)),
+            pl.BlockSpec((COUNT_ROWS, width), lambda c: (count_block, 0)),
+        ]
+        + [ANY_SPEC] * len(old),
+        out_specs=[
+            pl.BlockSpec((None, None, tall, width), lambda c: (b, 0, 0, c)),
+            pl.BlockSpec((None, None, tall, width), lambda c: (b, 0, c, 0)),
+        ],
+        out_shape=list(shapes),
+        input_output_aliases={3 + n: n for n in range(len(old))},
+        compiler_params=params_of(1),
+        cost_estimate=pl.CostEstimate(flops=0, transcendentals=0, bytes_accessed=8 * 2**20),
+        name="finish_feed",
+    )(feed, feed, feed, *old)
+
+
+def finish_rest(b, rest, feed, old, shapes):
+    tall, width = shapes[1].shape[2:]
+    count_block = (feed.shape[0] - COUNT_ROWS) // COUNT_ROWS
+    small_block = 7 * tall // SMALL_ROWS
+
+    def kernel(rest_ref, small_ref, count_ref, *refs):
+        qkv_to, out_to, taps_to, point_to, gain_to, shift_to = refs[-6:]
+        i = pl.program_id(0)
+        scales = 1.0 / count_ref[0:1, 0:8].astype(F32)
+        values = rest_ref[...].astype(F32)
+
+        @pl.when(i < 3)
+        def _():
+            qkv_to[...] = values * scales[:, 0:1]
+
+        @pl.when(i == 3)
+        def _():
+            out_to[...] = values * scales[:, 0:1]
+            small = small_ref[...].astype(F32)
+            row = lax.broadcasted_iota(jnp.int32, small.shape, 0)
+            which = jnp.where(row < 3, 1, jnp.where(row < 8, 2, jnp.where(row < 15, 3, 0)))
+            which = jnp.where(row >= 15, row - 15, which)
+            which = jnp.where(row >= 20, row - 20, which)
+            scale = jnp.zeros_like(small)
+            for k in range(KINDS):
+                scale = jnp.where(which == k, scales[:, k : k + 1], scale)
+            small = small * scale
+            taps_to[...] = small[:15, :tall]
+            gain_to[...] = small[15:20, :tall]
+            shift_to[...] = small[20:25, :tall]
+
+        for k in range(1, KINDS - 1):
+
+            @pl.when(i == 3 + k)
+            def _():
+                point_to[...] = values * scales[:, k : k + 1]
+
+    old = list(old)
+    return pl.pallas_call(
+        kernel,
+        grid=(7,),
+        in_specs=[
+            pl.BlockSpec((tall, width), lambda i: (i, 0)),
+            pl.BlockSpec((SMALL_ROWS, width), lambda i: (small_block, 0)),
+            pl.BlockSpec((COUNT_ROWS, width), lambda i: (count_block, 0)),
+        ]
+        + [ANY_SPEC] * len(old),
+        out_specs=[
+            pl.BlockSpec((None, None, tall, width), lambda i: (b, 0, 0, jnp.minimum(i, 2))),
+            pl.BlockSpec((None, None, tall, width), lambda i: (b, 0, 0, 0)),
+            pl.BlockSpec((None, None, 15, tall), lambda i: (b, 0, 0, 0)),
+            pl.BlockSpec(
+                (None, None, None, tall, width), lambda i: (b, 0, jnp.maximum(i - 4, 0), 0, 0)
+            ),
+            pl.BlockSpec((None, None, KINDS, tall), lambda i: (b, 0, 0, 0)),
+            pl.BlockSpec((None, None, KINDS, tall), lambda i: (b, 0, 0, 0)),
+        ],
+        out_shape=list(shapes),
+        input_output_aliases={3 + n: n for n in range(len(old))},
+        compiler_params=params_of(1),
+        cost_estimate=pl.CostEstimate(flops=0, transcendentals=0, bytes_accessed=8 * 2**20),
+        name="finish_rest",
+    )(rest, rest, feed, *old)
 
 
 def small_params(b, conv_taps, norm_gain, norm_bias):
@@ -1237,17 +1350,17 @@
     for h in both:
         back = exchange(y0[h])
         x1.append(exchange(move_rows(relay, [start(0, h)], [back], owners, False, "relay_x")))
+    y1, kept1 = zip(
+        *[owner_forward(HALVES + h, tables, x1[h], weights, smalls[1]) for h in both]
+    )
     dy1 = [
         exchange(
             move_rows(
-                send, [start(1, h)], [cotangent], owners, False, "send_cotangent", (x1[0],)
+                send, [start(1, h)], [cotangent], owners, False, "send_cotangent", (y1[h],)
             )
         )
         for h in both
     ]
-    y1, kept1 = zip(
-        *[owner_forward(HALVES + h, tables, x1[h], weights, smalls[1]) for h in both]
-    )
     dx1, feed1, rest1 = owner_backward(1, tables, x1, dy1, kept1, weights, smalls[1], groups)
     dy0 = []
     for h in both:
@@ -1261,36 +1374,28 @@
     dx_home = [exchange(dx0[h]) for h in both]
     input_grad = move_rows(send, starts, dx_home, seqs, True, "input_grad")
 
-    tall, deep, parts = width // groups, hidden // groups, hidden // FF_PART
-    finished, earlier = [None, None], None
+    tall, deep = width // groups, hidden // groups
+    grad = lambda *dims: jax.ShapeDtypeStruct((BLOCKS, 1) + dims, F32)
+    feed_shapes = (grad(tall, hidden), grad(deep, width))
+    rest_shapes = (
+        grad(tall, 3 * width),
+        grad(tall, width),
+        grad(15, tall),
+        grad(KINDS - 2, tall, width),
+        grad(KINDS, tall),
+        grad(KINDS, tall),
+    )
+    earlier, feeds, rests = None, (None, None), ()
     for b, feed, rest in ((1, feed1, rest1), (0, feed0, rest0)):
         if earlier is not None:
             feed = after(feed, (earlier,))
         feed = lax.psum_scatter(feed, "dp", scatter_dimension=0, tiled=False)
-        rest = after(rest, (feed,))
+        rest = after(rest, (feed,) if b else (feed, y_home[0], dx_home[0]))
         earlier = lax.psum_scatter(rest, "dp", scatter_dimension=0, tiled=False)
-        feed, rest = feed.astype(F32), earlier.astype(F32)
-        total = rest[-1, :KINDS]
-        small = rest[7 * tall : -1].reshape(-1)[: 25 * tall].reshape(25, tall)
-        up = feed[: parts * tall].reshape(parts, tall, FF_PART).transpose(1, 0, 2)
-        qkv = rest[: 3 * tall].reshape(3, tall, width).transpose(1, 0, 2)
-        point = rest[4 * tall : 7 * tall].reshape(KINDS - 2, tall, width)
-        tap_total = jnp.concatenate(
-            [jnp.broadcast_to(total[k], (2 * k + 1,)) for k in range(1, KINDS - 1)]
-        )
-        finished[b] = (
-            qkv.reshape(tall, 3 * width) / total[0],
-            rest[3 * tall : 4 * tall] / total[0],
-            up.reshape(tall, hidden) / total[KINDS - 1],
-            feed[parts * tall :] / total[KINDS - 1],
-            small[:15] / tap_total[:, None],
-            point / total[1 : KINDS - 1, None, None],
-            small[15:20] / total[:, None],
-            small[20:25] / total[:, None],
-        )
-    grads = tuple(
-        jnp.stack([finished[0][n], finished[1][n]])[:, None] for n in range(8)
-    )
+        feeds = finish_feed(b, feed, *feeds, feed_shapes)
+        rests = finish_rest(b, earlier, feed, rests, rest_shapes)
+    qkv, out, taps, point, gain, shift = rests
+    grads = (qkv, out, *feeds, taps, point, gain, shift)
     return (outputs, input_grad) + grads
 
 

time: 1710 us -> 1580 us (0.924)
  the two profiles are of different devices: /device:TPU:0 before, /device:TPU:16 now
where the time goes in v3:
time: 1580 us; the launch traced here: 1550 us
  waiting for transfers between devices  694 us (44%)
  Pallas kernels  687 us (43%)
  starting transfers between devices  130 us (8%)
  local copies, waits for them, and re-layouts  20.6 us (1%)
    all_to_all x17, waiting for transfers between devices, exchange(): return lax.all_to_all(rows, 'op', split_axis=0, concat_axis=0, tiled=True)  694 us
    pallas_call x4, Pallas kernels, feed_backward(): pl.pallas_call(kernel, grid_spec=pltpu.PrefetchScalarGridSpec(num_scalar_...  135 us
    pallas_call x4, Pallas kernels, attention_backward(): pl.pallas_call(kernel, grid_spec=pltpu.PrefetchScalarGridSpec(num_scalar_...  132 us
    all_to_all x17, starting transfers between devices, exchange(): return lax.all_to_all(rows, 'op', split_axis=0, concat_axis=0, tiled=True)  130 us
    pallas_call x4, Pallas kernels, conv_backward(): pl.pallas_call(kernel, grid_spec=pltpu.PrefetchScalarGridSpec(num_scalar_...  127 us
    pallas_call x4, Pallas kernels, feed_forward(): pl.pallas_call(kernel, grid_spec=pltpu.PrefetchScalarGridSpec(num_scalar_...  81.6 us
    pallas_call x4, Pallas kernels, conv_forward(): pl.pallas_call(kernel, grid_spec=pltpu.PrefetchScalarGridSpec(num_scalar_...  72.9 us
    pallas_call x4, Pallas kernels, attention_forward(): pl.pallas_call(kernel, grid_spec=pltpu.PrefetchScalarGridSpec(num_scalar_...  58.8 us
  transfers between devices with their start and end apart: 21, of which 15 were waited for; matrix products, arithmetic and copies ran while one was open for 1% of the time, Pallas kernels for 41%

profile of v3, /device:TPU:16, one launch (start us, length us, event | category | flops | bytes accessed | tf_op | source)
XLA Modules:
  0.0 1549.8 jit_solution(10474100943777542928)
XLA Ops:
  20.7 4.8 all-to-all-start.1
  30.2 66.9 %all-to-all-done.1.x_ref = bf16[8,512,768]{2,1,0:T(8,128)(2,1)} async-done(((bf16[8,512,768]{2,1,0:T(8,128)(2,1)}), bf16[8,512,768]{2,1,0:T(8,128)(2,1)}, u32[]{:S(2)}, u32[]{:S(2)}) %all-to-all-start.1) | async-done | bytes 6291488 | tf_op jit(solution)/shard_map/all_to_all | solution.py:1313
  97.1 4.8 all-to-all-start.4
  106.9 20.5 %feed_forward.4 = (bf16[8,512,768]{2,1,0:T(8,128)(2,1)}, bf16[3,512,3072]{2,1,0:T(8,128)(2,1)}, bf16[3,512,3072]{2,1,0:T(8,128)(2,1)}, bf16[3,512,768]{2,1,0:T(8,128)(2,1)}, f32[3,512,128]{2,1,0:T(8,128)}) custom-call(s32[60]{0:T(128)} %get-tuple-element.129.rows_ref, s32[32]{0:T(128)} %get-tuple-element.130.counts_ref, ...), custom_call_target="tpu_custom_call" | custom-call | flops 14495514624 | bytes 41943040 | tf_op jit(solution)/shard_map/feed_forward/pallas_call | solution.py:669
  127.4 12.9 attention_forward.4
  140.3 18.9 %conv_forward.4 = (bf16[8,512,768]{2,1,0:T(8,128)(2,1)}, bf16[9,512,768]{2,1,0:T(8,128)(2,1)}, bf16[9,512,768]{2,1,0:T(8,128)(2,1)}, f32[9,512,128]{2,1,0:T(8,128)}) custom-call(s32[60]{0:T(128)} %get-tuple-element.129.rows_ref, s32[32]{0:T(128)} %get-tuple-element.130.counts_ref, ...), custom_call_target="tpu_custom_call", output_to_operand_aliasing={{0}: (7, {})} | custom-call | flops 5435817984 | bytes 37748736 | tf_op jit(solution)/shard_map/conv_forward/pallas_call | solution.py:974
  159.2 14.2 all-to-all-done.4.x_ref
  173.4 5.0 all-to-all-start.2
  178.4 29.4 %feed_forward.6 = (bf16[8,512,768]{2,1,0:T(8,128)(2,1)}, bf16[3,512,3072]{2,1,0:T(8,128)(2,1)}, bf16[3,512,3072]{2,1,0:T(8,128)(2,1)}, bf16[3,512,768]{2,1,0:T(8,128)(2,1)}, f32[3,512,128]{2,1,0:T(8,128)}) custom-call(s32[60]{0:T(128)} %get-tuple-element.129.rows_ref, s32[32]{0:T(128)} %get-tuple-element.130.counts_ref, ...), custom_call_target="tpu_custom_call" | custom-call | flops 14495514624 | bytes 41943040 | tf_op jit(solution)/shard_map/feed_forward/pallas_call | solution.py:669
  207.8 12.9 attention_forward.6
  220.8 16.9 %conv_forward.6 = (bf16[8,512,768]{2,1,0:T(8,128)(2,1)}, bf16[9,512,768]{2,1,0:T(8,128)(2,1)}, bf16[9,512,768]{2,1,0:T(8,128)(2,1)}, f32[9,512,128]{2,1,0:T(8,128)}) custom-call(s32[60]{0:T(128)} %get-tuple-element.129.rows_ref, s32[32]{0:T(128)} %get-tuple-element.130.counts_ref, ...), custom_call_target="tpu_custom_call", output_to_operand_aliasing={{0}: (7, {})} | custom-call | flops 5435817984 | bytes 37748736 | tf_op jit(solution)/shard_map/conv_forward/pallas_call | solution.py:974
  237.7 12.4 all-to-all-done.2.refs_0_
  250.0 4.8 all-to-all-start.5
  254.8 4.7 relay_x.2
  259.5 66.9 %all-to-all-done.5.refs_0_ = bf16[8,512,768]{2,1,0:T(8,128)(2,1)} async-done(((bf16[8,512,768]{2,1,0:T(8,128)(2,1)}), bf16[8,512,768]{2,1,0:T(8,128)(2,1)}, u32[]{:S(2)}, u32[]{:S(2)}) %all-to-all-start.5) | async-done | bytes 6291488 | tf_op jit(solution)/shard_map/all_to_all | solution.py:1313
  326.4 4.8 all-to-all-start.3
  331.2 4.7 relay_x.3
  335.9 66.9 %all-to-all-done.3.x_ref = bf16[8,512,768]{2,1,0:T(8,128)(2,1)} async-done(((bf16[8,512,768]{2,1,0:T(8,128)(2,1)}), bf16[8,512,768]{2,1,0:T(8,128)(2,1)}, u32[]{:S(2)}, u32[]{:S(2)}) %all-to-all-start.3) | async-done | bytes 6291488 | tf_op jit(solution)/shard_map/all_to_all | solution.py:1313
  402.8 4.9 all-to-all-start.6
  409.0 11.0 feed_forward.5
  420.0 12.9 attention_forward.5
  432.9 21.7 %conv_forward.5 = (bf16[8,512,768]{2,1,0:T(8,128)(2,1)}, bf16[9,512,768]{2,1,0:T(8,128)(2,1)}, bf16[9,512,768]{2,1,0:T(8,128)(2,1)}, f32[9,512,128]{2,1,0:T(8,128)}) custom-call(s32[60]{0:T(128)} %get-tuple-element.129.rows_ref, s32[32]{0:T(128)} %get-tuple-element.130.counts_ref, ...), custom_call_target="tpu_custom_call", output_to_operand_aliasing={{0}: (7, {})} | custom-call | flops 5435817984 | bytes 37748736 | tf_op jit(solution)/shard_map/conv_forward/pallas_call | solution.py:974
  459.3 20.0 %all-to-all-done.6.x_ref = bf16[8,512,768]{2,1,0:T(8,128)(2,1)} async-done(((bf16[8,512,768]{2,1,0:T(8,128)(2,1)}), bf16[8,512,768]{2,1,0:T(8,128)(2,1)}, u32[]{:S(2)}, u32[]{:S(2)}) %all-to-all-start.6) | async-done | bytes 6291488 | tf_op jit(solution)/shard_map/all_to_all | solution.py:1313
  479.3 5.2 all-to-all-start.8
  484.5 20.6 %feed_forward.7 = (bf16[8,512,768]{2,1,0:T(8,128)(2,1)}, bf16[3,512,3072]{2,1,0:T(8,128)(2,1)}, bf16[3,512,3072]{2,1,0:T(8,128)(2,1)}, bf16[3,512,768]{2,1,0:T(8,128)(2,1)}, f32[3,512,128]{2,1,0:T(8,128)}) custom-call(s32[60]{0:T(128)} %get-tuple-element.129.rows_ref, s32[32]{0:T(128)} %get-tuple-element.130.counts_ref, ...), custom_call_target="tpu_custom_call" | custom-call | flops 14495514624 | bytes 41943040 | tf_op jit(solution)/shard_map/feed_forward/pallas_call | solution.py:669
  505.1 20.0 %attention_forward.7 = (bf16[8,512,768]{2,1,0:T(8,128)(2,1)}, bf16[3,512,2304]{2,1,0:T(8,128)(2,1)}, bf16[3,512,768]{2,1,0:T(8,128)(2,1)}, bf16[3,512,768]{2,1,0:T(8,128)(2,1)}, f32[3,512,128]{2,1,0:T(8,128)}) custom-call(s32[60]{0:T(128)} %get-tuple-element.129.rows_ref, s32[32]{0:T(128)} %get-tuple-element.130.counts_ref, ...), custom_call_target="tpu_custom_call", output_to_operand_aliasing={{0}: (7, {})} | custom-call | flops 19327352832 | bytes 31457280 | tf_op jit(solution)/shard_map/attention_forward/pallas_call | solution.py:375
  525.2 15.5 conv_forward.7
  540.6 4.7 send_cotangent.2
  545.3 10.8 all-to-all-done.8.dy_ref
  556.1 4.8 all-to-all-start.7
  560.9 20.0 %feed_backward.4 = (bf16[8,512,768]{2,1,0:T(8,128)(2,1)}, f32[8,768]{1,0:T(8,128)}, f32[768,3072]{1,0:T(8,128)}, f32[3072,768]{1,0:T(8,128)}) custom-call(s32[60]{0:T(128)} %get-tuple-element.129.rows_ref, s32[32]{0:T(128)} %get-tuple-element.130.counts_ref, bf16[8,512,768]{2,1,0:T(8,128)(2,1)} %all-to-all-done.3.x_ref, ...), custom_call_target="tpu_custom_call" | custom-call | flops 14495514624 | bytes 52428800 | tf_op jit(solution)/shard_map/feed_backward/pallas_call | solution.py:876
  580.9 51.6 %all-to-all-done.7.dy_ref = bf16[8,512,768]{2,1,0:T(8,128)(2,1)} async-done(((bf16[8,512,768]{2,1,0:T(8,128)(2,1)}), bf16[8,512,768]{2,1,0:T(8,128)(2,1)}, u32[]{:S(2)}, u32[]{:S(2)}) %all-to-all-start.7) | async-done | bytes 6291488 | tf_op jit(solution)/shard_map/all_to_all | solution.py:1313
  632.5 35.5 %feed_backward.5 = (bf16[8,512,768]{2,1,0:T(8,128)(2,1)}, f32[8,768]{1,0:T(8,128)}, bf16[4,1552,768]{2,1,0:T(8,128)(2,1)}) custom-call(s32[60]{0:T(128)} %get-tuple-element.129.rows_ref, s32[32]{0:T(128)} %get-tuple-element.130.counts_ref, bf16[8,512,768]{2,1,0:T(8,128)(2,1)} %all-to-all-done.6.x_ref, bf16[8,512,768]{2,1,0:T(8,128)(2,1)} %all-to-all-done.7.dy_ref, ...), custom_call_target="tpu_custom_call" | custom-call | flops 14495514624 | bytes 52428800 | tf_op jit(solution)/shard_map/feed_backward/pallas_call | solution.py:876
  668.0 28.9 %attention_backward.4 = (bf16[8,512,768]{2,1,0:T(8,128)(2,1)}, f32[8,768]{1,0:T(8,128)}, f32[768,2304]{1,0:T(8,128)}, f32[768,768]{1,0:T(8,128)}) custom-call(s32[60]{0:T(128)} %get-tuple-element.129.rows_ref, s32[32]{0:T(128)} %get-tuple-element.130.counts_ref, bf16[8,512,768]{2,1,0:T(8,128)(2,1)} %all-to-all-done.3.x_ref, ...), custom_call_target="tpu_custom_call", output_to_operand_aliasing={{0}: (11, {})} | custom-call | flops 19327352832 | bytes 41943040 | tf_op jit(solution)/shard_map/attention_backward/pallas_call | solution.py:564
  696.9 38.5 %conv_backward.4 = (bf16[8,512,768]{2,1,0:T(8,128)(2,1)}, f32[24,768]{1,0:T(8,128)}, f32[3,768,768]{2,1,0:T(8,128)}) custom-call(s32[60]{0:T(128)} %get-tuple-element.129.rows_ref, s32[32]{0:T(128)} %get-tuple-element.130.counts_ref, bf16[8,512,768]{2,1,0:T(8,128)(2,1)} %all-to-all-done.3.x_ref, ...), custom_call_target="tpu_custom_call", output_to_operand_aliasing={{0}: (10, {})} | custom-call | flops 8153726976 | bytes 52428800 | tf_op jit(solution)/shard_map/conv_backward/pallas_call | solution.py:1123
  735.5 28.8 %all-to-all-start.13 = ((bf16[8,512,768]{2,1,0:T(8,128)(2,1)}), bf16[8,512,768]{2,1,0:T(8,128)(2,1)}, u32[]{:S(2)}, u32[]{:S(2)}) async-start(bf16[8,512,768]{2,1,0:T(8,128)(2,1)} %get-tuple-element.177), calls=%async_computation.13 | async-start | bytes 12582912 | tf_op jit(solution)/shard_map/all_to_all | solution.py:1313
  766.3 46.8 %attention_backward.5 = (bf16[8,512,768]{2,1,0:T(8,128)(2,1)}, f32[8,768]{1,0:T(8,128)}, bf16[4,1376,768]{2,1,0:T(8,128)(2,1)}) custom-call(s32[60]{0:T(128)} %get-tuple-element.129.rows_ref, s32[32]{0:T(128)} %get-tuple-element.130.counts_ref, bf16[8,512,768]{2,1,0:T(8,128)(2,1)} %all-to-all-done.6.x_ref, ...), custom_call_target="tpu_custom_call", output_to_operand_aliasing={{0}: (13, {})} | custom-call | flops 19327352832 | bytes 41943040 | tf_op jit(solution)/shard_map/attention_backward/pallas_call | solution.py:564
  813.1 27.2 %conv_backward.5 = (bf16[8,512,768]{2,1,0:T(8,128)(2,1)}, f32[24,768]{1,0:T(8,128)}, bf16[4,1376,768]{2,1,0:T(8,128)(2,1)}) custom-call(s32[60]{0:T(128)} %get-tuple-element.129.rows_ref, s32[32]{0:T(128)} %get-tuple-element.130.counts_ref, bf16[8,512,768]{2,1,0:T(8,128)(2,1)} %all-to-all-done.6.x_ref, ...), custom_call_target="tpu_custom_call", output_to_operand_aliasing={{2}: (11, {}), {0}: (12, {})} | custom-call | flops 8153726976 | bytes 52428800 | tf_op jit(solution)/shard_map/conv_backward/pallas_call | solution.py:1123
  840.4 7.0 all-to-all-start.9
  851.0 4.7 relay_dx.3
  855.7 63.3 %all-to-all-done.9.refs_0_ = bf16[8,512,768]{2,1,0:T(8,128)(2,1)} async-done(((bf16[8,512,768]{2,1,0:T(8,128)(2,1)}), bf16[8,512,768]{2,1,0:T(8,128)(2,1)}, u32[]{:S(2)}, u32[]{:S(2)}) %all-to-all-start.9) | async-done | bytes 6291488 | tf_op jit(solution)/shard_map/all_to_all | solution.py:1313
  919.1 4.8 all-to-all-start.14
  923.8 5.3 relay_dx.2
  929.2 66.3 %all-to-all-done.14.dy_ref = bf16[8,512,768]{2,1,0:T(8,128)(2,1)} async-done(((bf16[8,512,768]{2,1,0:T(8,128)(2,1)}), bf16[8,512,768]{2,1,0:T(8,128)(2,1)}, u32[]{:S(2)}, u32[]{:S(2)}) %all-to-all-start.14) | async-done | bytes 6291488 | tf_op jit(solution)/shard_map/all_to_all | solution.py:1313
  995.4 4.8 all-to-all-start.10
  1000.2 31.8 %feed_backward.6 = (bf16[8,512,768]{2,1,0:T(8,128)(2,1)}, f32[8,768]{1,0:T(8,128)}, f32[768,3072]{1,0:T(8,128)}, f32[3072,768]{1,0:T(8,128)}) custom-call(s32[60]{0:T(128)} %get-tuple-element.129.rows_ref, s32[32]{0:T(128)} %get-tuple-element.130.counts_ref, bf16[8,512,768]{2,1,0:T(8,128)(2,1)} %all-to-all-done.1.x_ref, ...), custom_call_target="tpu_custom_call" | custom-call | flops 14495514624 | bytes 52428800 | tf_op jit(solution)/shard_map/feed_backward/pallas_call | solution.py:876
  1032.0 39.8 %all-to-all-done.10.refs_1_.dy_ref = bf16[8,512,768]{2,1,0:T(8,128)(2,1)} async-done(((bf16[8,512,768]{2,1,0:T(8,128)(2,1)}), bf16[8,512,768]{2,1,0:T(8,128)(2,1)}, u32[]{:S(2)}, u32[]{:S(2)}) %all-to-all-start.10) | async-done | bytes 6291488 | tf_op jit(solution)/shard_map/all_to_all | solution.py:1313
  1071.8 47.3 %feed_backward.7 = (bf16[8,512,768]{2,1,0:T(8,128)(2,1)}, f32[8,768]{1,0:T(8,128)}, bf16[4,1552,768]{2,1,0:T(8,128)(2,1)}) custom-call(s32[60]{0:T(128)} %get-tuple-element.129.rows_ref, s32[32]{0:T(128)} %get-tuple-element.130.counts_ref, bf16[8,512,768]{2,1,0:T(8,128)(2,1)} %all-to-all-done.4.x_ref, bf16[8,512,768]{2,1,0:T(8,128)(2,1)} %all-to-all-done.10.refs_1_.dy_ref, ...), custom_call_target="tpu_custom_call" | custom-call | flops 14495514624 | bytes 52428800 | tf_op jit(solution)/shard_map/feed_backward/pallas_call | solution.py:876
  1119.1 29.0 %attention_backward.6 = (bf16[8,512,768]{2,1,0:T(8,128)(2,1)}, f32[8,768]{1,0:T(8,128)}, f32[768,2304]{1,0:T(8,128)}, f32[768,768]{1,0:T(8,128)}) custom-call(s32[60]{0:T(128)} %get-tuple-element.129.rows_ref, s32[32]{0:T(128)} %get-tuple-element.130.counts_ref, bf16[8,512,768]{2,1,0:T(8,128)(2,1)} %all-to-all-done.1.x_ref, ...), custom_call_target="tpu_custom_call", output_to_operand_aliasing={{0}: (11, {})} | custom-call | flops 19327352832 | bytes 41943040 | tf_op jit(solution)/shard_map/attention_backward/pallas_call | solution.py:564
  1148.2 32.4 %conv_backward.6 = (bf16[8,512,768]{2,1,0:T(8,128)(2,1)}, f32[24,768]{1,0:T(8,128)}, f32[3,768,768]{2,1,0:T(8,128)}) custom-call(s32[60]{0:T(128)} %get-tuple-element.129.rows_ref, s32[32]{0:T(128)} %get-tuple-element.130.counts_ref, bf16[8,512,768]{2,1,0:T(8,128)(2,1)} %all-to-all-done.1.x_ref, ...), custom_call_target="tpu_custom_call", output_to_operand_aliasing={{0}: (10, {})} | custom-call | flops 8153726976 | bytes 52428800 | tf_op jit(solution)/shard_map/conv_backward/pallas_call | solution.py:1123
  1180.5 27.7 %all-to-all-start.15 = ((bf16[8,512,768]{2,1,0:T(8,128)(2,1)}), bf16[8,512,768]{2,1,0:T(8,128)(2,1)}, u32[]{:S(2)}, u32[]{:S(2)}) async-start(bf16[8,512,768]{2,1,0:T(8,128)(2,1)} %get-tuple-element.191), calls=%async_computation.15 | async-start | bytes 12582912 | tf_op jit(solution)/shard_map/all_to_all | solution.py:1313
  1208.2 71.7 %all-to-all-done.15.refs_0_.refs_3_ = bf16[8,512,768]{2,1,0:T(8,128)(2,1)} async-done(((bf16[8,512,768]{2,1,0:T(8,128)(2,1)}), bf16[8,512,768]{2,1,0:T(8,128)(2,1)}, u32[]{:S(2)}, u32[]{:S(2)}) %all-to-all-start.15) | async-done | bytes 6291488 | tf_op jit(solution)/shard_map/all_to_all | solution.py:1313
  1279.9 4.8 all-to-all-start.11
  1287.1 27.4 %attention_backward.7 = (bf16[8,512,768]{2,1,0:T(8,128)(2,1)}, f32[8,768]{1,0:T(8,128)}, bf16[4,1376,768]{2,1,0:T(8,128)(2,1)}) custom-call(s32[60]{0:T(128)} %get-tuple-element.129.rows_ref, s32[32]{0:T(128)} %get-tuple-element.130.counts_ref, bf16[8,512,768]{2,1,0:T(8,128)(2,1)} %all-to-all-done.4.x_ref, ...), custom_call_target="tpu_custom_call", output_to_operand_aliasing={{0}: (13, {})} | custom-call | flops 19327352832 | bytes 41943040 | tf_op jit(solution)/shard_map/attention_backward/pallas_call | solution.py:564
  1316.5 28.8 %conv_backward.7 = (bf16[8,512,768]{2,1,0:T(8,128)(2,1)}, f32[24,768]{1,0:T(8,128)}, bf16[4,1376,768]{2,1,0:T(8,128)(2,1)}) custom-call(s32[60]{0:T(128)} %get-tuple-element.129.rows_ref, s32[32]{0:T(128)} %get-tuple-element.130.counts_ref, bf16[8,512,768]{2,1,0:T(8,128)(2,1)} %all-to-all-done.4.x_ref, ...), custom_call_target="tpu_custom_call", output_to_operand_aliasing={{2}: (11, {}), {0}: (12, {})} | custom-call | flops 8153726976 | bytes 52428800 | tf_op jit(solution)/shard_map/conv_backward/pallas_call | solution.py:1123
  1348.2 8.1 all-to-all-done.11.refs_0_.refs_2_
  1356.3 4.8 all-to-all-start.16
  1361.1 71.6 %all-to-all-done.16.refs_1_ = bf16[8,512,768]{2,1,0:T(8,128)(2,1)} async-done(((bf16[8,512,768]{2,1,0:T(8,128)(2,1)}), bf16[8,512,768]{2,1,0:T(8,128)(2,1)}, u32[]{:S(2)}, u32[]{:S(2)}) %all-to-all-start.16) | async-done | bytes 6291488 | tf_op jit(solution)/shard_map/all_to_all | solution.py:1313
  1432.7 4.7 all-to-all-start.12
  1437.4 8.2 input_grad.1
  1445.7 63.4 %all-to-all-done.12.refs_1_ = bf16[8,512,768]{2,1,0:T(8,128)(2,1)} async-done(((bf16[8,512,768]{2,1,0:T(8,128)(2,1)}), bf16[8,512,768]{2,1,0:T(8,128)(2,1)}, u32[]{:S(2)}, u32[]{:S(2)}) %all-to-all-start.12) | async-done | bytes 6291488 | tf_op jit(solution)/shard_map/all_to_all | solution.py:1313
  1509.0 8.0 outputs.1
  1521.6 6.4 finish_rest.2
  1532.4 6.4 finish_rest.3
  (125 shorter events, 55.0 us)
Async XLA Ops:
  12.3 8.4 all-to-all-start
  20.7 76.4 %all-to-all-start.1 = ((bf16[8,512,768]{2,1,0:T(8,128)(2,1)}), bf16[8,512,768]{2,1,0:T(8,128)(2,1)}, u32[]{:S(2)}, u32[]{:S(2)}) async-start(bf16[8,512,768]{2,1,0:T(8,128)(2,1)} %send_inputs.2), calls=%async_computation.1 | async-start | bytes 12582912 | tf_op jit(solution)/shard_map/all_to_all | solution.py:1313
  30.1 71.7 %copy-start.4 = (bf16[2,1,5,768]{3,0,2,1:T(2,128)(2,1)S(1)}, bf16[2,1,5,768]{3,0,2,1:T(2,128)(2,1)}, u32[]{:S(2)}) copy-start(bf16[2,1,5,768]{3,0,2,1:T(2,128)(2,1)} %param.19) | copy-start | bytes 46084
  30.1 71.7 %copy-start.5 = (bf16[2,1,5,768]{3,0,2,1:T(2,128)(2,1)S(1)}, bf16[2,1,5,768]{3,0,2,1:T(2,128)(2,1)}, u32[]{:S(2)}) copy-start(bf16[2,1,5,768]{3,0,2,1:T(2,128)(2,1)} %param.20) | copy-start | bytes 46084
  30.2 71.8 %copy-start = (bf16[2,1,15,768]{3,0,2,1:T(2,128)(2,1)S(1)}, bf16[2,1,15,768]{3,0,2,1:T(2,128)(2,1)}, u32[]{:S(2)}) copy-start(bf16[2,1,15,768]{3,0,2,1:T(2,128)(2,1)} %param.17) | copy-start | bytes 138244
  97.1 76.4 %all-to-all-start.4 = ((bf16[8,512,768]{2,1,0:T(8,128)(2,1)}), bf16[8,512,768]{2,1,0:T(8,128)(2,1)}, u32[]{:S(2)}, u32[]{:S(2)}) async-start(bf16[8,512,768]{2,1,0:T(8,128)(2,1)} %send_inputs.3), calls=%async_computation.4 | async-start | bytes 12582912 | tf_op jit(solution)/shard_map/all_to_all | solution.py:1313
  173.4 76.6 %all-to-all-start.2 = ((bf16[8,512,768]{2,1,0:T(8,128)(2,1)}), bf16[8,512,768]{2,1,0:T(8,128)(2,1)}, u32[]{:S(2)}, u32[]{:S(2)}) async-start(bf16[8,512,768]{2,1,0:T(8,128)(2,1)} %get-tuple-element.134), calls=%async_computation.2 | async-start | bytes 12582912 | tf_op jit(solution)/shard_map/all_to_all | solution.py:1313
  250.0 76.4 %all-to-all-start.5 = ((bf16[8,512,768]{2,1,0:T(8,128)(2,1)}), bf16[8,512,768]{2,1,0:T(8,128)(2,1)}, u32[]{:S(2)}, u32[]{:S(2)}) async-start(bf16[8,512,768]{2,1,0:T(8,128)(2,1)} %get-tuple-element.140), calls=%async_computation.5 | async-start | bytes 12582912 | tf_op jit(solution)/shard_map/all_to_all | solution.py:1313
  326.4 76.4 %all-to-all-start.3 = ((bf16[8,512,768]{2,1,0:T(8,128)(2,1)}), bf16[8,512,768]{2,1,0:T(8,128)(2,1)}, u32[]{:S(2)}, u32[]{:S(2)}) async-start(bf16[8,512,768]{2,1,0:T(8,128)(2,1)} %relay_x.2), calls=%async_computation.3 | async-start | bytes 12582912 | tf_op jit(solution)/shard_map/all_to_all | solution.py:1313
  402.8 76.5 %all-to-all-start.6 = ((bf16[8,512,768]{2,1,0:T(8,128)(2,1)}), bf16[8,512,768]{2,1,0:T(8,128)(2,1)}, u32[]{:S(2)}, u32[]{:S(2)}) async-start(bf16[8,512,768]{2,1,0:T(8,128)(2,1)} %relay_x.3), calls=%async_computation.6 | async-start | bytes 12582912 | tf_op jit(solution)/shard_map/all_to_all | solution.py:1313
  479.3 76.8 %all-to-all-start.8 = ((bf16[8,512,768]{2,1,0:T(8,128)(2,1)}), bf16[8,512,768]{2,1,0:T(8,128)(2,1)}, u32[]{:S(2)}, u32[]{:S(2)}) async-start(bf16[8,512,768]{2,1,0:T(8,128)(2,1)} %send_cotangent.3), calls=%async_computation.8 | async-start | bytes 12582912 | tf_op jit(solution)/shard_map/all_to_all | solution.py:1313
  556.1 76.4 %all-to-all-start.7 = ((bf16[8,512,768]{2,1,0:T(8,128)(2,1)}), bf16[8,512,768]{2,1,0:T(8,128)(2,1)}, u32[]{:S(2)}, u32[]{:S(2)}) async-start(bf16[8,512,768]{2,1,0:T(8,128)(2,1)} %send_cotangent.2), calls=%async_computation.7 | async-start | bytes 12582912 | tf_op jit(solution)/shard_map/all_to_all | solution.py:1313
  560.9 290.1 %reduce-scatter.5.cloned.1.call-start = ((), (), s32[]{:S(2)}) async-start(), calls=%async_computation.21 | async-start | bytes 11919360 | tf_op jit(solution)/shard_map/reduce_scatter | solution.py:1392
  735.5 30.8 %copy-start.1 = (f32[24,768]{1,0:T(8,128)S(1)}, f32[24,768]{1,0:T(8,128)}, u32[]{:S(2)}) copy-start(f32[24,768]{1,0:T(8,128)} %get-tuple-element.221) | copy-start | bytes 221188
  735.5 104.9 %all-to-all-start.13 = ((bf16[8,512,768]{2,1,0:T(8,128)(2,1)}), bf16[8,512,768]{2,1,0:T(8,128)(2,1)}, u32[]{:S(2)}, u32[]{:S(2)}) async-start(bf16[8,512,768]{2,1,0:T(8,128)(2,1)} %get-tuple-element.177), calls=%async_computation.13 | async-start | bytes 12582912 | tf_op jit(solution)/shard_map/all_to_all | solution.py:1313
  840.4 9.3 copy-start.2
  840.4 78.7 %all-to-all-start.9 = ((bf16[8,512,768]{2,1,0:T(8,128)(2,1)}), bf16[8,512,768]{2,1,0:T(8,128)(2,1)}, u32[]{:S(2)}, u32[]{:S(2)}) async-start(bf16[8,512,768]{2,1,0:T(8,128)(2,1)} %get-tuple-element.176), calls=%async_computation.9 | async-start | bytes 12582912 | tf_op jit(solution)/shard_map/all_to_all | solution.py:1313
  847.4 271.7 %reduce-scatter.7.cloned.1.call-start = ((), (), s32[]{:S(2)}) async-start(), calls=%async_computation.22 | async-start | bytes 10567680 | tf_op jit(solution)/shard_map/reduce_scatter | solution.py:1394
  919.1 76.4 %all-to-all-start.14 = ((bf16[8,512,768]{2,1,0:T(8,128)(2,1)}), bf16[8,512,768]{2,1,0:T(8,128)(2,1)}, u32[]{:S(2)}, u32[]{:S(2)}) async-start(bf16[8,512,768]{2,1,0:T(8,128)(2,1)} %relay_dx.3), calls=%async_computation.14 | async-start | bytes 12582912 | tf_op jit(solution)/shard_map/all_to_all | solution.py:1313
  995.4 76.4 %all-to-all-start.10 = ((bf16[8,512,768]{2,1,0:T(8,128)(2,1)}), bf16[8,512,768]{2,1,0:T(8,128)(2,1)}, u32[]{:S(2)}, u32[]{:S(2)}) async-start(bf16[8,512,768]{2,1,0:T(8,128)(2,1)} %relay_dx.2), calls=%async_computation.10 | async-start | bytes 12582912 | tf_op jit(solution)/shard_map/all_to_all | solution.py:1313
  1000.2 356.1 %reduce-scatter.9.cloned.1.call-start = ((), (), s32[]{:S(2)}) async-start(), calls=%async_computation.23 | async-start | bytes 11919360 | tf_op jit(solution)/shard_map/reduce_scatter | solution.py:1392
  1180.5 99.4 %all-to-all-start.15 = ((bf16[8,512,768]{2,1,0:T(8,128)(2,1)}), bf16[8,512,768]{2,1,0:T(8,128)(2,1)}, u32[]{:S(2)}, u32[]{:S(2)}) async-start(bf16[8,512,768]{2,1,0:T(8,128)(2,1)} %get-tuple-element.191), calls=%async_computation.15 | async-start | bytes 12582912 | tf_op jit(solution)/shard_map/all_to_all | solution.py:1313
  1208.2 78.5 %copy-start.3 = (f32[24,768]{1,0:T(8,128)S(1)}, f32[24,768]{1,0:T(8,128)}, u32[]{:S(2)}) copy-start(f32[24,768]{1,0:T(8,128)} %get-tuple-element.213) | copy-start | bytes 221188
  1279.9 76.4 %all-to-all-start.11 = ((bf16[8,512,768]{2,1,0:T(8,128)(2,1)}), bf16[8,512,768]{2,1,0:T(8,128)(2,1)}, u32[]{:S(2)}, u32[]{:S(2)}) async-start(bf16[8,512,768]{2,1,0:T(8,128)(2,1)} %after.5), calls=%async_computation.11 | async-start | bytes 12582912 | tf_op jit(solution)/shard_map/all_to_all | solution.py:1313
  1284.7 247.7 %reduce-scatter.11.cloned.1.call-start = ((), (), s32[]{:S(2)}) async-start(), calls=%async_computation.24 | async-start | bytes 10567680 | tf_op jit(solution)/shard_map/reduce_scatter | solution.py:1394
  1356.3 76.4 %all-to-all-start.16 = ((bf16[8,512,768]{2,1,0:T(8,128)(2,1)}), bf16[8,512,768]{2,1,0:T(8,128)(2,1)}, u32[]{:S(2)}, u32[]{:S(2)}) async-start(bf16[8,512,768]{2,1,0:T(8,128)(2,1)} %get-tuple-element.211), calls=%async_computation.16 | async-start | bytes 12582912 | tf_op jit(solution)/shard_map/all_to_all | solution.py:1313
  1432.7 76.3 %all-to-all-start.12 = ((bf16[8,512,768]{2,1,0:T(8,128)(2,1)}), bf16[8,512,768]{2,1,0:T(8,128)(2,1)}, u32[]{:S(2)}, u32[]{:S(2)}) async-start(bf16[8,512,768]{2,1,0:T(8,128)(2,1)} %after.6), calls=%async_computation.12 | async-start | bytes 12582912 | tf_op jit(solution)/shard_map/all_to_all | solution.py:1313
Sparse Core Ops, SparseCore 0:
  668.1 176.3 reduce-scatter.4
  851.1 154.4 reduce-scatter.6
  1119.2 169.3 reduce-scatter.8
  1356.4 160.9 reduce-scatter.10

commit v4 on v3

--- a/solution.py
+++ b/solution.py
@@ -290,8 +290,8 @@
     rstd_ref[0] = jnp.broadcast_to(scale, rstd_ref.shape[1:])
 
 
-def norm_backward(dy_ref, zn_ref, rstd_ref, gain_row):
-    dy = dy_ref[0].astype(F32)
+def norm_backward(dy, zn_ref, rstd_ref, gain_row):
+    dy = dy.astype(F32)
     normed = zn_ref[0].astype(F32)
     scale = rstd_ref[0][:, :1]
     scaled = dy * gain_row
@@ -443,7 +443,7 @@
 
         @pl.when(here)
         def _():
-            dz, gain_grad, shift_grad = norm_backward(dy_ref, zn_ref, rstd_ref, gain[0:1, :])
+            dz, gain_grad, shift_grad = norm_backward(dy_ref[0], zn_ref, rstd_ref, gain[0:1, :])
             small_ref[0:1, :] += gain_grad
             small_ref[1:2, :] += shift_grad
             dz_scr[...] = dz
@@ -557,9 +557,11 @@
         out_shape.append(jax.ShapeDtypeStruct((groups, total_rows, width), BF16))
         in_specs += [ANY_SPEC, ANY_SPEC]
         args += list(sums)
-    in_specs.append(ANY_SPEC)
-    alias = {len(args): 0}
-    args.append(dx_in)
+    alias = {}
+    if dx_in is not None:
+        in_specs.append(ANY_SPEC)
+        alias = {len(args): 0}
+        args.append(dx_in)
     flops = 2 * OWN_CAP * length * width * (8 * width + 4 * length)
     return pl.pallas_call(
         kernel,
@@ -588,7 +590,7 @@
     )(*args)
 
 
-def feed_forward(part, tables, x, weights, norms, y_in):
+def feed_forward(part, tables, x, weights, norms, earlier):
     rows, counts = tables
     b = part // HALVES
     ffn_up, ffn_down = weights
@@ -646,11 +648,15 @@
     def out_row(c, i, r, n):
         return (r[base + jnp.where(c == parts - 1, i, 0)], 0, 0)
 
+    def place(i, n):
+        at = jnp.maximum(jnp.minimum(i, n[part * 8 + kind] - 1), 0)
+        return at if part == b * HALVES else at + n[b * HALVES * 8 + kind]
+
     def out_step(c, i, r, n):
-        return (jnp.where(c == parts - 1, jnp.maximum(jnp.minimum(i, n[part * 8 + kind] - 1), 0), 0), 0, 0)
+        return (place(jnp.where(c == parts - 1, i, 0), n), 0, 0)
 
     def part_step(c, i, r, n):
-        return (jnp.maximum(jnp.minimum(i, n[part * 8 + kind] - 1), 0), 0, c)
+        return (place(i, n), 0, c)
 
     seq = (1, length, width)
     in_specs = [
@@ -662,10 +668,10 @@
     ]
     args = [rows, counts, x, ffn_up, ffn_down, gains, shifts]
     alias = {}
-    if y_in is not None:
-        in_specs.append(pl.BlockSpec(memory_space=pl.ANY))
-        alias = {len(args): 0}
-        args.append(y_in)
+    for n, kept in enumerate(earlier or ()):
+        in_specs.append(ANY_SPEC)
+        alias[len(args)] = 1 + n
+        args.append(kept)
     return pl.pallas_call(
         kernel,
         grid_spec=pltpu.PrefetchScalarGridSpec(
@@ -686,10 +692,10 @@
         ),
         out_shape=[
             jax.ShapeDtypeStruct((slots, length, width), BF16),
-            jax.ShapeDtypeStruct((OWN_CAP, length, hidden), BF16),
-            jax.ShapeDtypeStruct((OWN_CAP, length, hidden), BF16),
-            jax.ShapeDtypeStruct((OWN_CAP, length, width), BF16),
-            jax.ShapeDtypeStruct((OWN_CAP, length, LANES), F32),
+            jax.ShapeDtypeStruct((OWN_CAP + 1, length, hidden), BF16),
+            jax.ShapeDtypeStruct((OWN_CAP + 1, length, hidden), BF16),
+            jax.ShapeDtypeStruct((OWN_CAP + 1, length, width), BF16),
+            jax.ShapeDtypeStruct((OWN_CAP + 1, length, LANES), F32),
         ],
         input_output_aliases=alias,
         compiler_params=params_of(2),
@@ -702,55 +708,89 @@
     )(*args)
 
 
-def feed_backward(part, tables, x, dy, kept, weights, gains, sums, packed):
+def feed_backward(b, tables, x, dy, kept, weights, gains, dx_first, groups, wait_for):
     rows, counts = tables
-    b = part // HALVES
     ffn_up, ffn_down = weights
     g, slope, zn, rstd = kept
-    slots, length, width = x.shape
+    slots, length, width = x[0].shape
     hidden = ffn_up.shape[-1]
     parts = hidden // FF_PART
     kind = KINDS - 1
-    base = part * SLOTS + kind * OWN_CAP
-    first = sums is None
-    groups = packed[0]
+    bases = [(b * HALVES + half) * SLOTS + kind * OWN_CAP for half in range(HALVES)]
     tall = width // groups
     deep = hidden // groups
+    shares = FF_PART // deep
+
+    def present(n, half):
+        return n[(b * HALVES + half) * 8 + kind]
 
     def kernel(
-        rows_ref, counts_ref, x_ref, dy_ref, g_ref, slope_ref, zn_ref, rstd_ref, up, down, gain, *rest
+        rows_ref,
+        counts_ref,
+        x_ref0,
+        x_ref1,
+        dy_ref0,
+        dy_ref1,
+        g_ref,
+        slope_ref,
+        zn_ref,
+        rstd_ref,
+        up,
+        down,
+        gain,
+        *rest,
     ):
-        if first:
-            dx_ref, small_ref, acc_up, acc_down = rest[:4]
-        else:
-            sum_up, sum_down, dx_ref, small_ref, packed_ref = rest[:5]
-            acc_up, acc_down, low_up, low_down, tally, sems = rest[-6:]
-        x_scr, dh_scr, dx_scr, da_scr = rest[-4:] if first else rest[-10:-6]
+        (
+        small_ref,
+        dx_ref0,
+        dx_ref1,
+        packed_ref,
+        x_scr,
+        dh_scr,
+        dx_scr,
+        da_scr,
+        acc_up,
+        acc_down,
+        low_up,
+        low_down,
+        low_dx,
+        tally,
+        sems,
+        dx_sem,
+        ) = rest[-16:]
         c, i = pl.program_id(0), pl.program_id(1)
+        n0 = present(counts_ref, 0)
+        total_n = n0 + present(counts_ref, 1)
+        in_first = i < n0
 
         @pl.when(jnp.logical_and(c == 0, i == 0))
         def _():
             small_ref[...] = jnp.zeros_like(small_ref)
+            lane = lax.broadcasted_iota(jnp.int32, (COUNT_ROWS, width), 1)
+            counted = jnp.zeros((COUNT_ROWS, width), F32)
+            for k in range(KINDS):
+                there = sum(counts_ref[(b * HALVES + half) * 8 + k] for half in range(HALVES))
+                counted = jnp.where(lane == k, there.astype(F32), counted)
+            tally[...] = counted.astype(BF16)
 
         @pl.when(i == 0)
         def _():
-            if first:
-                acc_up[...] = jnp.zeros_like(acc_up)
-                acc_down[...] = jnp.zeros_like(acc_down)
-            else:
-                acc_up[...] = sum_up[...]
-                acc_down[...] = sum_down[...]
-
-        @pl.when(i < counts_ref[part * 8 + kind])
+            acc_up[...] = jnp.zeros_like(acc_up)
+            acc_down[...] = jnp.zeros_like(acc_down)
+
+        @pl.when(i < total_n)
         def _():
             @pl.when(c == 0)
             def _():
                 dz, gain_grad, shift_grad = norm_backward(
-                    dy_ref, zn_ref, rstd_ref, gain[kind : kind + 1, :]
+                    jnp.where(in_first, dy_ref0[0], dy_ref1[0]),
+                    zn_ref,
+                    rstd_ref,
+                    gain[kind : kind + 1, :],
                 )
                 small_ref[0:1, :] += gain_grad
                 small_ref[1:2, :] += shift_grad
-                x_scr[i] = x_ref[0]
+                x_scr[i] = jnp.where(in_first, x_ref0[0], x_ref1[0])
                 dh_scr[i] = dz.astype(BF16)
                 dx_scr[i] = dz
 
@@ -769,67 +809,86 @@
 
             @pl.when(c == parts - 1)
             def _():
-                dx_ref[0] = total.astype(BF16)
-
-        if not first:
-
-            @pl.when(i == OWN_CAP - 1)
-            def _():
-                low_up[...] = acc_up[...].astype(BF16)
-                low_down[...] = acc_down[...].astype(BF16)
-                copies = [
-                    pltpu.make_async_copy(
-                        low_up.at[pl.ds(z * tall, tall)],
-                        packed_ref.at[z, pl.ds(c * tall, tall)],
-                        sems.at[z],
-                    )
-                    for z in range(groups)
-                ]
-                shares = FF_PART // deep
-                lane = lax.broadcasted_iota(jnp.int32, (COUNT_ROWS, width), 1)
-                counted = jnp.zeros((COUNT_ROWS, width), F32)
-                for k in range(KINDS):
-                    there = sum(counts_ref[(b * HALVES + half) * 8 + k] for half in range(HALVES))
-                    counted = jnp.where(lane == k, there.astype(F32), counted)
-                tally[...] = counted.astype(BF16)
-                copies += [
-                    pltpu.make_async_copy(
-                        tally,
-                        packed_ref.at[z, pl.ds(parts * tall + deep, COUNT_ROWS)],
-                        sems.at[groups + shares + z],
-                    )
-                    for z in range(groups)
-                ]
-                copies += [
-                    pltpu.make_async_copy(
-                        low_down.at[pl.ds(m * deep, deep)],
-                        packed_ref.at[c * shares + m, pl.ds(parts * tall, deep)],
-                        sems.at[groups + m],
-                    )
-                    for m in range(shares)
-                ]
-                for copy in copies:
+                low_dx[...] = total.astype(BF16)
+                for half, (inside, dx_ref) in enumerate(
+                    ((in_first, dx_ref0), (jnp.logical_not(in_first), dx_ref1))
+                ):
+
+                    @pl.when(inside)
+                    def _():
+                        row = rows_ref[bases[half] + jnp.where(in_first, i, jnp.maximum(i - n0, 0))]
+                        copy = pltpu.make_async_copy(low_dx, dx_ref.at[row], dx_sem)
+                        copy.start()
+                        copy.wait()
+
+        def copies():
+            pairs = [
+                (low_up.at[pl.ds(z * tall, tall)], packed_ref.at[z, pl.ds(c * tall, tall)])
+                for z in range(groups)
+            ]
+            pairs += [
+                (
+                    low_down.at[pl.ds(m * deep, deep)],
+                    packed_ref.at[c * shares + m, pl.ds(parts * tall, deep)],
+                )
+                for m in range(shares)
+            ]
+            return [
+                pltpu.make_async_copy(source, target, sems.at[n])
+                for n, (source, target) in enumerate(pairs)
+            ]
+
+        def tallies():
+            return [
+                pltpu.make_async_copy(
+                    tally,
+                    packed_ref.at[z, pl.ds(parts * tall + deep, COUNT_ROWS)],
+                    sems.at[groups + shares + z],
+                )
+                for z in range(groups)
+            ]
+
+        @pl.when(i == OWN_CAP - 1)
+        def _():
+            @pl.when(c > 0)
+            def _():
+                for copy in copies():
+                    copy.wait()
+
+            low_up[...] = acc_up[...].astype(BF16)
+            low_down[...] = acc_down[...].astype(BF16)
+            for copy in copies():
+                copy.start()
+
+            @pl.when(c == parts - 1)
+            def _():
+                for copy in tallies():
                     copy.start()
-                for copy in copies:
+                for copy in copies() + tallies():
                     copy.wait()
 
-    def in_row(c, i, r, n):
-        return (r[base + jnp.where(c == 0, i, OWN_CAP - 1)], 0, 0)
+    def first_row(c, i, r, n):
+        return (r[bases[0] + jnp.where(c == 0, i, OWN_CAP - 1)], 0, 0)
+
+    def second_row(c, i, r, n):
+        at = jnp.where(c == 0, i, OWN_CAP - 1) - present(n, 0)
+        return (r[bases[1] + jnp.maximum(at, 0)], 0, 0)
+
+    def last(n):
+        return present(n, 0) + present(n, 1) - 1
 
     def in_step(c, i, r, n):
-        last = jnp.maximum(n[part * 8 + kind] - 1, 0)
-        return (jnp.where(c == 0, jnp.minimum(i, last), last), 0, 0)
-
-    def out_row(c, i, r, n):
-        return (r[base + jnp.where(c == parts - 1, i, 0)], 0, 0)
+        return (jnp.where(c == 0, jnp.minimum(i, last(n)), last(n)), 0, 0)
 
     def part_step(c, i, r, n):
-        return (jnp.maximum(jnp.minimum(i, n[part * 8 + kind] - 1), 0), 0, c)
+        return (jnp.minimum(i, last(n)), 0, c)
 
     seq = (1, length, width)
     in_specs = [
-        pl.BlockSpec(seq, in_row),
-        pl.BlockSpec(seq, in_row),
+        pl.BlockSpec(seq, first_row),
+        pl.BlockSpec(seq, second_row),
+        pl.BlockSpec(seq, first_row),
+        pl.BlockSpec(seq, second_row),
         pl.BlockSpec((1, length, FF_PART), part_step),
         pl.BlockSpec((1, length, FF_PART), part_step),
         pl.BlockSpec(seq, in_step),
@@ -837,55 +896,48 @@
         pl.BlockSpec((None, None, width, FF_PART), lambda c, i, r, n: (b, 0, 0, c)),
         pl.BlockSpec((None, None, FF_PART, width), lambda c, i, r, n: (b, 0, c, 0)),
         pl.BlockSpec((8, width), lambda c, i, r, n: (0, 0)),
-    ]
-    args = [rows, counts, x, dy, g, slope, zn, rstd, ffn_up, ffn_down, gains]
-    up_spec = pl.BlockSpec((width, FF_PART), lambda c, i, r, n: (0, c))
-    down_spec = pl.BlockSpec((FF_PART, width), lambda c, i, r, n: (c, 0))
-    out_specs = [pl.BlockSpec(seq, out_row), pl.BlockSpec((8, width), lambda c, i, r, n: (0, 0))]
-    out_shape = [
-        jax.ShapeDtypeStruct((slots, length, width), BF16),
-        jax.ShapeDtypeStruct((8, width), F32),
-    ]
-    scratch = [
-        pltpu.VMEM((OWN_CAP, length, width), BF16),
-        pltpu.VMEM((OWN_CAP, length, width), BF16),
-        pltpu.VMEM((OWN_CAP, length, width), F32),
-        pltpu.VMEM((length, FF_PART), BF16),
-    ]
-    if first:
-        out_specs += [up_spec, down_spec]
-        out_shape += [
-            jax.ShapeDtypeStruct((width, hidden), F32),
-            jax.ShapeDtypeStruct((hidden, width), F32),
-        ]
-    else:
-        in_specs += [up_spec, down_spec]
-        args += list(sums)
-        out_specs.append(ANY_SPEC)
-        out_shape.append(
-            jax.ShapeDtypeStruct((groups, parts * tall + deep + COUNT_ROWS, width), BF16)
-        )
-        scratch += [
-            pltpu.VMEM((width, FF_PART), F32),
-            pltpu.VMEM((FF_PART, width), F32),
-            pltpu.VMEM((width, FF_PART), BF16),
-            pltpu.VMEM((FF_PART, width), BF16),
-            pltpu.VMEM((COUNT_ROWS, width), BF16),
-            pltpu.SemaphoreType.DMA((2 * groups + FF_PART // deep,)),
-        ]
+        ANY_SPEC,
+    ] + [ANY_SPEC] * len(wait_for)
+    args = [rows, counts, *x, *dy, g, slope, zn, rstd, ffn_up, ffn_down, gains, dx_first]
+    alias = {len(args) - 1: 1}
+    args += wait_for
     return pl.pallas_call(
         kernel,
         grid_spec=pltpu.PrefetchScalarGridSpec(
             num_scalar_prefetch=2,
             grid=(parts, OWN_CAP),
             in_specs=in_specs,
-            out_specs=out_specs,
-            scratch_shapes=scratch,
-        ),
-        out_shape=out_shape,
+            out_specs=[
+                pl.BlockSpec((8, width), lambda c, i, r, n: (0, 0)),
+                ANY_SPEC,
+                ANY_SPEC,
+                ANY_SPEC,
+            ],
+            scratch_shapes=[
+                pltpu.VMEM((OWN_CAP, length, width), BF16),
+                pltpu.VMEM((OWN_CAP, length, width), BF16),
+                pltpu.VMEM((OWN_CAP, length, width), F32),
+                pltpu.VMEM((length, FF_PART), BF16),
+                pltpu.VMEM((width, FF_PART), F32),
+                pltpu.VMEM((FF_PART, width), F32),
+                pltpu.VMEM((width, FF_PART), BF16),
+                pltpu.VMEM((FF_PART, width), BF16),
+                pltpu.VMEM((length, width), BF16),
+                pltpu.VMEM((COUNT_ROWS, width), BF16),
+                pltpu.SemaphoreType.DMA((2 * groups + shares,)),
+                pltpu.SemaphoreType.DMA,
+            ],
+        ),
+        out_shape=[
+            jax.ShapeDtypeStruct((8, width), F32),
+            jax.ShapeDtypeStruct((slots, length, width), BF16),
+            jax.ShapeDtypeStruct((slots, length, width), BF16),
+            jax.ShapeDtypeStruct((groups, parts * tall + deep + COUNT_ROWS, width), BF16),
+        ],
+        input_output_aliases=alias,
         compiler_params=params_of(2),
         cost_estimate=pl.CostEstimate(
-            flops=4 * OWN_CAP * length * width * hidden,
+            flops=7 * OWN_CAP * length * width * hidden,
             transcendentals=0,
             bytes_accessed=50 * 2**20,
         ),
@@ -1035,7 +1087,7 @@
             @pl.when(jnp.logical_and(which == kind - 1, j < counts_ref[part * 8 + kind]))
             def _():
                 dz, gain_grad, shift_grad = norm_backward(
-                    dy_ref, zn_ref, rstd_ref, gain[kind : kind + 1, :]
+                    dy_ref[0], zn_ref, rstd_ref, gain[kind : kind + 1, :]
                 )
                 small_ref[14 + kind : 15 + kind, :] += gain_grad
                 small_ref[17 + kind : 18 + kind, :] += shift_grad
@@ -1139,14 +1191,27 @@
     )(*args)
 
 
-def owner_forward(part, tables, x, weights, small_weights):
+def owner_forward(b, half, tables, x, weights, small_weights, earlier):
+    part = b * HALVES + half
     attn_qkv, attn_out, ffn_up, ffn_down, conv_point = weights
     taps, gains, shifts = small_weights
     norms = (gains, shifts)
-    y, g, slope, zn_f, rstd_f = feed_forward(part, tables, x, (ffn_up, ffn_down), norms, None)
-    y, qkv, o, zn_a, rstd_a = attention_forward(part, tables, x, (attn_qkv, attn_out), norms, y)
-    y, u, zn_c, rstd_c = conv_forward(part, tables, x, (taps, conv_point), norms, y)
-    return y, ((g, slope, zn_f, rstd_f), (qkv, o, zn_a, rstd_a), (u, zn_c, rstd_c))
+    y, *kept_f = feed_forward(part, tables, x, (ffn_up, ffn_down), norms, earlier)
+    y, *kept_a = attention_forward(part, tables, x, (attn_qkv, attn_out), norms, y)
+    y, *kept_c = conv_forward(part, tables, x, (taps, conv_point), norms, y)
+    return y, kept_f, kept_a, kept_c
+
+
+def both_forward(b, tables, x, weights, small_weights):
+    y, kept_a, kept_c, kept_f = [], [], [], None
+    for half in range(HALVES):
+        yh, kept_f, ka, kc = owner_forward(
+            b, half, tables, x[half], weights, small_weights, kept_f
+        )
+        y.append(yh)
+        kept_a.append(ka)
+        kept_c.append(kc)
+    return y, (kept_f, kept_a, kept_c)
 
 
 def join_small(small_f, small_a, small_c):
@@ -1163,41 +1228,32 @@
     )
 
 
-def owner_backward(b, tables, x, dy, kept, weights, small_weights, groups):
+def owner_backward(b, tables, x, dy, kept, weights, small_weights, groups, wait_for):
     attn_qkv, attn_out, ffn_up, ffn_down, conv_point = weights
     taps, gains, shifts = small_weights
+    kept_f, kept_a, kept_c = kept
     width = x[0].shape[-1]
     rest_rows = 7 * width // groups + SMALL_ROWS
-    dx, smalls = [None, None], [None, None]
-    sums = None
-    for half in range(HALVES):
-        part = b * HALVES + half
-        kept_f, kept_a, kept_c = kept[half]
-        xh, dyh = x[half], dy[half]
-        first = half == 0
-        if first:
-            d, small_f, *sum_f = feed_backward(
-                part, tables, xh, dyh, kept_f, (ffn_up, ffn_down), gains, None, (groups,)
-            )
-            d, small_a, *sum_a = attention_backward(
-                part, tables, xh, dyh, kept_a, (attn_qkv, attn_out), gains, d, None, None
-            )
-            d, small_c, sum_c = conv_backward(
-                part, tables, xh, dyh, kept_c, (taps, conv_point), gains, d, None, (groups,)
-            )
-        else:
-            d, small_f, feed_pack = feed_backward(
-                part, tables, xh, dyh, kept_f, (ffn_up, ffn_down), gains, sum_f, (groups,)
-            )
-            d, small_a, rest_pack = attention_backward(
-                part, tables, xh, dyh, kept_a, (attn_qkv, attn_out), gains, d, sum_a, (groups, rest_rows)
-            )
-            d, small_c, rest_pack = conv_backward(
-                part, tables, xh, dyh, kept_c, (taps, conv_point), gains, d, sum_c, (groups, rest_pack)
-            )
-        dx[half] = d
-        smalls[half] = join_small(small_f, small_a, small_c)
-    small = (smalls[0] + smalls[1]).astype(BF16).reshape(25, groups, width // groups)
+    attn, conv = (attn_qkv, attn_out), (taps, conv_point)
+    first, second = b * HALVES, b * HALVES + 1
+    d0, small_a0, *sum_a = attention_backward(
+        first, tables, x[0], dy[0], kept_a[0], attn, gains, None, None, None
+    )
+    d0, small_c0, sum_c = conv_backward(
+        first, tables, x[0], dy[0], kept_c[0], conv, gains, d0, None, (groups,)
+    )
+    small_f, d0, d1, feed_pack = feed_backward(
+        b, tables, x, dy, kept_f, (ffn_up, ffn_down), gains, d0, groups, wait_for
+    )
+    d1, small_a1, rest_pack = attention_backward(
+        second, tables, x[1], dy[1], kept_a[1], attn, gains, d1, sum_a, (groups, rest_rows)
+    )
+    d1, small_c1, rest_pack = conv_backward(
+        second, tables, x[1], dy[1], kept_c[1], conv, gains, d1, sum_c, (groups, rest_pack)
+    )
+    dx = (d0, d1)
+    small = join_small(small_f, small_a0 + small_a1, small_c0 + small_c1).astype(BF16)
+    small = small.reshape(25, groups, width // groups)
     small = small.transpose(1, 0, 2)
     small = jnp.pad(small, ((0, 0), (0, SMALL_ROWS - 25), (0, width - width // groups)))
     rest_pack = lax.dynamic_update_slice(rest_pack, small, (0, rest_rows - SMALL_ROWS, 0))
@@ -1313,6 +1369,10 @@
     return lax.all_to_all(rows, "op", split_axis=0, concat_axis=0, tiled=True)
 
 
+def group_sum(pack):
+    return lax.psum_scatter(pack, "dp", scatter_dimension=0, tiled=False)
+
+
 def per_device(
     inputs,
     candidate,
@@ -1345,14 +1405,12 @@
         exchange(move_rows(send, [start(0, h)], [inputs], owners, False, "send_inputs"))
         for h in both
     ]
-    y0, kept0 = zip(*[owner_forward(h, tables, x0[h], weights, smalls[0]) for h in both])
+    y0, kept0 = both_forward(0, tables, x0, weights, smalls[0])
     x1 = []
     for h in both:
         back = exchange(y0[h])
         x1.append(exchange(move_rows(relay, [start(0, h)], [back], owners, False, "relay_x")))
-    y1, kept1 = zip(
-        *[owner_forward(HALVES + h, tables, x1[h], weights, smalls[1]) for h in both]
-    )
+    y1, kept1 = both_forward(1, tables, x1, weights, smalls[1])
     dy1 = [
         exchange(
             move_rows(
@@ -1361,17 +1419,23 @@
         )
         for h in both
     ]
-    dx1, feed1, rest1 = owner_backward(1, tables, x1, dy1, kept1, weights, smalls[1], groups)
+    dx1, feed1, rest1 = owner_backward(1, tables, x1, dy1, kept1, weights, smalls[1], groups, ())
+    feed1 = group_sum(feed1)
+    rest1 = group_sum(rest1)
     dy0 = []
     for h in both:
         back = exchange(dx1[h])
         dy0.append(exchange(move_rows(relay, [start(1, h)], [back], owners, False, "relay_dx")))
-    dx0, feed0, rest0 = owner_backward(0, tables, x0, dy0, kept0, weights, smalls[0], groups)
+    dx0, feed0, rest0 = owner_backward(
+        0, tables, x0, dy0, kept0, weights, smalls[0], groups, (feed1,)
+    )
+    feed0 = group_sum(after(feed0, (rest1,)))
+    rest0 = group_sum(rest0)
     starts = [start(1, h) for h in both]
     y_home = [exchange(after(y1[h], (dy0[1],))) for h in both]
     outputs = move_rows(send, starts, y_home, seqs, True, "outputs")
     starts = [start(0, h) for h in both]
-    dx_home = [exchange(dx0[h]) for h in both]
+    dx_home = [exchange(dx0[0]), exchange(after(dx0[1], (feed0,)))]
     input_grad = move_rows(send, starts, dx_home, seqs, True, "input_grad")
 
     tall, deep = width // groups, hidden // groups
@@ -1385,15 +1449,10 @@
         grad(KINDS, tall),
         grad(KINDS, tall),
     )
-    earlier, feeds, rests = None, (None, None), ()
+    feeds, rests = (None, None), ()
     for b, feed, rest in ((1, feed1, rest1), (0, feed0, rest0)):
-        if earlier is not None:
-            feed = after(feed, (earlier,))
-        feed = lax.psum_scatter(feed, "dp", scatter_dimension=0, tiled=False)
-        rest = after(rest, (feed,) if b else (feed, y_home[0], dx_home[0]))
-        earlier = lax.psum_scatter(rest, "dp", scatter_dimension=0, tiled=False)
         feeds = finish_feed(b, feed, *feeds, feed_shapes)
-        rests = finish_rest(b, earlier, feed, rests, rest_shapes)
+        rests = finish_rest(b, rest, feed, rests, rest_shapes)
     qkv, out, taps, point, gain, shift = rests
     grads = (qkv, out, *feeds, taps, point, gain, shift)
     return (outputs, input_grad) + grads

time: 1580 us -> 1420 us (0.90)
  the two profiles are of different devices: /device:TPU:16 before, /device:TPU:0 now
where the time goes in v4:
time: 1420 us; the launch traced here: 1410 us
  Pallas kernels  624 us (44%)
  waiting for transfers between devices  558 us (39%)
  blocking collectives  102 us (7%)
  starting transfers between devices  91.6 us (6%)
  between operations  14.6 us (1%)
    all_to_all x16, waiting for transfers between devices, exchange(): return lax.all_to_all(rows, 'op', split_axis=0, concat_axis=0, tiled=True)  506 us
    pallas_call x4, Pallas kernels, conv_backward(): pl.pallas_call(kernel, grid_spec=pltpu.PrefetchScalarGridSpec(num_scalar_...  124 us
    pallas_call x4, Pallas kernels, attention_backward(): pl.pallas_call(kernel, grid_spec=pltpu.PrefetchScalarGridSpec(num_scalar_...  114 us
    all_to_all x1, blocking collectives, exchange(): return lax.all_to_all(rows, 'op', split_axis=0, concat_axis=0, tiled=True)  102 us
    pallas_call x2, Pallas kernels, feed_backward(): pl.pallas_call(kernel, grid_spec=pltpu.PrefetchScalarGridSpec(num_scalar_...  91.9 us
    all_to_all x16, starting transfers between devices, exchange(): return lax.all_to_all(rows, 'op', split_axis=0, concat_axis=0, tiled=True)  91.5 us
    pallas_call x4, Pallas kernels, feed_forward(): pl.pallas_call(kernel, grid_spec=pltpu.PrefetchScalarGridSpec(num_scalar_...  90 us
    pallas_call x4, Pallas kernels, conv_forward(): pl.pallas_call(kernel, grid_spec=pltpu.PrefetchScalarGridSpec(num_scalar_...  71.6 us
  transfers between devices with their start and end apart: 20, of which 15 were waited for; matrix products, arithmetic and copies ran while one was open for 1% of the time, Pallas kernels for 41%

profile of v4, /device:TPU:0, one launch (start us, length us, event | category | flops | bytes accessed | tf_op | source)
XLA Modules:
  0.0 1405.4 jit_solution(4310481117080249567)
XLA Ops:
  12.3 5.2 all-to-all-start
  22.1 4.8 all-to-all-start.1
  26.9 4.7 send_inputs.3
  31.6 66.9 %all-to-all-done.1.x_ref.x_ref0 = bf16[8,512,768]{2,1,0:T(8,128)(2,1)} async-done(((bf16[8,512,768]{2,1,0:T(8,128)(2,1)}), bf16[8,512,768]{2,1,0:T(8,128)(2,1)}, u32[]{:S(2)}, u32[]{:S(2)}) %all-to-all-start.1) | async-done | bytes 6291488 | tf_op jit(solution)/shard_map/all_to_all | solution.py:1369
  98.6 4.8 all-to-all-start.4
  108.4 29.2 %feed_forward.4 = (bf16[8,512,768]{2,1,0:T(8,128)(2,1)}, bf16[4,512,3072]{2,1,0:T(8,128)(2,1)}, bf16[4,512,3072]{2,1,0:T(8,128)(2,1)}, bf16[4,512,768]{2,1,0:T(8,128)(2,1)}, f32[4,512,128]{2,1,0:T(8,128)}) custom-call(s32[60]{0:T(128)} %get-tuple-element.123.rows_ref, s32[32]{0:T(128)} %get-tuple-element.124.counts_ref, ...), custom_call_target="tpu_custom_call" | custom-call | flops 14495514624 | bytes 41943040 | tf_op jit(solution)/shard_map/feed_forward/pallas_call | solution.py:675
  137.7 12.9 attention_forward.4
  150.6 15.8 %conv_forward.4 = (bf16[8,512,768]{2,1,0:T(8,128)(2,1)}, bf16[9,512,768]{2,1,0:T(8,128)(2,1)}, bf16[9,512,768]{2,1,0:T(8,128)(2,1)}, f32[9,512,128]{2,1,0:T(8,128)}) custom-call(s32[60]{0:T(128)} %get-tuple-element.123.rows_ref, s32[32]{0:T(128)} %get-tuple-element.124.counts_ref, ...), custom_call_target="tpu_custom_call", output_to_operand_aliasing={{0}: (7, {})} | custom-call | flops 5435817984 | bytes 37748736 | tf_op jit(solution)/shard_map/conv_forward/pallas_call | solution.py:1026
  166.4 8.5 all-to-all-done.4.x_ref.x_ref1
  174.9 4.9 all-to-all-start.2
  179.9 20.6 %feed_forward.6 = (bf16[8,512,768]{2,1,0:T(8,128)(2,1)}, bf16[4,512,3072]{2,1,0:T(8,128)(2,1)}, bf16[4,512,3072]{2,1,0:T(8,128)(2,1)}, bf16[4,512,768]{2,1,0:T(8,128)(2,1)}, f32[4,512,128]{2,1,0:T(8,128)}) custom-call(s32[60]{0:T(128)} %get-tuple-element.123.rows_ref, ...), custom_call_target="tpu_custom_call", output_to_operand_aliasing={{1}: (7, {}), {2}: (8, {}), {3}: (9, {}), {4}: (10, {})} | custom-call | flops 14495514624 | bytes 41943040 | tf_op jit(solution)/shard_map/feed_forward/pallas_call | solution.py:675
  200.4 13.0 attention_forward.6
  213.4 18.9 %conv_forward.6 = (bf16[8,512,768]{2,1,0:T(8,128)(2,1)}, bf16[9,512,768]{2,1,0:T(8,128)(2,1)}, bf16[9,512,768]{2,1,0:T(8,128)(2,1)}, f32[9,512,128]{2,1,0:T(8,128)}) custom-call(s32[60]{0:T(128)} %get-tuple-element.123.rows_ref, s32[32]{0:T(128)} %get-tuple-element.124.counts_ref, ...), custom_call_target="tpu_custom_call", output_to_operand_aliasing={{0}: (7, {})} | custom-call | flops 5435817984 | bytes 37748736 | tf_op jit(solution)/shard_map/conv_forward/pallas_call | solution.py:1026
  232.3 19.2 %all-to-all-done.2.refs_0_ = bf16[8,512,768]{2,1,0:T(8,128)(2,1)} async-done(((bf16[8,512,768]{2,1,0:T(8,128)(2,1)}), bf16[8,512,768]{2,1,0:T(8,128)(2,1)}, u32[]{:S(2)}, u32[]{:S(2)}) %all-to-all-start.2) | async-done | bytes 6291488 | tf_op jit(solution)/shard_map/all_to_all | solution.py:1369
  251.5 4.8 all-to-all-start.5
  256.3 4.7 relay_x.2
  260.9 66.9 %all-to-all-done.5.refs_0_ = bf16[8,512,768]{2,1,0:T(8,128)(2,1)} async-done(((bf16[8,512,768]{2,1,0:T(8,128)(2,1)}), bf16[8,512,768]{2,1,0:T(8,128)(2,1)}, u32[]{:S(2)}, u32[]{:S(2)}) %all-to-all-start.5) | async-done | bytes 6291488 | tf_op jit(solution)/shard_map/all_to_all | solution.py:1369
  327.8 4.7 all-to-all-start.3
  332.6 4.7 relay_x.3
  337.4 66.8 %all-to-all-done.3.x_ref.x_ref0 = bf16[8,512,768]{2,1,0:T(8,128)(2,1)} async-done(((bf16[8,512,768]{2,1,0:T(8,128)(2,1)}), bf16[8,512,768]{2,1,0:T(8,128)(2,1)}, u32[]{:S(2)}, u32[]{:S(2)}) %all-to-all-start.3) | async-done | bytes 6291488 | tf_op jit(solution)/shard_map/all_to_all | solution.py:1369
  404.2 5.0 all-to-all-start.6
  410.5 10.9 feed_forward.5
  421.4 12.9 attention_forward.5
  434.4 21.9 %conv_forward.5 = (bf16[8,512,768]{2,1,0:T(8,128)(2,1)}, bf16[9,512,768]{2,1,0:T(8,128)(2,1)}, bf16[9,512,768]{2,1,0:T(8,128)(2,1)}, f32[9,512,128]{2,1,0:T(8,128)}) custom-call(s32[60]{0:T(128)} %get-tuple-element.123.rows_ref, s32[32]{0:T(128)} %get-tuple-element.124.counts_ref, ...), custom_call_target="tpu_custom_call", output_to_operand_aliasing={{0}: (7, {})} | custom-call | flops 5435817984 | bytes 37748736 | tf_op jit(solution)/shard_map/conv_forward/pallas_call | solution.py:1026
  456.3 4.7 send_cotangent.3
  461.0 19.9 %all-to-all-done.6.x_ref.x_ref1 = bf16[8,512,768]{2,1,0:T(8,128)(2,1)} async-done(((bf16[8,512,768]{2,1,0:T(8,128)(2,1)}), bf16[8,512,768]{2,1,0:T(8,128)(2,1)}, u32[]{:S(2)}, u32[]{:S(2)}) %all-to-all-start.6) | async-done | bytes 6291488 | tf_op jit(solution)/shard_map/all_to_all | solution.py:1369
  480.8 5.0 all-to-all-start.8
  485.8 29.3 %feed_forward.7 = (bf16[8,512,768]{2,1,0:T(8,128)(2,1)}, bf16[4,512,3072]{2,1,0:T(8,128)(2,1)}, bf16[4,512,3072]{2,1,0:T(8,128)(2,1)}, bf16[4,512,768]{2,1,0:T(8,128)(2,1)}, f32[4,512,128]{2,1,0:T(8,128)}) custom-call(s32[60]{0:T(128)} %get-tuple-element.123.rows_ref, ...), custom_call_target="tpu_custom_call", output_to_operand_aliasing={{1}: (7, {}), {2}: (8, {}), {3}: (9, {}), {4}: (10, {})} | custom-call | flops 14495514624 | bytes 41943040 | tf_op jit(solution)/shard_map/feed_forward/pallas_call | solution.py:675
  515.1 12.9 attention_forward.7
  528.0 15.0 %conv_forward.7 = (bf16[8,512,768]{2,1,0:T(8,128)(2,1)}, bf16[9,512,768]{2,1,0:T(8,128)(2,1)}, bf16[9,512,768]{2,1,0:T(8,128)(2,1)}, f32[9,512,128]{2,1,0:T(8,128)}) custom-call(s32[60]{0:T(128)} %get-tuple-element.123.rows_ref, s32[32]{0:T(128)} %get-tuple-element.124.counts_ref, ...), custom_call_target="tpu_custom_call", output_to_operand_aliasing={{0}: (7, {})} | custom-call | flops 5435817984 | bytes 37748736 | tf_op jit(solution)/shard_map/conv_forward/pallas_call | solution.py:1026
  543.0 4.7 send_cotangent.2
  547.7 9.7 all-to-all-done.8.dy_ref.dy_ref0
  557.4 4.7 all-to-all-start.7
  562.2 29.0 %attention_backward.4 = (bf16[8,512,768]{2,1,0:T(8,128)(2,1)}, f32[8,768]{1,0:T(8,128)}, f32[768,2304]{1,0:T(8,128)}, f32[768,768]{1,0:T(8,128)}) custom-call(s32[60]{0:T(128)} %get-tuple-element.123.rows_ref, s32[32]{0:T(128)} %get-tuple-element.124.counts_ref, bf16[8,512,768]{2,1,0:T(8,128)(2,1)} %all-to-all-done.3.x_ref.x_ref0, ...), custom_call_target="tpu_custom_call" | custom-call | flops 19327352832 | bytes 41943040 | tf_op jit(solution)/shard_map/attention_backward/pallas_call | solution.py:566
  591.2 38.6 %conv_backward.4 = (bf16[8,512,768]{2,1,0:T(8,128)(2,1)}, f32[24,768]{1,0:T(8,128)}, f32[3,768,768]{2,1,0:T(8,128)}) custom-call(s32[60]{0:T(128)} %get-tuple-element.123.rows_ref, s32[32]{0:T(128)} %get-tuple-element.124.counts_ref, bf16[8,512,768]{2,1,0:T(8,128)(2,1)} %all-to-all-done.3.x_ref.x_ref0, ...), custom_call_target="tpu_custom_call", output_to_operand_aliasing={{0}: (10, {})} | custom-call | flops 8153726976 | bytes 52428800 | tf_op jit(solution)/shard_map/conv_backward/pallas_call | solution.py:1175
  633.8 43.2 %feed_backward.2 = (f32[8,768]{1,0:T(8,128)}, bf16[8,512,768]{2,1,0:T(8,128)(2,1)}, bf16[8,512,768]{2,1,0:T(8,128)(2,1)}, bf16[4,1552,768]{2,1,0:T(8,128)(2,1)}) custom-call(s32[60]{0:T(128)} %get-tuple-element.123.rows_ref, s32[32]{0:T(128)} %get-tuple-element.124.counts_ref, ...), custom_call_target="tpu_custom_call", output_to_operand_aliasing={{1}: (13, {})} | custom-call | flops 25367150592 | bytes 52428800 | tf_op jit(solution)/shard_map/feed_backward/pallas_call | solution.py:904
  677.0 10.4 all-to-all-start.13
  687.4 28.4 %attention_backward.5 = (bf16[8,512,768]{2,1,0:T(8,128)(2,1)}, f32[8,768]{1,0:T(8,128)}, bf16[4,1376,768]{2,1,0:T(8,128)(2,1)}) custom-call(s32[60]{0:T(128)} %get-tuple-element.123.rows_ref, s32[32]{0:T(128)} %get-tuple-element.124.counts_ref, bf16[8,512,768]{2,1,0:T(8,128)(2,1)} %all-to-all-done.6.x_ref.x_ref1, ...), custom_call_target="tpu_custom_call", output_to_operand_aliasing={{0}: (13, {})} | custom-call | flops 19327352832 | bytes 41943040 | tf_op jit(solution)/shard_map/attention_backward/pallas_call | solution.py:566
  715.8 25.6 %conv_backward.5 = (bf16[8,512,768]{2,1,0:T(8,128)(2,1)}, f32[24,768]{1,0:T(8,128)}, bf16[4,1376,768]{2,1,0:T(8,128)(2,1)}) custom-call(s32[60]{0:T(128)} %get-tuple-element.123.rows_ref, s32[32]{0:T(128)} %get-tuple-element.124.counts_ref, bf16[8,512,768]{2,1,0:T(8,128)(2,1)} %all-to-all-done.6.x_ref.x_ref1, ...), custom_call_target="tpu_custom_call", output_to_operand_aliasing={{2}: (11, {}), {0}: (12, {})} | custom-call | flops 8153726976 | bytes 52428800 | tf_op jit(solution)/shard_map/conv_backward/pallas_call | solution.py:1175
  741.3 17.7 %all-to-all-done.13.refs_0_ = bf16[8,512,768]{2,1,0:T(8,128)(2,1)} async-done(((bf16[8,512,768]{2,1,0:T(8,128)(2,1)}), bf16[8,512,768]{2,1,0:T(8,128)(2,1)}, u32[]{:S(2)}, u32[]{:S(2)}) %all-to-all-start.13) | async-done | bytes 6291488 | tf_op jit(solution)/shard_map/all_to_all | solution.py:1369
  759.1 9.9 all-to-all-start.9
  770.7 5.5 relay_dx.3
  776.2 64.5 %all-to-all-done.9.refs_0_ = bf16[8,512,768]{2,1,0:T(8,128)(2,1)} async-done(((bf16[8,512,768]{2,1,0:T(8,128)(2,1)}), bf16[8,512,768]{2,1,0:T(8,128)(2,1)}, u32[]{:S(2)}, u32[]{:S(2)}) %all-to-all-start.9) | async-done | bytes 6291488 | tf_op jit(solution)/shard_map/all_to_all | solution.py:1369
  840.7 4.8 all-to-all-start.14
  845.5 4.7 relay_dx.2
  850.2 66.9 %all-to-all-done.14.dy_ref.dy_ref0 = bf16[8,512,768]{2,1,0:T(8,128)(2,1)} async-done(((bf16[8,512,768]{2,1,0:T(8,128)(2,1)}), bf16[8,512,768]{2,1,0:T(8,128)(2,1)}, u32[]{:S(2)}, u32[]{:S(2)}) %all-to-all-start.14) | async-done | bytes 6291488 | tf_op jit(solution)/shard_map/all_to_all | solution.py:1369
  917.1 4.8 all-to-all-start.10
  921.9 29.3 %attention_backward.6 = (bf16[8,512,768]{2,1,0:T(8,128)(2,1)}, f32[8,768]{1,0:T(8,128)}, f32[768,2304]{1,0:T(8,128)}, f32[768,768]{1,0:T(8,128)}) custom-call(s32[60]{0:T(128)} %get-tuple-element.123.rows_ref, s32[32]{0:T(128)} %get-tuple-element.124.counts_ref, bf16[8,512,768]{2,1,0:T(8,128)(2,1)} %all-to-all-done.1.x_ref.x_ref0, ...), custom_call_target="tpu_custom_call" | custom-call | flops 19327352832 | bytes 41943040 | tf_op jit(solution)/shard_map/attention_backward/pallas_call | solution.py:566
  951.2 25.7 %conv_backward.6 = (bf16[8,512,768]{2,1,0:T(8,128)(2,1)}, f32[24,768]{1,0:T(8,128)}, f32[3,768,768]{2,1,0:T(8,128)}) custom-call(s32[60]{0:T(128)} %get-tuple-element.123.rows_ref, s32[32]{0:T(128)} %get-tuple-element.124.counts_ref, bf16[8,512,768]{2,1,0:T(8,128)(2,1)} %all-to-all-done.1.x_ref.x_ref0, ...), custom_call_target="tpu_custom_call", output_to_operand_aliasing={{0}: (10, {})} | custom-call | flops 8153726976 | bytes 52428800 | tf_op jit(solution)/shard_map/conv_backward/pallas_call | solution.py:1175
  977.0 16.5 %all-to-all-done.10.refs_1_.dy_ref1.dy_ref = bf16[8,512,768]{2,1,0:T(8,128)(2,1)} async-done(((bf16[8,512,768]{2,1,0:T(8,128)(2,1)}), bf16[8,512,768]{2,1,0:T(8,128)(2,1)}, u32[]{:S(2)}, u32[]{:S(2)}) %all-to-all-start.10) | async-done | bytes 6291488 | tf_op jit(solution)/shard_map/all_to_all | solution.py:1369
  993.5 48.7 %feed_backward.3 = (f32[8,768]{1,0:T(8,128)}, bf16[8,512,768]{2,1,0:T(8,128)(2,1)}, bf16[8,512,768]{2,1,0:T(8,128)(2,1)}, bf16[4,1552,768]{2,1,0:T(8,128)(2,1)}) custom-call(s32[60]{0:T(128)} %get-tuple-element.123.rows_ref, s32[32]{0:T(128)} %get-tuple-element.124.counts_ref, ...), custom_call_target="tpu_custom_call", output_to_operand_aliasing={{1}: (13, {})} | custom-call | flops 25367150592 | bytes 52428800 | tf_op jit(solution)/shard_map/feed_backward/pallas_call | solution.py:904
  1042.3 8.1 all-to-all-start.11
  1050.5 27.6 %attention_backward.7 = (bf16[8,512,768]{2,1,0:T(8,128)(2,1)}, f32[8,768]{1,0:T(8,128)}, bf16[4,1376,768]{2,1,0:T(8,128)(2,1)}) custom-call(s32[60]{0:T(128)} %get-tuple-element.123.rows_ref, s32[32]{0:T(128)} %get-tuple-element.124.counts_ref, bf16[8,512,768]{2,1,0:T(8,128)(2,1)} %all-to-all-done.4.x_ref.x_ref1, ...), custom_call_target="tpu_custom_call", output_to_operand_aliasing={{0}: (13, {})} | custom-call | flops 19327352832 | bytes 41943040 | tf_op jit(solution)/shard_map/attention_backward/pallas_call | solution.py:566
  1079.2 33.8 %conv_backward.7 = (bf16[8,512,768]{2,1,0:T(8,128)(2,1)}, f32[24,768]{1,0:T(8,128)}, bf16[4,1376,768]{2,1,0:T(8,128)(2,1)}) custom-call(s32[60]{0:T(128)} %get-tuple-element.123.rows_ref, s32[32]{0:T(128)} %get-tuple-element.124.counts_ref, bf16[8,512,768]{2,1,0:T(8,128)(2,1)} %all-to-all-done.4.x_ref.x_ref1, ...), custom_call_target="tpu_custom_call", output_to_operand_aliasing={{2}: (11, {}), {0}: (12, {})} | custom-call | flops 8153726976 | bytes 52428800 | tf_op jit(solution)/shard_map/conv_backward/pallas_call | solution.py:1175
  1115.1 7.0 all-to-all-done.11.refs_0_
  1122.1 101.6 %all_to_all.89.refs_1_ = bf16[8,512,768]{2,1,0:T(8,128)(2,1)} all-to-all(bf16[8,512,768]{2,1,0:T(8,128)(2,1)} %after.5), channel_id=1, replica_groups=mesh['dp'=4,'op'=8] {'op'}, dimensions={0} | all-to-all | bytes 12582912 | tf_op jit(solution)/shard_map/all_to_all | solution.py:1369
  1223.7 4.8 all-to-all-start.15
  1228.5 71.6 %all-to-all-done.15.refs_0_ = bf16[8,512,768]{2,1,0:T(8,128)(2,1)} async-done(((bf16[8,512,768]{2,1,0:T(8,128)(2,1)}), bf16[8,512,768]{2,1,0:T(8,128)(2,1)}, u32[]{:S(2)}, u32[]{:S(2)}) %all-to-all-start.15) | async-done | bytes 6291488 | tf_op jit(solution)/shard_map/all_to_all | solution.py:1369
  1300.1 4.8 all-to-all-start.16
  1304.9 8.1 outputs.1
  1313.0 6.4 finish_rest.2
  1323.9 51.8 %reduce-scatter.11.cloned.1.call-done = bf16[1,1376,768]{2,1,0:T(8,128)(2,1)} async-done(((bf16[4,1376,768]{2,1,0:T(8,128)(2,1)}), bf16[1,1376,768]{2,1,0:T(8,128)(2,1)}) %reduce-scatter.11.cloned.1.call-update) | async-done | bytes 2113552 | tf_op jit(solution)/shard_map/reduce_scatter | solution.py:1373
  1375.7 6.3 finish_rest.3
  1390.6 8.0 input_grad.1
  (105 shorter events, 37.9 us)
Async XLA Ops:
  12.3 9.8 all-to-all-start
  22.1 76.4 %all-to-all-start.1 = ((bf16[8,512,768]{2,1,0:T(8,128)(2,1)}), bf16[8,512,768]{2,1,0:T(8,128)(2,1)}, u32[]{:S(2)}, u32[]{:S(2)}) async-start(bf16[8,512,768]{2,1,0:T(8,128)(2,1)} %send_inputs.2), calls=%async_computation.1 | async-start | bytes 12582912 | tf_op jit(solution)/shard_map/all_to_all | solution.py:1369
  31.6 71.8 %copy-start.4 = (bf16[2,1,5,768]{3,0,2,1:T(2,128)(2,1)S(1)}, bf16[2,1,5,768]{3,0,2,1:T(2,128)(2,1)}, u32[]{:S(2)}) copy-start(bf16[2,1,5,768]{3,0,2,1:T(2,128)(2,1)} %param.19) | copy-start | bytes 46084
  31.6 71.8 %copy-start.5 = (bf16[2,1,5,768]{3,0,2,1:T(2,128)(2,1)S(1)}, bf16[2,1,5,768]{3,0,2,1:T(2,128)(2,1)}, u32[]{:S(2)}) copy-start(bf16[2,1,5,768]{3,0,2,1:T(2,128)(2,1)} %param.20) | copy-start | bytes 46084
  31.6 71.8 %copy-start = (bf16[2,1,15,768]{3,0,2,1:T(2,128)(2,1)S(1)}, bf16[2,1,15,768]{3,0,2,1:T(2,128)(2,1)}, u32[]{:S(2)}) copy-start(bf16[2,1,15,768]{3,0,2,1:T(2,128)(2,1)} %param.17) | copy-start | bytes 138244
  98.6 76.4 %all-to-all-start.4 = ((bf16[8,512,768]{2,1,0:T(8,128)(2,1)}), bf16[8,512,768]{2,1,0:T(8,128)(2,1)}, u32[]{:S(2)}, u32[]{:S(2)}) async-start(bf16[8,512,768]{2,1,0:T(8,128)(2,1)} %send_inputs.3), calls=%async_computation.4 | async-start | bytes 12582912 | tf_op jit(solution)/shard_map/all_to_all | solution.py:1369
  174.9 76.6 %all-to-all-start.2 = ((bf16[8,512,768]{2,1,0:T(8,128)(2,1)}), bf16[8,512,768]{2,1,0:T(8,128)(2,1)}, u32[]{:S(2)}, u32[]{:S(2)}) async-start(bf16[8,512,768]{2,1,0:T(8,128)(2,1)} %get-tuple-element.128), calls=%async_computation.2 | async-start | bytes 12582912 | tf_op jit(solution)/shard_map/all_to_all | solution.py:1369
  251.5 76.4 %all-to-all-start.5 = ((bf16[8,512,768]{2,1,0:T(8,128)(2,1)}), bf16[8,512,768]{2,1,0:T(8,128)(2,1)}, u32[]{:S(2)}, u32[]{:S(2)}) async-start(bf16[8,512,768]{2,1,0:T(8,128)(2,1)} %get-tuple-element.138), calls=%async_computation.5 | async-start | bytes 12582912 | tf_op jit(solution)/shard_map/all_to_all | solution.py:1369
  327.8 76.4 %all-to-all-start.3 = ((bf16[8,512,768]{2,1,0:T(8,128)(2,1)}), bf16[8,512,768]{2,1,0:T(8,128)(2,1)}, u32[]{:S(2)}, u32[]{:S(2)}) async-start(bf16[8,512,768]{2,1,0:T(8,128)(2,1)} %relay_x.2), calls=%async_computation.3 | async-start | bytes 12582912 | tf_op jit(solution)/shard_map/all_to_all | solution.py:1369
  404.2 76.6 %all-to-all-start.6 = ((bf16[8,512,768]{2,1,0:T(8,128)(2,1)}), bf16[8,512,768]{2,1,0:T(8,128)(2,1)}, u32[]{:S(2)}, u32[]{:S(2)}) async-start(bf16[8,512,768]{2,1,0:T(8,128)(2,1)} %relay_x.3), calls=%async_computation.6 | async-start | bytes 12582912 | tf_op jit(solution)/shard_map/all_to_all | solution.py:1369
  480.8 76.6 %all-to-all-start.8 = ((bf16[8,512,768]{2,1,0:T(8,128)(2,1)}), bf16[8,512,768]{2,1,0:T(8,128)(2,1)}, u32[]{:S(2)}, u32[]{:S(2)}) async-start(bf16[8,512,768]{2,1,0:T(8,128)(2,1)} %send_cotangent.3), calls=%async_computation.8 | async-start | bytes 12582912 | tf_op jit(solution)/shard_map/all_to_all | solution.py:1369
  557.4 76.3 %all-to-all-start.7 = ((bf16[8,512,768]{2,1,0:T(8,128)(2,1)}), bf16[8,512,768]{2,1,0:T(8,128)(2,1)}, u32[]{:S(2)}, u32[]{:S(2)}) async-start(bf16[8,512,768]{2,1,0:T(8,128)(2,1)} %send_cotangent.2), calls=%async_computation.7 | async-start | bytes 12582912 | tf_op jit(solution)/shard_map/all_to_all | solution.py:1369
  562.2 431.3 %reduce-scatter.5.cloned.1.call-start = ((), (), s32[]{:S(2)}) async-start(), calls=%async_computation.21 | async-start | bytes 11919360 | tf_op jit(solution)/shard_map/reduce_scatter | solution.py:1373
  677.0 82.1 %all-to-all-start.13 = ((bf16[8,512,768]{2,1,0:T(8,128)(2,1)}), bf16[8,512,768]{2,1,0:T(8,128)(2,1)}, u32[]{:S(2)}, u32[]{:S(2)}) async-start(bf16[8,512,768]{2,1,0:T(8,128)(2,1)} %get-tuple-element.173), calls=%async_computation.13 | async-start | bytes 12582912 | tf_op jit(solution)/shard_map/all_to_all | solution.py:1369
  759.1 10.0 copy-start.8
  759.1 10.0 copy-start.10
  759.1 10.2 copy-start.6
  759.1 10.4 copy-start.2
  759.1 10.4 copy-start.3
  759.1 81.6 %all-to-all-start.9 = ((bf16[8,512,768]{2,1,0:T(8,128)(2,1)}), bf16[8,512,768]{2,1,0:T(8,128)(2,1)}, u32[]{:S(2)}, u32[]{:S(2)}) async-start(bf16[8,512,768]{2,1,0:T(8,128)(2,1)} %get-tuple-element.172), calls=%async_computation.9 | async-start | bytes 12582912 | tf_op jit(solution)/shard_map/all_to_all | solution.py:1369
  769.0 273.2 %reduce-scatter.7.cloned.1.call-start = ((), (), s32[]{:S(2)}) async-start(), calls=%async_computation.22 | async-start | bytes 10567680 | tf_op jit(solution)/shard_map/reduce_scatter | solution.py:1373
  840.7 76.4 %all-to-all-start.14 = ((bf16[8,512,768]{2,1,0:T(8,128)(2,1)}), bf16[8,512,768]{2,1,0:T(8,128)(2,1)}, u32[]{:S(2)}, u32[]{:S(2)}) async-start(bf16[8,512,768]{2,1,0:T(8,128)(2,1)} %relay_dx.3), calls=%async_computation.14 | async-start | bytes 12582912 | tf_op jit(solution)/shard_map/all_to_all | solution.py:1369
  917.1 76.4 %all-to-all-start.10 = ((bf16[8,512,768]{2,1,0:T(8,128)(2,1)}), bf16[8,512,768]{2,1,0:T(8,128)(2,1)}, u32[]{:S(2)}, u32[]{:S(2)}) async-start(bf16[8,512,768]{2,1,0:T(8,128)(2,1)} %relay_dx.2), calls=%async_computation.10 | async-start | bytes 12582912 | tf_op jit(solution)/shard_map/all_to_all | solution.py:1369
  921.9 306.6 %reduce-scatter.9.cloned.1.call-start = ((), (), s32[]{:S(2)}) async-start(), calls=%async_computation.23 | async-start | bytes 11919360 | tf_op jit(solution)/shard_map/reduce_scatter | solution.py:1373
  1042.3 79.8 %all-to-all-start.11 = ((bf16[8,512,768]{2,1,0:T(8,128)(2,1)}), bf16[8,512,768]{2,1,0:T(8,128)(2,1)}, u32[]{:S(2)}, u32[]{:S(2)}) async-start(bf16[8,512,768]{2,1,0:T(8,128)(2,1)} %after.4), calls=%async_computation.11 | async-start | bytes 12582912 | tf_op jit(solution)/shard_map/all_to_all | solution.py:1369
  1050.4 325.3 %reduce-scatter.11.cloned.1.call-start = ((), (), s32[]{:S(2)}) async-start(), calls=%async_computation.24 | async-start | bytes 10567680 | tf_op jit(solution)/shard_map/reduce_scatter | solution.py:1373
  1050.5 27.6 %copy-start.9 = (f32[8,768]{1,0:T(8,128)S(1)}, f32[8,768]{1,0:T(8,128)}, u32[]{:S(2)}) copy-start(f32[8,768]{1,0:T(8,128)} %get-tuple-element.213) | copy-start | bytes 73732
  1050.5 28.5 %copy-start.7 = (f32[8,768]{1,0:T(8,128)S(1)}, f32[8,768]{1,0:T(8,128)}, u32[]{:S(2)}) copy-start(f32[8,768]{1,0:T(8,128)} %get-tuple-element.215) | copy-start | bytes 73732
  1079.2 33.8 %copy-start.1 = (f32[24,768]{1,0:T(8,128)S(1)}, f32[24,768]{1,0:T(8,128)}, u32[]{:S(2)}) copy-start(f32[24,768]{1,0:T(8,128)} %get-tuple-element.211) | copy-start | bytes 221188
  1223.7 76.4 %all-to-all-start.15 = ((bf16[8,512,768]{2,1,0:T(8,128)(2,1)}), bf16[8,512,768]{2,1,0:T(8,128)(2,1)}, u32[]{:S(2)}, u32[]{:S(2)}) async-start(bf16[8,512,768]{2,1,0:T(8,128)(2,1)} %get-tuple-element.188), calls=%async_computation.16 | async-start | bytes 12582912 | tf_op jit(solution)/shard_map/all_to_all | solution.py:1369
  1300.1 90.5 %all-to-all-start.16 = ((bf16[8,512,768]{2,1,0:T(8,128)(2,1)}), bf16[8,512,768]{2,1,0:T(8,128)(2,1)}, u32[]{:S(2)}, u32[]{:S(2)}) async-start(bf16[8,512,768]{2,1,0:T(8,128)(2,1)} %after.7), calls=%async_computation.19 | async-start | bytes 12582912 | tf_op jit(solution)/shard_map/all_to_all | solution.py:1369
Sparse Core Ops, SparseCore 0:
  677.1 171.8 reduce-scatter.4
  852.0 146.3 reduce-scatter.6
  1042.4 184.0 reduce-scatter.8
  1229.3 146.3 reduce-scatter.10

commit v5 on v4

--- a/solution.py
+++ b/solution.py
@@ -39,11 +39,69 @@
     return lax.dot_general(a, b, (((0,), (0,)), ((), ())), preferred_element_type=F32)
 
 
+def colour_home(owners, seqs, home, cand, color, partner, first, tally):
+    base = home * seqs
+
+    def clear_owner(o, _):
+        first[o] = -1
+        return 0
+
+    lax.fori_loop(0, BLOCKS * owners, clear_owner, 0)
+    for half in range(HALVES):
+        tally[half] = 0
+
+    def pair_up(j, _):
+        color[base + j] = -1
+        for b in range(BLOCKS):
+            o = b * owners + lax.rem(cand[(base + j) * BLOCKS + b], owners)
+            other = first[o]
+            partner[b * seqs + j] = other
+            first[o] = j
+
+            @pl.when(other >= 0)
+            def _():
+                partner[b * seqs + other] = j
+
+        return 0
+
+    lax.fori_loop(0, seqs, pair_up, 0)
+
+    def give(j, shade):
+        color[base + j] = shade
+        tally[shade] = tally[shade] + 1
+
+    def paint(j, _):
+        @pl.when(color[base + j] < 0)
+        def _():
+            shade = jnp.where(tally[0] > tally[1], 1, 0).astype(jnp.int32)
+            give(j, shade)
+            for side in range(2):
+
+                def more(state):
+                    return state[0] >= 0
+
+                def walk(state):
+                    now, use, tone = state
+                    then = partner[use * seqs + now]
+                    free = jnp.logical_and(then >= 0, color[base + jnp.maximum(then, 0)] < 0)
+
+                    @pl.when(free)
+                    def _():
+                        give(then, 1 - tone)
+
+                    return (jnp.where(free, then, -1), 1 - use, 1 - tone)
+
+                lax.while_loop(more, walk, (j, jnp.int32(side), shade))
+
+        return 0
+
+    lax.fori_loop(0, seqs, paint, 0)
+
+
 def home_kernel(owners, seqs, cand, send, relay, tags, color, partner, first, tally):
     for b in range(BLOCKS):
 
         def clear_owner(o, _):
-            first[b * owners + o] = -1
             for half in range(HALVES):
                 send[(b * HALVES + half) * owners + o] = -1
                 relay[(b * HALVES + half) * owners + o] = -1
@@ -51,55 +109,7 @@
             return 0
 
         lax.fori_loop(0, owners, clear_owner, 0)
-    for half in range(HALVES):
-        tally[half] = 0
-
-    def pair_up(j, _):
-        color[j] = -1
-        for b in range(BLOCKS):
-            o = b * owners + lax.rem(cand[j * BLOCKS + b], owners)
-            other = first[o]
-            partner[b * seqs + j] = other
-            first[o] = j
-
-            @pl.when(other >= 0)
-            def _():
-                partner[b * seqs + other] = j
-
-        return 0
-
-    lax.fori_loop(0, seqs, pair_up, 0)
-
-    def give(j, shade):
-        color[j] = shade
-        tally[shade] = tally[shade] + 1
-
-    def paint(j, _):
-        @pl.when(color[j] < 0)
-        def _():
-            shade = jnp.where(tally[0] > tally[1], 1, 0).astype(jnp.int32)
-            give(j, shade)
-            for side in range(2):
-
-                def more(state):
-                    return state[0] >= 0
-
-                def walk(state):
-                    now, use, tone = state
-                    after = partner[use * seqs + now]
-                    free = jnp.logical_and(after >= 0, color[jnp.maximum(after, 0)] < 0)
-
-                    @pl.when(free)
-                    def _():
-                        give(after, 1 - tone)
-
-                    return (jnp.where(free, after, -1), 1 - use, 1 - tone)
-
-                lax.while_loop(more, walk, (j, jnp.int32(side), shade))
-
-        return 0
-
-    lax.fori_loop(0, seqs, paint, 0)
+    colour_home(owners, seqs, 0, cand, color, partner, first, tally)
 
     def place(j, _):
         half = color[j]
@@ -115,6 +125,162 @@
         return 0
 
     lax.fori_loop(0, seqs, place, 0)
+
+
+ROUTES = 10
+TRIES = 24
+
+
+def route_kernel(
+    owners, seqs, cand, me_ref, out, ok, color, partner, first, tally, leave, goal, hops, spill
+):
+    me = me_ref[0]
+    square = owners * owners
+
+    def colour(home, _):
+        colour_home(owners, seqs, home, cand, color, partner, first, tally)
+        return 0
+
+    lax.fori_loop(0, owners, colour, 0)
+
+    def ends(q, _):
+        leave[q] = lax.rem(cand[q * BLOCKS], owners)
+        goal[q] = lax.rem(cand[q * BLOCKS + 1], owners)
+        return 0
+
+    lax.fori_loop(0, owners * seqs, ends, 0)
+
+    def attempt(state):
+        turn, _ = state
+
+        def clear(n, _):
+            hops[n] = -1
+            return 0
+
+        lax.fori_loop(0, 3 * square, clear, 0)
+
+        def direct(q, spilt):
+            at = color[q] * 2 * square + leave[q] * owners + goal[q]
+            free = hops[at] < 0
+
+            @pl.when(free)
+            def _():
+                hops[at] = q
+
+            @pl.when(jnp.logical_not(free))
+            def _():
+                spill[spilt] = q
+
+            return jnp.where(free, spilt, spilt + 1)
+
+        spilt = lax.fori_loop(0, owners * seqs, direct, jnp.int32(0))
+        begin = lax.rem(turn * 5, jnp.maximum(spilt, 1))
+
+        def two_hops(n, lost):
+            q = spill[lax.rem(begin + n, jnp.maximum(spilt, 1))]
+            o, p = leave[q], goal[q]
+            early = color[q] * square
+            shift = o * 3 + p * 5 + (n + 1) * turn
+
+            def look(s, found):
+                i = lax.rem(shift + s, owners)
+                a = early + o * owners + i
+                b = early + square + i * owners + p
+                good = jnp.logical_and(hops[a] < 0, hops[b] < 0)
+                return jnp.where(jnp.logical_and(good, found < 0), i, found)
+
+            i = lax.fori_loop(0, owners, look, jnp.int32(-1))
+
+            @pl.when(i >= 0)
+            def _():
+                hops[early + o * owners + i] = q
+                hops[early + square + i * owners + p] = q
+
+            return jnp.where(i >= 0, lost, lost + 1)
+
+        lost = lax.fori_loop(0, spilt, two_hops, jnp.int32(0))
+        return turn + 1, lost
+
+    def again(state):
+        return jnp.logical_and(state[0] < TRIES, state[1] > 0)
+
+    _, lost = lax.while_loop(again, attempt, (jnp.int32(0), jnp.int32(1)))
+    ok[0] = lost
+
+    def clear_out(n, _):
+        out[n] = -1
+        return 0
+
+    lax.fori_loop(0, ROUTES * owners, clear_out, 0)
+
+    def note(d, _):
+        def home(q):
+            return lax.div(q, seqs)
+
+        def put(table, at, value):
+            out[table * owners + at] = value
+
+        q = hops[me * owners + d]
+
+        @pl.when(q >= 0)
+        def _():
+            put(0, d, home(q))
+            put(9, home(q), d)
+
+        q1 = hops[square + me * owners + d]
+
+        @pl.when(q1 >= 0)
+        def _():
+            late = color[q1] == 1
+            put(1, d, jnp.where(late, owners + home(q1), leave[q1]))
+
+            @pl.when(late)
+            def _():
+                put(8, home(q1), owners + d)
+
+        q2 = hops[2 * square + me * owners + d]
+
+        @pl.when(q2 >= 0)
+        def _():
+            mine = leave[q2] == me
+            put(2, d, jnp.where(mine, home(q2), owners + leave[q2]))
+
+            @pl.when(mine)
+            def _():
+                put(8, home(q2), d)
+
+        r = hops[d * owners + me]
+
+        @pl.when(r >= 0)
+        def _():
+            there = goal[r] == me
+            put(7, d, jnp.where(there, home(r), owners + goal[r]))
+
+            @pl.when(there)
+            def _():
+                put(3, home(r), d)
+
+        r1 = hops[square + d * owners + me]
+
+        @pl.when(r1 >= 0)
+        def _():
+            late = color[r1] == 1
+            put(6, d, jnp.where(late, owners + goal[r1], home(r1)))
+
+            @pl.when(jnp.logical_not(late))
+            def _():
+                put(3, home(r1), owners + d)
+
+        r2 = hops[2 * square + d * owners + me]
+
+        @pl.when(r2 >= 0)
+        def _():
+            put(4, home(r2), d)
+            put(5, d, home(r2))
+
+        return 0
+
+    lax.fori_loop(0, owners, note, 0)
 
 
 SMEM_SPEC = pl.BlockSpec(memory_space=pltpu.SMEM)
@@ -196,6 +362,93 @@
         out_shape=[int_shape(BLOCKS * HALVES * SLOTS), int_shape(BLOCKS * HALVES * 8)],
         name="owner_tables",
     )(tags)
+
+
+def route_tables(cand, me, owners, seqs):
+    def kernel(*refs):
+        route_kernel(owners, seqs, *refs)
+
+    smem = lambda n: pltpu.SMEM((n,), jnp.int32)
+    return pl.pallas_call(
+        kernel,
+        in_specs=[SMEM_SPEC] * 2,
+        out_specs=[SMEM_SPEC] * 2,
+        out_shape=[int_shape(ROUTES * owners), int_shape(1)],
+        scratch_shapes=[
+            smem(owners * seqs),
+            smem(BLOCKS * seqs),
+            smem(BLOCKS * owners),
+            smem(HALVES),
+            smem(owners * seqs),
+            smem(owners * seqs),
+            smem(3 * owners * owners),
+            smem(owners * seqs),
+        ],
+        name="route_tables",
+    )(cand, me)
+
+
+def bring_rows(table, start, sources, name):
+    count, length, width = sources[0].shape
+
+    def kernel(table_ref, *refs):
+        ins = refs[: len(sources)]
+        out_ref, buf, sem_in, sem_out = refs[-4:]
+
+        def loads(n):
+            e = table_ref[start + n]
+            last = count * (len(sources) - 1)
+            for which, source in enumerate(ins):
+                low = count * which
+                here = e >= low
+                if low < last:
+                    here = jnp.logical_and(here, e < low + count)
+                row = jnp.clip(e - low, 0, count - 1)
+                yield here, pltpu.make_async_copy(source.at[row], buf.at[n], sem_in.at[n])
+
+        def store(n):
+            return pltpu.make_async_copy(buf.at[n], out_ref.at[n], sem_out.at[n])
+
+        for n in range(count):
+            for here, copy in loads(n):
+
+                @pl.when(here)
+                def _():
+                    copy.start()
+
+        for n in range(count):
+
+            @pl.when(table_ref[start + n] >= 0)
+            def _():
+                pltpu.make_async_copy(ins[0].at[0], buf.at[n], sem_in.at[n]).wait()
+                store(n).start()
+
+        for n in range(count):
+
+            @pl.when(table_ref[start + n] >= 0)
+            def _():
+                store(n).wait()
+
+    return pl.pallas_call(
+        kernel,
+        grid_spec=pltpu.PrefetchScalarGridSpec(
+            num_scalar_prefetch=1,
+            grid=(1,),
+            in_specs=[ANY_SPEC] * len(sources),
+            out_specs=ANY_SPEC,
+            scratch_shapes=[
+                pltpu.VMEM((count, length, width), BF16),
+                pltpu.SemaphoreType.DMA((count,)),
+                pltpu.SemaphoreType.DMA((count,)),
+            ],
+        ),
+        out_shape=jax.ShapeDtypeStruct((count, length, width), BF16),
+        compiler_params=params_of(1),
+        cost_estimate=pl.CostEstimate(
+            flops=0, transcendentals=0, bytes_accessed=4 * count * length * width
+        ),
+        name=name,
+    )(table, *sources)
 
 
 def move_rows(table, starts, sources, count, scatter, name, wait_for=()):
@@ -708,7 +961,7 @@
     )(*args)
 
 
-def feed_backward(b, tables, x, dy, kept, weights, gains, dx_first, groups, wait_for):
+def feed_backward(b, tables, x, dy, kept, weights, gains, dx_lead, lead, groups, wait_for):
     rows, counts = tables
     ffn_up, ffn_down = weights
     g, slope, zn, rstd = kept
@@ -898,8 +1151,8 @@
         pl.BlockSpec((8, width), lambda c, i, r, n: (0, 0)),
         ANY_SPEC,
     ] + [ANY_SPEC] * len(wait_for)
-    args = [rows, counts, *x, *dy, g, slope, zn, rstd, ffn_up, ffn_down, gains, dx_first]
-    alias = {len(args) - 1: 1}
+    args = [rows, counts, *x, *dy, g, slope, zn, rstd, ffn_up, ffn_down, gains, dx_lead]
+    alias = {len(args) - 1: 1 + lead}
     args += wait_for
     return pl.pallas_call(
         kernel,
@@ -1235,23 +1488,41 @@
     width = x[0].shape[-1]
     rest_rows = 7 * width // groups + SMALL_ROWS
     attn, conv = (attn_qkv, attn_out), (taps, conv_point)
-    first, second = b * HALVES, b * HALVES + 1
-    d0, small_a0, *sum_a = attention_backward(
-        first, tables, x[0], dy[0], kept_a[0], attn, gains, None, None, None
+    lead, other = 1, 0
+    first, second = b * HALVES + lead, b * HALVES + other
+    d_lead, small_a0, *sum_a = attention_backward(
+        first, tables, x[lead], dy[lead], kept_a[lead], attn, gains, None, None, None
     )
-    d0, small_c0, sum_c = conv_backward(
-        first, tables, x[0], dy[0], kept_c[0], conv, gains, d0, None, (groups,)
+    d_lead, small_c0, sum_c = conv_backward(
+        first, tables, x[lead], dy[lead], kept_c[lead], conv, gains, d_lead, None, (groups,)
     )
-    small_f, d0, d1, feed_pack = feed_backward(
-        b, tables, x, dy, kept_f, (ffn_up, ffn_down), gains, d0, groups, wait_for
+    small_f, *dx, feed_pack = feed_backward(
+        b, tables, x, dy, kept_f, (ffn_up, ffn_down), gains, d_lead, lead, groups, wait_for
     )
-    d1, small_a1, rest_pack = attention_backward(
-        second, tables, x[1], dy[1], kept_a[1], attn, gains, d1, sum_a, (groups, rest_rows)
+    dx[other], small_a1, rest_pack = attention_backward(
+        second,
+        tables,
+        x[other],
+        dy[other],
+        kept_a[other],
+        attn,
+        gains,
+        dx[other],
+        sum_a,
+        (groups, rest_rows),
     )
-    d1, small_c1, rest_pack = conv_backward(
-        second, tables, x[1], dy[1], kept_c[1], conv, gains, d1, sum_c, (groups, rest_pack)
+    dx[other], small_c1, rest_pack = conv_backward(
+        second,
+        tables,
+        x[other],
+        dy[other],
+        kept_c[other],
+        conv,
+        gains,
+        dx[other],
+        sum_c,
+        (groups, rest_pack),
     )
-    dx = (d0, d1)
     small = join_small(small_f, small_a0 + small_a1, small_c0 + small_c1).astype(BF16)
     small = small.reshape(25, groups, width // groups)
     small = small.transpose(1, 0, 2)
@@ -1293,7 +1564,7 @@
     )(feed, feed, feed, *old)
 
 
-def finish_rest(b, rest, feed, old, shapes):
+def finish_rest(b, rest, feed, old, shapes, wait_for):
     tall, width = shapes[1].shape[2:]
     count_block = (feed.shape[0] - COUNT_ROWS) // COUNT_ROWS
     small_block = 7 * tall // SMALL_ROWS
@@ -1339,7 +1610,7 @@
             pl.BlockSpec((SMALL_ROWS, width), lambda i: (small_block, 0)),
             pl.BlockSpec((COUNT_ROWS, width), lambda i: (count_block, 0)),
         ]
-        + [ANY_SPEC] * len(old),
+        + [ANY_SPEC] * (len(old) + len(wait_for)),
         out_specs=[
             pl.BlockSpec((None, None, tall, width), lambda i: (b, 0, 0, jnp.minimum(i, 2))),
             pl.BlockSpec((None, None, tall, width), lambda i: (b, 0, 0, 0)),
@@ -1355,7 +1626,7 @@
         compiler_params=params_of(1),
         cost_estimate=pl.CostEstimate(flops=0, transcendentals=0, bytes_accessed=8 * 2**20),
         name="finish_rest",
-    )(rest, rest, feed, *old)
+    )(rest, rest, feed, *old, *wait_for)
 
 
 def small_params(b, conv_taps, norm_gain, norm_bias):
@@ -1401,61 +1672,117 @@
     def start(b, half):
         return (b * HALVES + half) * owners
 
+    me = lax.axis_index("op").astype(jnp.int32)[None]
+    routed = owners < seqs
+    if routed:
+        everyone = lax.all_gather(candidate, "op", axis=0, tiled=True)
+        route, lost = route_tables(everyone.reshape(-1), me, owners, seqs)
+        lost = lax.psum(lost[0], "dp")
+
     x0 = [
-        exchange(move_rows(send, [start(0, h)], [inputs], owners, False, "send_inputs"))
-        for h in both
-    ]
-    y0, kept0 = both_forward(0, tables, x0, weights, smalls[0])
-    x1 = []
-    for h in both:
-        back = exchange(y0[h])
-        x1.append(exchange(move_rows(relay, [start(0, h)], [back], owners, False, "relay_x")))
-    y1, kept1 = both_forward(1, tables, x1, weights, smalls[1])
-    dy1 = [
         exchange(
-            move_rows(
-                send, [start(1, h)], [cotangent], owners, False, "send_cotangent", (y1[h],)
-            )
+            move_rows(send, [start(0, h)], [inputs], owners, False, "send_inputs", (route,) * h if routed else ())
         )
         for h in both
     ]
-    dx1, feed1, rest1 = owner_backward(1, tables, x1, dy1, kept1, weights, smalls[1], groups, ())
-    feed1 = group_sum(feed1)
-    rest1 = group_sum(rest1)
-    dy0 = []
-    for h in both:
-        back = exchange(dx1[h])
-        dy0.append(exchange(move_rows(relay, [start(1, h)], [back], owners, False, "relay_dx")))
-    dx0, feed0, rest0 = owner_backward(
-        0, tables, x0, dy0, kept0, weights, smalls[0], groups, (feed1,)
+    first = owner_forward(0, 0, tables, x0[0], weights, smalls[0], None)
+
+    def on_the_way(table, sources, name):
+        return bring_rows(route, table * owners, sources, name)
+
+    def straight_there(y):
+        hop0 = exchange(on_the_way(0, [y[0]], "hop_x"))
+        hop1 = exchange(on_the_way(1, [hop0, y[1]], "hop_x"))
+        hop2 = exchange(on_the_way(2, [y[1], hop1], "hop_x"))
+        return [on_the_way(3, [hop0, hop1], "land_x"), on_the_way(4, [hop2], "land_x")]
+
+    def straight_back(dx):
+        hop0 = exchange(on_the_way(5, [dx[1]], "hop_dx"))
+        hop1 = exchange(on_the_way(6, [dx[0], hop0], "hop_dx"))
+        hop2 = exchange(on_the_way(7, [dx[0], hop1], "hop_dx"))
+        return [on_the_way(9, [hop2], "land_dx"), on_the_way(8, [hop0, hop1], "land_dx")]
+
+    def home_there(y):
+        return [
+            exchange(move_rows(relay, [start(0, h)], [exchange(y[h])], owners, False, "relay_x"))
+            for h in both
+        ]
+
+    def home_back(dx):
+        return [
+            exchange(move_rows(relay, [start(1, h)], [exchange(dx[h])], owners, False, "relay_dx"))
+            for h in both
+        ]
+
+    def after_first(there, back, x0, first):
+        y00, kept_f, ka0, kc0 = first
+        y01, kept_f, ka1, kc1 = owner_forward(
+            0, 1, tables, x0[1], weights, smalls[0], kept_f
+        )
+        kept0 = (kept_f, [ka0, ka1], [kc0, kc1])
+        x1 = there([y00, y01])
+        y1, kept1 = both_forward(1, tables, x1, weights, smalls[1])
+        dy1 = [
+            exchange(
+                move_rows(
+                    send,
+                    [start(1, h)],
+                    [cotangent],
+                    owners,
+                    False,
+                    "send_cotangent",
+                    (y1[1 - h],),
+                )
+            )
+            for h in both
+        ]
+        dx1, feed1, rest1 = owner_backward(
+            1, tables, x1, dy1, kept1, weights, smalls[1], groups, ()
+        )
+        feed1 = group_sum(feed1)
+        rest1 = group_sum(rest1)
+        dy0 = back(dx1)
+        dx0, feed0, rest0 = owner_backward(
+            0, tables, x0, dy0, kept0, weights, smalls[0], groups, (feed1,)
+        )
+        feed0 = group_sum(feed0)
+        rest0 = group_sum(rest0)
+        y_home = [exchange(after(y1[h], (dy0[0],))) for h in both]
+        outputs = move_rows(send, [start(1, h) for h in both], y_home, seqs, True, "outputs")
+        dx_home = [
+            exchange(after(dx0[0], (feed0,))),
+            exchange(after(dx0[1], (rest1,))),
+        ]
+        input_grad = move_rows(
+            send, [start(0, h) for h in both], dx_home, seqs, True, "input_grad"
+        )
+        tall, deep = width // groups, hidden // groups
+        grad = lambda *dims: jax.ShapeDtypeStruct((BLOCKS, 1) + dims, F32)
+        feed_shapes = (grad(tall, hidden), grad(deep, width))
+        rest_shapes = (
+            grad(tall, 3 * width),
+            grad(tall, width),
+            grad(15, tall),
+            grad(KINDS - 2, tall, width),
+            grad(KINDS, tall),
+            grad(KINDS, tall),
+        )
+        feeds = finish_feed(1, feed1, None, None, feed_shapes)
+        rests = finish_rest(1, rest1, feed1, (), rest_shapes, ())
+        feeds = finish_feed(0, feed0, *feeds, feed_shapes)
+        rests = finish_rest(0, rest0, feed0, rests, rest_shapes, (outputs, input_grad, feeds[0]))
+        qkv, out, taps, point, gain, shift = rests
+        return (outputs, input_grad, qkv, out, *feeds, taps, point, gain, shift)
+
+    if not routed:
+        return after_first(home_there, home_back, x0, first)
+    return lax.cond(
+        lost == 0,
+        lambda x0, first: after_first(straight_there, straight_back, x0, first),
+        lambda x0, first: after_first(home_there, home_back, x0, first),
+        x0,
+        first,
     )
-    feed0 = group_sum(after(feed0, (rest1,)))
-    rest0 = group_sum(rest0)
-    starts = [start(1, h) for h in both]
-    y_home = [exchange(after(y1[h], (dy0[1],))) for h in both]
-    outputs = move_rows(send, starts, y_home, seqs, True, "outputs")
-    starts = [start(0, h) for h in both]
-    dx_home = [exchange(dx0[0]), exchange(after(dx0[1], (feed0,)))]
-    input_grad = move_rows(send, starts, dx_home, seqs, True, "input_grad")
-
-    tall, deep = width // groups, hidden // groups
-    grad = lambda *dims: jax.ShapeDtypeStruct((BLOCKS, 1) + dims, F32)
-    feed_shapes = (grad(tall, hidden), grad(deep, width))
-    rest_shapes = (
-        grad(tall, 3 * width),
-        grad(tall, width),
-        grad(15, tall),
-        grad(KINDS - 2, tall, width),
-        grad(KINDS, tall),
-        grad(KINDS, tall),
-    )
-    feeds, rests = (None, None), ()
-    for b, feed, rest in ((1, feed1, rest1), (0, feed0, rest0)):
-        feeds = finish_feed(b, feed, *feeds, feed_shapes)
-        rests = finish_rest(b, rest, feed, rests, rest_shapes)
-    qkv, out, taps, point, gain, shift = rests
-    grads = (qkv, out, *feeds, taps, point, gain, shift)
-    return (outputs, input_grad) + grads
 
 
 def solution(mesh):

time: 1420 us -> 1360 us (0.958)
  waiting for transfers between devices: 558 us -> 344 us
  blocking collectives: 102 us -> 252 us
    all_to_all x16 -> x13, waiting for transfers between devices: 506 us -> 273 us  [exchange(): return lax.all_to_all(rows, 'op', split_axis=0, concat_axis=0, tiled=True)]
    all_gather x0 -> x1, blocking collectives: none -> 74.5 us  [per_device(): everyone = lax.all_gather(candidate, 'op', axis=0, tiled=True)]
    pallas_call x0 -> x11, Pallas kernels: none -> 59.6 us  [the longest x10 42.9 us: bring_rows(): pl.pallas_call(kernel, grid_spec=pltpu.PrefetchScalarGridSpec(num_scalar_...]
    all_to_all x1 -> x2, blocking collectives: 102 us -> 154 us  [exchange(): return lax.all_to_all(rows, 'op', split_axis=0, concat_axis=0, tiled=True)]
    pallas_call x4, Pallas kernels: 114 us -> 80.7 us  [attention_backward(): pl.pallas_call(kernel, grid_spec=pltpu.PrefetchScalarGridSpec(num_scalar_...]
    psum x0 -> x1, blocking collectives: none -> 23.6 us  [per_device(): lost = lax.psum(lost[0], 'dp')]
    pallas_call x10 -> x6, Pallas kernels: 54.4 us -> 34.1 us  [move_rows(): pl.pallas_call(kernel, grid_spec=pltpu.PrefetchScalarGridSpec(num_scalar_...]
    reduce_scatter x4, waiting for transfers between devices: 51.8 us -> 70.4 us  [group_sum(): return lax.psum_scatter(pack, 'dp', scatter_dimension=0, tiled=False)]
  transfers between devices with their start and end apart: 20 -> 17, of which waited for: 15 -> 11; matrix products, arithmetic and copies ran while one was open for 1% -> 1% of each run, Pallas kernels for 41% -> 41%
where the time goes in v5:
time: 1360 us; the launch traced here: 1350 us
  Pallas kernels  616 us (45%)
  waiting for transfers between devices  344 us (25%)
  blocking collectives  252 us (19%)
  starting transfers between devices  95.5 us (7%)
  between operations  14.9 us (1%)
    all_to_all x13, waiting for transfers between devices, exchange(): return lax.all_to_all(rows, 'op', split_axis=0, concat_axis=0, tiled=True)  273 us
    all_to_all x2, blocking collectives, exchange(): return lax.all_to_all(rows, 'op', split_axis=0, concat_axis=0, tiled=True)  154 us
    pallas_call x4, Pallas kernels, conv_backward(): pl.pallas_call(kernel, grid_spec=pltpu.PrefetchScalarGridSpec(num_scalar_...  131 us
    all_to_all x13, starting transfers between devices, exchange(): return lax.all_to_all(rows, 'op', split_axis=0, concat_axis=0, tiled=True)  95.3 us
    pallas_call x2, Pallas kernels, feed_backward(): pl.pallas_call(kernel, grid_spec=pltpu.PrefetchScalarGridSpec(num_scalar_...  91.4 us
    pallas_call x4, Pallas kernels, feed_forward(): pl.pallas_call(kernel, grid_spec=pltpu.PrefetchScalarGridSpec(num_scalar_...  82.2 us
    pallas_call x4, Pallas kernels, attention_backward(): pl.pallas_call(kernel, grid_spec=pltpu.PrefetchScalarGridSpec(num_scalar_...  80.7 us
    pallas_call x4, Pallas kernels, conv_forward(): pl.pallas_call(kernel, grid_spec=pltpu.PrefetchScalarGridSpec(num_scalar_...  74.5 us
  transfers between devices with their start and end apart: 17, of which 11 were waited for; matrix products, arithmetic and copies ran while one was open for 1% of the time, Pallas kernels for 41%

profile of v5, /device:TPU:0, one launch (start us, length us, event | category | flops | bytes accessed | tf_op | source)
XLA Modules:
  0.0 1346.6 jit_solution(5173313060940384923)
XLA Ops:
  12.4 5.2 all-to-all-start.26
  22.2 4.8 all-to-all-start.27
  27.0 74.5 %all-gather = s32[8,12,2]{1,2,0:T(2,128)S(1)} all-gather(s32[1,12,2]{1,2,0:T(2,128)S(1)} %bitcast.62), channel_id=1, replica_groups=mesh['dp'=4,'op'=8] {'op'}, dimensions={0}, use_global_device_ids=true | all-gather | bytes 864 | tf_op jit(solution)/shard_map/all_gather | solution.py:1678
  102.4 16.8 %route_tables.1 = (s32[80]{0:T(128)S(1)}, s32[1]{0:T(128)}) custom-call(s32[192]{0:T(256)} %reshape.106.refs_0_, s32[1]{0:T(128)} %bitcast.13.refs_1_), custom_call_target="tpu_custom_call" | custom-call | tf_op jit(solution)/shard_map/route_tables/pallas_call | solution.py:372
  124.2 4.8 all-to-all-start.28
  129.1 23.6 %psum.7 = s32[]{:T(128)} all-reduce(s32[]{:T(128)} %bitcast.14), channel_id=1, replica_groups=mesh['dp'=4,'op'=8] {'dp'}, use_global_device_ids=true, to_apply=%region_0.1 | all-reduce | flops 1 | bytes 8 | tf_op jit(solution)/shard_map/psum | solution.py:1680
  157.3 28.8 %feed_forward.13 = (bf16[8,512,768]{2,1,0:T(8,128)(2,1)}, bf16[4,512,3072]{2,1,0:T(8,128)(2,1)}, bf16[4,512,3072]{2,1,0:T(8,128)(2,1)}, bf16[4,512,768]{2,1,0:T(8,128)(2,1)S(1)}, f32[4,512,128]{2,1,0:T(8,128)}) custom-call(s32[60]{0:T(128)S(1)} %get-tuple-element.397.rows_ref, s32[32]{0:T(128)S(1)} %get-tuple-element.398.counts_ref, ...), custom_call_target="tpu_custom_call" | custom-call | flops 14495514624 | bytes 41943040 | tf_op jit(solution)/shard_map/feed_forward/pallas_call | solution.py:928
  186.1 5.5 attention_forward.13
  191.5 18.3 %conv_forward.13 = (bf16[8,512,768]{2,1,0:T(8,128)(2,1)}, bf16[9,512,768]{2,1,0:T(8,128)(2,1)}, bf16[9,512,768]{2,1,0:T(8,128)(2,1)}, f32[9,512,128]{2,1,0:T(8,128)}) custom-call(s32[60]{0:T(128)S(1)} %get-tuple-element.397.rows_ref, s32[32]{0:T(128)S(1)} %get-tuple-element.398.counts_ref, ...), custom_call_target="tpu_custom_call", output_to_operand_aliasing={{0}: (7, {})} | custom-call | flops 5435817984 | bytes 37748736 | tf_op jit(solution)/shard_map/conv_forward/pallas_call | solution.py:1279
  209.8 1126.0 %conditional.1 = (f32[2,1,192,2304]{3,2,1,0:T(8,128)}, f32[2,1,192,768]{3,2,1,0:T(8,128)}, f32[2,1,192,3072]{3,2,1,0:T(8,128)}, f32[2,1,768,768]{3,2,1,0:T(8,128...) conditional(s32[]{:T(128)} %convert_element_type.48, ...), branch_computations={%region_1.6_spmd, %region_6.11_spmd} | conditional | flops 278434742272 | bytes 1449890048 | solution.py:1779
  217.3 4.6 hop_x.3
  221.8 8.5 all-to-all-start.14
  230.3 10.6 feed_forward.10
  240.9 13.2 attention_forward.10
  254.2 21.8 %conv_forward.10 = (bf16[8,512,768]{2,1,0:T(8,128)(2,1)}, bf16[9,512,768]{2,1,0:T(8,128)(2,1)}, bf16[9,512,768]{2,1,0:T(8,128)(2,1)}, f32[9,512,128]{2,1,0:T(8,128)}) custom-call(s32[60]{0:T(128)S(1)} %get-tuple-element.243.rows_ref, s32[32]{0:T(128)S(1)} %get-tuple-element.244.counts_ref, ...), custom_call_target="tpu_custom_call", output_to_operand_aliasing={{0}: (7, {})} | custom-call | flops 5435817984 | bytes 37748736 | tf_op jit(solution)/shard_map/cond/branch_1_fun/conv_forward/pallas_call | solution.py:1279
  275.9 26.0 %all-to-all-done.14.refs_0_ = bf16[8,512,768]{2,1,0:T(8,128)(2,1)} async-done(((bf16[8,512,768]{2,1,0:T(8,128)(2,1)}), bf16[8,512,768]{2,1,0:T(8,128)(2,1)}, u32[]{:S(2)}, u32[]{:S(2)}) %all-to-all-start.14) | async-done | bytes 6291488 | tf_op jit(solution)/shard_map/cond/branch_1_fun/all_to_all | solution.py:1640
  305.2 76.9 %all_to_all.123.refs_1_ = bf16[8,512,768]{2,1,0:T(8,128)(2,1)} all-to-all(bf16[8,512,768]{2,1,0:T(8,128)(2,1)} %hop_x.4), channel_id=1, replica_groups=mesh['dp'=4,'op'=8] {'op'}, dimensions={0} | all-to-all | bytes 12582912 | tf_op jit(solution)/shard_map/cond/branch_1_fun/all_to_all | solution.py:1640
  382.1 4.6 hop_x.5
  386.6 4.9 all-to-all-start.16
  391.6 4.6 land_x.2.x_ref.x_ref0
  396.2 10.9 feed_forward.11
  407.1 5.1 attention_forward.11
  412.2 20.5 %conv_forward.11 = (bf16[8,512,768]{2,1,0:T(8,128)(2,1)}, bf16[9,512,768]{2,1,0:T(8,128)(2,1)}, bf16[9,512,768]{2,1,0:T(8,128)(2,1)}, f32[9,512,128]{2,1,0:T(8,128)}) custom-call(s32[60]{0:T(128)S(1)} %get-tuple-element.243.rows_ref, s32[32]{0:T(128)S(1)} %get-tuple-element.244.counts_ref, ...), custom_call_target="tpu_custom_call", output_to_operand_aliasing={{0}: (7, {})} | custom-call | flops 5435817984 | bytes 37748736 | tf_op jit(solution)/shard_map/cond/branch_1_fun/conv_forward/pallas_call | solution.py:1279
  432.7 4.6 send_cotangent.7
  437.2 25.9 %all-to-all-done.16.refs_0_ = bf16[8,512,768]{2,1,0:T(8,128)(2,1)} async-done(((bf16[8,512,768]{2,1,0:T(8,128)(2,1)}), bf16[8,512,768]{2,1,0:T(8,128)(2,1)}, u32[]{:S(2)}, u32[]{:S(2)}) %all-to-all-start.16) | async-done | bytes 6291488 | tf_op jit(solution)/shard_map/cond/branch_1_fun/all_to_all | solution.py:1640
  463.2 5.0 all-to-all-start.18
  468.2 4.6 land_x.3.x_ref.x_ref1
  472.8 31.8 %feed_forward.12 = (bf16[8,512,768]{2,1,0:T(8,128)(2,1)}, bf16[4,512,3072]{2,1,0:T(8,128)(2,1)}, bf16[4,512,3072]{2,1,0:T(8,128)(2,1)}, bf16[4,512,768]{2,1,0:T(8,128)(2,1)}, f32[4,512,128]{2,1,0:T(8,128)}) custom-call(s32[60]{0:T(128)S(1)} %get-tuple-element.243.rows_ref, ...), custom_call_target="tpu_custom_call", output_to_operand_aliasing={{1}: (7, {}), {2}: (8, {}), {3}: (9, {}), {4}: (10, {})} | custom-call | flops 14495514624 | bytes 41943040 | tf_op jit(solution)/shard_map/cond/branch_1_fun/feed_forward/pallas_call | solution.py:928
  504.6 12.4 attention_forward.12
  517.0 14.1 %conv_forward.12 = (bf16[8,512,768]{2,1,0:T(8,128)(2,1)}, bf16[9,512,768]{2,1,0:T(8,128)(2,1)}, bf16[9,512,768]{2,1,0:T(8,128)(2,1)}, f32[9,512,128]{2,1,0:T(8,128)}) custom-call(s32[60]{0:T(128)S(1)} %get-tuple-element.243.rows_ref, s32[32]{0:T(128)S(1)} %get-tuple-element.244.counts_ref, ...), custom_call_target="tpu_custom_call", output_to_operand_aliasing={{0}: (7, {})} | custom-call | flops 5435817984 | bytes 37748736 | tf_op jit(solution)/shard_map/cond/branch_1_fun/conv_forward/pallas_call | solution.py:1279
  531.0 4.6 send_cotangent.6
  539.8 4.7 all-to-all-start.17
  544.6 28.4 %attention_backward.12 = (bf16[8,512,768]{2,1,0:T(8,128)(2,1)}, f32[8,768]{1,0:T(8,128)}, f32[768,2304]{1,0:T(8,128)}, f32[768,768]{1,0:T(8,128)}) custom-call(s32[60]{0:T(128)S(1)} %get-tuple-element.243.rows_ref, s32[32]{0:T(128)S(1)} %get-tuple-element.244.counts_ref, bf16[8,512,768]{2,1,0:T(8,128)(2,1)} %land_x.3.x_ref.x_ref1, ...), custom_call_target="tpu_custom_call" | custom-call | flops 19327352832 | bytes 41943040 | tf_op jit(solution)/shard_map/cond/branch_1_fun/attention_backward/pallas_call | solution.py:819
  573.0 23.4 %conv_backward.12 = (bf16[8,512,768]{2,1,0:T(8,128)(2,1)}, f32[24,768]{1,0:T(8,128)}, f32[3,768,768]{2,1,0:T(8,128)}) custom-call(s32[60]{0:T(128)S(1)} %get-tuple-element.243.rows_ref, s32[32]{0:T(128)S(1)} %get-tuple-element.244.counts_ref, bf16[8,512,768]{2,1,0:T(8,128)(2,1)} %land_x.3.x_ref.x_ref1, ...), custom_call_target="tpu_custom_call", output_to_operand_aliasing={{0}: (10, {})} | custom-call | flops 8153726976 | bytes 52428800 | tf_op jit(solution)/shard_map/cond/branch_1_fun/conv_backward/pallas_call | solution.py:1428
  596.5 19.7 %all-to-all-done.17.dy_ref0.dy_ref = bf16[8,512,768]{2,1,0:T(8,128)(2,1)} async-done(((bf16[8,512,768]{2,1,0:T(8,128)(2,1)}), bf16[8,512,768]{2,1,0:T(8,128)(2,1)}, u32[]{:S(2)}, u32[]{:S(2)}) %all-to-all-start.17) | async-done | bytes 6291488 | tf_op jit(solution)/shard_map/cond/branch_1_fun/all_to_all | solution.py:1640
  616.2 48.6 %feed_backward.6 = (f32[8,768]{1,0:T(8,128)}, bf16[8,512,768]{2,1,0:T(8,128)(2,1)}, bf16[8,512,768]{2,1,0:T(8,128)(2,1)}, bf16[4,1552,768]{2,1,0:T(8,128)(2,1)}) custom-call(s32[60]{0:T(128)S(1)} %get-tuple-element.243.rows_ref, s32[32]{0:T(128)S(1)} %get-tuple-element.244.counts_ref, ...), custom_call_target="tpu_custom_call", output_to_operand_aliasing={{2}: (13, {})} | custom-call | flops 25367150592 | bytes 52428800 | tf_op jit(solution)/shard_map/cond/branch_1_fun/feed_backward/pallas_call | solution.py:1157
  664.8 4.6 hop_dx.3
  669.4 10.2 all-to-all-start.19
  679.6 11.9 attention_backward.13
  692.7 36.9 %conv_backward.13 = (bf16[8,512,768]{2,1,0:T(8,128)(2,1)}, f32[24,768]{1,0:T(8,128)}, bf16[4,1376,768]{2,1,0:T(8,128)(2,1)}) custom-call(s32[60]{0:T(128)S(1)} %get-tuple-element.243.rows_ref, s32[32]{0:T(128)S(1)} %get-tuple-element.244.counts_ref, bf16[8,512,768]{2,1,0:T(8,128)(2,1)} %land_x.2.x_ref.x_ref0, ...), custom_call_target="tpu_custom_call", output_to_operand_aliasing={{2}: (11, {}), {0}: (12, {})} | custom-call | flops 8153726976 | bytes 52428800 | tf_op jit(solution)/shard_map/cond/branch_1_fun/conv_backward/pallas_call | solution.py:1428
  731.7 20.1 %all-to-all-done.19.refs_1_.refs_0_ = bf16[8,512,768]{2,1,0:T(8,128)(2,1)} async-done(((bf16[8,512,768]{2,1,0:T(8,128)(2,1)}), bf16[8,512,768]{2,1,0:T(8,128)(2,1)}, u32[]{:S(2)}, u32[]{:S(2)}) %all-to-all-start.19) | async-done | bytes 6291488 | tf_op jit(solution)/shard_map/cond/branch_1_fun/all_to_all | solution.py:1640
  755.3 76.9 %all_to_all.124.refs_1_ = bf16[8,512,768]{2,1,0:T(8,128)(2,1)} all-to-all(bf16[8,512,768]{2,1,0:T(8,128)(2,1)} %hop_dx.4), channel_id=1, replica_groups=mesh['dp'=4,'op'=8] {'op'}, dimensions={0} | all-to-all | bytes 12582912 | tf_op jit(solution)/shard_map/cond/branch_1_fun/all_to_all | solution.py:1640
  836.0 4.8 all-to-all-start.21
  840.8 4.7 land_dx.3.dy_ref.dy_ref1
  845.5 28.6 %attention_backward.14 = (bf16[8,512,768]{2,1,0:T(8,128)(2,1)}, f32[8,768]{1,0:T(8,128)}, f32[768,2304]{1,0:T(8,128)}, f32[768,768]{1,0:T(8,128)}) custom-call(s32[60]{0:T(128)S(1)} %get-tuple-element.243.rows_ref, s32[32]{0:T(128)S(1)} %get-tuple-element.244.counts_ref, bf16[8,512,768]{2,1,0:T(8,128)(2,1)} %get-tuple-element.247.x_ref.x_ref1, ...), custom_call_target="tpu_custom_call" | custom-call | flops 19327352832 | bytes 41943040 | tf_op jit(solution)/shard_map/cond/branch_1_fun/attention_backward/pallas_call | solution.py:819
  874.2 38.5 %conv_backward.14 = (bf16[8,512,768]{2,1,0:T(8,128)(2,1)}, f32[24,768]{1,0:T(8,128)}, f32[3,768,768]{2,1,0:T(8,128)}) custom-call(s32[60]{0:T(128)S(1)} %get-tuple-element.243.rows_ref, s32[32]{0:T(128)S(1)} %get-tuple-element.244.counts_ref, bf16[8,512,768]{2,1,0:T(8,128)(2,1)} %get-tuple-element.247.x_ref.x_ref1, ...), custom_call_target="tpu_custom_call", output_to_operand_aliasing={{0}: (10, {})} | custom-call | flops 8153726976 | bytes 52428800 | tf_op jit(solution)/shard_map/cond/branch_1_fun/conv_backward/pallas_call | solution.py:1428
  912.8 4.9 land_dx.2.refs_1_.dy_ref0.dy_ref
  917.7 42.8 %feed_backward.7 = (f32[8,768]{1,0:T(8,128)}, bf16[8,512,768]{2,1,0:T(8,128)(2,1)}, bf16[8,512,768]{2,1,0:T(8,128)(2,1)}, bf16[4,1552,768]{2,1,0:T(8,128)(2,1)}) custom-call(s32[60]{0:T(128)S(1)} %get-tuple-element.243.rows_ref, s32[32]{0:T(128)S(1)} %get-tuple-element.244.counts_ref, ...), custom_call_target="tpu_custom_call", output_to_operand_aliasing={{2}: (13, {})} | custom-call | flops 25367150592 | bytes 52428800 | tf_op jit(solution)/shard_map/cond/branch_1_fun/feed_backward/pallas_call | solution.py:1157
  960.6 10.5 all-to-all-start.22
  971.1 11.8 attention_backward.15
  984.1 32.2 %conv_backward.15 = (bf16[8,512,768]{2,1,0:T(8,128)(2,1)}, f32[24,768]{1,0:T(8,128)}, bf16[4,1376,768]{2,1,0:T(8,128)(2,1)}) custom-call(s32[60]{0:T(128)S(1)} %get-tuple-element.243.rows_ref, s32[32]{0:T(128)S(1)} %get-tuple-element.244.counts_ref, ...), custom_call_target="tpu_custom_call", output_to_operand_aliasing={{2}: (11, {}), {0}: (12, {})} | custom-call | flops 8153726976 | bytes 52428800 | tf_op jit(solution)/shard_map/cond/branch_1_fun/conv_backward/pallas_call | solution.py:1428
  1018.4 24.4 %all-to-all-done.22.refs_0_ = bf16[8,512,768]{2,1,0:T(8,128)(2,1)} async-done(((bf16[8,512,768]{2,1,0:T(8,128)(2,1)}), bf16[8,512,768]{2,1,0:T(8,128)(2,1)}, u32[]{:S(2)}, u32[]{:S(2)}) %all-to-all-start.22) | async-done | bytes 6291488 | tf_op jit(solution)/shard_map/cond/branch_1_fun/all_to_all | solution.py:1640
  1042.7 22.5 %all-to-all-start.23 = ((bf16[8,512,768]{2,1,0:T(8,128)(2,1)}), bf16[8,512,768]{2,1,0:T(8,128)(2,1)}, u32[]{:S(2)}, u32[]{:S(2)}) async-start(bf16[8,512,768]{2,1,0:T(8,128)(2,1)} %after.13), calls=%async_computation.27 | async-start | bytes 12582912 | tf_op jit(solution)/shard_map/cond/branch_1_fun/all_to_all | solution.py:1640
  1065.3 71.7 %all-to-all-done.23.refs_1_ = bf16[8,512,768]{2,1,0:T(8,128)(2,1)} async-done(((bf16[8,512,768]{2,1,0:T(8,128)(2,1)}), bf16[8,512,768]{2,1,0:T(8,128)(2,1)}, u32[]{:S(2)}, u32[]{:S(2)}) %all-to-all-start.23) | async-done | bytes 6291488 | tf_op jit(solution)/shard_map/cond/branch_1_fun/all_to_all | solution.py:1640
  1137.0 4.8 all-to-all-start.25
  1141.7 38.8 %reduce-scatter.19.cloned.1.call-done = bf16[1,1552,768]{2,1,0:T(8,128)(2,1)} async-done(((bf16[4,1552,768]{2,1,0:T(8,128)(2,1)}), bf16[1,1552,768]{2,1,0:T(8,128)(2,1)}) %reduce-scatter.19.cloned.1.call-update) | async-done | bytes 2383888 | tf_op jit(solution)/shard_map/cond/branch_1_fun/reduce_scatter | solution.py:1644
  1180.5 32.8 %all-to-all-done.25.refs_1_ = bf16[8,512,768]{2,1,0:T(8,128)(2,1)} async-done(((bf16[8,512,768]{2,1,0:T(8,128)(2,1)}), bf16[8,512,768]{2,1,0:T(8,128)(2,1)}, u32[]{:S(2)}, u32[]{:S(2)}) %all-to-all-start.25) | async-done | bytes 6291488 | tf_op jit(solution)/shard_map/cond/branch_1_fun/all_to_all | solution.py:1640
  1213.3 4.8 all-to-all-start.24
  1218.1 6.4 finish_rest.6
  1229.0 8.0 outputs.3.refs_6_
  1241.5 48.2 %all-to-all-done.24.refs_0_ = bf16[8,512,768]{2,1,0:T(8,128)(2,1)} async-done(((bf16[8,512,768]{2,1,0:T(8,128)(2,1)}), bf16[8,512,768]{2,1,0:T(8,128)(2,1)}, u32[]{:S(2)}, u32[]{:S(2)}) %all-to-all-start.24) | async-done | bytes 6291488 | tf_op jit(solution)/shard_map/cond/branch_1_fun/all_to_all | solution.py:1640
  1289.7 7.9 input_grad.3.refs_7_
  1297.6 31.6 %reduce-scatter.23.cloned.1.call-done = bf16[1,1376,768]{2,1,0:T(8,128)(2,1)} async-done(((bf16[4,1376,768]{2,1,0:T(8,128)(2,1)}), bf16[1,1376,768]{2,1,0:T(8,128)(2,1)}) %reduce-scatter.23.cloned.1.call-update) | async-done | bytes 2113552 | tf_op jit(solution)/shard_map/cond/branch_1_fun/reduce_scatter | solution.py:1644
  1329.2 6.3 finish_rest.7
  (135 shorter events, 54.0 us)
Async XLA Ops:
  12.4 9.8 all-to-all-start.26
  22.2 4.8 copy-start.39
  22.2 102.1 %all-to-all-start.27 = ((bf16[8,512,768]{2,1,0:T(8,128)(2,1)}), bf16[8,512,768]{2,1,0:T(8,128)(2,1)}, u32[]{:S(2)}, u32[]{:S(2)}) async-start(bf16[8,512,768]{2,1,0:T(8,128)(2,1)} %send_inputs.2), calls=%async_computation.35 | async-start | bytes 12582912 | tf_op jit(solution)/shard_map/all_to_all | solution.py:1640
  119.1 0.5 copy-start.20
  124.2 4.8 copy-start.22
  124.2 29.1 %copy-start.23 = (bf16[2,1,5,768]{3,0,2,1:T(2,128)(2,1)S(1)}, bf16[2,1,5,768]{3,0,2,1:T(2,128)(2,1)}, u32[]{:S(2)}) copy-start(bf16[2,1,5,768]{3,0,2,1:T(2,128)(2,1)} %param.22) | copy-start | bytes 46084
  124.2 29.2 %copy-start.14 = (bf16[2,1,15,768]{3,0,2,1:T(2,128)(2,1)S(1)}, bf16[2,1,15,768]{3,0,2,1:T(2,128)(2,1)}, u32[]{:S(2)}) copy-start(bf16[2,1,15,768]{3,0,2,1:T(2,128)(2,1)} %param.19) | copy-start | bytes 138244
  124.2 85.5 %all-to-all-start.28 = ((bf16[8,512,768]{2,1,0:T(8,128)(2,1)}), bf16[8,512,768]{2,1,0:T(8,128)(2,1)}, u32[]{:S(2)}, u32[]{:S(2)}) async-start(bf16[8,512,768]{2,1,0:T(8,128)(2,1)} %send_inputs.3), calls=%async_computation.36 | async-start | bytes 12582912 | tf_op jit(solution)/shard_map/all_to_all | solution.py:1640
  191.5 18.3 %copy-start.21 = (s32[80]{0:T(128)S(1)}, s32[80]{0:T(128)}, u32[]{:S(2)}) copy-start(s32[80]{0:T(128)} %copy-done.20) | copy-start | bytes 964
  217.2 36.9 %copy-start.8 = (f32[16,768]{1,0:T(8,128)}, f32[16,768]{1,0:T(8,128)S(1)}, u32[]{:S(2)}) copy-start(f32[16,768]{1,0:T(8,128)S(1)} %get-tuple-element.249.taps_ref) | copy-start | bytes 147460 | tf_op jit(solution)/shard_map/cond
  217.2 36.9 %copy-start.12 = (f32[8,768]{1,0:T(8,128)}, f32[8,768]{1,0:T(8,128)S(1)}, u32[]{:S(2)}) copy-start(f32[8,768]{1,0:T(8,128)S(1)} %get-tuple-element.250.gain) | copy-start | bytes 73732 | tf_op jit(solution)/shard_map/cond
  217.2 313.8 %copy-start.26 = (s32[32]{0:T(128)}, s32[32]{0:T(128)S(1)}, u32[]{:S(2)}) copy-start(s32[32]{0:T(128)S(1)} %get-tuple-element.242.table_ref) | copy-start | bytes 388 | tf_op jit(solution)/shard_map/cond
  221.8 80.1 %all-to-all-start.14 = ((bf16[8,512,768]{2,1,0:T(8,128)(2,1)}), bf16[8,512,768]{2,1,0:T(8,128)(2,1)}, u32[]{:S(2)}, u32[]{:S(2)}) async-start(bf16[8,512,768]{2,1,0:T(8,128)(2,1)} %hop_x.3), calls=%async_computation.18 | async-start | bytes 12582912 | tf_op jit(solution)/shard_map/cond/branch_1_fun/all_to_all | solution.py:1640
  240.9 13.2 copy-start.2
  386.6 76.5 %all-to-all-start.16 = ((bf16[8,512,768]{2,1,0:T(8,128)(2,1)}), bf16[8,512,768]{2,1,0:T(8,128)(2,1)}, u32[]{:S(2)}, u32[]{:S(2)}) async-start(bf16[8,512,768]{2,1,0:T(8,128)(2,1)} %hop_x.5), calls=%async_computation.20 | async-start | bytes 12582912 | tf_op jit(solution)/shard_map/cond/branch_1_fun/all_to_all | solution.py:1640
  396.1 10.9 copy-start.41
  463.2 76.6 %all-to-all-start.18 = ((bf16[8,512,768]{2,1,0:T(8,128)(2,1)}), bf16[8,512,768]{2,1,0:T(8,128)(2,1)}, u32[]{:S(2)}, u32[]{:S(2)}) async-start(bf16[8,512,768]{2,1,0:T(8,128)(2,1)} %send_cotangent.7), calls=%async_computation.22 | async-start | bytes 12582912 | tf_op jit(solution)/shard_map/cond/branch_1_fun/all_to_all | solution.py:1640
  539.8 76.3 %all-to-all-start.17 = ((bf16[8,512,768]{2,1,0:T(8,128)(2,1)}), bf16[8,512,768]{2,1,0:T(8,128)(2,1)}, u32[]{:S(2)}, u32[]{:S(2)}) async-start(bf16[8,512,768]{2,1,0:T(8,128)(2,1)} %send_cotangent.6), calls=%async_computation.21 | async-start | bytes 12582912 | tf_op jit(solution)/shard_map/cond/branch_1_fun/all_to_all | solution.py:1640
  544.6 373.1 %reduce-scatter.17.cloned.1.call-start = ((), (), s32[]{:S(2)}) async-start(), calls=%async_computation.41 | async-start | bytes 11919360 | tf_op jit(solution)/shard_map/cond/branch_1_fun/reduce_scatter | solution.py:1644
  669.4 82.4 %all-to-all-start.19 = ((bf16[8,512,768]{2,1,0:T(8,128)(2,1)}), bf16[8,512,768]{2,1,0:T(8,128)(2,1)}, u32[]{:S(2)}, u32[]{:S(2)}) async-start(bf16[8,512,768]{2,1,0:T(8,128)(2,1)} %hop_dx.3), calls=%async_computation.23 | async-start | bytes 12582912 | tf_op jit(solution)/shard_map/cond/branch_1_fun/all_to_all | solution.py:1640
  679.5 385.7 %reduce-scatter.21.cloned.1.call-start = ((), (), s32[]{:S(2)}) async-start(), calls=%async_computation.43 | async-start | bytes 10567680 | tf_op jit(solution)/shard_map/cond/branch_1_fun/reduce_scatter | solution.py:1644
  679.6 11.9 copy-start.33
  679.6 12.9 copy-start.29
  692.7 36.9 %copy-start.16 = (f32[24,768]{1,0:T(8,128)S(1)}, f32[24,768]{1,0:T(8,128)}, u32[]{:S(2)}) copy-start(f32[24,768]{1,0:T(8,128)} %get-tuple-element.337) | copy-start | bytes 221188 | tf_op jit(solution)/shard_map/cond
  836.0 76.8 %all-to-all-start.21 = ((bf16[8,512,768]{2,1,0:T(8,128)(2,1)}), bf16[8,512,768]{2,1,0:T(8,128)(2,1)}, u32[]{:S(2)}, u32[]{:S(2)}) async-start(bf16[8,512,768]{2,1,0:T(8,128)(2,1)} %hop_dx.5), calls=%async_computation.25 | async-start | bytes 12582912 | tf_op jit(solution)/shard_map/cond/branch_1_fun/all_to_all | solution.py:1640
  840.7 4.8 copy-start.13
  840.8 339.7 %reduce-scatter.19.cloned.1.call-start = ((), (), s32[]{:S(2)}) async-start(), calls=%async_computation.42 | async-start | bytes 11919360 | tf_op jit(solution)/shard_map/cond/branch_1_fun/reduce_scatter | solution.py:1644
  845.5 28.7 %copy-start.9 = (f32[16,768]{1,0:T(8,128)S(1)}, f32[16,768]{1,0:T(8,128)}, u32[]{:S(2)}) copy-start(f32[16,768]{1,0:T(8,128)} %copy-done.8) | copy-start | bytes 147460 | tf_op jit(solution)/shard_map/cond
  912.8 4.9 copy-start.3
  960.6 10.5 copy-start.43
  960.6 82.2 %all-to-all-start.22 = ((bf16[8,512,768]{2,1,0:T(8,128)(2,1)}), bf16[8,512,768]{2,1,0:T(8,128)(2,1)}, u32[]{:S(2)}, u32[]{:S(2)}) async-start(bf16[8,512,768]{2,1,0:T(8,128)(2,1)} %after.12), calls=%async_computation.26 | async-start | bytes 12582912 | tf_op jit(solution)/shard_map/cond/branch_1_fun/all_to_all | solution.py:1640
  971.1 358.2 %reduce-scatter.23.cloned.1.call-start = ((), (), s32[]{:S(2)}) async-start(), calls=%async_computation.44 | async-start | bytes 10567680 | tf_op jit(solution)/shard_map/cond/branch_1_fun/reduce_scatter | solution.py:1644
  971.1 11.8 copy-start.34
  971.1 12.8 copy-start.31
  971.1 13.0 copy-start.5
  984.1 32.2 %copy-start.17 = (f32[24,768]{1,0:T(8,128)S(1)}, f32[24,768]{1,0:T(8,128)}, u32[]{:S(2)}) copy-start(f32[24,768]{1,0:T(8,128)} %get-tuple-element.343) | copy-start | bytes 221188 | tf_op jit(solution)/shard_map/cond
  1042.7 94.2 %all-to-all-start.23 = ((bf16[8,512,768]{2,1,0:T(8,128)(2,1)}), bf16[8,512,768]{2,1,0:T(8,128)(2,1)}, u32[]{:S(2)}, u32[]{:S(2)}) async-start(bf16[8,512,768]{2,1,0:T(8,128)(2,1)} %after.13), calls=%async_computation.27 | async-start | bytes 12582912 | tf_op jit(solution)/shard_map/cond/branch_1_fun/all_to_all | solution.py:1640
  1137.0 76.4 %all-to-all-start.25 = ((bf16[8,512,768]{2,1,0:T(8,128)(2,1)}), bf16[8,512,768]{2,1,0:T(8,128)(2,1)}, u32[]{:S(2)}, u32[]{:S(2)}) async-start(bf16[8,512,768]{2,1,0:T(8,128)(2,1)} %after.15), calls=%async_computation.32 | async-start | bytes 12582912 | tf_op jit(solution)/shard_map/cond/branch_1_fun/all_to_all | solution.py:1640
  1213.3 76.4 %all-to-all-start.24 = ((bf16[8,512,768]{2,1,0:T(8,128)(2,1)}), bf16[8,512,768]{2,1,0:T(8,128)(2,1)}, u32[]{:S(2)}, u32[]{:S(2)}) async-start(bf16[8,512,768]{2,1,0:T(8,128)(2,1)} %after.14), calls=%async_computation.30 | async-start | bytes 12582912 | tf_op jit(solution)/shard_map/cond/branch_1_fun/all_to_all | solution.py:1640
  1218.1 10.9 copy-start.27
Sparse Core Ops, SparseCore 0:
  664.9 183.3 reduce-scatter.16
  851.3 146.3 reduce-scatter.20
  1000.2 180.2 reduce-scatter.18
  1182.8 146.3 reduce-scatter.22

commit v6 on v5

--- a/solution.py
+++ b/solution.py
@@ -1665,8 +1665,14 @@
     weights = (attn_qkv, attn_out, ffn_up, ffn_down, conv_point)
     smalls = [small_params(b, conv_taps, norm_gain, norm_bias) for b in range(BLOCKS)]
     send, relay, tags = home_tables(candidate.reshape(-1), owners, seqs)
-    arrived = exchange(tags.reshape(owners, BLOCKS * HALVES))
-    tables = owner_tables(arrived.reshape(-1), owners)
+    marks = BLOCKS * HALVES
+    told = jnp.concatenate(
+        [tags.reshape(owners, marks), jnp.broadcast_to(candidate.reshape(1, -1), (owners, BLOCKS * seqs))],
+        axis=1,
+    )
+    told = exchange(told)
+    everyone = told[:, marks:].reshape(-1)
+    tables = owner_tables(told[:, :marks].reshape(-1), owners)
     both = range(HALVES)
 
     def start(b, half):
@@ -1675,23 +1681,23 @@
     me = lax.axis_index("op").astype(jnp.int32)[None]
     routed = owners < seqs
     if routed:
-        everyone = lax.all_gather(candidate, "op", axis=0, tiled=True)
-        route, lost = route_tables(everyone.reshape(-1), me, owners, seqs)
-        lost = lax.psum(lost[0], "dp")
+        route, lost = route_tables(everyone, me, owners, seqs)
+        lost = lax.psum(lost, "dp")
 
     x0 = [
         exchange(
-            move_rows(send, [start(0, h)], [inputs], owners, False, "send_inputs", (route,) * h if routed else ())
+            move_rows(send, [start(0, h)], [inputs], owners, False, "send_inputs", (lost,) * h if routed else ())
         )
         for h in both
     ]
     first = owner_forward(0, 0, tables, x0[0], weights, smalls[0], None)
+    leaving = bring_rows(route, 0, [first[0]], "hop_x") if routed else None
 
     def on_the_way(table, sources, name):
         return bring_rows(route, table * owners, sources, name)
 
     def straight_there(y):
-        hop0 = exchange(on_the_way(0, [y[0]], "hop_x"))
+        hop0 = exchange(leaving)
         hop1 = exchange(on_the_way(1, [hop0, y[1]], "hop_x"))
         hop2 = exchange(on_the_way(2, [y[1], hop1], "hop_x"))
         return [on_the_way(3, [hop0, hop1], "land_x"), on_the_way(4, [hop2], "land_x")]
@@ -1777,7 +1783,7 @@
     if not routed:
         return after_first(home_there, home_back, x0, first)
     return lax.cond(
-        lost == 0,
+        lost[0] == 0,
         lambda x0, first: after_first(straight_there, straight_back, x0, first),
         lambda x0, first: after_first(home_there, home_back, x0, first),
         x0,

time: 1360 us -> 1320 us (0.971)
  the two profiles are of different devices: /device:TPU:0 before, /device:TPU:24 now
where the time goes in v6:
time: 1320 us; the launch traced here: 1310 us
  Pallas kernels  693 us (52%)
  waiting for transfers between devices  319 us (24%)
  blocking collectives  170 us (13%)
  starting transfers between devices  88.6 us (7%)
  between operations  14.9 us (1%)
    all_to_all x13, waiting for transfers between devices, exchange(): return lax.all_to_all(rows, 'op', split_axis=0, concat_axis=0, tiled=True)  319 us
    all_to_all x2, blocking collectives, exchange(): return lax.all_to_all(rows, 'op', split_axis=0, concat_axis=0, tiled=True)  164 us
    pallas_call x4, Pallas kernels, conv_backward(): pl.pallas_call(kernel, grid_spec=pltpu.PrefetchScalarGridSpec(num_scalar_...  117 us
    pallas_call x4, Pallas kernels, attention_backward(): pl.pallas_call(kernel, grid_spec=pltpu.PrefetchScalarGridSpec(num_scalar_...  116 us
    pallas_call x4, Pallas kernels, feed_forward(): pl.pallas_call(kernel, grid_spec=pltpu.PrefetchScalarGridSpec(num_scalar_...  98.6 us
    pallas_call x2, Pallas kernels, feed_backward(): pl.pallas_call(kernel, grid_spec=pltpu.PrefetchScalarGridSpec(num_scalar_...  96.7 us
    all_to_all x13, starting transfers between devices, exchange(): return lax.all_to_all(rows, 'op', split_axis=0, concat_axis=0, tiled=True)  88.4 us
    pallas_call x4, Pallas kernels, conv_forward(): pl.pallas_call(kernel, grid_spec=pltpu.PrefetchScalarGridSpec(num_scalar_...  66.5 us
  transfers between devices with their start and end apart: 17, of which 11 were waited for; matrix products, arithmetic and copies ran while one was open for 1% of the time, Pallas kernels for 48%

profile of v6, /device:TPU:24, one launch (start us, length us, event | category | flops | bytes accessed | tf_op | source)
XLA Modules:
  0.0 1308.6 jit_solution(1144313728658631164)
XLA Ops:
  21.5 4.8 all-to-all-start.27
  27.0 41.2 %route_tables.1 = (s32[80]{0:T(128)S(1)}, s32[1]{0:T(128)}) custom-call(s32[192]{0:T(256)} %reshape.114.refs_0_, s32[1]{0:T(128)} %bitcast.14.refs_1_), custom_call_target="tpu_custom_call" | custom-call | tf_op jit(solution)/shard_map/route_tables/pallas_call | solution.py:372
  68.2 6.3 psum.7.refs_1_
  74.5 5.2 send_inputs.3
  79.7 18.2 %all-to-all-done.27.x_ref = bf16[8,512,768]{2,1,0:T(8,128)(2,1)} async-done(((bf16[8,512,768]{2,1,0:T(8,128)(2,1)}), bf16[8,512,768]{2,1,0:T(8,128)(2,1)}, u32[]{:S(2)}, u32[]{:S(2)}) %all-to-all-start.27) | async-done | bytes 6291488 | tf_op jit(solution)/shard_map/all_to_all | solution.py:1640
  97.9 4.8 all-to-all-start.28
  106.1 28.8 %feed_forward.13 = (bf16[8,512,768]{2,1,0:T(8,128)(2,1)}, bf16[4,512,3072]{2,1,0:T(8,128)(2,1)}, bf16[4,512,3072]{2,1,0:T(8,128)(2,1)}, bf16[4,512,768]{2,1,0:T(8,128)(2,1)S(1)}, f32[4,512,128]{2,1,0:T(8,128)}) custom-call(s32[60]{0:T(128)S(1)} %get-tuple-element.397.rows_ref, s32[32]{0:T(128)S(1)} %get-tuple-element.398.counts_ref, ...), custom_call_target="tpu_custom_call" | custom-call | flops 14495514624 | bytes 41943040 | tf_op jit(solution)/shard_map/feed_forward/pallas_call | solution.py:928
  134.9 5.6 attention_forward.13
  140.5 18.1 %conv_forward.13 = (bf16[8,512,768]{2,1,0:T(8,128)(2,1)}, bf16[9,512,768]{2,1,0:T(8,128)(2,1)}, bf16[9,512,768]{2,1,0:T(8,128)(2,1)}, f32[9,512,128]{2,1,0:T(8,128)}) custom-call(s32[60]{0:T(128)S(1)} %get-tuple-element.397.rows_ref, s32[32]{0:T(128)S(1)} %get-tuple-element.398.counts_ref, ...), custom_call_target="tpu_custom_call", output_to_operand_aliasing={{0}: (7, {})} | custom-call | flops 5435817984 | bytes 37748736 | tf_op jit(solution)/shard_map/conv_forward/pallas_call | solution.py:1279
  163.2 11.1 all-to-all-done.28
  174.3 1123.5 %conditional.1 = (f32[2,1,192,2304]{3,2,1,0:T(8,128)}, f32[2,1,192,768]{3,2,1,0:T(8,128)}, f32[2,1,192,3072]{3,2,1,0:T(8,128)}, f32[2,1,768,768]{3,2,1,0:T(8,128...) conditional(s32[]{:T(128)} %bitcast.15, ...), branch_computations={%region_1.6_spmd, %region_6.11_spmd} | conditional | flops 278434742272 | bytes 1437307136 | solution.py:1785
  181.6 4.8 all-to-all-start.14
  186.4 20.1 %feed_forward.10 = (bf16[8,512,768]{2,1,0:T(8,128)(2,1)}, bf16[4,512,3072]{2,1,0:T(8,128)(2,1)}, bf16[4,512,3072]{2,1,0:T(8,128)(2,1)}, bf16[4,512,768]{2,1,0:T(8,128)(2,1)S(1)}, f32[4,512,128]{2,1,0:T(8,128)}) custom-call(s32[60]{0:T(128)S(1)} %get-tuple-element.243.rows_ref, ...), custom_call_target="tpu_custom_call", output_to_operand_aliasing={{1}: (7, {}), {2}: (8, {}), {3}: (9, {}), {4}: (10, {})} | custom-call | flops 14495514624 | bytes 41943040 | tf_op jit(solution)/shard_map/cond/branch_1_fun/feed_forward/pallas_call | solution.py:928
  206.6 27.4 %attention_forward.10 = (bf16[8,512,768]{2,1,0:T(8,128)(2,1)}, bf16[3,512,2304]{2,1,0:T(8,128)(2,1)}, bf16[3,512,768]{2,1,0:T(8,128)(2,1)}, bf16[3,512,768]{2,1,0:T(8,128)(2,1)}, f32[3,512,128]{2,1,0:T(8,128)}) custom-call(s32[60]{0:T(128)S(1)} %get-tuple-element.243.rows_ref, s32[32]{0:T(128)S(1)} %get-tuple-element.244.counts_ref, ...), custom_call_target="tpu_custom_call", output_to_operand_aliasing={{0}: (7, {})} | custom-call | flops 19327352832 | bytes 31457280 | tf_op jit(solution)/shard_map/cond/branch_1_fun/attention_forward/pallas_call | solution.py:628
  234.0 14.1 %conv_forward.10 = (bf16[8,512,768]{2,1,0:T(8,128)(2,1)}, bf16[9,512,768]{2,1,0:T(8,128)(2,1)}, bf16[9,512,768]{2,1,0:T(8,128)(2,1)}, f32[9,512,128]{2,1,0:T(8,128)}) custom-call(s32[60]{0:T(128)S(1)} %get-tuple-element.243.rows_ref, s32[32]{0:T(128)S(1)} %get-tuple-element.244.counts_ref, ...), custom_call_target="tpu_custom_call", output_to_operand_aliasing={{0}: (7, {})} | custom-call | flops 5435817984 | bytes 37748736 | tf_op jit(solution)/shard_map/cond/branch_1_fun/conv_forward/pallas_call | solution.py:1279
  248.1 10.0 all-to-all-done.14.refs_0_
  261.8 76.9 %all_to_all.126.refs_1_ = bf16[8,512,768]{2,1,0:T(8,128)(2,1)} all-to-all(bf16[8,512,768]{2,1,0:T(8,128)(2,1)} %hop_x.3), channel_id=1, replica_groups=mesh['dp'=4,'op'=8] {'op'}, dimensions={0} | all-to-all | bytes 12582912 | tf_op jit(solution)/shard_map/cond/branch_1_fun/all_to_all | solution.py:1640
  338.6 5.4 hop_x.4
  344.0 4.9 all-to-all-start.16
  349.0 4.6 land_x.2.x_ref.x_ref0
  353.6 29.3 %feed_forward.11 = (bf16[8,512,768]{2,1,0:T(8,128)(2,1)}, bf16[4,512,3072]{2,1,0:T(8,128)(2,1)}, bf16[4,512,3072]{2,1,0:T(8,128)(2,1)}, bf16[4,512,768]{2,1,0:T(8,128)(2,1)}, f32[4,512,128]{2,1,0:T(8,128)}) custom-call(s32[60]{0:T(128)S(1)} %get-tuple-element.243.rows_ref, s32[32]{0:T(128)S(1)} %get-tuple-element.244.counts_ref, ...), custom_call_target="tpu_custom_call" | custom-call | flops 14495514624 | bytes 41943040 | tf_op jit(solution)/shard_map/cond/branch_1_fun/feed_forward/pallas_call | solution.py:928
  382.9 12.4 attention_forward.11
  395.3 15.3 %conv_forward.11 = (bf16[8,512,768]{2,1,0:T(8,128)(2,1)}, bf16[9,512,768]{2,1,0:T(8,128)(2,1)}, bf16[9,512,768]{2,1,0:T(8,128)(2,1)}, f32[9,512,128]{2,1,0:T(8,128)}) custom-call(s32[60]{0:T(128)S(1)} %get-tuple-element.243.rows_ref, s32[32]{0:T(128)S(1)} %get-tuple-element.244.counts_ref, ...), custom_call_target="tpu_custom_call", output_to_operand_aliasing={{0}: (7, {})} | custom-call | flops 5435817984 | bytes 37748736 | tf_op jit(solution)/shard_map/cond/branch_1_fun/conv_forward/pallas_call | solution.py:1279
  410.6 4.6 send_cotangent.7
  415.2 5.4 all-to-all-done.16.refs_0_
  420.6 5.0 all-to-all-start.18
  430.2 20.4 %feed_forward.12 = (bf16[8,512,768]{2,1,0:T(8,128)(2,1)}, bf16[4,512,3072]{2,1,0:T(8,128)(2,1)}, bf16[4,512,3072]{2,1,0:T(8,128)(2,1)}, bf16[4,512,768]{2,1,0:T(8,128)(2,1)}, f32[4,512,128]{2,1,0:T(8,128)}) custom-call(s32[60]{0:T(128)S(1)} %get-tuple-element.243.rows_ref, ...), custom_call_target="tpu_custom_call", output_to_operand_aliasing={{1}: (7, {}), {2}: (8, {}), {3}: (9, {}), {4}: (10, {})} | custom-call | flops 14495514624 | bytes 41943040 | tf_op jit(solution)/shard_map/cond/branch_1_fun/feed_forward/pallas_call | solution.py:928
  450.6 5.1 attention_forward.12
  455.7 19.0 %conv_forward.12 = (bf16[8,512,768]{2,1,0:T(8,128)(2,1)}, bf16[9,512,768]{2,1,0:T(8,128)(2,1)}, bf16[9,512,768]{2,1,0:T(8,128)(2,1)}, f32[9,512,128]{2,1,0:T(8,128)}) custom-call(s32[60]{0:T(128)S(1)} %get-tuple-element.243.rows_ref, s32[32]{0:T(128)S(1)} %get-tuple-element.244.counts_ref, ...), custom_call_target="tpu_custom_call", output_to_operand_aliasing={{0}: (7, {})} | custom-call | flops 5435817984 | bytes 37748736 | tf_op jit(solution)/shard_map/cond/branch_1_fun/conv_forward/pallas_call | solution.py:1279
  474.7 4.6 send_cotangent.6
  479.3 18.0 %all-to-all-done.18.dy_ref.dy_ref1 = bf16[8,512,768]{2,1,0:T(8,128)(2,1)} async-done(((bf16[8,512,768]{2,1,0:T(8,128)(2,1)}), bf16[8,512,768]{2,1,0:T(8,128)(2,1)}, u32[]{:S(2)}, u32[]{:S(2)}) %all-to-all-start.18) | async-done | bytes 6291488 | tf_op jit(solution)/shard_map/cond/branch_1_fun/all_to_all | solution.py:1640
  497.2 4.8 all-to-all-start.17
  502.1 10.9 attention_backward.12
  513.0 34.1 %conv_backward.12 = (bf16[8,512,768]{2,1,0:T(8,128)(2,1)}, f32[24,768]{1,0:T(8,128)}, f32[3,768,768]{2,1,0:T(8,128)}) custom-call(s32[60]{0:T(128)S(1)} %get-tuple-element.243.rows_ref, s32[32]{0:T(128)S(1)} %get-tuple-element.244.counts_ref, bf16[8,512,768]{2,1,0:T(8,128)(2,1)} %land_x.3.x_ref.x_ref1, ...), custom_call_target="tpu_custom_call", output_to_operand_aliasing={{0}: (10, {})} | custom-call | flops 8153726976 | bytes 52428800 | tf_op jit(solution)/shard_map/cond/branch_1_fun/conv_backward/pallas_call | solution.py:1428
  547.1 26.5 %all-to-all-done.17.dy_ref0.dy_ref = bf16[8,512,768]{2,1,0:T(8,128)(2,1)} async-done(((bf16[8,512,768]{2,1,0:T(8,128)(2,1)}), bf16[8,512,768]{2,1,0:T(8,128)(2,1)}, u32[]{:S(2)}, u32[]{:S(2)}) %all-to-all-start.17) | async-done | bytes 6291488 | tf_op jit(solution)/shard_map/cond/branch_1_fun/all_to_all | solution.py:1640
  573.6 48.6 %feed_backward.6 = (f32[8,768]{1,0:T(8,128)}, bf16[8,512,768]{2,1,0:T(8,128)(2,1)}, bf16[8,512,768]{2,1,0:T(8,128)(2,1)}, bf16[4,1552,768]{2,1,0:T(8,128)(2,1)}) custom-call(s32[60]{0:T(128)S(1)} %get-tuple-element.243.rows_ref, s32[32]{0:T(128)S(1)} %get-tuple-element.244.counts_ref, ...), custom_call_target="tpu_custom_call", output_to_operand_aliasing={{2}: (13, {})} | custom-call | flops 25367150592 | bytes 52428800 | tf_op jit(solution)/shard_map/cond/branch_1_fun/feed_backward/pallas_call | solution.py:1157
  622.2 4.6 hop_dx.3
  626.8 4.7 all-to-all-start.19
  631.6 27.0 %attention_backward.13 = (bf16[8,512,768]{2,1,0:T(8,128)(2,1)}, f32[8,768]{1,0:T(8,128)}, bf16[4,1376,768]{2,1,0:T(8,128)(2,1)}) custom-call(s32[60]{0:T(128)S(1)} %get-tuple-element.243.rows_ref, s32[32]{0:T(128)S(1)} %get-tuple-element.244.counts_ref, bf16[8,512,768]{2,1,0:T(8,128)(2,1)} %land_x.2.x_ref.x_ref0, ...), custom_call_target="tpu_custom_call", output_to_operand_aliasing={{0}: (13, {})} | custom-call | flops 19327352832 | bytes 41943040 | tf_op jit(solution)/shard_map/cond/branch_1_fun/attention_backward/pallas_call | solution.py:819
  659.8 26.3 %conv_backward.13 = (bf16[8,512,768]{2,1,0:T(8,128)(2,1)}, f32[24,768]{1,0:T(8,128)}, bf16[4,1376,768]{2,1,0:T(8,128)(2,1)}) custom-call(s32[60]{0:T(128)S(1)} %get-tuple-element.243.rows_ref, s32[32]{0:T(128)S(1)} %get-tuple-element.244.counts_ref, bf16[8,512,768]{2,1,0:T(8,128)(2,1)} %land_x.2.x_ref.x_ref0, ...), custom_call_target="tpu_custom_call", output_to_operand_aliasing={{2}: (11, {}), {0}: (12, {})} | custom-call | flops 8153726976 | bytes 52428800 | tf_op jit(solution)/shard_map/cond/branch_1_fun/conv_backward/pallas_call | solution.py:1428
  688.2 14.9 %all-to-all-done.19.refs_1_.refs_0_ = bf16[8,512,768]{2,1,0:T(8,128)(2,1)} async-done(((bf16[8,512,768]{2,1,0:T(8,128)(2,1)}), bf16[8,512,768]{2,1,0:T(8,128)(2,1)}, u32[]{:S(2)}, u32[]{:S(2)}) %all-to-all-start.19) | async-done | bytes 6291488 | tf_op jit(solution)/shard_map/cond/branch_1_fun/all_to_all | solution.py:1640
  703.1 4.6 hop_dx.4
  707.7 86.8 %all_to_all.127.refs_1_ = bf16[8,512,768]{2,1,0:T(8,128)(2,1)} all-to-all(bf16[8,512,768]{2,1,0:T(8,128)(2,1)} %hop_dx.4), channel_id=1, replica_groups=mesh['dp'=4,'op'=8] {'op'}, dimensions={0} | all-to-all | bytes 12582912 | tf_op jit(solution)/shard_map/cond/branch_1_fun/all_to_all | solution.py:1640
  794.6 4.6 hop_dx.5
  799.2 4.8 all-to-all-start.21
  804.1 4.6 land_dx.3.dy_ref.dy_ref1
  808.6 65.2 %attention_backward.14 = (bf16[8,512,768]{2,1,0:T(8,128)(2,1)}, f32[8,768]{1,0:T(8,128)}, f32[768,2304]{1,0:T(8,128)}, f32[768,768]{1,0:T(8,128)}) custom-call(s32[60]{0:T(128)S(1)} %get-tuple-element.243.rows_ref, s32[32]{0:T(128)S(1)} %get-tuple-element.244.counts_ref, bf16[8,512,768]{2,1,0:T(8,128)(2,1)} %get-tuple-element.247.x_ref.x_ref1, ...), custom_call_target="tpu_custom_call" | custom-call | flops 19327352832 | bytes 41943040 | tf_op jit(solution)/shard_map/cond/branch_1_fun/attention_backward/pallas_call | solution.py:819
  873.9 23.6 %conv_backward.14 = (bf16[8,512,768]{2,1,0:T(8,128)(2,1)}, f32[24,768]{1,0:T(8,128)}, f32[3,768,768]{2,1,0:T(8,128)}) custom-call(s32[60]{0:T(128)S(1)} %get-tuple-element.243.rows_ref, s32[32]{0:T(128)S(1)} %get-tuple-element.244.counts_ref, bf16[8,512,768]{2,1,0:T(8,128)(2,1)} %get-tuple-element.247.x_ref.x_ref1, ...), custom_call_target="tpu_custom_call", output_to_operand_aliasing={{0}: (10, {})} | custom-call | flops 8153726976 | bytes 52428800 | tf_op jit(solution)/shard_map/cond/branch_1_fun/conv_backward/pallas_call | solution.py:1428
  897.5 4.8 land_dx.2.refs_1_.dy_ref0.dy_ref
  902.4 48.2 %feed_backward.7 = (f32[8,768]{1,0:T(8,128)}, bf16[8,512,768]{2,1,0:T(8,128)(2,1)}, bf16[8,512,768]{2,1,0:T(8,128)(2,1)}, bf16[4,1552,768]{2,1,0:T(8,128)(2,1)}) custom-call(s32[60]{0:T(128)S(1)} %get-tuple-element.243.rows_ref, s32[32]{0:T(128)S(1)} %get-tuple-element.244.counts_ref, ...), custom_call_target="tpu_custom_call", output_to_operand_aliasing={{2}: (13, {})} | custom-call | flops 25367150592 | bytes 52428800 | tf_op jit(solution)/shard_map/cond/branch_1_fun/feed_backward/pallas_call | solution.py:1157
  950.6 4.9 all-to-all-start.22
  955.6 12.7 attention_backward.15
  969.4 32.5 %conv_backward.15 = (bf16[8,512,768]{2,1,0:T(8,128)(2,1)}, f32[24,768]{1,0:T(8,128)}, bf16[4,1376,768]{2,1,0:T(8,128)(2,1)}) custom-call(s32[60]{0:T(128)S(1)} %get-tuple-element.243.rows_ref, s32[32]{0:T(128)S(1)} %get-tuple-element.244.counts_ref, ...), custom_call_target="tpu_custom_call", output_to_operand_aliasing={{2}: (11, {}), {0}: (12, {})} | custom-call | flops 8153726976 | bytes 52428800 | tf_op jit(solution)/shard_map/cond/branch_1_fun/conv_backward/pallas_call | solution.py:1428
  1004.1 23.0 %all-to-all-done.22.refs_0_ = bf16[8,512,768]{2,1,0:T(8,128)(2,1)} async-done(((bf16[8,512,768]{2,1,0:T(8,128)(2,1)}), bf16[8,512,768]{2,1,0:T(8,128)(2,1)}, u32[]{:S(2)}, u32[]{:S(2)}) %all-to-all-start.22) | async-done | bytes 6291488 | tf_op jit(solution)/shard_map/cond/branch_1_fun/all_to_all | solution.py:1640
  1027.1 31.6 %all-to-all-start.23 = ((bf16[8,512,768]{2,1,0:T(8,128)(2,1)}), bf16[8,512,768]{2,1,0:T(8,128)(2,1)}, u32[]{:S(2)}, u32[]{:S(2)}) async-start(bf16[8,512,768]{2,1,0:T(8,128)(2,1)} %after.13), calls=%async_computation.27 | async-start | bytes 12582912 | tf_op jit(solution)/shard_map/cond/branch_1_fun/all_to_all | solution.py:1640
  1058.8 71.7 %all-to-all-done.23.refs_1_ = bf16[8,512,768]{2,1,0:T(8,128)(2,1)} async-done(((bf16[8,512,768]{2,1,0:T(8,128)(2,1)}), bf16[8,512,768]{2,1,0:T(8,128)(2,1)}, u32[]{:S(2)}, u32[]{:S(2)}) %all-to-all-start.23) | async-done | bytes 6291488 | tf_op jit(solution)/shard_map/cond/branch_1_fun/all_to_all | solution.py:1640
  1130.4 4.8 all-to-all-start.25
  1135.3 71.6 %all-to-all-done.25.refs_1_ = bf16[8,512,768]{2,1,0:T(8,128)(2,1)} async-done(((bf16[8,512,768]{2,1,0:T(8,128)(2,1)}), bf16[8,512,768]{2,1,0:T(8,128)(2,1)}, u32[]{:S(2)}, u32[]{:S(2)}) %all-to-all-start.25) | async-done | bytes 6291488 | tf_op jit(solution)/shard_map/cond/branch_1_fun/all_to_all | solution.py:1640
  1206.8 4.8 all-to-all-start.24
  1211.6 6.4 finish_rest.6
  1222.5 8.0 outputs.3.refs_6_
  1235.0 48.2 %all-to-all-done.24.refs_0_ = bf16[8,512,768]{2,1,0:T(8,128)(2,1)} async-done(((bf16[8,512,768]{2,1,0:T(8,128)(2,1)}), bf16[8,512,768]{2,1,0:T(8,128)(2,1)}, u32[]{:S(2)}, u32[]{:S(2)}) %all-to-all-start.24) | async-done | bytes 6291488 | tf_op jit(solution)/shard_map/cond/branch_1_fun/all_to_all | solution.py:1640
  1283.2 7.9 input_grad.3.refs_7_
  1291.1 6.4 finish_rest.7
  (132 shorter events, 50.3 us)
Async XLA Ops:
  11.1 63.4 %copy-start.22 = (s32[32]{0:T(128)}, s32[32]{0:T(128)S(1)}, u32[]{:S(2)}) copy-start(s32[32]{0:T(128)S(1)} %get-tuple-element.399.table_ref) | copy-start | bytes 388
  13.2 8.3 all-to-all-start.26
  21.5 76.4 %all-to-all-start.27 = ((bf16[8,512,768]{2,1,0:T(8,128)(2,1)}), bf16[8,512,768]{2,1,0:T(8,128)(2,1)}, u32[]{:S(2)}, u32[]{:S(2)}) async-start(bf16[8,512,768]{2,1,0:T(8,128)(2,1)} %send_inputs.2), calls=%async_computation.35 | async-start | bytes 12582912 | tf_op jit(solution)/shard_map/all_to_all | solution.py:1640
  79.7 23.0 %copy-start.20 = (bf16[2,1,5,768]{3,0,2,1:T(2,128)(2,1)S(1)}, bf16[2,1,5,768]{3,0,2,1:T(2,128)(2,1)}, u32[]{:S(2)}) copy-start(bf16[2,1,5,768]{3,0,2,1:T(2,128)(2,1)} %param.21) | copy-start | bytes 46084
  79.7 23.1 %copy-start.21 = (bf16[2,1,5,768]{3,0,2,1:T(2,128)(2,1)S(1)}, bf16[2,1,5,768]{3,0,2,1:T(2,128)(2,1)}, u32[]{:S(2)}) copy-start(bf16[2,1,5,768]{3,0,2,1:T(2,128)(2,1)} %param.22) | copy-start | bytes 46084
  79.7 23.1 %copy-start.14 = (bf16[2,1,15,768]{3,0,2,1:T(2,128)(2,1)S(1)}, bf16[2,1,15,768]{3,0,2,1:T(2,128)(2,1)}, u32[]{:S(2)}) copy-start(bf16[2,1,15,768]{3,0,2,1:T(2,128)(2,1)} %param.19) | copy-start | bytes 138244
  97.9 76.4 %all-to-all-start.28 = ((bf16[8,512,768]{2,1,0:T(8,128)(2,1)}), bf16[8,512,768]{2,1,0:T(8,128)(2,1)}, u32[]{:S(2)}, u32[]{:S(2)}) async-start(bf16[8,512,768]{2,1,0:T(8,128)(2,1)} %send_inputs.3), calls=%async_computation.36 | async-start | bytes 12582912 | tf_op jit(solution)/shard_map/all_to_all | solution.py:1640
  158.6 15.7 %copy-start.23 = (s32[32]{0:T(128)S(1)}, s32[32]{0:T(128)}, u32[]{:S(2)}) copy-start(s32[32]{0:T(128)} %copy-done.22) | copy-start | bytes 388
  181.6 52.4 %copy-start.8 = (f32[16,768]{1,0:T(8,128)}, f32[16,768]{1,0:T(8,128)S(1)}, u32[]{:S(2)}) copy-start(f32[16,768]{1,0:T(8,128)S(1)} %get-tuple-element.249.taps_ref) | copy-start | bytes 147460 | tf_op jit(solution)/shard_map/cond
  181.6 52.4 %copy-start.12 = (f32[8,768]{1,0:T(8,128)}, f32[8,768]{1,0:T(8,128)S(1)}, u32[]{:S(2)}) copy-start(f32[8,768]{1,0:T(8,128)S(1)} %get-tuple-element.250.gain) | copy-start | bytes 73732 | tf_op jit(solution)/shard_map/cond
  181.6 293.1 %copy-start.26 = (s32[32]{0:T(128)}, s32[32]{0:T(128)S(1)}, u32[]{:S(2)}) copy-start(s32[32]{0:T(128)S(1)} %get-tuple-element.242.table_ref) | copy-start | bytes 388 | tf_op jit(solution)/shard_map/cond
  181.6 76.4 %all-to-all-start.14 = ((bf16[8,512,768]{2,1,0:T(8,128)(2,1)}), bf16[8,512,768]{2,1,0:T(8,128)(2,1)}, u32[]{:S(2)}, u32[]{:S(2)}) async-start(bf16[8,512,768]{2,1,0:T(8,128)(2,1)} %get-tuple-element.246), calls=%async_computation.18 | async-start | bytes 12582912 | tf_op jit(solution)/shard_map/cond/branch_1_fun/all_to_all | solution.py:1640
  206.6 27.4 %copy-start.2 = (bf16[4,512,768]{2,1,0:T(8,128)(2,1)}, bf16[4,512,768]{2,1,0:T(8,128)(2,1)S(1)}, u32[]{:S(2)}) copy-start(bf16[4,512,768]{2,1,0:T(8,128)(2,1)S(1)} %get-tuple-element.326.zn_ref) | copy-start | bytes 9437188 | tf_op jit(solution)/shard_map/cond
  344.0 76.5 %all-to-all-start.16 = ((bf16[8,512,768]{2,1,0:T(8,128)(2,1)}), bf16[8,512,768]{2,1,0:T(8,128)(2,1)}, u32[]{:S(2)}, u32[]{:S(2)}) async-start(bf16[8,512,768]{2,1,0:T(8,128)(2,1)} %hop_x.4), calls=%async_computation.20 | async-start | bytes 12582912 | tf_op jit(solution)/shard_map/cond/branch_1_fun/all_to_all | solution.py:1640
  353.6 29.3 %copy-start.40 = (bf16[2,1,768,768]{3,2,1,0:T(8,128)(2,1)S(1)}, bf16[2,1,768,768]{3,2,1,0:T(8,128)(2,1)}, u32[]{:S(2)}) copy-start(bf16[2,1,768,768]{3,2,1,0:T(8,128)(2,1)} %get-tuple-element.253.out_w) | copy-start | bytes 7077892 | tf_op jit(solution)/shard_map/cond
  420.6 76.6 %all-to-all-start.18 = ((bf16[8,512,768]{2,1,0:T(8,128)(2,1)}), bf16[8,512,768]{2,1,0:T(8,128)(2,1)}, u32[]{:S(2)}, u32[]{:S(2)}) async-start(bf16[8,512,768]{2,1,0:T(8,128)(2,1)} %send_cotangent.7), calls=%async_computation.22 | async-start | bytes 12582912 | tf_op jit(solution)/shard_map/cond/branch_1_fun/all_to_all | solution.py:1640
  497.2 76.4 %all-to-all-start.17 = ((bf16[8,512,768]{2,1,0:T(8,128)(2,1)}), bf16[8,512,768]{2,1,0:T(8,128)(2,1)}, u32[]{:S(2)}, u32[]{:S(2)}) async-start(bf16[8,512,768]{2,1,0:T(8,128)(2,1)} %send_cotangent.6), calls=%async_computation.21 | async-start | bytes 12582912 | tf_op jit(solution)/shard_map/cond/branch_1_fun/all_to_all | solution.py:1640
  502.0 400.4 %reduce-scatter.17.cloned.1.call-start = ((), (), s32[]{:S(2)}) async-start(), calls=%async_computation.41 | async-start | bytes 11919360 | tf_op jit(solution)/shard_map/cond/branch_1_fun/reduce_scatter | solution.py:1644
  626.8 76.3 %all-to-all-start.19 = ((bf16[8,512,768]{2,1,0:T(8,128)(2,1)}), bf16[8,512,768]{2,1,0:T(8,128)(2,1)}, u32[]{:S(2)}, u32[]{:S(2)}) async-start(bf16[8,512,768]{2,1,0:T(8,128)(2,1)} %hop_dx.3), calls=%async_computation.23 | async-start | bytes 12582912 | tf_op jit(solution)/shard_map/cond/branch_1_fun/all_to_all | solution.py:1640
  631.5 427.2 %reduce-scatter.21.cloned.1.call-start = ((), (), s32[]{:S(2)}) async-start(), calls=%async_computation.43 | async-start | bytes 10567680 | tf_op jit(solution)/shard_map/cond/branch_1_fun/reduce_scatter | solution.py:1644
  631.6 27.1 %copy-start.33 = (f32[8,768]{1,0:T(8,128)S(1)}, f32[8,768]{1,0:T(8,128)}, u32[]{:S(2)}) copy-start(f32[8,768]{1,0:T(8,128)} %get-tuple-element.339) | copy-start | bytes 73732 | tf_op jit(solution)/shard_map/cond
  631.6 28.0 %copy-start.29 = (f32[8,768]{1,0:T(8,128)S(1)}, f32[8,768]{1,0:T(8,128)}, u32[]{:S(2)}) copy-start(f32[8,768]{1,0:T(8,128)} %get-tuple-element.341) | copy-start | bytes 73732 | tf_op jit(solution)/shard_map/cond
  659.8 26.3 %copy-start.16 = (f32[24,768]{1,0:T(8,128)S(1)}, f32[24,768]{1,0:T(8,128)}, u32[]{:S(2)}) copy-start(f32[24,768]{1,0:T(8,128)} %get-tuple-element.337) | copy-start | bytes 221188 | tf_op jit(solution)/shard_map/cond
  799.2 98.3 %all-to-all-start.21 = ((bf16[8,512,768]{2,1,0:T(8,128)(2,1)}), bf16[8,512,768]{2,1,0:T(8,128)(2,1)}, u32[]{:S(2)}, u32[]{:S(2)}) async-start(bf16[8,512,768]{2,1,0:T(8,128)(2,1)} %hop_dx.5), calls=%async_computation.25 | async-start | bytes 12582912 | tf_op jit(solution)/shard_map/cond/branch_1_fun/all_to_all | solution.py:1640
  804.0 4.6 copy-start.13
  804.0 331.2 %reduce-scatter.19.cloned.1.call-start = ((), (), s32[]{:S(2)}) async-start(), calls=%async_computation.42 | async-start | bytes 11919360 | tf_op jit(solution)/shard_map/cond/branch_1_fun/reduce_scatter | solution.py:1644
  808.6 65.2 %copy-start.9 = (f32[16,768]{1,0:T(8,128)S(1)}, f32[16,768]{1,0:T(8,128)}, u32[]{:S(2)}) copy-start(f32[16,768]{1,0:T(8,128)} %copy-done.8) | copy-start | bytes 147460 | tf_op jit(solution)/shard_map/cond
  897.5 4.9 copy-start.3
  950.6 5.0 copy-start.42
  950.6 76.5 %all-to-all-start.22 = ((bf16[8,512,768]{2,1,0:T(8,128)(2,1)}), bf16[8,512,768]{2,1,0:T(8,128)(2,1)}, u32[]{:S(2)}, u32[]{:S(2)}) async-start(bf16[8,512,768]{2,1,0:T(8,128)(2,1)} %after.12), calls=%async_computation.26 | async-start | bytes 12582912 | tf_op jit(solution)/shard_map/cond/branch_1_fun/all_to_all | solution.py:1640
  955.5 335.6 %reduce-scatter.23.cloned.1.call-start = ((), (), s32[]{:S(2)}) async-start(), calls=%async_computation.44 | async-start | bytes 10567680 | tf_op jit(solution)/shard_map/cond/branch_1_fun/reduce_scatter | solution.py:1644
  955.6 12.7 copy-start.34
  955.6 13.7 %copy-start.31 = (f32[8,768]{1,0:T(8,128)S(1)}, f32[8,768]{1,0:T(8,128)}, u32[]{:S(2)}) copy-start(f32[8,768]{1,0:T(8,128)} %get-tuple-element.347) | copy-start | bytes 73732 | tf_op jit(solution)/shard_map/cond
  955.6 13.8 %copy-start.5 = (f32[9,512,128]{2,1,0:T(8,128)S(1)}, f32[9,512,128]{2,1,0:T(8,128)}, u32[]{:S(2)}) copy-start(f32[9,512,128]{2,1,0:T(8,128)} %get-tuple-element.308.rstd_ref) | copy-start | bytes 7077892 | tf_op jit(solution)/shard_map/cond
  969.4 32.6 %copy-start.17 = (f32[24,768]{1,0:T(8,128)S(1)}, f32[24,768]{1,0:T(8,128)}, u32[]{:S(2)}) copy-start(f32[24,768]{1,0:T(8,128)} %get-tuple-element.343) | copy-start | bytes 221188 | tf_op jit(solution)/shard_map/cond
  1027.1 103.3 %all-to-all-start.23 = ((bf16[8,512,768]{2,1,0:T(8,128)(2,1)}), bf16[8,512,768]{2,1,0:T(8,128)(2,1)}, u32[]{:S(2)}, u32[]{:S(2)}) async-start(bf16[8,512,768]{2,1,0:T(8,128)(2,1)} %after.13), calls=%async_computation.27 | async-start | bytes 12582912 | tf_op jit(solution)/shard_map/cond/branch_1_fun/all_to_all | solution.py:1640
  1130.4 76.4 %all-to-all-start.25 = ((bf16[8,512,768]{2,1,0:T(8,128)(2,1)}), bf16[8,512,768]{2,1,0:T(8,128)(2,1)}, u32[]{:S(2)}, u32[]{:S(2)}) async-start(bf16[8,512,768]{2,1,0:T(8,128)(2,1)} %after.15), calls=%async_computation.32 | async-start | bytes 12582912 | tf_op jit(solution)/shard_map/cond/branch_1_fun/all_to_all | solution.py:1640
  1206.8 76.4 %all-to-all-start.24 = ((bf16[8,512,768]{2,1,0:T(8,128)(2,1)}), bf16[8,512,768]{2,1,0:T(8,128)(2,1)}, u32[]{:S(2)}, u32[]{:S(2)}) async-start(bf16[8,512,768]{2,1,0:T(8,128)(2,1)} %after.14), calls=%async_computation.30 | async-start | bytes 12582912 | tf_op jit(solution)/shard_map/cond/branch_1_fun/all_to_all | solution.py:1640
  1211.6 10.9 copy-start.27
Sparse Core Ops, SparseCore 0:
  622.3 176.2 reduce-scatter.16
  801.5 146.2 reduce-scatter.20
  950.7 163.6 reduce-scatter.18
  1116.8 146.2 reduce-scatter.22

commit v7 on v6

--- a/solution.py
+++ b/solution.py
@@ -15,7 +15,6 @@
 FF_SUB = 256
 LANES = 128
 SMALL_ROWS = 32
-COUNT_ROWS = 16
 BF16 = jnp.bfloat16
 F32 = jnp.float32
 VMEM_BYTES = 60 * 2**20
@@ -1007,10 +1006,9 @@
         low_up,
         low_down,
         low_dx,
-        tally,
         sems,
         dx_sem,
-        ) = rest[-16:]
+        ) = rest[-15:]
         c, i = pl.program_id(0), pl.program_id(1)
         n0 = present(counts_ref, 0)
         total_n = n0 + present(counts_ref, 1)
@@ -1019,12 +1017,6 @@
         @pl.when(jnp.logical_and(c == 0, i == 0))
         def _():
             small_ref[...] = jnp.zeros_like(small_ref)
-            lane = lax.broadcasted_iota(jnp.int32, (COUNT_ROWS, width), 1)
-            counted = jnp.zeros((COUNT_ROWS, width), F32)
-            for k in range(KINDS):
-                there = sum(counts_ref[(b * HALVES + half) * 8 + k] for half in range(HALVES))
-                counted = jnp.where(lane == k, there.astype(F32), counted)
-            tally[...] = counted.astype(BF16)
 
         @pl.when(i == 0)
         def _():
@@ -1091,16 +1083,6 @@
                 for n, (source, target) in enumerate(pairs)
             ]
 
-        def tallies():
-            return [
-                pltpu.make_async_copy(
-                    tally,
-                    packed_ref.at[z, pl.ds(parts * tall + deep, COUNT_ROWS)],
-                    sems.at[groups + shares + z],
-                )
-                for z in range(groups)
-            ]
-
         @pl.when(i == OWN_CAP - 1)
         def _():
             @pl.when(c > 0)
@@ -1115,9 +1097,7 @@
 
             @pl.when(c == parts - 1)
             def _():
-                for copy in tallies():
-                    copy.start()
-                for copy in copies() + tallies():
+                for copy in copies():
                     copy.wait()
 
     def first_row(c, i, r, n):
@@ -1176,8 +1156,7 @@
                 pltpu.VMEM((width, FF_PART), BF16),
                 pltpu.VMEM((FF_PART, width), BF16),
                 pltpu.VMEM((length, width), BF16),
-                pltpu.VMEM((COUNT_ROWS, width), BF16),
-                pltpu.SemaphoreType.DMA((2 * groups + shares,)),
+                pltpu.SemaphoreType.DMA((groups + shares,)),
                 pltpu.SemaphoreType.DMA,
             ],
         ),
@@ -1185,7 +1164,7 @@
             jax.ShapeDtypeStruct((8, width), F32),
             jax.ShapeDtypeStruct((slots, length, width), BF16),
             jax.ShapeDtypeStruct((slots, length, width), BF16),
-            jax.ShapeDtypeStruct((groups, parts * tall + deep + COUNT_ROWS, width), BF16),
+            jax.ShapeDtypeStruct((groups, parts * tall + deep, width), BF16),
         ],
         input_output_aliases=alias,
         compiler_params=params_of(2),
@@ -1531,14 +1510,13 @@
     return dx, feed_pack, rest_pack
 
 
-def finish_feed(b, feed, up_out, down_out, shapes):
+def finish_feed(b, feed, totals, up_out, down_out, shapes):
     parts = shapes[0].shape[-1] // FF_PART
     tall, width = shapes[0].shape[2], FF_PART
-    count_block = 2 * parts * tall // COUNT_ROWS
 
     def kernel(up_ref, down_ref, count_ref, *rest):
         up_to, down_to = rest[-2:]
-        scale = 1.0 / count_ref[0:1, KINDS - 1 : KINDS].astype(F32)
+        scale = 1.0 / count_ref[b : b + 1, KINDS - 1 : KINDS]
         up_to[...] = up_ref[...].astype(F32) * scale
         down_to[...] = down_ref[...].astype(F32) * scale
 
@@ -1549,7 +1527,7 @@
         in_specs=[
             pl.BlockSpec((tall, width), lambda c: (c, 0)),
             pl.BlockSpec((tall, width), lambda c: (parts + c, 0)),
-            pl.BlockSpec((COUNT_ROWS, width), lambda c: (count_block, 0)),
+            pl.BlockSpec((BLOCKS, 8), lambda c: (0, 0)),
         ]
         + [ANY_SPEC] * len(old),
         out_specs=[
@@ -1561,18 +1539,17 @@
         compiler_params=params_of(1),
         cost_estimate=pl.CostEstimate(flops=0, transcendentals=0, bytes_accessed=8 * 2**20),
         name="finish_feed",
-    )(feed, feed, feed, *old)
-
-
-def finish_rest(b, rest, feed, old, shapes, wait_for):
+    )(feed, feed, totals, *old)
+
+
+def finish_rest(b, rest, totals, old, shapes, wait_for):
     tall, width = shapes[1].shape[2:]
-    count_block = (feed.shape[0] - COUNT_ROWS) // COUNT_ROWS
     small_block = 7 * tall // SMALL_ROWS
 
     def kernel(rest_ref, small_ref, count_ref, *refs):
         qkv_to, out_to, taps_to, point_to, gain_to, shift_to = refs[-6:]
         i = pl.program_id(0)
-        scales = 1.0 / count_ref[0:1, 0:8].astype(F32)
+        scales = 1.0 / jnp.maximum(count_ref[b : b + 1, :], 1.0)
         values = rest_ref[...].astype(F32)
 
         @pl.when(i < 3)
@@ -1591,9 +1568,11 @@
             for k in range(KINDS):
                 scale = jnp.where(which == k, scales[:, k : k + 1], scale)
             small = small * scale
-            taps_to[...] = small[:15, :tall]
-            gain_to[...] = small[15:20, :tall]
-            shift_to[...] = small[20:25, :tall]
+            for r in range(15):
+                taps_to[r] = small[r : r + 1, :tall]
+            for r in range(KINDS):
+                gain_to[r] = small[15 + r : 16 + r, :tall]
+                shift_to[r] = small[20 + r : 21 + r, :tall]
 
         for k in range(1, KINDS - 1):
 
@@ -1608,25 +1587,25 @@
         in_specs=[
             pl.BlockSpec((tall, width), lambda i: (i, 0)),
             pl.BlockSpec((SMALL_ROWS, width), lambda i: (small_block, 0)),
-            pl.BlockSpec((COUNT_ROWS, width), lambda i: (count_block, 0)),
+            pl.BlockSpec((BLOCKS, 8), lambda i: (0, 0)),
         ]
         + [ANY_SPEC] * (len(old) + len(wait_for)),
         out_specs=[
             pl.BlockSpec((None, None, tall, width), lambda i: (b, 0, 0, jnp.minimum(i, 2))),
             pl.BlockSpec((None, None, tall, width), lambda i: (b, 0, 0, 0)),
-            pl.BlockSpec((None, None, 15, tall), lambda i: (b, 0, 0, 0)),
+            pl.BlockSpec((None, 15, 1, tall), lambda i: (b, 0, 0, 0)),
             pl.BlockSpec(
                 (None, None, None, tall, width), lambda i: (b, 0, jnp.maximum(i - 4, 0), 0, 0)
             ),
-            pl.BlockSpec((None, None, KINDS, tall), lambda i: (b, 0, 0, 0)),
-            pl.BlockSpec((None, None, KINDS, tall), lambda i: (b, 0, 0, 0)),
+            pl.BlockSpec((None, KINDS, 1, tall), lambda i: (b, 0, 0, 0)),
+            pl.BlockSpec((None, KINDS, 1, tall), lambda i: (b, 0, 0, 0)),
         ],
         out_shape=list(shapes),
         input_output_aliases={3 + n: n for n in range(len(old))},
         compiler_params=params_of(1),
         cost_estimate=pl.CostEstimate(flops=0, transcendentals=0, bytes_accessed=8 * 2**20),
         name="finish_rest",
-    )(rest, rest, feed, *old, *wait_for)
+    )(rest, rest, totals, *old, *wait_for)
 
 
 def small_params(b, conv_taps, norm_gain, norm_bias):
@@ -1682,7 +1661,10 @@
     routed = owners < seqs
     if routed:
         route, lost = route_tables(everyone, me, owners, seqs)
-        lost = lax.psum(lost, "dp")
+    else:
+        lost = jnp.zeros((1,), jnp.int32)
+    lost = lax.psum(jnp.concatenate([lost, tables[1]]), "dp")
+    totals = lost[1:].reshape(BLOCKS, HALVES, 8).sum(axis=1).astype(F32)
 
     x0 = [
         exchange(
@@ -1768,16 +1750,17 @@
         rest_shapes = (
             grad(tall, 3 * width),
             grad(tall, width),
-            grad(15, tall),
+            jax.ShapeDtypeStruct((BLOCKS, 15, 1, tall), F32),
             grad(KINDS - 2, tall, width),
-            grad(KINDS, tall),
-            grad(KINDS, tall),
+            jax.ShapeDtypeStruct((BLOCKS, KINDS, 1, tall), F32),
+            jax.ShapeDtypeStruct((BLOCKS, KINDS, 1, tall), F32),
         )
-        feeds = finish_feed(1, feed1, None, None, feed_shapes)
-        rests = finish_rest(1, rest1, feed1, (), rest_shapes, ())
-        feeds = finish_feed(0, feed0, *feeds, feed_shapes)
-        rests = finish_rest(0, rest0, feed0, rests, rest_shapes, (outputs, input_grad, feeds[0]))
+        feeds = finish_feed(1, feed1, totals, None, None, feed_shapes)
+        rests = finish_rest(1, rest1, totals, (), rest_shapes, ())
+        feeds = finish_feed(0, feed0, totals, *feeds, feed_shapes)
+        rests = finish_rest(0, rest0, totals, rests, rest_shapes, (outputs, input_grad, feeds[0]))
         qkv, out, taps, point, gain, shift = rests
+        taps, gain, shift = (rows.transpose(0, 2, 1, 3) for rows in (taps, gain, shift))
         return (outputs, input_grad, qkv, out, *feeds, taps, point, gain, shift)
 
     if not routed:

time: 1320 us -> 1330 us (level)
  the two profiles are of different devices: /device:TPU:24 before, /device:TPU:0 now
where the time goes in v7:
time: 1330 us; the launch traced here: 1310 us
  Pallas kernels  684 us (51%)
  waiting for transfers between devices  293 us (22%)
  blocking collectives  168 us (13%)
  starting transfers between devices  92 us (7%)
  local copies, waits for them, and re-layouts  44.8 us (3%)
  between operations  14.3 us (1%)
    all_to_all x13, waiting for transfers between devices, exchange(): return lax.all_to_all(rows, 'op', split_axis=0, concat_axis=0, tiled=True)  292 us
    all_to_all x2, blocking collectives, exchange(): return lax.all_to_all(rows, 'op', split_axis=0, concat_axis=0, tiled=True)  154 us
    pallas_call x4, Pallas kernels, attention_backward(): pl.pallas_call(kernel, grid_spec=pltpu.PrefetchScalarGridSpec(num_scalar_...  132 us
    pallas_call x4, Pallas kernels, conv_backward(): pl.pallas_call(kernel, grid_spec=pltpu.PrefetchScalarGridSpec(num_scalar_...  128 us
    all_to_all x13, starting transfers between devices, exchange(): return lax.all_to_all(rows, 'op', split_axis=0, concat_axis=0, tiled=True)  91.9 us
    pallas_call x2, Pallas kernels, feed_backward(): pl.pallas_call(kernel, grid_spec=pltpu.PrefetchScalarGridSpec(num_scalar_...  85.7 us
    pallas_call x4, Pallas kernels, feed_forward(): pl.pallas_call(kernel, grid_spec=pltpu.PrefetchScalarGridSpec(num_scalar_...  80.2 us
    pallas_call x4, Pallas kernels, conv_forward(): pl.pallas_call(kernel, grid_spec=pltpu.PrefetchScalarGridSpec(num_scalar_...  72.8 us
  transfers between devices with their start and end apart: 17, of which 11 were waited for; matrix products, arithmetic and copies ran while one was open for 3% of the time, Pallas kernels for 48%

profile of v7, /device:TPU:0, one launch (start us, length us, event | category | flops | bytes accessed | tf_op | source)
XLA Modules:
  0.0 1309.5 jit_solution(12781114448036814471)
XLA Ops:
  13.2 5.2 all-to-all-start.26
  22.9 4.8 all-to-all-start.27
  31.0 25.4 %route_tables.1 = (s32[80]{0:T(128)S(1)}, s32[1]{0:T(128)}) custom-call(s32[192]{0:T(256)} %reshape.117.refs_0_, s32[1]{0:T(128)} %bitcast.14.refs_1_), custom_call_target="tpu_custom_call" | custom-call | tf_op jit(solution)/shard_map/route_tables/pallas_call | solution.py:371
  57.1 14.0 %psum.7.refs_1_ = s32[33]{0:T(128)} all-reduce(s32[33]{0:T(128)S(1)} %pad_add_fusion.1), channel_id=1, replica_groups=mesh['dp'=4,'op'=8] {'dp'}, use_global_device_ids=true, to_apply=%region_0.1 | all-reduce | flops 33 | bytes 264 | tf_op jit(solution)/shard_map/psum | solution.py:1666
  75.7 23.6 %all-to-all-done.27.x_ref = bf16[8,512,768]{2,1,0:T(8,128)(2,1)} async-done(((bf16[8,512,768]{2,1,0:T(8,128)(2,1)}), bf16[8,512,768]{2,1,0:T(8,128)(2,1)}, u32[]{:S(2)}, u32[]{:S(2)}) %all-to-all-start.27) | async-done | bytes 6291488 | tf_op jit(solution)/shard_map/all_to_all | solution.py:1619
  99.3 4.8 all-to-all-start.28
  105.2 20.1 %feed_forward.13 = (bf16[8,512,768]{2,1,0:T(8,128)(2,1)}, bf16[4,512,3072]{2,1,0:T(8,128)(2,1)}, bf16[4,512,3072]{2,1,0:T(8,128)(2,1)}, bf16[4,512,768]{2,1,0:T(8,128)(2,1)S(1)}, f32[4,512,128]{2,1,0:T(8,128)}) custom-call(s32[60]{0:T(128)S(1)} %get-tuple-element.404.rows_ref, s32[32]{0:T(128)S(1)} %get-tuple-element.403.counts_ref, ...), custom_call_target="tpu_custom_call" | custom-call | flops 14495514624 | bytes 41943040 | tf_op jit(solution)/shard_map/feed_forward/pallas_call | solution.py:927
  125.3 12.7 attention_forward.13
  138.0 18.3 %conv_forward.13 = (bf16[8,512,768]{2,1,0:T(8,128)(2,1)}, bf16[9,512,768]{2,1,0:T(8,128)(2,1)}, bf16[9,512,768]{2,1,0:T(8,128)(2,1)}, f32[9,512,128]{2,1,0:T(8,128)}) custom-call(s32[60]{0:T(128)S(1)} %get-tuple-element.404.rows_ref, s32[32]{0:T(128)S(1)} %get-tuple-element.403.counts_ref, ...), custom_call_target="tpu_custom_call", output_to_operand_aliasing={{0}: (7, {})} | custom-call | flops 5435817984 | bytes 37748736 | tf_op jit(solution)/shard_map/conv_forward/pallas_call | solution.py:1258
  156.3 4.6 hop_x.5
  160.9 14.8 %all-to-all-done.28 = bf16[8,512,768]{2,1,0:T(8,128)(2,1)} async-done(((bf16[8,512,768]{2,1,0:T(8,128)(2,1)}), bf16[8,512,768]{2,1,0:T(8,128)(2,1)}, u32[]{:S(2)}, u32[]{:S(2)}) %all-to-all-start.28) | async-done | bytes 6291488 | tf_op jit(solution)/shard_map/all_to_all | solution.py:1619
  175.7 1122.3 %conditional.1 = (f32[2,1,192,3072]{3,2,1,0:T(8,128)}, f32[2,1,192,3072]{3,2,1,0:T(8,128)}, bf16[12,512,768]{2,1,0:T(8,128)(2,1)}, bf16[12,512,768]{2,1,0:T(8,12...) conditional(s32[]{:T(128)} %bitcast.15, ...), branch_computations={%region_2.7_spmd, %region_7.12_spmd} | conditional | flops 278434742272 | bytes 1575968384 | solution.py:1768
  183.1 4.8 all-to-all-start.14
  187.8 20.1 %feed_forward.10 = (bf16[8,512,768]{2,1,0:T(8,128)(2,1)}, bf16[4,512,3072]{2,1,0:T(8,128)(2,1)}, bf16[4,512,3072]{2,1,0:T(8,128)(2,1)}, bf16[4,512,768]{2,1,0:T(8,128)(2,1)S(1)}, f32[4,512,128]{2,1,0:T(8,128)}) custom-call(s32[60]{0:T(128)S(1)} %get-tuple-element.248.rows_ref, ...), custom_call_target="tpu_custom_call", output_to_operand_aliasing={{1}: (7, {}), {2}: (8, {}), {3}: (9, {}), {4}: (10, {})} | custom-call | flops 14495514624 | bytes 41943040 | tf_op jit(solution)/shard_map/cond/branch_1_fun/feed_forward/pallas_call | solution.py:927
  207.9 13.2 %attention_forward.10 = (bf16[8,512,768]{2,1,0:T(8,128)(2,1)}, bf16[3,512,2304]{2,1,0:T(8,128)(2,1)}, bf16[3,512,768]{2,1,0:T(8,128)(2,1)}, bf16[3,512,768]{2,1,0:T(8,128)(2,1)}, f32[3,512,128]{2,1,0:T(8,128)}) custom-call(s32[60]{0:T(128)S(1)} %get-tuple-element.248.rows_ref, s32[32]{0:T(128)S(1)} %get-tuple-element.249.counts_ref, ...), custom_call_target="tpu_custom_call", output_to_operand_aliasing={{0}: (7, {})} | custom-call | flops 19327352832 | bytes 31457280 | tf_op jit(solution)/shard_map/cond/branch_1_fun/attention_forward/pallas_call | solution.py:627
  221.2 19.0 %conv_forward.10 = (bf16[8,512,768]{2,1,0:T(8,128)(2,1)}, bf16[9,512,768]{2,1,0:T(8,128)(2,1)}, bf16[9,512,768]{2,1,0:T(8,128)(2,1)}, f32[9,512,128]{2,1,0:T(8,128)}) custom-call(s32[60]{0:T(128)S(1)} %get-tuple-element.248.rows_ref, s32[32]{0:T(128)S(1)} %get-tuple-element.249.counts_ref, ...), custom_call_target="tpu_custom_call", output_to_operand_aliasing={{0}: (7, {})} | custom-call | flops 5435817984 | bytes 37748736 | tf_op jit(solution)/shard_map/cond/branch_1_fun/conv_forward/pallas_call | solution.py:1258
  240.1 19.3 %all-to-all-done.14.refs_0_ = bf16[8,512,768]{2,1,0:T(8,128)(2,1)} async-done(((bf16[8,512,768]{2,1,0:T(8,128)(2,1)}), bf16[8,512,768]{2,1,0:T(8,128)(2,1)}, u32[]{:S(2)}, u32[]{:S(2)}) %all-to-all-start.14) | async-done | bytes 6291488 | tf_op jit(solution)/shard_map/cond/branch_1_fun/all_to_all | solution.py:1619
  263.2 76.9 %all_to_all.126.refs_1_ = bf16[8,512,768]{2,1,0:T(8,128)(2,1)} all-to-all(bf16[8,512,768]{2,1,0:T(8,128)(2,1)} %hop_x.3), channel_id=1, replica_groups=mesh['dp'=4,'op'=8] {'op'}, dimensions={0} | all-to-all | bytes 12582912 | tf_op jit(solution)/shard_map/cond/branch_1_fun/all_to_all | solution.py:1619
  343.8 5.0 all-to-all-start.16
  348.8 4.6 land_x.2.x_ref.x_ref0
  353.4 10.9 feed_forward.11
  364.3 26.6 %attention_forward.11 = (bf16[8,512,768]{2,1,0:T(8,128)(2,1)}, bf16[3,512,2304]{2,1,0:T(8,128)(2,1)}, bf16[3,512,768]{2,1,0:T(8,128)(2,1)}, bf16[3,512,768]{2,1,0:T(8,128)(2,1)}, f32[3,512,128]{2,1,0:T(8,128)}) custom-call(s32[60]{0:T(128)S(1)} %get-tuple-element.248.rows_ref, s32[32]{0:T(128)S(1)} %get-tuple-element.249.counts_ref, ...), custom_call_target="tpu_custom_call", output_to_operand_aliasing={{0}: (7, {})} | custom-call | flops 19327352832 | bytes 31457280 | tf_op jit(solution)/shard_map/cond/branch_1_fun/attention_forward/pallas_call | solution.py:627
  391.0 16.6 %conv_forward.11 = (bf16[8,512,768]{2,1,0:T(8,128)(2,1)}, bf16[9,512,768]{2,1,0:T(8,128)(2,1)}, bf16[9,512,768]{2,1,0:T(8,128)(2,1)}, f32[9,512,128]{2,1,0:T(8,128)}) custom-call(s32[60]{0:T(128)S(1)} %get-tuple-element.248.rows_ref, s32[32]{0:T(128)S(1)} %get-tuple-element.249.counts_ref, ...), custom_call_target="tpu_custom_call", output_to_operand_aliasing={{0}: (7, {})} | custom-call | flops 5435817984 | bytes 37748736 | tf_op jit(solution)/shard_map/cond/branch_1_fun/conv_forward/pallas_call | solution.py:1258
  407.6 4.6 send_cotangent.7
  412.1 8.3 all-to-all-done.16.refs_0_
  420.4 5.0 all-to-all-start.18
  430.0 29.1 %feed_forward.12 = (bf16[8,512,768]{2,1,0:T(8,128)(2,1)}, bf16[4,512,3072]{2,1,0:T(8,128)(2,1)}, bf16[4,512,3072]{2,1,0:T(8,128)(2,1)}, bf16[4,512,768]{2,1,0:T(8,128)(2,1)}, f32[4,512,128]{2,1,0:T(8,128)}) custom-call(s32[60]{0:T(128)S(1)} %get-tuple-element.248.rows_ref, ...), custom_call_target="tpu_custom_call", output_to_operand_aliasing={{1}: (7, {}), {2}: (8, {}), {3}: (9, {}), {4}: (10, {})} | custom-call | flops 14495514624 | bytes 41943040 | tf_op jit(solution)/shard_map/cond/branch_1_fun/feed_forward/pallas_call | solution.py:927
  459.1 5.1 attention_forward.12
  464.2 18.9 %conv_forward.12 = (bf16[8,512,768]{2,1,0:T(8,128)(2,1)}, bf16[9,512,768]{2,1,0:T(8,128)(2,1)}, bf16[9,512,768]{2,1,0:T(8,128)(2,1)}, f32[9,512,128]{2,1,0:T(8,128)}) custom-call(s32[60]{0:T(128)S(1)} %get-tuple-element.248.rows_ref, s32[32]{0:T(128)S(1)} %get-tuple-element.249.counts_ref, ...), custom_call_target="tpu_custom_call", output_to_operand_aliasing={{0}: (7, {})} | custom-call | flops 5435817984 | bytes 37748736 | tf_op jit(solution)/shard_map/cond/branch_1_fun/conv_forward/pallas_call | solution.py:1258
  487.7 9.4 all-to-all-done.18.dy_ref.dy_ref1
  497.0 4.8 all-to-all-start.17
  501.8 10.9 attention_backward.12
  512.8 32.5 %conv_backward.12 = (bf16[8,512,768]{2,1,0:T(8,128)(2,1)}, f32[24,768]{1,0:T(8,128)}, f32[3,768,768]{2,1,0:T(8,128)}) custom-call(s32[60]{0:T(128)S(1)} %get-tuple-element.248.rows_ref, s32[32]{0:T(128)S(1)} %get-tuple-element.249.counts_ref, bf16[8,512,768]{2,1,0:T(8,128)(2,1)} %land_x.3.x_ref.x_ref1, ...), custom_call_target="tpu_custom_call", output_to_operand_aliasing={{0}: (10, {})} | custom-call | flops 8153726976 | bytes 52428800 | tf_op jit(solution)/shard_map/cond/branch_1_fun/conv_backward/pallas_call | solution.py:1407
  545.3 28.1 %all-to-all-done.17.dy_ref0.dy_ref = bf16[8,512,768]{2,1,0:T(8,128)(2,1)} async-done(((bf16[8,512,768]{2,1,0:T(8,128)(2,1)}), bf16[8,512,768]{2,1,0:T(8,128)(2,1)}, u32[]{:S(2)}, u32[]{:S(2)}) %all-to-all-start.17) | async-done | bytes 6291488 | tf_op jit(solution)/shard_map/cond/branch_1_fun/all_to_all | solution.py:1619
  573.4 43.0 %feed_backward.6 = (f32[8,768]{1,0:T(8,128)}, bf16[8,512,768]{2,1,0:T(8,128)(2,1)}, bf16[8,512,768]{2,1,0:T(8,128)(2,1)}, bf16[4,1536,768]{2,1,0:T(8,128)(2,1)}) custom-call(s32[60]{0:T(128)S(1)} %get-tuple-element.248.rows_ref, s32[32]{0:T(128)S(1)} %get-tuple-element.249.counts_ref, ...), custom_call_target="tpu_custom_call", output_to_operand_aliasing={{2}: (13, {})} | custom-call | flops 25367150592 | bytes 52428800 | tf_op jit(solution)/shard_map/cond/branch_1_fun/feed_backward/pallas_call | solution.py:1137
  620.9 4.9 all-to-all-start.19
  625.9 65.2 %attention_backward.13 = (bf16[8,512,768]{2,1,0:T(8,128)(2,1)}, f32[8,768]{1,0:T(8,128)}, bf16[4,1376,768]{2,1,0:T(8,128)(2,1)}) custom-call(s32[60]{0:T(128)S(1)} %get-tuple-element.248.rows_ref, s32[32]{0:T(128)S(1)} %get-tuple-element.249.counts_ref, bf16[8,512,768]{2,1,0:T(8,128)(2,1)} %land_x.2.x_ref.x_ref0, ...), custom_call_target="tpu_custom_call", output_to_operand_aliasing={{0}: (13, {})} | custom-call | flops 19327352832 | bytes 41943040 | tf_op jit(solution)/shard_map/cond/branch_1_fun/attention_backward/pallas_call | solution.py:818
  692.3 30.4 %conv_backward.13 = (bf16[8,512,768]{2,1,0:T(8,128)(2,1)}, f32[24,768]{1,0:T(8,128)}, bf16[4,1376,768]{2,1,0:T(8,128)(2,1)}) custom-call(s32[60]{0:T(128)S(1)} %get-tuple-element.248.rows_ref, s32[32]{0:T(128)S(1)} %get-tuple-element.249.counts_ref, bf16[8,512,768]{2,1,0:T(8,128)(2,1)} %land_x.2.x_ref.x_ref0, ...), custom_call_target="tpu_custom_call", output_to_operand_aliasing={{2}: (11, {}), {0}: (12, {})} | custom-call | flops 8153726976 | bytes 52428800 | tf_op jit(solution)/shard_map/cond/branch_1_fun/conv_backward/pallas_call | solution.py:1407
  728.0 76.9 %all_to_all.127.refs_1_ = bf16[8,512,768]{2,1,0:T(8,128)(2,1)} all-to-all(bf16[8,512,768]{2,1,0:T(8,128)(2,1)} %hop_dx.4), channel_id=1, replica_groups=mesh['dp'=4,'op'=8] {'op'}, dimensions={0} | all-to-all | bytes 12582912 | tf_op jit(solution)/shard_map/cond/branch_1_fun/all_to_all | solution.py:1619
  804.9 5.4 hop_dx.5
  810.3 4.8 all-to-all-start.21
  815.2 4.6 land_dx.3.dy_ref.dy_ref1
  819.9 28.6 %attention_backward.14 = (bf16[8,512,768]{2,1,0:T(8,128)(2,1)}, f32[8,768]{1,0:T(8,128)}, f32[768,2304]{1,0:T(8,128)}, f32[768,768]{1,0:T(8,128)}) custom-call(s32[60]{0:T(128)S(1)} %get-tuple-element.248.rows_ref, s32[32]{0:T(128)S(1)} %get-tuple-element.249.counts_ref, bf16[8,512,768]{2,1,0:T(8,128)(2,1)} %get-tuple-element.252.x_ref.x_ref1, ...), custom_call_target="tpu_custom_call" | custom-call | flops 19327352832 | bytes 41943040 | tf_op jit(solution)/shard_map/cond/branch_1_fun/attention_backward/pallas_call | solution.py:818
  848.5 32.6 %conv_backward.14 = (bf16[8,512,768]{2,1,0:T(8,128)(2,1)}, f32[24,768]{1,0:T(8,128)}, f32[3,768,768]{2,1,0:T(8,128)}) custom-call(s32[60]{0:T(128)S(1)} %get-tuple-element.248.rows_ref, s32[32]{0:T(128)S(1)} %get-tuple-element.249.counts_ref, bf16[8,512,768]{2,1,0:T(8,128)(2,1)} %get-tuple-element.252.x_ref.x_ref1, ...), custom_call_target="tpu_custom_call", output_to_operand_aliasing={{0}: (10, {})} | custom-call | flops 8153726976 | bytes 52428800 | tf_op jit(solution)/shard_map/cond/branch_1_fun/conv_backward/pallas_call | solution.py:1407
  881.1 5.7 all-to-all-done.21.refs_0_
  891.4 42.7 %feed_backward.7 = (f32[8,768]{1,0:T(8,128)}, bf16[8,512,768]{2,1,0:T(8,128)(2,1)}, bf16[8,512,768]{2,1,0:T(8,128)(2,1)}, bf16[4,1536,768]{2,1,0:T(8,128)(2,1)}) custom-call(s32[60]{0:T(128)S(1)} %get-tuple-element.248.rows_ref, s32[32]{0:T(128)S(1)} %get-tuple-element.249.counts_ref, ...), custom_call_target="tpu_custom_call", output_to_operand_aliasing={{2}: (13, {})} | custom-call | flops 25367150592 | bytes 52428800 | tf_op jit(solution)/shard_map/cond/branch_1_fun/feed_backward/pallas_call | solution.py:1137
  934.1 18.9 %all-to-all-start.22 = ((bf16[8,512,768]{2,1,0:T(8,128)(2,1)}), bf16[8,512,768]{2,1,0:T(8,128)(2,1)}, u32[]{:S(2)}, u32[]{:S(2)}) async-start(bf16[8,512,768]{2,1,0:T(8,128)(2,1)} %after.12), calls=%async_computation.26 | async-start | bytes 12582912 | tf_op jit(solution)/shard_map/cond/branch_1_fun/all_to_all | solution.py:1619
  953.1 27.2 %attention_backward.15 = (bf16[8,512,768]{2,1,0:T(8,128)(2,1)}, f32[8,768]{1,0:T(8,128)}, bf16[4,1376,768]{2,1,0:T(8,128)(2,1)}) custom-call(s32[60]{0:T(128)S(1)} %get-tuple-element.248.rows_ref, s32[32]{0:T(128)S(1)} %get-tuple-element.249.counts_ref, bf16[8,512,768]{2,1,0:T(8,128)(2,1)} %get-tuple-element.310.x_ref0.x_ref, ...), custom_call_target="tpu_custom_call", output_to_operand_aliasing={{0}: (13, {})} | custom-call | flops 19327352832 | bytes 41943040 | tf_op jit(solution)/shard_map/cond/branch_1_fun/attention_backward/pallas_call | solution.py:818
  981.5 32.1 %conv_backward.15 = (bf16[8,512,768]{2,1,0:T(8,128)(2,1)}, f32[24,768]{1,0:T(8,128)}, bf16[4,1376,768]{2,1,0:T(8,128)(2,1)}) custom-call(s32[60]{0:T(128)S(1)} %get-tuple-element.248.rows_ref, s32[32]{0:T(128)S(1)} %get-tuple-element.249.counts_ref, ...), custom_call_target="tpu_custom_call", output_to_operand_aliasing={{2}: (11, {}), {0}: (12, {})} | custom-call | flops 8153726976 | bytes 52428800 | tf_op jit(solution)/shard_map/cond/branch_1_fun/conv_backward/pallas_call | solution.py:1407
  1015.7 9.1 all-to-all-done.22.refs_0_
  1024.7 19.4 %all-to-all-start.23 = ((bf16[8,512,768]{2,1,0:T(8,128)(2,1)}), bf16[8,512,768]{2,1,0:T(8,128)(2,1)}, u32[]{:S(2)}, u32[]{:S(2)}) async-start(bf16[8,512,768]{2,1,0:T(8,128)(2,1)} %after.13), calls=%async_computation.27 | async-start | bytes 12582912 | tf_op jit(solution)/shard_map/cond/branch_1_fun/all_to_all | solution.py:1619
  1044.2 71.7 %all-to-all-done.23.refs_1_ = bf16[8,512,768]{2,1,0:T(8,128)(2,1)} async-done(((bf16[8,512,768]{2,1,0:T(8,128)(2,1)}), bf16[8,512,768]{2,1,0:T(8,128)(2,1)}, u32[]{:S(2)}, u32[]{:S(2)}) %all-to-all-start.23) | async-done | bytes 6291488 | tf_op jit(solution)/shard_map/cond/branch_1_fun/all_to_all | solution.py:1619
  1115.8 4.8 all-to-all-start.25
  1120.6 71.5 %all-to-all-done.25.refs_1_ = bf16[8,512,768]{2,1,0:T(8,128)(2,1)} async-done(((bf16[8,512,768]{2,1,0:T(8,128)(2,1)}), bf16[8,512,768]{2,1,0:T(8,128)(2,1)}, u32[]{:S(2)}, u32[]{:S(2)}) %all-to-all-start.25) | async-done | bytes 6291488 | tf_op jit(solution)/shard_map/cond/branch_1_fun/all_to_all | solution.py:1619
  1192.2 4.8 all-to-all-start.24
  1197.0 6.0 finish_rest.6
  1203.0 4.6 finish_feed.6
  1207.6 7.9 outputs.3.refs_6_
  1215.6 8.0 copy.327
  1228.1 5.1 copy.312
  1237.6 31.0 %all-to-all-done.24.refs_0_ = bf16[8,512,768]{2,1,0:T(8,128)(2,1)} async-done(((bf16[8,512,768]{2,1,0:T(8,128)(2,1)}), bf16[8,512,768]{2,1,0:T(8,128)(2,1)}, u32[]{:S(2)}, u32[]{:S(2)}) %all-to-all-start.24) | async-done | bytes 6291488 | tf_op jit(solution)/shard_map/cond/branch_1_fun/all_to_all | solution.py:1619
  1268.6 8.0 input_grad.3.refs_7_
  1276.6 8.0 copy.328
  1284.7 6.0 finish_rest.7
  (179 shorter events, 76.1 us)
Async XLA Ops:
  11.1 60.0 %copy-start.38 = (s32[32]{0:T(128)}, s32[32]{0:T(128)S(1)}, u32[]{:S(2)}) copy-start(s32[32]{0:T(128)S(1)} %get-tuple-element.405.table_ref) | copy-start | bytes 388
  13.2 9.8 all-to-all-start.26
  22.9 76.4 %all-to-all-start.27 = ((bf16[8,512,768]{2,1,0:T(8,128)(2,1)}), bf16[8,512,768]{2,1,0:T(8,128)(2,1)}, u32[]{:S(2)}, u32[]{:S(2)}) async-start(bf16[8,512,768]{2,1,0:T(8,128)(2,1)} %send_inputs.2), calls=%async_computation.35 | async-start | bytes 12582912 | tf_op jit(solution)/shard_map/all_to_all | solution.py:1619
  75.7 28.4 %copy-start.36 = (bf16[2,1,5,768]{3,0,2,1:T(2,128)(2,1)S(1)}, bf16[2,1,5,768]{3,0,2,1:T(2,128)(2,1)}, u32[]{:S(2)}) copy-start(bf16[2,1,5,768]{3,0,2,1:T(2,128)(2,1)} %param.21) | copy-start | bytes 46084
  75.7 28.5 %copy-start.37 = (bf16[2,1,5,768]{3,0,2,1:T(2,128)(2,1)S(1)}, bf16[2,1,5,768]{3,0,2,1:T(2,128)(2,1)}, u32[]{:S(2)}) copy-start(bf16[2,1,5,768]{3,0,2,1:T(2,128)(2,1)} %param.22) | copy-start | bytes 46084
  75.7 28.6 %copy-start.26 = (bf16[2,1,15,768]{3,0,2,1:T(2,128)(2,1)S(1)}, bf16[2,1,15,768]{3,0,2,1:T(2,128)(2,1)}, u32[]{:S(2)}) copy-start(bf16[2,1,15,768]{3,0,2,1:T(2,128)(2,1)} %param.19) | copy-start | bytes 138244
  75.7 28.7 %copy-start.58 = (s32[33]{0:T(128)S(1)}, s32[33]{0:T(128)}, u32[]{:S(2)}) copy-start(s32[33]{0:T(128)} %psum.7.refs_1_) | copy-start | bytes 400
  99.3 76.4 %all-to-all-start.28 = ((bf16[8,512,768]{2,1,0:T(8,128)(2,1)}), bf16[8,512,768]{2,1,0:T(8,128)(2,1)}, u32[]{:S(2)}, u32[]{:S(2)}) async-start(bf16[8,512,768]{2,1,0:T(8,128)(2,1)} %send_inputs.3), calls=%async_computation.36 | async-start | bytes 12582912 | tf_op jit(solution)/shard_map/all_to_all | solution.py:1619
  156.3 19.4 %copy-start.39 = (s32[32]{0:T(128)S(1)}, s32[32]{0:T(128)}, u32[]{:S(2)}) copy-start(s32[32]{0:T(128)} %copy-done.38) | copy-start | bytes 388
  183.0 38.1 %copy-start.17 = (f32[16,768]{1,0:T(8,128)}, f32[16,768]{1,0:T(8,128)S(1)}, u32[]{:S(2)}) copy-start(f32[16,768]{1,0:T(8,128)S(1)} %get-tuple-element.254.taps_ref) | copy-start | bytes 147460 | tf_op jit(solution)/shard_map/cond
  183.0 38.1 %copy-start.21 = (f32[8,768]{1,0:T(8,128)}, f32[8,768]{1,0:T(8,128)S(1)}, u32[]{:S(2)}) copy-start(f32[8,768]{1,0:T(8,128)S(1)} %get-tuple-element.255.gain) | copy-start | bytes 73732 | tf_op jit(solution)/shard_map/cond
  183.1 300.1 %copy-start.42 = (s32[32]{0:T(128)}, s32[32]{0:T(128)S(1)}, u32[]{:S(2)}) copy-start(s32[32]{0:T(128)S(1)} %get-tuple-element.247.table_ref) | copy-start | bytes 388 | tf_op jit(solution)/shard_map/cond
  183.1 76.4 %all-to-all-start.14 = ((bf16[8,512,768]{2,1,0:T(8,128)(2,1)}), bf16[8,512,768]{2,1,0:T(8,128)(2,1)}, u32[]{:S(2)}, u32[]{:S(2)}) async-start(bf16[8,512,768]{2,1,0:T(8,128)(2,1)} %get-tuple-element.251), calls=%async_computation.18 | async-start | bytes 12582912 | tf_op jit(solution)/shard_map/cond/branch_1_fun/all_to_all | solution.py:1619
  207.9 13.2 %copy-start.8 = (bf16[4,512,768]{2,1,0:T(8,128)(2,1)}, bf16[4,512,768]{2,1,0:T(8,128)(2,1)S(1)}, u32[]{:S(2)}) copy-start(bf16[4,512,768]{2,1,0:T(8,128)(2,1)S(1)} %get-tuple-element.331.zn_ref) | copy-start | bytes 9437188 | tf_op jit(solution)/shard_map/cond
  343.8 76.6 %all-to-all-start.16 = ((bf16[8,512,768]{2,1,0:T(8,128)(2,1)}), bf16[8,512,768]{2,1,0:T(8,128)(2,1)}, u32[]{:S(2)}, u32[]{:S(2)}) async-start(bf16[8,512,768]{2,1,0:T(8,128)(2,1)} %hop_x.4), calls=%async_computation.20 | async-start | bytes 12582912 | tf_op jit(solution)/shard_map/cond/branch_1_fun/all_to_all | solution.py:1619
  353.4 10.9 copy-start.60
  420.4 76.6 %all-to-all-start.18 = ((bf16[8,512,768]{2,1,0:T(8,128)(2,1)}), bf16[8,512,768]{2,1,0:T(8,128)(2,1)}, u32[]{:S(2)}, u32[]{:S(2)}) async-start(bf16[8,512,768]{2,1,0:T(8,128)(2,1)} %send_cotangent.7), calls=%async_computation.22 | async-start | bytes 12582912 | tf_op jit(solution)/shard_map/cond/branch_1_fun/all_to_all | solution.py:1619
  497.0 76.4 %all-to-all-start.17 = ((bf16[8,512,768]{2,1,0:T(8,128)(2,1)}), bf16[8,512,768]{2,1,0:T(8,128)(2,1)}, u32[]{:S(2)}, u32[]{:S(2)}) async-start(bf16[8,512,768]{2,1,0:T(8,128)(2,1)} %send_cotangent.6), calls=%async_computation.21 | async-start | bytes 12582912 | tf_op jit(solution)/shard_map/cond/branch_1_fun/all_to_all | solution.py:1619
  501.8 389.6 %reduce-scatter.17.cloned.1.call-start = ((), (), s32[]{:S(2)}) async-start(), calls=%async_computation.41 | async-start | bytes 11796480 | tf_op jit(solution)/shard_map/cond/branch_1_fun/reduce_scatter | solution.py:1623
  620.9 103.8 %all-to-all-start.19 = ((bf16[8,512,768]{2,1,0:T(8,128)(2,1)}), bf16[8,512,768]{2,1,0:T(8,128)(2,1)}, u32[]{:S(2)}, u32[]{:S(2)}) async-start(bf16[8,512,768]{2,1,0:T(8,128)(2,1)} %hop_dx.3), calls=%async_computation.23 | async-start | bytes 12582912 | tf_op jit(solution)/shard_map/cond/branch_1_fun/all_to_all | solution.py:1619
  625.9 418.3 %reduce-scatter.21.cloned.1.call-start = ((), (), s32[]{:S(2)}) async-start(), calls=%async_computation.43 | async-start | bytes 10567680 | tf_op jit(solution)/shard_map/cond/branch_1_fun/reduce_scatter | solution.py:1623
  625.9 65.2 %copy-start.50 = (f32[8,768]{1,0:T(8,128)S(1)}, f32[8,768]{1,0:T(8,128)}, u32[]{:S(2)}) copy-start(f32[8,768]{1,0:T(8,128)} %get-tuple-element.344) | copy-start | bytes 73732 | tf_op jit(solution)/shard_map/cond
  625.9 66.2 %copy-start.46 = (f32[8,768]{1,0:T(8,128)S(1)}, f32[8,768]{1,0:T(8,128)}, u32[]{:S(2)}) copy-start(f32[8,768]{1,0:T(8,128)} %get-tuple-element.346) | copy-start | bytes 73732 | tf_op jit(solution)/shard_map/cond
  692.3 30.4 %copy-start.32 = (f32[24,768]{1,0:T(8,128)S(1)}, f32[24,768]{1,0:T(8,128)}, u32[]{:S(2)}) copy-start(f32[24,768]{1,0:T(8,128)} %get-tuple-element.342) | copy-start | bytes 221188 | tf_op jit(solution)/shard_map/cond
  810.3 76.4 %all-to-all-start.21 = ((bf16[8,512,768]{2,1,0:T(8,128)(2,1)}), bf16[8,512,768]{2,1,0:T(8,128)(2,1)}, u32[]{:S(2)}, u32[]{:S(2)}) async-start(bf16[8,512,768]{2,1,0:T(8,128)(2,1)} %hop_dx.5), calls=%async_computation.25 | async-start | bytes 12582912 | tf_op jit(solution)/shard_map/cond/branch_1_fun/all_to_all | solution.py:1619
  815.2 4.7 copy-start.22
  815.2 305.4 %reduce-scatter.19.cloned.1.call-start = ((), (), s32[]{:S(2)}) async-start(), calls=%async_computation.42 | async-start | bytes 11796480 | tf_op jit(solution)/shard_map/cond/branch_1_fun/reduce_scatter | solution.py:1623
  819.8 28.6 %copy-start.18 = (f32[16,768]{1,0:T(8,128)S(1)}, f32[16,768]{1,0:T(8,128)}, u32[]{:S(2)}) copy-start(f32[16,768]{1,0:T(8,128)} %copy-done.17) | copy-start | bytes 147460 | tf_op jit(solution)/shard_map/cond
  881.1 10.3 copy-start.9
  934.1 19.0 %copy-start.62 = (f32[3,512,128]{2,1,0:T(8,128)S(1)}, f32[3,512,128]{2,1,0:T(8,128)}, u32[]{:S(2)}) copy-start(f32[3,512,128]{2,1,0:T(8,128)} %get-tuple-element.326.rstd_ref) | copy-start | bytes 2359300 | tf_op jit(solution)/shard_map/cond
  934.1 90.6 %all-to-all-start.22 = ((bf16[8,512,768]{2,1,0:T(8,128)(2,1)}), bf16[8,512,768]{2,1,0:T(8,128)(2,1)}, u32[]{:S(2)}, u32[]{:S(2)}) async-start(bf16[8,512,768]{2,1,0:T(8,128)(2,1)} %after.12), calls=%async_computation.26 | async-start | bytes 12582912 | tf_op jit(solution)/shard_map/cond/branch_1_fun/all_to_all | solution.py:1619
  953.0 331.6 %reduce-scatter.23.cloned.1.call-start = ((), (), s32[]{:S(2)}) async-start(), calls=%async_computation.44 | async-start | bytes 10567680 | tf_op jit(solution)/shard_map/cond/branch_1_fun/reduce_scatter | solution.py:1623
  953.1 27.2 %copy-start.51 = (f32[8,768]{1,0:T(8,128)S(1)}, f32[8,768]{1,0:T(8,128)}, u32[]{:S(2)}) copy-start(f32[8,768]{1,0:T(8,128)} %get-tuple-element.350) | copy-start | bytes 73732 | tf_op jit(solution)/shard_map/cond
  953.1 28.2 %copy-start.48 = (f32[8,768]{1,0:T(8,128)S(1)}, f32[8,768]{1,0:T(8,128)}, u32[]{:S(2)}) copy-start(f32[8,768]{1,0:T(8,128)} %get-tuple-element.352) | copy-start | bytes 73732 | tf_op jit(solution)/shard_map/cond
  953.1 28.4 %copy-start.11 = (f32[9,512,128]{2,1,0:T(8,128)S(1)}, f32[9,512,128]{2,1,0:T(8,128)}, u32[]{:S(2)}) copy-start(f32[9,512,128]{2,1,0:T(8,128)} %get-tuple-element.313.rstd_ref) | copy-start | bytes 7077892 | tf_op jit(solution)/shard_map/cond
  981.5 32.1 %copy-start.33 = (f32[24,768]{1,0:T(8,128)S(1)}, f32[24,768]{1,0:T(8,128)}, u32[]{:S(2)}) copy-start(f32[24,768]{1,0:T(8,128)} %get-tuple-element.348) | copy-start | bytes 221188 | tf_op jit(solution)/shard_map/cond
  1024.7 91.1 %all-to-all-start.23 = ((bf16[8,512,768]{2,1,0:T(8,128)(2,1)}), bf16[8,512,768]{2,1,0:T(8,128)(2,1)}, u32[]{:S(2)}, u32[]{:S(2)}) async-start(bf16[8,512,768]{2,1,0:T(8,128)(2,1)} %after.13), calls=%async_computation.27 | async-start | bytes 12582912 | tf_op jit(solution)/shard_map/cond/branch_1_fun/all_to_all | solution.py:1619
  1115.8 76.4 %all-to-all-start.25 = ((bf16[8,512,768]{2,1,0:T(8,128)(2,1)}), bf16[8,512,768]{2,1,0:T(8,128)(2,1)}, u32[]{:S(2)}, u32[]{:S(2)}) async-start(bf16[8,512,768]{2,1,0:T(8,128)(2,1)} %after.15), calls=%async_computation.32 | async-start | bytes 12582912 | tf_op jit(solution)/shard_map/cond/branch_1_fun/all_to_all | solution.py:1619
  1120.6 76.4 %copy-start.30 = (f32[2,8]{1,0:T(2,128)S(1)}, f32[2,8]{1,0:T(2,128)}, u32[]{:S(2)}) copy-start(f32[2,8]{1,0:T(2,128)} %get-tuple-element.353.count_ref) | copy-start | bytes 196 | tf_op jit(solution)/shard_map/cond
  1192.2 76.4 %all-to-all-start.24 = ((bf16[8,512,768]{2,1,0:T(8,128)(2,1)}), bf16[8,512,768]{2,1,0:T(8,128)(2,1)}, u32[]{:S(2)}, u32[]{:S(2)}) async-start(bf16[8,512,768]{2,1,0:T(8,128)(2,1)} %after.14), calls=%async_computation.30 | async-start | bytes 12582912 | tf_op jit(solution)/shard_map/cond/branch_1_fun/all_to_all | solution.py:1619
  1197.0 10.6 copy-start.43
  1228.1 5.1 slice-start.2
  1228.1 5.1 slice-start.3
  1290.6 4.1 copy-start.1
  1290.6 4.1 copy-start.28
  1290.6 2.1 copy-start.5
  1290.6 2.2 copy-start.25
  1290.6 3.6 copy-start.3
  1298.0 2.2 copy-start.12
  1298.0 3.3 copy-start.13
  1298.0 4.4 copy-start.14
  1298.0 4.7 copy-start.23
  1298.0 4.7 copy-start.44
  1298.0 4.6 copy-start.54
  1298.1 4.6 copy-start.55
Sparse Core Ops, SparseCore 0:
  616.5 182.8 reduce-scatter.16
  802.3 146.3 reduce-scatter.20
  951.6 162.0 reduce-scatter.18
  1115.9 146.3 reduce-scatter.22

commit v8 on v7

--- a/solution.py
+++ b/solution.py
@@ -1760,18 +1760,22 @@
         feeds = finish_feed(0, feed0, totals, *feeds, feed_shapes)
         rests = finish_rest(0, rest0, totals, rests, rest_shapes, (outputs, input_grad, feeds[0]))
         qkv, out, taps, point, gain, shift = rests
-        taps, gain, shift = (rows.transpose(0, 2, 1, 3) for rows in (taps, gain, shift))
         return (outputs, input_grad, qkv, out, *feeds, taps, point, gain, shift)
 
+    def in_place(results):
+        turned = [rows.transpose(0, 2, 1, 3) if n in (6, 8, 9) else rows for n, rows in enumerate(results)]
+        return tuple(turned)
+
     if not routed:
-        return after_first(home_there, home_back, x0, first)
-    return lax.cond(
+        return in_place(after_first(home_there, home_back, x0, first))
+    results = lax.cond(
         lost[0] == 0,
         lambda x0, first: after_first(straight_there, straight_back, x0, first),
         lambda x0, first: after_first(home_there, home_back, x0, first),
         x0,
         first,
     )
+    return in_place(results)
 
 
 def solution(mesh):

time: 1330 us -> 1300 us (0.977)
  local copies, waits for them, and re-layouts: 44.8 us -> 7.54 us
  waiting for transfers between devices: 293 us -> 310 us
  Pallas kernels: 684 us -> 700 us
    cond x62 -> x36, local copies, waits for them, and re-layouts: 32.7 us -> 0.08 us
    pallas_call x4, Pallas kernels: 128 us -> 107 us  [conv_backward(): pl.pallas_call(kernel, grid_spec=pltpu.PrefetchScalarGridSpec(num_scalar_...]
    pallas_call x4, Pallas kernels: 132 us -> 152 us  [attention_backward(): pl.pallas_call(kernel, grid_spec=pltpu.PrefetchScalarGridSpec(num_scalar_...]
    pallas_call x4, Pallas kernels: 80.2 us -> 98.6 us  [feed_forward(): pl.pallas_call(kernel, grid_spec=pltpu.PrefetchScalarGridSpec(num_scalar_...]
    all_to_all x13, waiting for transfers between devices: 292 us -> 309 us  [exchange(): return lax.all_to_all(rows, 'op', split_axis=0, concat_axis=0, tiled=True)]
  transfers between devices with their start and end apart: 17 -> 17, of which waited for: 11 -> 10; matrix products, arithmetic and copies ran while one was open for 3% -> 1% of each run, Pallas kernels for 48% -> 49%
where the time goes in v8:
time: 1300 us; the launch traced here: 1290 us
  Pallas kernels  700 us (54%)
  waiting for transfers between devices  310 us (24%)
  blocking collectives  163 us (13%)
  starting transfers between devices  78.8 us (6%)
  between operations  14.3 us (1%)
    all_to_all x13, waiting for transfers between devices, exchange(): return lax.all_to_all(rows, 'op', split_axis=0, concat_axis=0, tiled=True)  309 us
    all_to_all x2, blocking collectives, exchange(): return lax.all_to_all(rows, 'op', split_axis=0, concat_axis=0, tiled=True)  154 us
    pallas_call x4, Pallas kernels, attention_backward(): pl.pallas_call(kernel, grid_spec=pltpu.PrefetchScalarGridSpec(num_scalar_...  152 us
    pallas_call x4, Pallas kernels, conv_backward(): pl.pallas_call(kernel, grid_spec=pltpu.PrefetchScalarGridSpec(num_scalar_...  107 us
    pallas_call x4, Pallas kernels, feed_forward(): pl.pallas_call(kernel, grid_spec=pltpu.PrefetchScalarGridSpec(num_scalar_...  98.6 us
    pallas_call x2, Pallas kernels, feed_backward(): pl.pallas_call(kernel, grid_spec=pltpu.PrefetchScalarGridSpec(num_scalar_...  96.7 us
    all_to_all x13, starting transfers between devices, exchange(): return lax.all_to_all(rows, 'op', split_axis=0, concat_axis=0, tiled=True)  78.7 us
    pallas_call x4, Pallas kernels, attention_forward(): pl.pallas_call(kernel, grid_spec=pltpu.PrefetchScalarGridSpec(num_scalar_...  64.6 us
  transfers between devices with their start and end apart: 17, of which 10 were waited for; matrix products, arithmetic and copies ran while one was open for 1% of the time, Pallas kernels for 49%

profile of v8, /device:TPU:0, one launch (start us, length us, event | category | flops | bytes accessed | tf_op | source)
XLA Modules:
  0.0 1287.2 jit_solution(13093923171127784789)
XLA Ops:
  13.2 5.2 all-to-all-start.26
  18.4 4.5 send_inputs.2
  22.9 4.8 all-to-all-start.27
  31.0 16.4 %route_tables.1 = (s32[80]{0:T(128)S(1)}, s32[1]{0:T(128)}) custom-call(s32[192]{0:T(256)} %reshape.117.refs_0_, s32[1]{0:T(128)} %bitcast.14.refs_1_), custom_call_target="tpu_custom_call" | custom-call | tf_op jit(solution)/shard_map/route_tables/pallas_call | solution.py:371
  48.1 9.3 psum.7.refs_1_
  57.4 4.5 send_inputs.3
  62.0 37.3 %all-to-all-done.27.x_ref = bf16[8,512,768]{2,1,0:T(8,128)(2,1)} async-done(((bf16[8,512,768]{2,1,0:T(8,128)(2,1)}), bf16[8,512,768]{2,1,0:T(8,128)(2,1)}, u32[]{:S(2)}, u32[]{:S(2)}) %all-to-all-start.27) | async-done | bytes 6291488 | tf_op jit(solution)/shard_map/all_to_all | solution.py:1619
  99.3 4.8 all-to-all-start.28
  105.2 20.1 %feed_forward.13 = (bf16[8,512,768]{2,1,0:T(8,128)(2,1)}, bf16[4,512,3072]{2,1,0:T(8,128)(2,1)}, bf16[4,512,3072]{2,1,0:T(8,128)(2,1)}, bf16[4,512,768]{2,1,0:T(8,128)(2,1)S(1)}, f32[4,512,128]{2,1,0:T(8,128)}) custom-call(s32[60]{0:T(128)S(1)} %get-tuple-element.414.rows_ref, s32[32]{0:T(128)S(1)} %get-tuple-element.413.counts_ref, ...), custom_call_target="tpu_custom_call" | custom-call | flops 14495514624 | bytes 41943040 | tf_op jit(solution)/shard_map/feed_forward/pallas_call | solution.py:927
  125.3 26.9 %attention_forward.13 = (bf16[8,512,768]{2,1,0:T(8,128)(2,1)}, bf16[3,512,2304]{2,1,0:T(8,128)(2,1)}, bf16[3,512,768]{2,1,0:T(8,128)(2,1)}, bf16[3,512,768]{2,1,0:T(8,128)(2,1)}, f32[3,512,128]{2,1,0:T(8,128)}) custom-call(s32[60]{0:T(128)S(1)} %get-tuple-element.414.rows_ref, s32[32]{0:T(128)S(1)} %get-tuple-element.413.counts_ref, ...), custom_call_target="tpu_custom_call", output_to_operand_aliasing={{0}: (7, {})} | custom-call | flops 19327352832 | bytes 31457280 | tf_op jit(solution)/shard_map/attention_forward/pallas_call | solution.py:627
  152.2 13.5 %conv_forward.13 = (bf16[8,512,768]{2,1,0:T(8,128)(2,1)}, bf16[9,512,768]{2,1,0:T(8,128)(2,1)}, bf16[9,512,768]{2,1,0:T(8,128)(2,1)}, f32[9,512,128]{2,1,0:T(8,128)}) custom-call(s32[60]{0:T(128)S(1)} %get-tuple-element.414.rows_ref, s32[32]{0:T(128)S(1)} %get-tuple-element.413.counts_ref, ...), custom_call_target="tpu_custom_call", output_to_operand_aliasing={{0}: (7, {})} | custom-call | flops 5435817984 | bytes 37748736 | tf_op jit(solution)/shard_map/conv_forward/pallas_call | solution.py:1258
  165.7 4.6 hop_x.5
  170.3 5.4 all-to-all-done.28
  175.7 1104.7 %conditional.1 = (bf16[12,512,768]{2,1,0:T(8,128)(2,1)}, bf16[12,512,768]{2,1,0:T(8,128)(2,1)}, f32[2,1,192,2304]{3,2,1,0:T(8,128)}, f32[2,1,192,768]{3,2,1,0:T(...) conditional(s32[]{:T(128)} %bitcast.15, ...), branch_computations={%region_2.7_spmd, %region_7.12_spmd} | conditional | flops 278434742272 | bytes 1436570368 | solution.py:1771
  183.1 4.8 all-to-all-start.14
  187.8 28.9 %feed_forward.10 = (bf16[8,512,768]{2,1,0:T(8,128)(2,1)}, bf16[4,512,3072]{2,1,0:T(8,128)(2,1)}, bf16[4,512,3072]{2,1,0:T(8,128)(2,1)}, bf16[4,512,768]{2,1,0:T(8,128)(2,1)S(1)}, f32[4,512,128]{2,1,0:T(8,128)}) custom-call(s32[60]{0:T(128)S(1)} %get-tuple-element.248.rows_ref, ...), custom_call_target="tpu_custom_call", output_to_operand_aliasing={{1}: (7, {}), {2}: (8, {}), {3}: (9, {}), {4}: (10, {})} | custom-call | flops 14495514624 | bytes 41943040 | tf_op jit(solution)/shard_map/cond/branch_1_fun/feed_forward/pallas_call | solution.py:927
  216.7 5.9 attention_forward.10
  222.6 16.9 %conv_forward.10 = (bf16[8,512,768]{2,1,0:T(8,128)(2,1)}, bf16[9,512,768]{2,1,0:T(8,128)(2,1)}, bf16[9,512,768]{2,1,0:T(8,128)(2,1)}, f32[9,512,128]{2,1,0:T(8,128)}) custom-call(s32[60]{0:T(128)S(1)} %get-tuple-element.248.rows_ref, s32[32]{0:T(128)S(1)} %get-tuple-element.249.counts_ref, ...), custom_call_target="tpu_custom_call", output_to_operand_aliasing={{0}: (7, {})} | custom-call | flops 5435817984 | bytes 37748736 | tf_op jit(solution)/shard_map/cond/branch_1_fun/conv_forward/pallas_call | solution.py:1258
  239.6 19.9 %all-to-all-done.14.refs_0_ = bf16[8,512,768]{2,1,0:T(8,128)(2,1)} async-done(((bf16[8,512,768]{2,1,0:T(8,128)(2,1)}), bf16[8,512,768]{2,1,0:T(8,128)(2,1)}, u32[]{:S(2)}, u32[]{:S(2)}) %all-to-all-start.14) | async-done | bytes 6291488 | tf_op jit(solution)/shard_map/cond/branch_1_fun/all_to_all | solution.py:1619
  262.7 76.9 %all_to_all.126.refs_1_ = bf16[8,512,768]{2,1,0:T(8,128)(2,1)} all-to-all(bf16[8,512,768]{2,1,0:T(8,128)(2,1)} %hop_x.3), channel_id=1, replica_groups=mesh['dp'=4,'op'=8] {'op'}, dimensions={0} | all-to-all | bytes 12582912 | tf_op jit(solution)/shard_map/cond/branch_1_fun/all_to_all | solution.py:1619
  343.3 4.9 all-to-all-start.16
  348.2 4.6 land_x.2.x_ref.x_ref0
  352.8 20.5 %feed_forward.11 = (bf16[8,512,768]{2,1,0:T(8,128)(2,1)}, bf16[4,512,3072]{2,1,0:T(8,128)(2,1)}, bf16[4,512,3072]{2,1,0:T(8,128)(2,1)}, bf16[4,512,768]{2,1,0:T(8,128)(2,1)}, f32[4,512,128]{2,1,0:T(8,128)}) custom-call(s32[60]{0:T(128)S(1)} %get-tuple-element.248.rows_ref, s32[32]{0:T(128)S(1)} %get-tuple-element.249.counts_ref, ...), custom_call_target="tpu_custom_call" | custom-call | flops 14495514624 | bytes 41943040 | tf_op jit(solution)/shard_map/cond/branch_1_fun/feed_forward/pallas_call | solution.py:927
  373.3 19.4 %attention_forward.11 = (bf16[8,512,768]{2,1,0:T(8,128)(2,1)}, bf16[3,512,2304]{2,1,0:T(8,128)(2,1)}, bf16[3,512,768]{2,1,0:T(8,128)(2,1)}, bf16[3,512,768]{2,1,0:T(8,128)(2,1)}, f32[3,512,128]{2,1,0:T(8,128)}) custom-call(s32[60]{0:T(128)S(1)} %get-tuple-element.248.rows_ref, s32[32]{0:T(128)S(1)} %get-tuple-element.249.counts_ref, ...), custom_call_target="tpu_custom_call", output_to_operand_aliasing={{0}: (7, {})} | custom-call | flops 19327352832 | bytes 31457280 | tf_op jit(solution)/shard_map/cond/branch_1_fun/attention_forward/pallas_call | solution.py:627
  392.8 16.3 %conv_forward.11 = (bf16[8,512,768]{2,1,0:T(8,128)(2,1)}, bf16[9,512,768]{2,1,0:T(8,128)(2,1)}, bf16[9,512,768]{2,1,0:T(8,128)(2,1)}, f32[9,512,128]{2,1,0:T(8,128)}) custom-call(s32[60]{0:T(128)S(1)} %get-tuple-element.248.rows_ref, s32[32]{0:T(128)S(1)} %get-tuple-element.249.counts_ref, ...), custom_call_target="tpu_custom_call", output_to_operand_aliasing={{0}: (7, {})} | custom-call | flops 5435817984 | bytes 37748736 | tf_op jit(solution)/shard_map/cond/branch_1_fun/conv_forward/pallas_call | solution.py:1258
  409.1 4.5 send_cotangent.7
  413.6 6.2 all-to-all-done.16.refs_0_
  419.8 5.0 all-to-all-start.18
  424.9 4.6 land_x.3.x_ref.x_ref1
  429.4 29.1 %feed_forward.12 = (bf16[8,512,768]{2,1,0:T(8,128)(2,1)}, bf16[4,512,3072]{2,1,0:T(8,128)(2,1)}, bf16[4,512,3072]{2,1,0:T(8,128)(2,1)}, bf16[4,512,768]{2,1,0:T(8,128)(2,1)}, f32[4,512,128]{2,1,0:T(8,128)}) custom-call(s32[60]{0:T(128)S(1)} %get-tuple-element.248.rows_ref, ...), custom_call_target="tpu_custom_call", output_to_operand_aliasing={{1}: (7, {}), {2}: (8, {}), {3}: (9, {}), {4}: (10, {})} | custom-call | flops 14495514624 | bytes 41943040 | tf_op jit(solution)/shard_map/cond/branch_1_fun/feed_forward/pallas_call | solution.py:927
  458.5 12.4 attention_forward.12
  471.0 15.3 %conv_forward.12 = (bf16[8,512,768]{2,1,0:T(8,128)(2,1)}, bf16[9,512,768]{2,1,0:T(8,128)(2,1)}, bf16[9,512,768]{2,1,0:T(8,128)(2,1)}, f32[9,512,128]{2,1,0:T(8,128)}) custom-call(s32[60]{0:T(128)S(1)} %get-tuple-element.248.rows_ref, s32[32]{0:T(128)S(1)} %get-tuple-element.249.counts_ref, ...), custom_call_target="tpu_custom_call", output_to_operand_aliasing={{0}: (7, {})} | custom-call | flops 5435817984 | bytes 37748736 | tf_op jit(solution)/shard_map/cond/branch_1_fun/conv_forward/pallas_call | solution.py:1258
  486.3 4.6 send_cotangent.6
  490.9 5.6 all-to-all-done.18.dy_ref.dy_ref1
  496.5 4.7 all-to-all-start.17
  501.3 28.5 %attention_backward.12 = (bf16[8,512,768]{2,1,0:T(8,128)(2,1)}, f32[8,768]{1,0:T(8,128)}, f32[768,2304]{1,0:T(8,128)}, f32[768,768]{1,0:T(8,128)}) custom-call(s32[60]{0:T(128)S(1)} %get-tuple-element.248.rows_ref, s32[32]{0:T(128)S(1)} %get-tuple-element.249.counts_ref, bf16[8,512,768]{2,1,0:T(8,128)(2,1)} %land_x.3.x_ref.x_ref1, ...), custom_call_target="tpu_custom_call" | custom-call | flops 19327352832 | bytes 41943040 | tf_op jit(solution)/shard_map/cond/branch_1_fun/attention_backward/pallas_call | solution.py:818
  529.8 25.6 %conv_backward.12 = (bf16[8,512,768]{2,1,0:T(8,128)(2,1)}, f32[24,768]{1,0:T(8,128)}, f32[3,768,768]{2,1,0:T(8,128)}) custom-call(s32[60]{0:T(128)S(1)} %get-tuple-element.248.rows_ref, s32[32]{0:T(128)S(1)} %get-tuple-element.249.counts_ref, bf16[8,512,768]{2,1,0:T(8,128)(2,1)} %land_x.3.x_ref.x_ref1, ...), custom_call_target="tpu_custom_call", output_to_operand_aliasing={{0}: (10, {})} | custom-call | flops 8153726976 | bytes 52428800 | tf_op jit(solution)/shard_map/cond/branch_1_fun/conv_backward/pallas_call | solution.py:1407
  555.4 17.4 %all-to-all-done.17.dy_ref0.dy_ref = bf16[8,512,768]{2,1,0:T(8,128)(2,1)} async-done(((bf16[8,512,768]{2,1,0:T(8,128)(2,1)}), bf16[8,512,768]{2,1,0:T(8,128)(2,1)}, u32[]{:S(2)}, u32[]{:S(2)}) %all-to-all-start.17) | async-done | bytes 6291488 | tf_op jit(solution)/shard_map/cond/branch_1_fun/all_to_all | solution.py:1619
  572.8 48.5 %feed_backward.6 = (f32[8,768]{1,0:T(8,128)}, bf16[8,512,768]{2,1,0:T(8,128)(2,1)}, bf16[8,512,768]{2,1,0:T(8,128)(2,1)}, bf16[4,1536,768]{2,1,0:T(8,128)(2,1)}) custom-call(s32[60]{0:T(128)S(1)} %get-tuple-element.248.rows_ref, s32[32]{0:T(128)S(1)} %get-tuple-element.249.counts_ref, ...), custom_call_target="tpu_custom_call", output_to_operand_aliasing={{2}: (13, {})} | custom-call | flops 25367150592 | bytes 52428800 | tf_op jit(solution)/shard_map/cond/branch_1_fun/feed_backward/pallas_call | solution.py:1137
  621.3 4.6 hop_dx.3
  625.9 14.1 %all-to-all-start.19 = ((bf16[8,512,768]{2,1,0:T(8,128)(2,1)}), bf16[8,512,768]{2,1,0:T(8,128)(2,1)}, u32[]{:S(2)}, u32[]{:S(2)}) async-start(bf16[8,512,768]{2,1,0:T(8,128)(2,1)} %hop_dx.3), calls=%async_computation.23 | async-start | bytes 12582912 | tf_op jit(solution)/shard_map/cond/branch_1_fun/all_to_all | solution.py:1619
  640.1 46.9 %attention_backward.13 = (bf16[8,512,768]{2,1,0:T(8,128)(2,1)}, f32[8,768]{1,0:T(8,128)}, bf16[4,1376,768]{2,1,0:T(8,128)(2,1)}) custom-call(s32[60]{0:T(128)S(1)} %get-tuple-element.248.rows_ref, s32[32]{0:T(128)S(1)} %get-tuple-element.249.counts_ref, bf16[8,512,768]{2,1,0:T(8,128)(2,1)} %land_x.2.x_ref.x_ref0, ...), custom_call_target="tpu_custom_call", output_to_operand_aliasing={{0}: (13, {})} | custom-call | flops 19327352832 | bytes 41943040 | tf_op jit(solution)/shard_map/cond/branch_1_fun/attention_backward/pallas_call | solution.py:818
  688.2 29.1 %conv_backward.13 = (bf16[8,512,768]{2,1,0:T(8,128)(2,1)}, f32[24,768]{1,0:T(8,128)}, bf16[4,1376,768]{2,1,0:T(8,128)(2,1)}) custom-call(s32[60]{0:T(128)S(1)} %get-tuple-element.248.rows_ref, s32[32]{0:T(128)S(1)} %get-tuple-element.249.counts_ref, bf16[8,512,768]{2,1,0:T(8,128)(2,1)} %land_x.2.x_ref.x_ref0, ...), custom_call_target="tpu_custom_call", output_to_operand_aliasing={{2}: (11, {}), {0}: (12, {})} | custom-call | flops 8153726976 | bytes 52428800 | tf_op jit(solution)/shard_map/cond/branch_1_fun/conv_backward/pallas_call | solution.py:1407
  722.8 76.9 %all_to_all.127.refs_1_ = bf16[8,512,768]{2,1,0:T(8,128)(2,1)} all-to-all(bf16[8,512,768]{2,1,0:T(8,128)(2,1)} %hop_dx.4), channel_id=1, replica_groups=mesh['dp'=4,'op'=8] {'op'}, dimensions={0} | all-to-all | bytes 12582912 | tf_op jit(solution)/shard_map/cond/branch_1_fun/all_to_all | solution.py:1619
  803.3 4.8 all-to-all-start.21
  808.1 5.4 land_dx.3.dy_ref.dy_ref1
  813.6 10.9 attention_backward.14
  824.5 28.8 %conv_backward.14 = (bf16[8,512,768]{2,1,0:T(8,128)(2,1)}, f32[24,768]{1,0:T(8,128)}, f32[3,768,768]{2,1,0:T(8,128)}) custom-call(s32[60]{0:T(128)S(1)} %get-tuple-element.248.rows_ref, s32[32]{0:T(128)S(1)} %get-tuple-element.249.counts_ref, bf16[8,512,768]{2,1,0:T(8,128)(2,1)} %get-tuple-element.252.x_ref.x_ref1, ...), custom_call_target="tpu_custom_call", output_to_operand_aliasing={{0}: (10, {})} | custom-call | flops 8153726976 | bytes 52428800 | tf_op jit(solution)/shard_map/cond/branch_1_fun/conv_backward/pallas_call | solution.py:1407
  853.3 26.3 %all-to-all-done.21.refs_0_ = bf16[8,512,768]{2,1,0:T(8,128)(2,1)} async-done(((bf16[8,512,768]{2,1,0:T(8,128)(2,1)}), bf16[8,512,768]{2,1,0:T(8,128)(2,1)}, u32[]{:S(2)}, u32[]{:S(2)}) %all-to-all-start.21) | async-done | bytes 6291488 | tf_op jit(solution)/shard_map/cond/branch_1_fun/all_to_all | solution.py:1619
  879.6 5.3 land_dx.2.refs_1_.dy_ref0.dy_ref
  885.0 48.2 %feed_backward.7 = (f32[8,768]{1,0:T(8,128)}, bf16[8,512,768]{2,1,0:T(8,128)(2,1)}, bf16[8,512,768]{2,1,0:T(8,128)(2,1)}, bf16[4,1536,768]{2,1,0:T(8,128)(2,1)}) custom-call(s32[60]{0:T(128)S(1)} %get-tuple-element.248.rows_ref, s32[32]{0:T(128)S(1)} %get-tuple-element.249.counts_ref, ...), custom_call_target="tpu_custom_call", output_to_operand_aliasing={{2}: (13, {})} | custom-call | flops 25367150592 | bytes 52428800 | tf_op jit(solution)/shard_map/cond/branch_1_fun/feed_backward/pallas_call | solution.py:1137
  933.3 11.3 all-to-all-start.22
  944.7 65.6 %attention_backward.15 = (bf16[8,512,768]{2,1,0:T(8,128)(2,1)}, f32[8,768]{1,0:T(8,128)}, bf16[4,1376,768]{2,1,0:T(8,128)(2,1)}) custom-call(s32[60]{0:T(128)S(1)} %get-tuple-element.248.rows_ref, s32[32]{0:T(128)S(1)} %get-tuple-element.249.counts_ref, bf16[8,512,768]{2,1,0:T(8,128)(2,1)} %get-tuple-element.310.x_ref0.x_ref, ...), custom_call_target="tpu_custom_call", output_to_operand_aliasing={{0}: (13, {})} | custom-call | flops 19327352832 | bytes 41943040 | tf_op jit(solution)/shard_map/cond/branch_1_fun/attention_backward/pallas_call | solution.py:818
  1011.4 23.2 %conv_backward.15 = (bf16[8,512,768]{2,1,0:T(8,128)(2,1)}, f32[24,768]{1,0:T(8,128)}, bf16[4,1376,768]{2,1,0:T(8,128)(2,1)}) custom-call(s32[60]{0:T(128)S(1)} %get-tuple-element.248.rows_ref, s32[32]{0:T(128)S(1)} %get-tuple-element.249.counts_ref, ...), custom_call_target="tpu_custom_call", output_to_operand_aliasing={{2}: (11, {}), {0}: (12, {})} | custom-call | flops 8153726976 | bytes 52428800 | tf_op jit(solution)/shard_map/cond/branch_1_fun/conv_backward/pallas_call | solution.py:1407
  1036.7 4.8 all-to-all-start.23
  1041.6 71.6 %all-to-all-done.23.refs_1_ = bf16[8,512,768]{2,1,0:T(8,128)(2,1)} async-done(((bf16[8,512,768]{2,1,0:T(8,128)(2,1)}), bf16[8,512,768]{2,1,0:T(8,128)(2,1)}, u32[]{:S(2)}, u32[]{:S(2)}) %all-to-all-start.23) | async-done | bytes 6291488 | tf_op jit(solution)/shard_map/cond/branch_1_fun/all_to_all | solution.py:1619
  1113.1 4.8 all-to-all-start.25
  1117.9 71.5 %all-to-all-done.25.refs_1_ = bf16[8,512,768]{2,1,0:T(8,128)(2,1)} async-done(((bf16[8,512,768]{2,1,0:T(8,128)(2,1)}), bf16[8,512,768]{2,1,0:T(8,128)(2,1)}, u32[]{:S(2)}, u32[]{:S(2)}) %all-to-all-start.25) | async-done | bytes 6291488 | tf_op jit(solution)/shard_map/cond/branch_1_fun/all_to_all | solution.py:1619
  1189.5 4.7 all-to-all-start.24
  1194.3 6.4 finish_rest.6
  1205.2 8.0 outputs.3.refs_6_
  1217.6 48.2 %all-to-all-done.24.refs_0_ = bf16[8,512,768]{2,1,0:T(8,128)(2,1)} async-done(((bf16[8,512,768]{2,1,0:T(8,128)(2,1)}), bf16[8,512,768]{2,1,0:T(8,128)(2,1)}, u32[]{:S(2)}, u32[]{:S(2)}) %all-to-all-start.24) | async-done | bytes 6291488 | tf_op jit(solution)/shard_map/cond/branch_1_fun/all_to_all | solution.py:1619
  1265.8 7.9 input_grad.3.refs_7_
  1273.8 6.4 finish_rest.7
  (138 shorter events, 40.5 us)
Async XLA Ops:
  11.1 46.3 %copy-start.24 = (s32[32]{0:T(128)}, s32[32]{0:T(128)S(1)}, u32[]{:S(2)}) copy-start(s32[32]{0:T(128)S(1)} %get-tuple-element.415.table_ref) | copy-start | bytes 388
  13.2 9.8 all-to-all-start.26
  22.9 76.4 %all-to-all-start.27 = ((bf16[8,512,768]{2,1,0:T(8,128)(2,1)}), bf16[8,512,768]{2,1,0:T(8,128)(2,1)}, u32[]{:S(2)}, u32[]{:S(2)}) async-start(bf16[8,512,768]{2,1,0:T(8,128)(2,1)} %send_inputs.2), calls=%async_computation.35 | async-start | bytes 12582912 | tf_op jit(solution)/shard_map/all_to_all | solution.py:1619
  62.0 42.1 %copy-start.22 = (bf16[2,1,5,768]{3,0,2,1:T(2,128)(2,1)S(1)}, bf16[2,1,5,768]{3,0,2,1:T(2,128)(2,1)}, u32[]{:S(2)}) copy-start(bf16[2,1,5,768]{3,0,2,1:T(2,128)(2,1)} %param.21) | copy-start | bytes 46084
  62.0 42.2 %copy-start.23 = (bf16[2,1,5,768]{3,0,2,1:T(2,128)(2,1)S(1)}, bf16[2,1,5,768]{3,0,2,1:T(2,128)(2,1)}, u32[]{:S(2)}) copy-start(bf16[2,1,5,768]{3,0,2,1:T(2,128)(2,1)} %param.22) | copy-start | bytes 46084
  62.0 42.3 %copy-start.14 = (bf16[2,1,15,768]{3,0,2,1:T(2,128)(2,1)S(1)}, bf16[2,1,15,768]{3,0,2,1:T(2,128)(2,1)}, u32[]{:S(2)}) copy-start(bf16[2,1,15,768]{3,0,2,1:T(2,128)(2,1)} %param.19) | copy-start | bytes 138244
  62.0 42.4 %copy-start.41 = (s32[33]{0:T(128)S(1)}, s32[33]{0:T(128)}, u32[]{:S(2)}) copy-start(s32[33]{0:T(128)} %psum.7.refs_1_) | copy-start | bytes 400
  99.3 76.4 %all-to-all-start.28 = ((bf16[8,512,768]{2,1,0:T(8,128)(2,1)}), bf16[8,512,768]{2,1,0:T(8,128)(2,1)}, u32[]{:S(2)}, u32[]{:S(2)}) async-start(bf16[8,512,768]{2,1,0:T(8,128)(2,1)} %send_inputs.3), calls=%async_computation.36 | async-start | bytes 12582912 | tf_op jit(solution)/shard_map/all_to_all | solution.py:1619
  165.7 10.0 copy-start.25
  183.0 39.6 %copy-start.8 = (f32[16,768]{1,0:T(8,128)}, f32[16,768]{1,0:T(8,128)S(1)}, u32[]{:S(2)}) copy-start(f32[16,768]{1,0:T(8,128)S(1)} %get-tuple-element.254.taps_ref) | copy-start | bytes 147460 | tf_op jit(solution)/shard_map/cond
  183.0 39.6 %copy-start.12 = (f32[8,768]{1,0:T(8,128)}, f32[8,768]{1,0:T(8,128)S(1)}, u32[]{:S(2)}) copy-start(f32[8,768]{1,0:T(8,128)S(1)} %get-tuple-element.255.gain) | copy-start | bytes 73732 | tf_op jit(solution)/shard_map/cond
  183.0 303.2 %copy-start.28 = (s32[32]{0:T(128)}, s32[32]{0:T(128)S(1)}, u32[]{:S(2)}) copy-start(s32[32]{0:T(128)S(1)} %get-tuple-element.247.table_ref) | copy-start | bytes 388 | tf_op jit(solution)/shard_map/cond
  183.1 76.4 %all-to-all-start.14 = ((bf16[8,512,768]{2,1,0:T(8,128)(2,1)}), bf16[8,512,768]{2,1,0:T(8,128)(2,1)}, u32[]{:S(2)}, u32[]{:S(2)}) async-start(bf16[8,512,768]{2,1,0:T(8,128)(2,1)} %get-tuple-element.251), calls=%async_computation.18 | async-start | bytes 12582912 | tf_op jit(solution)/shard_map/cond/branch_1_fun/all_to_all | solution.py:1619
  216.7 5.9 copy-start.2
  343.3 76.6 %all-to-all-start.16 = ((bf16[8,512,768]{2,1,0:T(8,128)(2,1)}), bf16[8,512,768]{2,1,0:T(8,128)(2,1)}, u32[]{:S(2)}, u32[]{:S(2)}) async-start(bf16[8,512,768]{2,1,0:T(8,128)(2,1)} %hop_x.4), calls=%async_computation.20 | async-start | bytes 12582912 | tf_op jit(solution)/shard_map/cond/branch_1_fun/all_to_all | solution.py:1619
  352.8 20.5 %copy-start.43 = (bf16[2,1,768,768]{3,2,1,0:T(8,128)(2,1)S(1)}, bf16[2,1,768,768]{3,2,1,0:T(8,128)(2,1)}, u32[]{:S(2)}) copy-start(bf16[2,1,768,768]{3,2,1,0:T(8,128)(2,1)} %get-tuple-element.258.out_w) | copy-start | bytes 7077892 | tf_op jit(solution)/shard_map/cond
  419.8 76.6 %all-to-all-start.18 = ((bf16[8,512,768]{2,1,0:T(8,128)(2,1)}), bf16[8,512,768]{2,1,0:T(8,128)(2,1)}, u32[]{:S(2)}, u32[]{:S(2)}) async-start(bf16[8,512,768]{2,1,0:T(8,128)(2,1)} %send_cotangent.7), calls=%async_computation.22 | async-start | bytes 12582912 | tf_op jit(solution)/shard_map/cond/branch_1_fun/all_to_all | solution.py:1619
  496.5 76.4 %all-to-all-start.17 = ((bf16[8,512,768]{2,1,0:T(8,128)(2,1)}), bf16[8,512,768]{2,1,0:T(8,128)(2,1)}, u32[]{:S(2)}, u32[]{:S(2)}) async-start(bf16[8,512,768]{2,1,0:T(8,128)(2,1)} %send_cotangent.6), calls=%async_computation.21 | async-start | bytes 12582912 | tf_op jit(solution)/shard_map/cond/branch_1_fun/all_to_all | solution.py:1619
  501.2 383.8 %reduce-scatter.17.cloned.1.call-start = ((), (), s32[]{:S(2)}) async-start(), calls=%async_computation.41 | async-start | bytes 11796480 | tf_op jit(solution)/shard_map/cond/branch_1_fun/reduce_scatter | solution.py:1623
  625.9 93.5 %all-to-all-start.19 = ((bf16[8,512,768]{2,1,0:T(8,128)(2,1)}), bf16[8,512,768]{2,1,0:T(8,128)(2,1)}, u32[]{:S(2)}, u32[]{:S(2)}) async-start(bf16[8,512,768]{2,1,0:T(8,128)(2,1)} %hop_dx.3), calls=%async_computation.23 | async-start | bytes 12582912 | tf_op jit(solution)/shard_map/cond/branch_1_fun/all_to_all | solution.py:1619
  640.0 401.5 %reduce-scatter.21.cloned.1.call-start = ((), (), s32[]{:S(2)}) async-start(), calls=%async_computation.43 | async-start | bytes 10567680 | tf_op jit(solution)/shard_map/cond/branch_1_fun/reduce_scatter | solution.py:1623
  640.1 47.0 %copy-start.35 = (f32[8,768]{1,0:T(8,128)S(1)}, f32[8,768]{1,0:T(8,128)}, u32[]{:S(2)}) copy-start(f32[8,768]{1,0:T(8,128)} %get-tuple-element.344) | copy-start | bytes 73732 | tf_op jit(solution)/shard_map/cond
  640.1 47.9 %copy-start.31 = (f32[8,768]{1,0:T(8,128)S(1)}, f32[8,768]{1,0:T(8,128)}, u32[]{:S(2)}) copy-start(f32[8,768]{1,0:T(8,128)} %get-tuple-element.346) | copy-start | bytes 73732 | tf_op jit(solution)/shard_map/cond
  688.2 29.1 %copy-start.18 = (f32[24,768]{1,0:T(8,128)S(1)}, f32[24,768]{1,0:T(8,128)}, u32[]{:S(2)}) copy-start(f32[24,768]{1,0:T(8,128)} %get-tuple-element.342) | copy-start | bytes 221188 | tf_op jit(solution)/shard_map/cond
  803.3 76.4 %all-to-all-start.21 = ((bf16[8,512,768]{2,1,0:T(8,128)(2,1)}), bf16[8,512,768]{2,1,0:T(8,128)(2,1)}, u32[]{:S(2)}, u32[]{:S(2)}) async-start(bf16[8,512,768]{2,1,0:T(8,128)(2,1)} %hop_dx.5), calls=%async_computation.25 | async-start | bytes 12582912 | tf_op jit(solution)/shard_map/cond/branch_1_fun/all_to_all | solution.py:1619
  808.0 5.5 copy-start.13
  808.1 309.8 %reduce-scatter.19.cloned.1.call-start = ((), (), s32[]{:S(2)}) async-start(), calls=%async_computation.42 | async-start | bytes 11796480 | tf_op jit(solution)/shard_map/cond/branch_1_fun/reduce_scatter | solution.py:1623
  813.6 11.0 copy-start.9
  853.3 31.7 %copy-start.3 = (bf16[4,512,768]{2,1,0:T(8,128)(2,1)S(1)}, bf16[4,512,768]{2,1,0:T(8,128)(2,1)}, u32[]{:S(2)}) copy-start(bf16[4,512,768]{2,1,0:T(8,128)(2,1)} %copy-done.2) | copy-start | bytes 9437188 | tf_op jit(solution)/shard_map/cond
  933.3 11.4 copy-start.45
  933.3 103.5 %all-to-all-start.22 = ((bf16[8,512,768]{2,1,0:T(8,128)(2,1)}), bf16[8,512,768]{2,1,0:T(8,128)(2,1)}, u32[]{:S(2)}, u32[]{:S(2)}) async-start(bf16[8,512,768]{2,1,0:T(8,128)(2,1)} %after.12), calls=%async_computation.26 | async-start | bytes 12582912 | tf_op jit(solution)/shard_map/cond/branch_1_fun/all_to_all | solution.py:1619
  944.6 329.1 %reduce-scatter.23.cloned.1.call-start = ((), (), s32[]{:S(2)}) async-start(), calls=%async_computation.44 | async-start | bytes 10567680 | tf_op jit(solution)/shard_map/cond/branch_1_fun/reduce_scatter | solution.py:1623
  944.7 65.6 %copy-start.36 = (f32[8,768]{1,0:T(8,128)S(1)}, f32[8,768]{1,0:T(8,128)}, u32[]{:S(2)}) copy-start(f32[8,768]{1,0:T(8,128)} %get-tuple-element.350) | copy-start | bytes 73732 | tf_op jit(solution)/shard_map/cond
  944.7 66.6 %copy-start.33 = (f32[8,768]{1,0:T(8,128)S(1)}, f32[8,768]{1,0:T(8,128)}, u32[]{:S(2)}) copy-start(f32[8,768]{1,0:T(8,128)} %get-tuple-element.352) | copy-start | bytes 73732 | tf_op jit(solution)/shard_map/cond
  944.7 66.8 %copy-start.5 = (f32[9,512,128]{2,1,0:T(8,128)S(1)}, f32[9,512,128]{2,1,0:T(8,128)}, u32[]{:S(2)}) copy-start(f32[9,512,128]{2,1,0:T(8,128)} %get-tuple-element.313.rstd_ref) | copy-start | bytes 7077892 | tf_op jit(solution)/shard_map/cond
  1011.4 23.2 %copy-start.19 = (f32[24,768]{1,0:T(8,128)S(1)}, f32[24,768]{1,0:T(8,128)}, u32[]{:S(2)}) copy-start(f32[24,768]{1,0:T(8,128)} %get-tuple-element.348) | copy-start | bytes 221188 | tf_op jit(solution)/shard_map/cond
  1036.7 76.4 %all-to-all-start.23 = ((bf16[8,512,768]{2,1,0:T(8,128)(2,1)}), bf16[8,512,768]{2,1,0:T(8,128)(2,1)}, u32[]{:S(2)}, u32[]{:S(2)}) async-start(bf16[8,512,768]{2,1,0:T(8,128)(2,1)} %after.13), calls=%async_computation.27 | async-start | bytes 12582912 | tf_op jit(solution)/shard_map/cond/branch_1_fun/all_to_all | solution.py:1619
  1113.1 76.4 %all-to-all-start.25 = ((bf16[8,512,768]{2,1,0:T(8,128)(2,1)}), bf16[8,512,768]{2,1,0:T(8,128)(2,1)}, u32[]{:S(2)}, u32[]{:S(2)}) async-start(bf16[8,512,768]{2,1,0:T(8,128)(2,1)} %after.15), calls=%async_computation.32 | async-start | bytes 12582912 | tf_op jit(solution)/shard_map/cond/branch_1_fun/all_to_all | solution.py:1619
  1117.9 76.3 %copy-start.16 = (f32[2,8]{1,0:T(2,128)S(1)}, f32[2,8]{1,0:T(2,128)}, u32[]{:S(2)}) copy-start(f32[2,8]{1,0:T(2,128)} %get-tuple-element.353.count_ref) | copy-start | bytes 196 | tf_op jit(solution)/shard_map/cond
  1189.5 76.4 %all-to-all-start.24 = ((bf16[8,512,768]{2,1,0:T(8,128)(2,1)}), bf16[8,512,768]{2,1,0:T(8,128)(2,1)}, u32[]{:S(2)}, u32[]{:S(2)}) async-start(bf16[8,512,768]{2,1,0:T(8,128)(2,1)} %after.14), calls=%async_computation.30 | async-start | bytes 12582912 | tf_op jit(solution)/shard_map/cond/branch_1_fun/all_to_all | solution.py:1619
  1194.2 10.9 copy-start.29
Sparse Core Ops, SparseCore 0:
  621.4 178.4 reduce-scatter.16
  802.9 146.3 reduce-scatter.20
  952.2 162.0 reduce-scatter.18
  1116.5 146.3 reduce-scatter.22

commit v9 on v8

--- a/solution.py
+++ b/solution.py
@@ -98,13 +98,22 @@
 
 
 def home_kernel(owners, seqs, cand, send, relay, tags, color, partner, first, tally):
+    told = BLOCKS * (HALVES + seqs)
+
+    def tell(n, _):
+        value = cand[n]
+        for o in range(owners):
+            tags[o * told + BLOCKS * HALVES + n] = value
+        return 0
+
+    lax.fori_loop(0, BLOCKS * seqs, tell, 0)
     for b in range(BLOCKS):
 
         def clear_owner(o, _):
             for half in range(HALVES):
                 send[(b * HALVES + half) * owners + o] = -1
                 relay[(b * HALVES + half) * owners + o] = -1
-                tags[o * BLOCKS * HALVES + b * HALVES + half] = KINDS
+                tags[o * told + b * HALVES + half] = KINDS
             return 0
 
         lax.fori_loop(0, owners, clear_owner, 0)
@@ -118,7 +127,7 @@
             o = lax.rem(c, owners)
             spots.append(o)
             send[(b * HALVES + half) * owners + o] = j
-            tags[o * BLOCKS * HALVES + b * HALVES + half] = lax.div(c, owners)
+            tags[o * told + b * HALVES + half] = lax.div(c, owners)
         relay[half * owners + spots[1]] = spots[0]
         relay[(HALVES + half) * owners + spots[0]] = spots[1]
         return 0
@@ -299,7 +308,11 @@
         kernel,
         in_specs=[SMEM_SPEC],
         out_specs=[SMEM_SPEC] * 3,
-        out_shape=[int_shape(size)] * 3,
+        out_shape=[
+            int_shape(size),
+            int_shape(size),
+            int_shape(owners * BLOCKS * (HALVES + seqs)),
+        ],
         scratch_shapes=[
             pltpu.SMEM((seqs,), jnp.int32),
             pltpu.SMEM((BLOCKS * seqs,), jnp.int32),
@@ -1544,68 +1557,57 @@
 
 def finish_rest(b, rest, totals, old, shapes, wait_for):
     tall, width = shapes[1].shape[2:]
-    small_block = 7 * tall // SMALL_ROWS
-
-    def kernel(rest_ref, small_ref, count_ref, *refs):
+
+    def kernel(rest_ref, count_ref, *refs):
         qkv_to, out_to, taps_to, point_to, gain_to, shift_to = refs[-6:]
-        i = pl.program_id(0)
         scales = 1.0 / jnp.maximum(count_ref[b : b + 1, :], 1.0)
-        values = rest_ref[...].astype(F32)
-
-        @pl.when(i < 3)
-        def _():
-            qkv_to[...] = values * scales[:, 0:1]
-
-        @pl.when(i == 3)
-        def _():
-            out_to[...] = values * scales[:, 0:1]
-            small = small_ref[...].astype(F32)
-            row = lax.broadcasted_iota(jnp.int32, small.shape, 0)
-            which = jnp.where(row < 3, 1, jnp.where(row < 8, 2, jnp.where(row < 15, 3, 0)))
-            which = jnp.where(row >= 15, row - 15, which)
-            which = jnp.where(row >= 20, row - 20, which)
-            scale = jnp.zeros_like(small)
-            for k in range(KINDS):
-                scale = jnp.where(which == k, scales[:, k : k + 1], scale)
-            small = small * scale
-            for r in range(15):
-                taps_to[r] = small[r : r + 1, :tall]
-            for r in range(KINDS):
-                gain_to[r] = small[15 + r : 16 + r, :tall]
-                shift_to[r] = small[20 + r : 21 + r, :tall]
-
+
+        def piece(n, k):
+            return rest_ref[n * tall : (n + 1) * tall, :].astype(F32) * scales[:, k : k + 1]
+
+        for n in range(3):
+            qkv_to[:, n * width : (n + 1) * width] = piece(n, 0)
+        out_to[...] = piece(3, 0)
         for k in range(1, KINDS - 1):
-
-            @pl.when(i == 3 + k)
-            def _():
-                point_to[...] = values * scales[:, k : k + 1]
+            point_to[k - 1] = piece(3 + k, k)
+        small = rest_ref[7 * tall : 7 * tall + SMALL_ROWS, :].astype(F32)
+        row = lax.broadcasted_iota(jnp.int32, small.shape, 0)
+        which = jnp.where(row < 3, 1, jnp.where(row < 8, 2, jnp.where(row < 15, 3, 0)))
+        which = jnp.where(row >= 15, row - 15, which)
+        which = jnp.where(row >= 20, row - 20, which)
+        scale = jnp.zeros_like(small)
+        for k in range(KINDS):
+            scale = jnp.where(which == k, scales[:, k : k + 1], scale)
+        small = small * scale
+        for r in range(15):
+            taps_to[r] = small[r : r + 1, :tall]
+        for r in range(KINDS):
+            gain_to[r] = small[15 + r : 16 + r, :tall]
+            shift_to[r] = small[20 + r : 21 + r, :tall]
 
     old = list(old)
     return pl.pallas_call(
         kernel,
-        grid=(7,),
+        grid=(1,),
         in_specs=[
-            pl.BlockSpec((tall, width), lambda i: (i, 0)),
-            pl.BlockSpec((SMALL_ROWS, width), lambda i: (small_block, 0)),
+            pl.BlockSpec(rest.shape, lambda i: (0, 0)),
             pl.BlockSpec((BLOCKS, 8), lambda i: (0, 0)),
         ]
         + [ANY_SPEC] * (len(old) + len(wait_for)),
         out_specs=[
-            pl.BlockSpec((None, None, tall, width), lambda i: (b, 0, 0, jnp.minimum(i, 2))),
+            pl.BlockSpec((None, None, tall, 3 * width), lambda i: (b, 0, 0, 0)),
             pl.BlockSpec((None, None, tall, width), lambda i: (b, 0, 0, 0)),
             pl.BlockSpec((None, 15, 1, tall), lambda i: (b, 0, 0, 0)),
-            pl.BlockSpec(
-                (None, None, None, tall, width), lambda i: (b, 0, jnp.maximum(i - 4, 0), 0, 0)
-            ),
+            pl.BlockSpec((None, None, KINDS - 2, tall, width), lambda i: (b, 0, 0, 0, 0)),
             pl.BlockSpec((None, KINDS, 1, tall), lambda i: (b, 0, 0, 0)),
             pl.BlockSpec((None, KINDS, 1, tall), lambda i: (b, 0, 0, 0)),
         ],
         out_shape=list(shapes),
-        input_output_aliases={3 + n: n for n in range(len(old))},
+        input_output_aliases={2 + n: n for n in range(len(old))},
         compiler_params=params_of(1),
         cost_estimate=pl.CostEstimate(flops=0, transcendentals=0, bytes_accessed=8 * 2**20),
         name="finish_rest",
-    )(rest, rest, totals, *old, *wait_for)
+    )(rest, totals, *old, *wait_for)
 
 
 def small_params(b, conv_taps, norm_gain, norm_bias):
@@ -1645,10 +1647,7 @@
     smalls = [small_params(b, conv_taps, norm_gain, norm_bias) for b in range(BLOCKS)]
     send, relay, tags = home_tables(candidate.reshape(-1), owners, seqs)
     marks = BLOCKS * HALVES
-    told = jnp.concatenate(
-        [tags.reshape(owners, marks), jnp.broadcast_to(candidate.reshape(1, -1), (owners, BLOCKS * seqs))],
-        axis=1,
-    )
+    told = tags.reshape(owners, -1)
     told = exchange(told)
     everyone = told[:, marks:].reshape(-1)
     tables = owner_tables(told[:, :marks].reshape(-1), owners)

time: 1300 us -> 1300 us (level)
  Pallas kernels: 700 us -> 649 us
  starting transfers between devices: 78.8 us -> 112 us
  waiting for transfers between devices: 310 us -> 331 us
    pallas_call x4, Pallas kernels: 152 us -> 94.3 us  [attention_backward(): pl.pallas_call(kernel, grid_spec=pltpu.PrefetchScalarGridSpec(num_scalar_...]
    all_to_all x13, starting transfers between devices: 78.7 us -> 112 us  [exchange(): return lax.all_to_all(rows, 'op', split_axis=0, concat_axis=0, tiled=True)]
    pallas_call x4, Pallas kernels: 64.6 us -> 43.5 us  [attention_forward(): pl.pallas_call(kernel, grid_spec=pltpu.PrefetchScalarGridSpec(num_scalar_...]
    all_to_all x13, waiting for transfers between devices: 309 us -> 330 us  [exchange(): return lax.all_to_all(rows, 'op', split_axis=0, concat_axis=0, tiled=True)]
    pallas_call x4, Pallas kernels: 107 us -> 126 us  [conv_backward(): pl.pallas_call(kernel, grid_spec=pltpu.PrefetchScalarGridSpec(num_scalar_...]
  transfers between devices with their start and end apart: 17 -> 17, of which waited for: 10 -> 12; matrix products, arithmetic and copies ran while one was open for 1% -> 1% of each run, Pallas kernels for 49% -> 45%
where the time goes in v9:
time: 1300 us
  Pallas kernels  649 us (50%)
  waiting for transfers between devices  331 us (25%)
  blocking collectives  171 us (13%)
  starting transfers between devices  112 us (9%)
  between operations  14.3 us (1%)
    all_to_all x13, waiting for transfers between devices, exchange(): return lax.all_to_all(rows, 'op', split_axis=0, concat_axis=0, tiled=True)  330 us
    all_to_all x2, blocking collectives, exchange(): return lax.all_to_all(rows, 'op', split_axis=0, concat_axis=0, tiled=True)  160 us
    pallas_call x4, Pallas kernels, conv_backward(): pl.pallas_call(kernel, grid_spec=pltpu.PrefetchScalarGridSpec(num_scalar_...  126 us
    all_to_all x13, starting transfers between devices, exchange(): return lax.all_to_all(rows, 'op', split_axis=0, concat_axis=0, tiled=True)  112 us
    pallas_call x2, Pallas kernels, feed_backward(): pl.pallas_call(kernel, grid_spec=pltpu.PrefetchScalarGridSpec(num_scalar_...  96.6 us
    pallas_call x4, Pallas kernels, attention_backward(): pl.pallas_call(kernel, grid_spec=pltpu.PrefetchScalarGridSpec(num_scalar_...  94.3 us
    pallas_call x4, Pallas kernels, feed_forward(): pl.pallas_call(kernel, grid_spec=pltpu.PrefetchScalarGridSpec(num_scalar_...  91.7 us
    pallas_call x4, Pallas kernels, conv_forward(): pl.pallas_call(kernel, grid_spec=pltpu.PrefetchScalarGridSpec(num_scalar_...  72.4 us
  transfers between devices with their start and end apart: 17, of which 12 were waited for; matrix products, arithmetic and copies ran while one was open for 1% of the time, Pallas kernels for 45%

profile of v9, /device:TPU:0, one launch (start us, length us, event | category | flops | bytes accessed | tf_op | source)
XLA Modules:
  0.0 1296.8 jit_solution(15779500800728746389)
XLA Ops:
  12.7 5.2 all-to-all-start.26
  17.8 4.5 send_inputs.2
  22.4 4.8 all-to-all-start.27
  30.4 24.7 %route_tables.1 = (s32[80]{0:T(128)S(1)}, s32[1]{0:T(128)}) custom-call(s32[192]{0:T(256)} %reshape.113.refs_0_, s32[1]{0:T(128)} %bitcast.13.refs_1_), custom_call_target="tpu_custom_call" | custom-call | tf_op jit(solution)/shard_map/route_tables/pallas_call | solution.py:384
  55.8 11.1 psum.7.refs_1_
  67.0 4.5 send_inputs.3
  71.6 27.2 %all-to-all-done.27.x_ref = bf16[8,512,768]{2,1,0:T(8,128)(2,1)} async-done(((bf16[8,512,768]{2,1,0:T(8,128)(2,1)}), bf16[8,512,768]{2,1,0:T(8,128)(2,1)}, u32[]{:S(2)}, u32[]{:S(2)}) %all-to-all-start.27) | async-done | bytes 6291488 | tf_op jit(solution)/shard_map/all_to_all | solution.py:1621
  98.8 4.8 all-to-all-start.28
  104.7 31.5 %feed_forward.13 = (bf16[8,512,768]{2,1,0:T(8,128)(2,1)}, bf16[4,512,3072]{2,1,0:T(8,128)(2,1)}, bf16[4,512,3072]{2,1,0:T(8,128)(2,1)}, bf16[4,512,768]{2,1,0:T(8,128)(2,1)S(1)}, f32[4,512,128]{2,1,0:T(8,128)}) custom-call(s32[60]{0:T(128)S(1)} %get-tuple-element.414.rows_ref, s32[32]{0:T(128)S(1)} %get-tuple-element.413.counts_ref, ...), custom_call_target="tpu_custom_call" | custom-call | flops 14495514624 | bytes 41943040 | tf_op jit(solution)/shard_map/feed_forward/pallas_call | solution.py:940
  136.2 12.8 attention_forward.13
  148.9 13.8 %conv_forward.13 = (bf16[8,512,768]{2,1,0:T(8,128)(2,1)}, bf16[9,512,768]{2,1,0:T(8,128)(2,1)}, bf16[9,512,768]{2,1,0:T(8,128)(2,1)}, f32[9,512,128]{2,1,0:T(8,128)}) custom-call(s32[60]{0:T(128)S(1)} %get-tuple-element.414.rows_ref, s32[32]{0:T(128)S(1)} %get-tuple-element.413.counts_ref, ...), custom_call_target="tpu_custom_call", output_to_operand_aliasing={{0}: (7, {})} | custom-call | flops 5435817984 | bytes 37748736 | tf_op jit(solution)/shard_map/conv_forward/pallas_call | solution.py:1271
  162.7 4.6 hop_x.5
  167.3 7.8 all-to-all-done.28
  175.2 1114.8 %conditional.1 = (bf16[12,512,768]{2,1,0:T(8,128)(2,1)}, bf16[12,512,768]{2,1,0:T(8,128)(2,1)}, f32[2,1,192,2304]{3,2,1,0:T(8,128)}, f32[2,1,192,768]{3,2,1,0:T(...) conditional(s32[]{:T(128)} %bitcast.14, ...), branch_computations={%region_2.7_spmd, %region_7.12_spmd} | conditional | flops 278434742272 | bytes 1436570368 | solution.py:1770
  182.5 4.8 all-to-all-start.14
  187.3 10.5 feed_forward.10
  197.9 5.9 attention_forward.10
  203.8 23.6 %conv_forward.10 = (bf16[8,512,768]{2,1,0:T(8,128)(2,1)}, bf16[9,512,768]{2,1,0:T(8,128)(2,1)}, bf16[9,512,768]{2,1,0:T(8,128)(2,1)}, f32[9,512,128]{2,1,0:T(8,128)}) custom-call(s32[60]{0:T(128)S(1)} %get-tuple-element.248.rows_ref, s32[32]{0:T(128)S(1)} %get-tuple-element.249.counts_ref, ...), custom_call_target="tpu_custom_call", output_to_operand_aliasing={{0}: (7, {})} | custom-call | flops 5435817984 | bytes 37748736 | tf_op jit(solution)/shard_map/cond/branch_1_fun/conv_forward/pallas_call | solution.py:1271
  227.4 31.5 %all-to-all-done.14.refs_0_ = bf16[8,512,768]{2,1,0:T(8,128)(2,1)} async-done(((bf16[8,512,768]{2,1,0:T(8,128)(2,1)}), bf16[8,512,768]{2,1,0:T(8,128)(2,1)}, u32[]{:S(2)}, u32[]{:S(2)}) %all-to-all-start.14) | async-done | bytes 6291488 | tf_op jit(solution)/shard_map/cond/branch_1_fun/all_to_all | solution.py:1621
  262.7 76.9 %all_to_all.126.refs_1_ = bf16[8,512,768]{2,1,0:T(8,128)(2,1)} all-to-all(bf16[8,512,768]{2,1,0:T(8,128)(2,1)} %hop_x.3), channel_id=1, replica_groups=mesh['dp'=4,'op'=8] {'op'}, dimensions={0} | all-to-all | bytes 12582912 | tf_op jit(solution)/shard_map/cond/branch_1_fun/all_to_all | solution.py:1621
  343.3 4.9 all-to-all-start.16
  348.3 4.6 land_x.2.x_ref.x_ref0
  352.9 20.5 %feed_forward.11 = (bf16[8,512,768]{2,1,0:T(8,128)(2,1)}, bf16[4,512,3072]{2,1,0:T(8,128)(2,1)}, bf16[4,512,3072]{2,1,0:T(8,128)(2,1)}, bf16[4,512,768]{2,1,0:T(8,128)(2,1)}, f32[4,512,128]{2,1,0:T(8,128)}) custom-call(s32[60]{0:T(128)S(1)} %get-tuple-element.248.rows_ref, s32[32]{0:T(128)S(1)} %get-tuple-element.249.counts_ref, ...), custom_call_target="tpu_custom_call" | custom-call | flops 14495514624 | bytes 41943040 | tf_op jit(solution)/shard_map/cond/branch_1_fun/feed_forward/pallas_call | solution.py:940
  373.4 12.4 attention_forward.11
  385.8 18.3 %conv_forward.11 = (bf16[8,512,768]{2,1,0:T(8,128)(2,1)}, bf16[9,512,768]{2,1,0:T(8,128)(2,1)}, bf16[9,512,768]{2,1,0:T(8,128)(2,1)}, f32[9,512,128]{2,1,0:T(8,128)}) custom-call(s32[60]{0:T(128)S(1)} %get-tuple-element.248.rows_ref, s32[32]{0:T(128)S(1)} %get-tuple-element.249.counts_ref, ...), custom_call_target="tpu_custom_call", output_to_operand_aliasing={{0}: (7, {})} | custom-call | flops 5435817984 | bytes 37748736 | tf_op jit(solution)/shard_map/cond/branch_1_fun/conv_forward/pallas_call | solution.py:1271
  404.1 4.6 send_cotangent.7
  408.7 11.1 all-to-all-done.16.refs_0_
  419.9 5.0 all-to-all-start.18
  424.9 4.6 land_x.3.x_ref.x_ref1
  429.5 29.1 %feed_forward.12 = (bf16[8,512,768]{2,1,0:T(8,128)(2,1)}, bf16[4,512,3072]{2,1,0:T(8,128)(2,1)}, bf16[4,512,3072]{2,1,0:T(8,128)(2,1)}, bf16[4,512,768]{2,1,0:T(8,128)(2,1)}, f32[4,512,128]{2,1,0:T(8,128)}) custom-call(s32[60]{0:T(128)S(1)} %get-tuple-element.248.rows_ref, ...), custom_call_target="tpu_custom_call", output_to_operand_aliasing={{1}: (7, {}), {2}: (8, {}), {3}: (9, {}), {4}: (10, {})} | custom-call | flops 14495514624 | bytes 41943040 | tf_op jit(solution)/shard_map/cond/branch_1_fun/feed_forward/pallas_call | solution.py:940
  458.6 12.4 attention_forward.12
  471.0 16.7 %conv_forward.12 = (bf16[8,512,768]{2,1,0:T(8,128)(2,1)}, bf16[9,512,768]{2,1,0:T(8,128)(2,1)}, bf16[9,512,768]{2,1,0:T(8,128)(2,1)}, f32[9,512,128]{2,1,0:T(8,128)}) custom-call(s32[60]{0:T(128)S(1)} %get-tuple-element.248.rows_ref, s32[32]{0:T(128)S(1)} %get-tuple-element.249.counts_ref, ...), custom_call_target="tpu_custom_call", output_to_operand_aliasing={{0}: (7, {})} | custom-call | flops 5435817984 | bytes 37748736 | tf_op jit(solution)/shard_map/cond/branch_1_fun/conv_forward/pallas_call | solution.py:1271
  487.7 4.6 send_cotangent.6
  496.5 4.7 all-to-all-start.17
  501.3 28.5 %attention_backward.12 = (bf16[8,512,768]{2,1,0:T(8,128)(2,1)}, f32[8,768]{1,0:T(8,128)}, f32[768,2304]{1,0:T(8,128)}, f32[768,768]{1,0:T(8,128)}) custom-call(s32[60]{0:T(128)S(1)} %get-tuple-element.248.rows_ref, s32[32]{0:T(128)S(1)} %get-tuple-element.249.counts_ref, bf16[8,512,768]{2,1,0:T(8,128)(2,1)} %land_x.3.x_ref.x_ref1, ...), custom_call_target="tpu_custom_call" | custom-call | flops 19327352832 | bytes 41943040 | tf_op jit(solution)/shard_map/cond/branch_1_fun/attention_backward/pallas_call | solution.py:831
  529.8 27.7 %conv_backward.12 = (bf16[8,512,768]{2,1,0:T(8,128)(2,1)}, f32[24,768]{1,0:T(8,128)}, f32[3,768,768]{2,1,0:T(8,128)}) custom-call(s32[60]{0:T(128)S(1)} %get-tuple-element.248.rows_ref, s32[32]{0:T(128)S(1)} %get-tuple-element.249.counts_ref, bf16[8,512,768]{2,1,0:T(8,128)(2,1)} %land_x.3.x_ref.x_ref1, ...), custom_call_target="tpu_custom_call", output_to_operand_aliasing={{0}: (10, {})} | custom-call | flops 8153726976 | bytes 52428800 | tf_op jit(solution)/shard_map/cond/branch_1_fun/conv_backward/pallas_call | solution.py:1420
  557.5 15.4 %all-to-all-done.17.dy_ref0.dy_ref = bf16[8,512,768]{2,1,0:T(8,128)(2,1)} async-done(((bf16[8,512,768]{2,1,0:T(8,128)(2,1)}), bf16[8,512,768]{2,1,0:T(8,128)(2,1)}, u32[]{:S(2)}, u32[]{:S(2)}) %all-to-all-start.17) | async-done | bytes 6291488 | tf_op jit(solution)/shard_map/cond/branch_1_fun/all_to_all | solution.py:1621
  572.8 48.5 %feed_backward.6 = (f32[8,768]{1,0:T(8,128)}, bf16[8,512,768]{2,1,0:T(8,128)(2,1)}, bf16[8,512,768]{2,1,0:T(8,128)(2,1)}, bf16[4,1536,768]{2,1,0:T(8,128)(2,1)}) custom-call(s32[60]{0:T(128)S(1)} %get-tuple-element.248.rows_ref, s32[32]{0:T(128)S(1)} %get-tuple-element.249.counts_ref, ...), custom_call_target="tpu_custom_call", output_to_operand_aliasing={{2}: (13, {})} | custom-call | flops 25367150592 | bytes 52428800 | tf_op jit(solution)/shard_map/cond/branch_1_fun/feed_backward/pallas_call | solution.py:1150
  621.4 4.6 hop_dx.3
  625.9 12.9 all-to-all-start.19
  638.9 27.5 %attention_backward.13 = (bf16[8,512,768]{2,1,0:T(8,128)(2,1)}, f32[8,768]{1,0:T(8,128)}, bf16[4,1376,768]{2,1,0:T(8,128)(2,1)}) custom-call(s32[60]{0:T(128)S(1)} %get-tuple-element.248.rows_ref, s32[32]{0:T(128)S(1)} %get-tuple-element.249.counts_ref, bf16[8,512,768]{2,1,0:T(8,128)(2,1)} %land_x.2.x_ref.x_ref0, ...), custom_call_target="tpu_custom_call", output_to_operand_aliasing={{0}: (13, {})} | custom-call | flops 19327352832 | bytes 41943040 | tf_op jit(solution)/shard_map/cond/branch_1_fun/attention_backward/pallas_call | solution.py:831
  667.7 31.9 %conv_backward.13 = (bf16[8,512,768]{2,1,0:T(8,128)(2,1)}, f32[24,768]{1,0:T(8,128)}, bf16[4,1376,768]{2,1,0:T(8,128)(2,1)}) custom-call(s32[60]{0:T(128)S(1)} %get-tuple-element.248.rows_ref, s32[32]{0:T(128)S(1)} %get-tuple-element.249.counts_ref, bf16[8,512,768]{2,1,0:T(8,128)(2,1)} %land_x.2.x_ref.x_ref0, ...), custom_call_target="tpu_custom_call", output_to_operand_aliasing={{2}: (11, {}), {0}: (12, {})} | custom-call | flops 8153726976 | bytes 52428800 | tf_op jit(solution)/shard_map/cond/branch_1_fun/conv_backward/pallas_call | solution.py:1420
  701.6 9.0 all-to-all-done.19.refs_1_.refs_0_
  713.8 82.9 %all_to_all.127.refs_1_ = bf16[8,512,768]{2,1,0:T(8,128)(2,1)} all-to-all(bf16[8,512,768]{2,1,0:T(8,128)(2,1)} %hop_dx.4), channel_id=1, replica_groups=mesh['dp'=4,'op'=8] {'op'}, dimensions={0} | all-to-all | bytes 12582912 | tf_op jit(solution)/shard_map/cond/branch_1_fun/all_to_all | solution.py:1621
  796.7 5.4 hop_dx.5
  802.1 4.8 all-to-all-start.21
  807.0 4.6 land_dx.3.dy_ref.dy_ref1
  811.6 10.9 attention_backward.14
  822.6 42.0 %conv_backward.14 = (bf16[8,512,768]{2,1,0:T(8,128)(2,1)}, f32[24,768]{1,0:T(8,128)}, f32[3,768,768]{2,1,0:T(8,128)}) custom-call(s32[60]{0:T(128)S(1)} %get-tuple-element.248.rows_ref, s32[32]{0:T(128)S(1)} %get-tuple-element.249.counts_ref, bf16[8,512,768]{2,1,0:T(8,128)(2,1)} %get-tuple-element.252.x_ref.x_ref1, ...), custom_call_target="tpu_custom_call", output_to_operand_aliasing={{0}: (10, {})} | custom-call | flops 8153726976 | bytes 52428800 | tf_op jit(solution)/shard_map/cond/branch_1_fun/conv_backward/pallas_call | solution.py:1420
  864.6 13.9 %all-to-all-done.21.refs_0_ = bf16[8,512,768]{2,1,0:T(8,128)(2,1)} async-done(((bf16[8,512,768]{2,1,0:T(8,128)(2,1)}), bf16[8,512,768]{2,1,0:T(8,128)(2,1)}, u32[]{:S(2)}, u32[]{:S(2)}) %all-to-all-start.21) | async-done | bytes 6291488 | tf_op jit(solution)/shard_map/cond/branch_1_fun/all_to_all | solution.py:1621
  878.5 4.6 land_dx.2.refs_1_.dy_ref0.dy_ref
  883.1 48.1 %feed_backward.7 = (f32[8,768]{1,0:T(8,128)}, bf16[8,512,768]{2,1,0:T(8,128)(2,1)}, bf16[8,512,768]{2,1,0:T(8,128)(2,1)}, bf16[4,1536,768]{2,1,0:T(8,128)(2,1)}) custom-call(s32[60]{0:T(128)S(1)} %get-tuple-element.248.rows_ref, s32[32]{0:T(128)S(1)} %get-tuple-element.249.counts_ref, ...), custom_call_target="tpu_custom_call", output_to_operand_aliasing={{2}: (13, {})} | custom-call | flops 25367150592 | bytes 52428800 | tf_op jit(solution)/shard_map/cond/branch_1_fun/feed_backward/pallas_call | solution.py:1150
  931.2 20.9 %all-to-all-start.22 = ((bf16[8,512,768]{2,1,0:T(8,128)(2,1)}), bf16[8,512,768]{2,1,0:T(8,128)(2,1)}, u32[]{:S(2)}, u32[]{:S(2)}) async-start(bf16[8,512,768]{2,1,0:T(8,128)(2,1)} %after.12), calls=%async_computation.26 | async-start | bytes 12582912 | tf_op jit(solution)/shard_map/cond/branch_1_fun/all_to_all | solution.py:1621
  952.3 27.3 %attention_backward.15 = (bf16[8,512,768]{2,1,0:T(8,128)(2,1)}, f32[8,768]{1,0:T(8,128)}, bf16[4,1376,768]{2,1,0:T(8,128)(2,1)}) custom-call(s32[60]{0:T(128)S(1)} %get-tuple-element.248.rows_ref, s32[32]{0:T(128)S(1)} %get-tuple-element.249.counts_ref, bf16[8,512,768]{2,1,0:T(8,128)(2,1)} %get-tuple-element.310.x_ref0.x_ref, ...), custom_call_target="tpu_custom_call", output_to_operand_aliasing={{0}: (13, {})} | custom-call | flops 19327352832 | bytes 41943040 | tf_op jit(solution)/shard_map/cond/branch_1_fun/attention_backward/pallas_call | solution.py:831
  980.8 24.6 %conv_backward.15 = (bf16[8,512,768]{2,1,0:T(8,128)(2,1)}, f32[24,768]{1,0:T(8,128)}, bf16[4,1376,768]{2,1,0:T(8,128)(2,1)}) custom-call(s32[60]{0:T(128)S(1)} %get-tuple-element.248.rows_ref, s32[32]{0:T(128)S(1)} %get-tuple-element.249.counts_ref, ...), custom_call_target="tpu_custom_call", output_to_operand_aliasing={{2}: (11, {}), {0}: (12, {})} | custom-call | flops 8153726976 | bytes 52428800 | tf_op jit(solution)/shard_map/cond/branch_1_fun/conv_backward/pallas_call | solution.py:1420
  1007.4 16.5 %all-to-all-done.22.refs_0_ = bf16[8,512,768]{2,1,0:T(8,128)(2,1)} async-done(((bf16[8,512,768]{2,1,0:T(8,128)(2,1)}), bf16[8,512,768]{2,1,0:T(8,128)(2,1)}, u32[]{:S(2)}, u32[]{:S(2)}) %all-to-all-start.22) | async-done | bytes 6291488 | tf_op jit(solution)/shard_map/cond/branch_1_fun/all_to_all | solution.py:1621
  1023.9 29.4 %all-to-all-start.23 = ((bf16[8,512,768]{2,1,0:T(8,128)(2,1)}), bf16[8,512,768]{2,1,0:T(8,128)(2,1)}, u32[]{:S(2)}, u32[]{:S(2)}) async-start(bf16[8,512,768]{2,1,0:T(8,128)(2,1)} %after.13), calls=%async_computation.27 | async-start | bytes 12582912 | tf_op jit(solution)/shard_map/cond/branch_1_fun/all_to_all | solution.py:1621
  1053.3 71.7 %all-to-all-done.23.refs_1_ = bf16[8,512,768]{2,1,0:T(8,128)(2,1)} async-done(((bf16[8,512,768]{2,1,0:T(8,128)(2,1)}), bf16[8,512,768]{2,1,0:T(8,128)(2,1)}, u32[]{:S(2)}, u32[]{:S(2)}) %all-to-all-start.23) | async-done | bytes 6291488 | tf_op jit(solution)/shard_map/cond/branch_1_fun/all_to_all | solution.py:1621
  1125.0 5.0 all-to-all-start.25
  1130.0 71.5 %all-to-all-done.25.refs_1_ = bf16[8,512,768]{2,1,0:T(8,128)(2,1)} async-done(((bf16[8,512,768]{2,1,0:T(8,128)(2,1)}), bf16[8,512,768]{2,1,0:T(8,128)(2,1)}, u32[]{:S(2)}, u32[]{:S(2)}) %all-to-all-start.25) | async-done | bytes 6291488 | tf_op jit(solution)/shard_map/cond/branch_1_fun/all_to_all | solution.py:1621
  1201.5 4.7 all-to-all-start.24
  1214.7 8.2 outputs.3.refs_6_
  1227.4 50.5 %all-to-all-done.24.refs_0_ = bf16[8,512,768]{2,1,0:T(8,128)(2,1)} async-done(((bf16[8,512,768]{2,1,0:T(8,128)(2,1)}), bf16[8,512,768]{2,1,0:T(8,128)(2,1)}, u32[]{:S(2)}, u32[]{:S(2)}) %all-to-all-start.24) | async-done | bytes 6291488 | tf_op jit(solution)/shard_map/cond/branch_1_fun/all_to_all | solution.py:1621
  1277.9 7.9 input_grad.3.refs_7_
  (136 shorter events, 48.8 us)
Async XLA Ops:
  11.3 55.7 %copy-start.24 = (s32[32]{0:T(128)}, s32[32]{0:T(128)S(1)}, u32[]{:S(2)}) copy-start(s32[32]{0:T(128)S(1)} %get-tuple-element.415.table_ref) | copy-start | bytes 388
  12.7 9.8 all-to-all-start.26
  22.4 76.4 %all-to-all-start.27 = ((bf16[8,512,768]{2,1,0:T(8,128)(2,1)}), bf16[8,512,768]{2,1,0:T(8,128)(2,1)}, u32[]{:S(2)}, u32[]{:S(2)}) async-start(bf16[8,512,768]{2,1,0:T(8,128)(2,1)} %send_inputs.2), calls=%async_computation.35 | async-start | bytes 12582912 | tf_op jit(solution)/shard_map/all_to_all | solution.py:1621
  71.5 32.1 %copy-start.22 = (bf16[2,1,5,768]{3,0,2,1:T(2,128)(2,1)S(1)}, bf16[2,1,5,768]{3,0,2,1:T(2,128)(2,1)}, u32[]{:S(2)}) copy-start(bf16[2,1,5,768]{3,0,2,1:T(2,128)(2,1)} %param.21) | copy-start | bytes 46084
  71.5 32.1 %copy-start.23 = (bf16[2,1,5,768]{3,0,2,1:T(2,128)(2,1)S(1)}, bf16[2,1,5,768]{3,0,2,1:T(2,128)(2,1)}, u32[]{:S(2)}) copy-start(bf16[2,1,5,768]{3,0,2,1:T(2,128)(2,1)} %param.22) | copy-start | bytes 46084
  71.5 32.2 %copy-start.14 = (bf16[2,1,15,768]{3,0,2,1:T(2,128)(2,1)S(1)}, bf16[2,1,15,768]{3,0,2,1:T(2,128)(2,1)}, u32[]{:S(2)}) copy-start(bf16[2,1,15,768]{3,0,2,1:T(2,128)(2,1)} %param.19) | copy-start | bytes 138244
  71.6 32.3 %copy-start.41 = (s32[33]{0:T(128)S(1)}, s32[33]{0:T(128)}, u32[]{:S(2)}) copy-start(s32[33]{0:T(128)} %psum.7.refs_1_) | copy-start | bytes 400
  98.8 76.4 %all-to-all-start.28 = ((bf16[8,512,768]{2,1,0:T(8,128)(2,1)}), bf16[8,512,768]{2,1,0:T(8,128)(2,1)}, u32[]{:S(2)}, u32[]{:S(2)}) async-start(bf16[8,512,768]{2,1,0:T(8,128)(2,1)} %send_inputs.3), calls=%async_computation.36 | async-start | bytes 12582912 | tf_op jit(solution)/shard_map/all_to_all | solution.py:1621
  162.7 12.4 copy-start.25
  182.5 21.3 %copy-start.8 = (f32[16,768]{1,0:T(8,128)}, f32[16,768]{1,0:T(8,128)S(1)}, u32[]{:S(2)}) copy-start(f32[16,768]{1,0:T(8,128)S(1)} %get-tuple-element.254.taps_ref) | copy-start | bytes 147460 | tf_op jit(solution)/shard_map/cond
  182.5 21.3 %copy-start.12 = (f32[8,768]{1,0:T(8,128)}, f32[8,768]{1,0:T(8,128)S(1)}, u32[]{:S(2)}) copy-start(f32[8,768]{1,0:T(8,128)S(1)} %get-tuple-element.255.gain) | copy-start | bytes 73732 | tf_op jit(solution)/shard_map/cond
  182.5 305.2 %copy-start.28 = (s32[32]{0:T(128)}, s32[32]{0:T(128)S(1)}, u32[]{:S(2)}) copy-start(s32[32]{0:T(128)S(1)} %get-tuple-element.247.table_ref) | copy-start | bytes 388 | tf_op jit(solution)/shard_map/cond
  182.5 76.4 %all-to-all-start.14 = ((bf16[8,512,768]{2,1,0:T(8,128)(2,1)}), bf16[8,512,768]{2,1,0:T(8,128)(2,1)}, u32[]{:S(2)}, u32[]{:S(2)}) async-start(bf16[8,512,768]{2,1,0:T(8,128)(2,1)} %get-tuple-element.251), calls=%async_computation.18 | async-start | bytes 12582912 | tf_op jit(solution)/shard_map/cond/branch_1_fun/all_to_all | solution.py:1621
  197.9 5.9 copy-start.2
  343.3 76.6 %all-to-all-start.16 = ((bf16[8,512,768]{2,1,0:T(8,128)(2,1)}), bf16[8,512,768]{2,1,0:T(8,128)(2,1)}, u32[]{:S(2)}, u32[]{:S(2)}) async-start(bf16[8,512,768]{2,1,0:T(8,128)(2,1)} %hop_x.4), calls=%async_computation.20 | async-start | bytes 12582912 | tf_op jit(solution)/shard_map/cond/branch_1_fun/all_to_all | solution.py:1621
  352.9 20.5 %copy-start.43 = (bf16[2,1,768,768]{3,2,1,0:T(8,128)(2,1)S(1)}, bf16[2,1,768,768]{3,2,1,0:T(8,128)(2,1)}, u32[]{:S(2)}) copy-start(bf16[2,1,768,768]{3,2,1,0:T(8,128)(2,1)} %get-tuple-element.258.out_w) | copy-start | bytes 7077892 | tf_op jit(solution)/shard_map/cond
  419.9 76.6 %all-to-all-start.18 = ((bf16[8,512,768]{2,1,0:T(8,128)(2,1)}), bf16[8,512,768]{2,1,0:T(8,128)(2,1)}, u32[]{:S(2)}, u32[]{:S(2)}) async-start(bf16[8,512,768]{2,1,0:T(8,128)(2,1)} %send_cotangent.7), calls=%async_computation.22 | async-start | bytes 12582912 | tf_op jit(solution)/shard_map/cond/branch_1_fun/all_to_all | solution.py:1621
  496.5 76.4 %all-to-all-start.17 = ((bf16[8,512,768]{2,1,0:T(8,128)(2,1)}), bf16[8,512,768]{2,1,0:T(8,128)(2,1)}, u32[]{:S(2)}, u32[]{:S(2)}) async-start(bf16[8,512,768]{2,1,0:T(8,128)(2,1)} %send_cotangent.6), calls=%async_computation.21 | async-start | bytes 12582912 | tf_op jit(solution)/shard_map/cond/branch_1_fun/all_to_all | solution.py:1621
  501.2 381.9 %reduce-scatter.17.cloned.1.call-start = ((), (), s32[]{:S(2)}) async-start(), calls=%async_computation.41 | async-start | bytes 11796480 | tf_op jit(solution)/shard_map/cond/branch_1_fun/reduce_scatter | solution.py:1625
  625.9 84.6 %all-to-all-start.19 = ((bf16[8,512,768]{2,1,0:T(8,128)(2,1)}), bf16[8,512,768]{2,1,0:T(8,128)(2,1)}, u32[]{:S(2)}, u32[]{:S(2)}) async-start(bf16[8,512,768]{2,1,0:T(8,128)(2,1)} %hop_dx.3), calls=%async_computation.23 | async-start | bytes 12582912 | tf_op jit(solution)/shard_map/cond/branch_1_fun/all_to_all | solution.py:1621
  638.9 414.4 %reduce-scatter.21.cloned.1.call-start = ((), (), s32[]{:S(2)}) async-start(), calls=%async_computation.43 | async-start | bytes 10567680 | tf_op jit(solution)/shard_map/cond/branch_1_fun/reduce_scatter | solution.py:1625
  638.9 27.6 %copy-start.35 = (f32[8,768]{1,0:T(8,128)S(1)}, f32[8,768]{1,0:T(8,128)}, u32[]{:S(2)}) copy-start(f32[8,768]{1,0:T(8,128)} %get-tuple-element.344) | copy-start | bytes 73732 | tf_op jit(solution)/shard_map/cond
  638.9 28.5 %copy-start.31 = (f32[8,768]{1,0:T(8,128)S(1)}, f32[8,768]{1,0:T(8,128)}, u32[]{:S(2)}) copy-start(f32[8,768]{1,0:T(8,128)} %get-tuple-element.346) | copy-start | bytes 73732 | tf_op jit(solution)/shard_map/cond
  667.7 31.9 %copy-start.18 = (f32[24,768]{1,0:T(8,128)S(1)}, f32[24,768]{1,0:T(8,128)}, u32[]{:S(2)}) copy-start(f32[24,768]{1,0:T(8,128)} %get-tuple-element.342) | copy-start | bytes 221188 | tf_op jit(solution)/shard_map/cond
  802.1 76.4 %all-to-all-start.21 = ((bf16[8,512,768]{2,1,0:T(8,128)(2,1)}), bf16[8,512,768]{2,1,0:T(8,128)(2,1)}, u32[]{:S(2)}, u32[]{:S(2)}) async-start(bf16[8,512,768]{2,1,0:T(8,128)(2,1)} %hop_dx.5), calls=%async_computation.25 | async-start | bytes 12582912 | tf_op jit(solution)/shard_map/cond/branch_1_fun/all_to_all | solution.py:1621
  806.9 4.7 copy-start.13
  806.9 323.0 %reduce-scatter.19.cloned.1.call-start = ((), (), s32[]{:S(2)}) async-start(), calls=%async_computation.42 | async-start | bytes 11796480 | tf_op jit(solution)/shard_map/cond/branch_1_fun/reduce_scatter | solution.py:1625
  811.6 11.0 copy-start.9
  864.6 18.5 %copy-start.3 = (bf16[4,512,768]{2,1,0:T(8,128)(2,1)S(1)}, bf16[4,512,768]{2,1,0:T(8,128)(2,1)}, u32[]{:S(2)}) copy-start(bf16[4,512,768]{2,1,0:T(8,128)(2,1)} %copy-done.2) | copy-start | bytes 9437188 | tf_op jit(solution)/shard_map/cond
  931.2 21.0 %copy-start.45 = (f32[3,512,128]{2,1,0:T(8,128)S(1)}, f32[3,512,128]{2,1,0:T(8,128)}, u32[]{:S(2)}) copy-start(f32[3,512,128]{2,1,0:T(8,128)} %get-tuple-element.326.rstd_ref) | copy-start | bytes 2359300 | tf_op jit(solution)/shard_map/cond
  931.2 92.6 %all-to-all-start.22 = ((bf16[8,512,768]{2,1,0:T(8,128)(2,1)}), bf16[8,512,768]{2,1,0:T(8,128)(2,1)}, u32[]{:S(2)}, u32[]{:S(2)}) async-start(bf16[8,512,768]{2,1,0:T(8,128)(2,1)} %after.12), calls=%async_computation.26 | async-start | bytes 12582912 | tf_op jit(solution)/shard_map/cond/branch_1_fun/all_to_all | solution.py:1621
  952.2 333.6 %reduce-scatter.23.cloned.1.call-start = ((), (), s32[]{:S(2)}) async-start(), calls=%async_computation.44 | async-start | bytes 10567680 | tf_op jit(solution)/shard_map/cond/branch_1_fun/reduce_scatter | solution.py:1625
  952.2 27.4 %copy-start.36 = (f32[8,768]{1,0:T(8,128)S(1)}, f32[8,768]{1,0:T(8,128)}, u32[]{:S(2)}) copy-start(f32[8,768]{1,0:T(8,128)} %get-tuple-element.350) | copy-start | bytes 73732 | tf_op jit(solution)/shard_map/cond
  952.2 28.3 %copy-start.33 = (f32[8,768]{1,0:T(8,128)S(1)}, f32[8,768]{1,0:T(8,128)}, u32[]{:S(2)}) copy-start(f32[8,768]{1,0:T(8,128)} %get-tuple-element.352) | copy-start | bytes 73732 | tf_op jit(solution)/shard_map/cond
  952.3 28.5 %copy-start.5 = (f32[9,512,128]{2,1,0:T(8,128)S(1)}, f32[9,512,128]{2,1,0:T(8,128)}, u32[]{:S(2)}) copy-start(f32[9,512,128]{2,1,0:T(8,128)} %get-tuple-element.313.rstd_ref) | copy-start | bytes 7077892 | tf_op jit(solution)/shard_map/cond
  980.8 24.6 %copy-start.19 = (f32[24,768]{1,0:T(8,128)S(1)}, f32[24,768]{1,0:T(8,128)}, u32[]{:S(2)}) copy-start(f32[24,768]{1,0:T(8,128)} %get-tuple-element.348) | copy-start | bytes 221188 | tf_op jit(solution)/shard_map/cond
  1023.9 101.1 %all-to-all-start.23 = ((bf16[8,512,768]{2,1,0:T(8,128)(2,1)}), bf16[8,512,768]{2,1,0:T(8,128)(2,1)}, u32[]{:S(2)}, u32[]{:S(2)}) async-start(bf16[8,512,768]{2,1,0:T(8,128)(2,1)} %after.13), calls=%async_computation.27 | async-start | bytes 12582912 | tf_op jit(solution)/shard_map/cond/branch_1_fun/all_to_all | solution.py:1621
  1125.0 76.6 %all-to-all-start.25 = ((bf16[8,512,768]{2,1,0:T(8,128)(2,1)}), bf16[8,512,768]{2,1,0:T(8,128)(2,1)}, u32[]{:S(2)}, u32[]{:S(2)}) async-start(bf16[8,512,768]{2,1,0:T(8,128)(2,1)} %after.15), calls=%async_computation.32 | async-start | bytes 12582912 | tf_op jit(solution)/shard_map/cond/branch_1_fun/all_to_all | solution.py:1621
  1130.0 76.3 %copy-start.16 = (f32[2,8]{1,0:T(2,128)S(1)}, f32[2,8]{1,0:T(2,128)}, u32[]{:S(2)}) copy-start(f32[2,8]{1,0:T(2,128)} %get-tuple-element.353.count_ref) | copy-start | bytes 196 | tf_op jit(solution)/shard_map/cond
  1201.5 76.4 %all-to-all-start.24 = ((bf16[8,512,768]{2,1,0:T(8,128)(2,1)}), bf16[8,512,768]{2,1,0:T(8,128)(2,1)}, u32[]{:S(2)}, u32[]{:S(2)}) async-start(bf16[8,512,768]{2,1,0:T(8,128)(2,1)} %after.14), calls=%async_computation.30 | async-start | bytes 12582912 | tf_op jit(solution)/shard_map/cond/branch_1_fun/all_to_all | solution.py:1621
  1206.3 8.4 copy-start.29
Sparse Core Ops, SparseCore 0:
  621.5 174.0 reduce-scatter.16
  798.5 146.3 reduce-scatter.20
  947.9 170.6 reduce-scatter.18
  1120.8 146.3 reduce-scatter.22
